TPU v7x, 32 devices: a whole 2x2x4 slice. The times are simulated.
32 devices in a mesh: mem: 8 (over y, x, core), lat: 4 (over z).
Axes of the slice: x: 2, y: 2, z: 4, core: 2. Of those that a mesh axis runs over, the one named last changes fastest.
Arguments:
- members: bfloat16 [80, 2, 4, 32, 1152], P('mem', None, None, 'lat'), may hold values from -0.625 to 0.625
- alpha: float32 [80, 4, 32, 1152], P('mem', None, 'lat'), may hold values from -6 to 6
- zonal_loc: bfloat16 [1152, 1152], replicated
- merid_coef: float32 [32, 9], replicated, may hold values from 0.1 to 0.6
- slot_tile: int32 [4, 8, 3], P('lat', 'mem'), may hold values from 0 to 17, as said below
- obs_count: int32 [4, 8, 3], P('lat', 'mem'), may hold values from 0 to 4096, as said below
- obs_index: int32 [4, 8, 3, 4096], P('lat', 'mem'), may hold values from 0 to 16383
- obs_value: float32 [4, 8, 3, 4096], P('lat', 'mem'), may hold values from -6 to 6
- obs_weight: float32 [4, 8, 3, 4096], P('lat', 'mem'), may hold values from 0.5 to 4
Outputs:
- analysis_alpha: float32 [80, 4, 32, 1152], P('mem', None, 'lat')
Inputs may be any that keep to these rules, and one draw needn't show every extreme that they name: `slot_tile`: within each band every tile 0..17 stands in exactly one slot; a device owns at most 3 tiles of a band, and in every band one device owns exactly 3. Unused slots hold tile 0. `obs_count`: zero exactly in unused slots; a used slot holds 4096, 2048 or 1024 live observations, and each band has a slot with 4096.
All inputs are finite; a program needn't handle non-finite values.
Results may differ from a plain program's by a relative error of at most 0.00065.
Values may be sent and summed in bfloat16 or wider, within the bound.
No kernel may reach another device: no remote copies, remote signals or barrier semaphores. Data moves between devices by JAX's collectives and lax.ppermute only.
A program may use at most 64 MiB of HBM per device.

v0:
```python
import jax
import jax.numpy as jnp
from jax import lax
from jax.sharding import PartitionSpec as P

TLON = 128
ITERS = 2


step_size = 0.3


def padded_2(cells, sides, width):
    for axis, dim in sides:
        count = lax.axis_size(axis)
        ends = count - 1
        head = lax.slice_in_dim(cells, 0, width, axis=dim)
        tail = lax.slice_in_dim(cells, cells.shape[dim] - width, cells.shape[dim], axis=dim)
        cells = jnp.concatenate(
            [
                lax.ppermute(tail, axis, [(i, (i + 1) % count) for i in range(ends)]),
                cells,
                lax.ppermute(head, axis, [((i + 1) % count, i) for i in range(ends)]),
            ],
            axis=dim,
        )
    return cells


def meridional(field_pad, coeffs, row_count, half_band):
    running = jnp.zeros(field_pad.shape[:2] + (row_count, field_pad.shape[3]), jnp.float32)
    for offset in range(-half_band, half_band + 1):
        running = (
            running
            + coeffs[:, offset + half_band][None, None, :, None]
            * field_pad[:, :, half_band + offset : half_band + offset + row_count]
        )
    return running


def meridional_back(back_pad, coeffs, row_count, half_band):
    running = jnp.zeros(back_pad.shape[:2] + (row_count, back_pad.shape[3]), jnp.float32)
    for offset in range(-half_band, half_band + 1):
        running = (
            running
            + coeffs[half_band - offset : half_band - offset + row_count, offset + half_band][
                None, None, :, None
            ]
            * back_pad[:, :, half_band - offset : half_band - offset + row_count]
        )
    return running


def fine_tile(coarse):
    inner_rows = coarse.shape[2] - 2
    tile_half = coarse.shape[3] - 1
    even_rows = 0.75 * coarse[:, :, 1:-1] + 0.25 * coarse[:, :, :-2]
    odd_rows = 0.75 * coarse[:, :, 1:-1] + 0.25 * coarse[:, :, 2:]
    merid = jnp.stack([even_rows, odd_rows], axis=3).reshape(
        coarse.shape[0], coarse.shape[1], 2 * inner_rows, coarse.shape[3]
    )
    even_cols = merid[..., :tile_half]
    odd_cols = 0.5 * (merid[..., :tile_half] + merid[..., 1 : tile_half + 1])
    return jnp.stack([even_cols, odd_cols], axis=-1).reshape(
        merid.shape[0], merid.shape[1], merid.shape[2], 2 * tile_half
    )


def tile_windows(field_in, tile_half):
    tile_count = field_in.shape[3] // tile_half
    pieces = field_in.reshape(
        field_in.shape[0], field_in.shape[1], field_in.shape[2], tile_count, tile_half
    )
    following = jnp.roll(pieces[..., :1], -1, axis=3)
    joined = jnp.concatenate([pieces, following], axis=4)
    return joined.transpose(3, 0, 1, 2, 4)


def clamp_poles(field_in, band_index, band_count):
    lower_row = jnp.where(band_index == 0, field_in[:, :, 1], field_in[:, :, 0])
    upper_row = jnp.where(band_index == band_count - 1, field_in[:, :, -2], field_in[:, :, -1])
    return jnp.concatenate(
        [lower_row[:, :, None], field_in[:, :, 1:-1], upper_row[:, :, None]], axis=2
    )


def clamp_back(field_in, band_index, band_count):
    at_south = band_index == 0
    at_north = band_index == band_count - 1
    first_row = jnp.where(at_south, field_in[:, :, 1] + field_in[:, :, 0], field_in[:, :, 1])
    lower_row = jnp.where(at_south, jnp.float32(0.0), field_in[:, :, 0])
    last_row = jnp.where(at_north, field_in[:, :, -2] + field_in[:, :, -1], field_in[:, :, -2])
    upper_row = jnp.where(at_north, jnp.float32(0.0), field_in[:, :, -1])
    return jnp.concatenate(
        [
            lower_row[:, :, None],
            first_row[:, :, None],
            field_in[:, :, 2:-2],
            last_row[:, :, None],
            upper_row[:, :, None],
        ],
        axis=2,
    )


def add_arrived(interior, arrived):
    interior = interior.at[:, :, 0].add(arrived[:, :, 0])
    return interior.at[:, :, -1].add(arrived[:, :, 3])


def body(
    members, alpha, zonal_loc, merid_coef, slot_tile, obs_count, obs_index, obs_value, obs_weight
):
    half_band = merid_coef.shape[1] // 2
    band_rows = alpha.shape[2]
    lon_cells = alpha.shape[3]
    band_index = lax.axis_index("lat")
    band_count = lax.axis_size("lat")
    member_groups = lax.axis_size("mem")
    coef_wide = jnp.pad(merid_coef, ((half_band + 1, half_band + 1), (0, 0)))
    rim_rows = 0
    wide_rows = band_rows + 2 * rim_rows
    forward_coef = lax.dynamic_slice_in_dim(
        coef_wide, band_index * band_rows - rim_rows + half_band + 1, wide_rows, 0
    )
    adjoint_coef = lax.dynamic_slice_in_dim(
        coef_wide, band_index * band_rows + 1, band_rows + 2 * half_band, 0
    )
    tile_half = TLON // 2
    tile_ids = slot_tile.reshape(-1)
    live_counts = obs_count.reshape(-1)
    slot_count = tile_ids.shape[0]
    obs_points = obs_index.reshape(slot_count, -1)
    values = obs_value.reshape(slot_count, -1)
    weights = obs_weight.reshape(slot_count, -1)
    slot_obs = obs_points.shape[1]
    owner_table = lax.all_gather(slot_tile, "mem", axis=1, tiled=True).reshape(-1)
    current = alpha
    for iteration in range(ITERS):
        padded = padded_2(current, (("lat", 2),), half_band)
        spread = meridional(padded, forward_coef, wide_rows, half_band).astype(jnp.bfloat16)
        zonal_out = jnp.dot(
            spread.reshape(-1, lon_cells), zonal_loc, preferred_element_type=jnp.float32
        ).reshape(spread.shape)
        partial_value = jnp.sum(members * zonal_out[:, None], axis=0)
        partial_value = padded_2(partial_value, (("lat", 2),), 1)
        chosen = jnp.take(tile_windows(partial_value, tile_half), owner_table, axis=0)
        chosen = chosen.reshape((member_groups, slot_count) + chosen.shape[1:])
        own_windows = lax.psum_scatter(chosen, "mem", scatter_dimension=0, tiled=True)[0]
        adjoint_acc = jnp.zeros(partial_value.shape[:3] + (lon_cells + 1,), jnp.float32)
        for slot_index in range(slot_count):
            col_start = tile_ids[slot_index] * tile_half
            coarse = clamp_poles(own_windows[slot_index], band_index, band_count)
            fine_field, pullback = jax.vjp(fine_tile, coarse)
            flat_tile = fine_field.reshape(-1)
            active = jnp.arange(slot_obs, dtype=jnp.int32) < live_counts[slot_index]
            residual = jnp.where(
                active,
                weights[slot_index] * (flat_tile[obs_points[slot_index]] - values[slot_index]),
                jnp.float32(0.0),
            )
            fine_grad = (
                jnp.zeros(flat_tile.shape, jnp.float32).at[obs_points[slot_index]].add(residual)
            )
            (coarse_grad,) = pullback(fine_grad.reshape(fine_field.shape))
            window = lax.dynamic_slice_in_dim(adjoint_acc, col_start, tile_half + 1, 3)
            adjoint_acc = lax.dynamic_update_slice_in_dim(
                adjoint_acc, window + coarse_grad, col_start, 3
            )
        folded = adjoint_acc[..., :lon_cells].at[..., 0].add(adjoint_acc[..., lon_cells])
        folded = clamp_back(folded, band_index, band_count)
        summed_back = lax.psum(folded, "mem")
        edge_rows = jnp.stack([summed_back[:, :, 0], summed_back[:, :, -1]], axis=2)
        arrived = padded_2(edge_rows, (("lat", 2),), 1)
        adjoint = add_arrived(summed_back[:, :, 1:-1], arrived)
        weighted = jnp.sum(members * adjoint[None], axis=1).astype(jnp.bfloat16)
        zonal_back = lax.dot_general(
            weighted.reshape(-1, lon_cells),
            zonal_loc,
            (((1,), (1,)), ((), ())),
            preferred_element_type=jnp.float32,
        ).reshape(weighted.shape)
        back_pad = padded_2(zonal_back, (("lat", 2),), half_band)
        gradient = current + meridional_back(back_pad, adjoint_coef, band_rows, half_band)
        current = current - step_size * gradient
    return current


def solution(mesh):
    in_specs = (
        P("mem", None, None, "lat", None),
        P("mem", None, "lat", None),
        P(),
        P(),
        P("lat", "mem", None),
        P("lat", "mem", None),
        P("lat", "mem", None, None),
        P("lat", "mem", None, None),
        P("lat", "mem", None, None),
    )
    out_specs = P("mem", None, "lat", None)
    return jax.shard_map(body, mesh=mesh, in_specs=in_specs, out_specs=out_specs, check_vma=False)
```

profile of v0, /device:TPU:0, one launch (start us, length us, event | category | flops | bytes accessed | tf_op | source)
XLA Modules:
  0.0 800.2 jit_solution(3041865562264348950)
XLA Ops:
  6.6 3.1 fusion.176
  11.0 6.4 collective-permute-start
  18.0 9.2 %all_gather.3 = s32[1,8,3]{2,0,1:T(1,128)S(1)} all-gather(s32[1,1,3]{2,0,1:T(1,128)S(1)} %bitcast.273), channel_id=1, replica_groups=mesh['mem'=8,'lat'=4] {'mem'}, dimensions={1}, use_global_device_ids=true | all-gather | bytes 108 | tf_op jit(solution)/shard_map/all_gather | solution.py:137
  37.1 5.4 fusion.16
  42.9 2.6 collective-permute-start.2
  49.9 2.0 collective-permute-done.3
  56.0 2.2 gather_fusion.6
  61.2 37.8 %reduce-scatter.3.cloned.1.call-done = f32[1,3,2,4,10,65]{5,4,3,2,1,0:T(8,128)} async-done(((f32[8,3,2,4,10,65]{5,4,3,2,1,0:T(8,128)}), f32[1,3,2,4,10,65]{5,4,3,2,1,0:T(8,128)}) %reduce-scatter.3.cloned.1.call-update) | async-done | bytes 62416 | tf_op jit(solution)/shard_map/reduce_scatter | solution.py:149
  100.2 2.8 copy.169
  102.9 4.0 reshape.530
  107.0 23.0 %gather_fusion.2 = f32[4096]{0:T(1024)S(1)} fusion(f32[16384]{0:T(1024)S(1)} %reshape.530, s32[4096]{0:T(1024)S(1)} %copy-done.11), kind=kCustom, calls=%fused_computation.4 | custom fusion | bytes 49152 | tf_op jit(solution)/shard_map/gather | solution.py:159
  130.7 22.5 %scatter_custom_fusion.2 = f32[16384]{0:T(1024)S(1)} fusion(s32[4096]{0:T(1024)} %bitcast.271, f32[4096]{0:T(1024)S(1)} %multiply_select_fusion.3, f32[]{:T(128)} %constant.179.clone.1), kind=kCustom, calls=%fused_computation.344 | custom fusion | flops 4096 | bytes 66048 | tf_op jit(solution)/shard_map/scatter-add | solution.py:163
  153.3 5.6 reshape_reshape.20
  158.8 6.8 fusion.3
  167.3 2.7 copy.165
  170.0 4.0 reshape.527
  174.0 23.0 %gather_fusion.1 = f32[4096]{0:T(1024)S(1)} fusion(f32[16384]{0:T(1024)S(1)} %reshape.527, s32[4096]{0:T(1024)S(1)} %copy-done.10), kind=kCustom, calls=%fused_computation.3 | custom fusion | bytes 49152 | tf_op jit(solution)/shard_map/gather | solution.py:159
  197.7 22.2 %scatter_custom_fusion.1 = f32[16384]{0:T(1024)S(1)} fusion(s32[4096]{0:T(1024)} %bitcast.268, f32[4096]{0:T(1024)S(1)} %multiply_select_fusion.4, f32[]{:T(128)} %constant.179.clone.1), kind=kCustom, calls=%fused_computation.346 | custom fusion | flops 4096 | bytes 66048 | tf_op jit(solution)/shard_map/scatter-add | solution.py:163
  220.0 5.5 reshape_reshape.19
  225.5 6.8 fusion.4
  233.9 2.7 copy.160
  236.7 4.0 reshape.524
  240.7 23.0 %gather_fusion = f32[4096]{0:T(1024)S(1)} fusion(f32[16384]{0:T(1024)S(1)} %reshape.524, s32[4096]{0:T(1024)S(1)} %copy-done.9), kind=kCustom, calls=%fused_computation.2 | custom fusion | bytes 49152 | tf_op jit(solution)/shard_map/gather | solution.py:159
  264.3 22.3 %scatter_custom_fusion = f32[16384]{0:T(1024)S(1)} fusion(s32[4096]{0:T(1024)} %bitcast.265, f32[4096]{0:T(1024)S(1)} %multiply_select_fusion.5, f32[]{:T(128)} %constant.179.clone.1), kind=kCustom, calls=%fused_computation.348 | custom fusion | flops 4096 | bytes 66048 | tf_op jit(solution)/shard_map/scatter-add | solution.py:163
  286.6 5.5 reshape_reshape.18
  292.2 6.8 fusion.5
  309.8 56.3 %all-reduce.46.cloned.1.call-done = f32[2,4,10,1152]{3,2,1,0:T(8,128)} async-done(((f32[2,4,10,1152]{3,2,1,0:T(8,128)}), f32[2,4,10,1152]{3,2,1,0:T(8,128)}) %all-reduce.46.cloned.1.call-update) | async-done | bytes 368656 | tf_op jit(solution)/shard_map/psum | solution.py:172
  367.2 3.3 collective-permute-start.4
  374.1 2.3 collective-permute-done.5
  382.4 5.4 collective-permute-start.7
  388.1 11.0 %collective-permute-done.6 = f32[10,4,4,1152]{3,2,1,0:T(4,128)S(1)} collective-permute-done((f32[10,4,4,1152]{3,2,1,0:T(4,128)}, f32[10,4,4,1152]{3,2,1,0:T(4,128)S(1)}, u32[]{:S(2)}, u32[]{:S(2)}) %collective-permute-start.6) | collective-permute-done | bytes 737312 | tf_op jit(solution)/shard_map/ppermute | solution.py:23
  400.4 10.8 %fusion.68 = f32[10,4,8,1152]{3,2,1,0:T(8,128)S(1)} fusion(f32[10,4,8,1152]{3,2,1,0:T(8,128)} %param.24, f32[10,4,8,1152]{3,2,1,0:T(8,128)} %copy-done.6, f32[10,4,4,1152]{3,2,1,0:T(4,128)} %collective-permute-done.7, f32[10,4,4,1152]{3,2,1,0:T(4,128)S(1)} %collective-permute-done.6, f32[8]{0:T(128)S(1)} %get-tuple-element.217, ...), kind=kLoop, calls=%fused_computation.140 | loop fusion | flops 10321920 | bytes 5898528 | tf_op jit(solution)/shard_map/sub | solution.py:185
  411.5 4.4 collective-permute-start.8
  417.8 10.3 %collective-permute-done.8 = f32[10,4,4,1152]{3,2,1,0:T(4,128)S(1)} collective-permute-done((f32[10,4,4,1152]{3,2,1,0:T(4,128)S(1)}, f32[10,4,4,1152]{3,2,1,0:T(4,128)S(1)}, u32[]{:S(2)}, u32[]{:S(2)}) %collective-permute-start.8) | collective-permute-done | bytes 737312 | tf_op jit(solution)/shard_map/ppermute | solution.py:21
  428.1 4.3 collective-permute-done.9
  432.5 3.7 fusion.12
  436.5 3.4 collective-permute-start.10
  441.5 4.2 collective-permute-done.11
  449.1 2.2 gather_fusion.7
  454.2 36.3 %reduce-scatter.5.cloned.1.call-done = f32[1,3,2,4,10,65]{5,4,3,2,1,0:T(8,128)} async-done(((f32[8,3,2,4,10,65]{5,4,3,2,1,0:T(8,128)}), f32[1,3,2,4,10,65]{5,4,3,2,1,0:T(8,128)}) %reduce-scatter.5.cloned.1.call-update) | async-done | bytes 62416 | tf_op jit(solution)/shard_map/reduce_scatter | solution.py:149
  491.8 2.8 copy.186
  494.5 4.0 reshape.541
  498.5 23.0 %gather_fusion.5 = f32[4096]{0:T(1024)S(1)} fusion(f32[16384]{0:T(1024)S(1)} %reshape.541, s32[4096]{0:T(1024)S(1)} %copy-done.11), kind=kCustom, calls=%fused_computation.7 | custom fusion | bytes 49152 | tf_op jit(solution)/shard_map/gather | solution.py:159
  522.2 22.2 %scatter_custom_fusion.5 = f32[16384]{0:T(1024)S(1)} fusion(s32[4096]{0:T(1024)} %bitcast.272, f32[4096]{0:T(1024)S(1)} %multiply_select_fusion, f32[]{:T(128)} %constant.179.clone.1), kind=kCustom, calls=%fused_computation.338 | custom fusion | flops 4096 | bytes 66048 | tf_op jit(solution)/shard_map/scatter-add | solution.py:163
  544.5 5.6 reshape_reshape.23
  550.1 6.8 fusion
  558.5 2.8 copy.182
  561.2 4.0 reshape.538
  565.2 23.0 %gather_fusion.4 = f32[4096]{0:T(1024)S(1)} fusion(f32[16384]{0:T(1024)S(1)} %reshape.538, s32[4096]{0:T(1024)S(1)} %copy-done.10), kind=kCustom, calls=%fused_computation.6 | custom fusion | bytes 49152 | tf_op jit(solution)/shard_map/gather | solution.py:159
  588.9 22.3 %scatter_custom_fusion.4 = f32[16384]{0:T(1024)S(1)} fusion(s32[4096]{0:T(1024)} %bitcast.269, f32[4096]{0:T(1024)S(1)} %multiply_select_fusion.1, f32[]{:T(128)} %constant.179.clone.1), kind=kCustom, calls=%fused_computation.340 | custom fusion | flops 4096 | bytes 66048 | tf_op jit(solution)/shard_map/scatter-add | solution.py:163
  611.2 5.6 reshape_reshape.22
  616.8 6.8 fusion.1
  625.2 2.8 copy.178
  627.9 4.0 reshape.535
  632.0 23.0 %gather_fusion.3 = f32[4096]{0:T(1024)S(1)} fusion(f32[16384]{0:T(1024)S(1)} %reshape.535, s32[4096]{0:T(1024)S(1)} %copy-done.9), kind=kCustom, calls=%fused_computation.5 | custom fusion | bytes 49152 | tf_op jit(solution)/shard_map/gather | solution.py:159
  655.6 22.3 %scatter_custom_fusion.3 = f32[16384]{0:T(1024)S(1)} fusion(s32[4096]{0:T(1024)} %bitcast.266, f32[4096]{0:T(1024)S(1)} %multiply_select_fusion.2, f32[]{:T(128)} %constant.179.clone.1), kind=kCustom, calls=%fused_computation.342 | custom fusion | flops 4096 | bytes 66048 | tf_op jit(solution)/shard_map/scatter-add | solution.py:163
  677.9 5.6 reshape_reshape.21
  683.5 6.8 fusion.2
  700.3 56.2 %all-reduce.48.cloned.1.call-done = f32[2,4,10,1152]{3,2,1,0:T(8,128)} async-done(((f32[2,4,10,1152]{3,2,1,0:T(8,128)}), f32[2,4,10,1152]{3,2,1,0:T(8,128)}) %all-reduce.48.cloned.1.call-update) | async-done | bytes 368656 | tf_op jit(solution)/shard_map/psum | solution.py:172
  757.6 3.3 collective-permute-start.12
  764.5 2.3 collective-permute-done.13
  771.7 4.6 collective-permute-start.15
  776.3 11.8 %collective-permute-done.14 = f32[10,4,4,1152]{3,2,1,0:T(4,128)S(1)} collective-permute-done((f32[10,4,4,1152]{3,2,1,0:T(4,128)S(1)}, f32[10,4,4,1152]{3,2,1,0:T(4,128)S(1)}, u32[]{:S(2)}, u32[]{:S(2)}) %collective-permute-start.14) | collective-permute-done | bytes 737312 | tf_op jit(solution)/shard_map/ppermute | solution.py:23
  789.5 3.8 fusion.24
  (313 shorter events, 87.6 us)
Async XLA Ops:
  6.5 30.5 %copy-start = (bf16[1152,1152]{1,0:T(8,128)(2,1)S(1)}, bf16[1152,1152]{1,0:T(8,128)(2,1)}, u32[]{:S(2)}) copy-start(bf16[1152,1152]{1,0:T(8,128)(2,1)} %param.25) | copy-start | bytes 7962628
  6.5 10.9 %copy-start.26 = (s32[1,1,3]{2,1,0:T(1,128)S(1)}, s32[1,1,3]{2,1,0:T(1,128)}, u32[]{:S(2)}) copy-start(s32[1,1,3]{2,1,0:T(1,128)} %param.27) | copy-start | bytes 40
  6.5 21.9 %copy-start.22 = (s32[1,1,3,4096]{3,1,2,0:T(1,128)S(1)}, s32[1,1,3,4096]{3,1,2,0:T(1,128)}, u32[]{:S(2)}) copy-start(s32[1,1,3,4096]{3,1,2,0:T(1,128)} %param.29) | copy-start | bytes 147460
  6.5 23.2 %copy-start.23 = (f32[1,1,3,4096]{3,1,2,0:T(1,128)S(1)}, f32[1,1,3,4096]{3,1,2,0:T(1,128)}, u32[]{:S(2)}) copy-start(f32[1,1,3,4096]{3,1,2,0:T(1,128)} %param.31) | copy-start | bytes 147460
  6.5 23.8 %copy-start.27 = (s32[1,1,3]{2,1,0:T(1,128)S(1)}, s32[1,1,3]{2,1,0:T(1,128)}, u32[]{:S(2)}) copy-start(s32[1,1,3]{2,1,0:T(1,128)} %param.28) | copy-start | bytes 40
  6.5 25.6 %copy-start.12 = (f32[32,9]{0,1:T(8,128)S(1)}, f32[32,9]{0,1:T(8,128)}, u32[]{:S(2)}) copy-start(f32[32,9]{0,1:T(8,128)} %param.26) | copy-start | bytes 3460
  6.6 92.4 %reduce-scatter.3.cloned.1.call-start = ((), (), s32[]{:S(2)}) async-start(), calls=%async_computation.2 | async-start | bytes 1769472 | tf_op jit(solution)/shard_map/reduce_scatter | solution.py:149
  9.7 25.8 %collective-permute-start.1 = (f32[10,4,4,1152]{3,2,1,0:T(4,128)}, f32[10,4,4,1152]{3,2,1,0:T(4,128)}, u32[]{:S(2)}, u32[]{:S(2)}) collective-permute-start(f32[10,4,4,1152]{3,2,1,0:T(4,128)} %get-tuple-element.96), channel_id=1, source_target_pairs={{1,0},{2,1},{3,2},{5,4},{6,5},{7,6},{9,8},{10,9},{11,10},{13,12},{... | collective-permute-start | bytes 2211848 | tf_op jit(solution)/shard_map/ppermute | solution.py:23
  11.0 25.9 %collective-permute-start = (f32[10,4,4,1152]{3,2,1,0:T(4,128)S(1)}, f32[10,4,4,1152]{3,2,1,0:T(4,128)}, u32[]{:S(2)}, u32[]{:S(2)}) collective-permute-start(f32[10,4,4,1152]{3,2,1,0:T(4,128)S(1)} %get-tuple-element.97), channel_id=1, source_target_pairs={{0,1},{1,2},{2,3},{4,5},{5,6},{6,7},{8,9},{9,10},{10,11},{12,13},{... | collective-permute-start | bytes 2211848 | tf_op jit(solution)/shard_map/ppermute | solution.py:21
  28.5 6.9 copy-start.19
  28.5 6.9 copy-start.20
  32.8 4.2 copy-start.54
  32.8 4.2 copy-start.56
  37.1 5.4 copy-start.1
  42.9 6.3 collective-permute-start.2
  45.5 6.4 collective-permute-start.3
  61.1 305.0 %all-reduce.46.cloned.1.call-start = ((), (), s32[]{:S(2)}) async-start(), calls=%async_computation.3 | async-start | bytes 1179648 | tf_op jit(solution)/shard_map/psum | solution.py:172
  107.0 23.1 %copy-start.8 = (f32[1,1,1,4096]{3,1,2,0:T(1,128)S(1)}, f32[1,1,1,4096]{3,1,2,0:T(1,128)}, u32[]{:S(2)}) copy-start(f32[1,1,1,4096]{3,1,2,0:T(1,128)} %get-tuple-element.160) | copy-start | bytes 49156
  174.0 23.1 %copy-start.7 = (f32[1,1,1,4096]{3,1,2,0:T(1,128)S(1)}, f32[1,1,1,4096]{3,1,2,0:T(1,128)}, u32[]{:S(2)}) copy-start(f32[1,1,1,4096]{3,1,2,0:T(1,128)} %get-tuple-element.162) | copy-start | bytes 49156
  309.8 180.7 %reduce-scatter.5.cloned.1.call-start = ((), (), s32[]{:S(2)}) async-start(), calls=%async_computation.4 | async-start | bytes 1769472 | tf_op jit(solution)/shard_map/reduce_scatter | solution.py:149
  367.2 5.7 collective-permute-start.4
  370.5 5.9 collective-permute-start.5
  379.5 8.3 %copy-start.13 = (f32[32,9]{0,1:T(8,128)S(1)}, f32[32,9]{0,1:T(8,128)}, u32[]{:S(2)}) copy-start(f32[32,9]{0,1:T(8,128)} %param.26) | copy-start | bytes 3460
  379.5 20.8 %copy-start.28 = (f32[8]{0:T(128)S(1)}, f32[8]{0:T(128)}, u32[]{:S(2)}) copy-start(f32[8]{0:T(128)} %get-tuple-element.200) | copy-start | bytes 100
  379.5 20.8 %copy-start.30 = (f32[8]{0:T(128)S(1)}, f32[8]{0:T(128)}, u32[]{:S(2)}) copy-start(f32[8]{0:T(128)} %get-tuple-element.206) | copy-start | bytes 100
  381.1 17.9 %collective-permute-start.6 = (f32[10,4,4,1152]{3,2,1,0:T(4,128)}, f32[10,4,4,1152]{3,2,1,0:T(4,128)S(1)}, u32[]{:S(2)}, u32[]{:S(2)}) collective-permute-start(f32[10,4,4,1152]{3,2,1,0:T(4,128)} %get-tuple-element.94), channel_id=1, source_target_pairs={{1,0},{2,1},{3,2},{5,4},{6,5},{7,6},{9,8},{10,9},{11,10},{13,12},{... | collective-permute-start | bytes 2211848 | tf_op jit(solution)/shard_map/ppermute | solution.py:23
  382.4 17.9 %collective-permute-start.7 = (f32[10,4,4,1152]{3,2,1,0:T(4,128)}, f32[10,4,4,1152]{3,2,1,0:T(4,128)}, u32[]{:S(2)}, u32[]{:S(2)}) collective-permute-start(f32[10,4,4,1152]{3,2,1,0:T(4,128)} %get-tuple-element.95), channel_id=1, source_target_pairs={{0,1},{1,2},{2,3},{4,5},{5,6},{6,7},{8,9},{9,10},{10,11},{12,13},{... | collective-permute-start | bytes 2211848 | tf_op jit(solution)/shard_map/ppermute | solution.py:21
  387.9 23.2 %copy-start.32 = (f32[8]{0:T(128)}, f32[8]{0:T(128)S(1)}, u32[]{:S(2)}) copy-start(f32[8]{0:T(128)S(1)} %get-tuple-element.215) | copy-start | bytes 100
  387.9 23.2 %copy-start.34 = (f32[8]{0:T(128)}, f32[8]{0:T(128)S(1)}, u32[]{:S(2)}) copy-start(f32[8]{0:T(128)S(1)} %get-tuple-element.216) | copy-start | bytes 100
  387.9 23.2 %copy-start.36 = (f32[8]{0:T(128)}, f32[8]{0:T(128)S(1)}, u32[]{:S(2)}) copy-start(f32[8]{0:T(128)S(1)} %get-tuple-element.217) | copy-start | bytes 100
  388.1 23.1 %copy-start.38 = (f32[8]{0:T(128)}, f32[8]{0:T(128)S(1)}, u32[]{:S(2)}) copy-start(f32[8]{0:T(128)S(1)} %get-tuple-element.211) | copy-start | bytes 100
  388.1 23.1 %copy-start.40 = (f32[8]{0:T(128)}, f32[8]{0:T(128)S(1)}, u32[]{:S(2)}) copy-start(f32[8]{0:T(128)S(1)} %get-tuple-element.212) | copy-start | bytes 100
  388.1 23.1 %copy-start.42 = (f32[8]{0:T(128)}, f32[8]{0:T(128)S(1)}, u32[]{:S(2)}) copy-start(f32[8]{0:T(128)S(1)} %get-tuple-element.213) | copy-start | bytes 100
  388.1 23.1 %copy-start.44 = (f32[8]{0:T(128)}, f32[8]{0:T(128)S(1)}, u32[]{:S(2)}) copy-start(f32[8]{0:T(128)S(1)} %get-tuple-element.214) | copy-start | bytes 100
  411.2 21.2 %copy-start.4 = (f32[10,4,8,1152]{3,2,1,0:T(8,128)}, f32[10,4,8,1152]{3,2,1,0:T(8,128)S(1)}, u32[]{:S(2)}) copy-start(f32[10,4,8,1152]{3,2,1,0:T(8,128)S(1)} %fusion.68) | copy-start | bytes 4423684
  411.2 21.2 %copy-start.49 = (f32[8]{0:T(128)S(1)}, f32[8]{0:T(128)}, u32[]{:S(2)}) copy-start(f32[8]{0:T(128)} %copy-done.48) | copy-start | bytes 100
  411.2 21.2 %copy-start.51 = (f32[8]{0:T(128)S(1)}, f32[8]{0:T(128)}, u32[]{:S(2)}) copy-start(f32[8]{0:T(128)} %copy-done.50) | copy-start | bytes 100
  411.2 21.2 %copy-start.53 = (f32[8]{0:T(128)S(1)}, f32[8]{0:T(128)}, u32[]{:S(2)}) copy-start(f32[8]{0:T(128)} %copy-done.52) | copy-start | bytes 100
  411.3 21.2 %copy-start.55 = (f32[8]{0:T(128)S(1)}, f32[8]{0:T(128)}, u32[]{:S(2)}) copy-start(f32[8]{0:T(128)} %copy-done.54) | copy-start | bytes 100
  411.3 21.2 %copy-start.57 = (f32[8]{0:T(128)S(1)}, f32[8]{0:T(128)}, u32[]{:S(2)}) copy-start(f32[8]{0:T(128)} %copy-done.56) | copy-start | bytes 100
  411.3 21.2 %copy-start.59 = (f32[8]{0:T(128)S(1)}, f32[8]{0:T(128)}, u32[]{:S(2)}) copy-start(f32[8]{0:T(128)} %copy-done.58) | copy-start | bytes 100
  411.3 21.2 %copy-start.61 = (f32[8]{0:T(128)S(1)}, f32[8]{0:T(128)}, u32[]{:S(2)}) copy-start(f32[8]{0:T(128)} %copy-done.60) | copy-start | bytes 100
  411.3 21.2 %copy-start.63 = (f32[8]{0:T(128)S(1)}, f32[8]{0:T(128)}, u32[]{:S(2)}) copy-start(f32[8]{0:T(128)} %copy-done.62) | copy-start | bytes 100
  411.3 21.2 %copy-start.65 = (f32[8]{0:T(128)S(1)}, f32[8]{0:T(128)}, u32[]{:S(2)}) copy-start(f32[8]{0:T(128)} %copy-done.64) | copy-start | bytes 100
  411.5 16.5 %collective-permute-start.8 = (f32[10,4,4,1152]{3,2,1,0:T(4,128)S(1)}, f32[10,4,4,1152]{3,2,1,0:T(4,128)S(1)}, u32[]{:S(2)}, u32[]{:S(2)}) collective-permute-start(f32[10,4,4,1152]{3,2,1,0:T(4,128)S(1)} %get-tuple-element.92), channel_id=1, source_target_pairs={{0,1},{1,2},{2,3},{4,5},{5,6},{6,7},{8,9},{9,10},{10,11},{12,13},{... | collective-permute-start | bytes 2211848 | tf_op jit(solution)/shard_map/ppermute | solution.py:21
  416.0 20.2 %copy-start.2 = (bf16[10,2,4,8,1152]{4,3,2,1,0:T(8,128)(2,1)S(1)}, bf16[10,2,4,8,1152]{4,3,2,1,0:T(8,128)(2,1)}, u32[]{:S(2)}) copy-start(bf16[10,2,4,8,1152]{4,3,2,1,0:T(8,128)(2,1)} %param.23) | copy-start | bytes 4423684
  416.0 16.4 %collective-permute-start.9 = (f32[10,4,4,1152]{3,2,1,0:T(4,128)S(1)}, f32[10,4,4,1152]{3,2,1,0:T(4,128)S(1)}, u32[]{:S(2)}, u32[]{:S(2)}) collective-permute-start(f32[10,4,4,1152]{3,2,1,0:T(4,128)S(1)} %get-tuple-element.93), channel_id=1, source_target_pairs={{1,0},{2,1},{3,2},{5,4},{6,5},{7,6},{9,8},{10,9},{11,10},{13,12},{... | collective-permute-start | bytes 2211848 | tf_op jit(solution)/shard_map/ppermute | solution.py:23
  436.5 5.0 collective-permute-start.10
  439.9 5.9 collective-permute-start.11
  454.1 302.4 %all-reduce.48.cloned.1.call-start = ((), (), s32[]{:S(2)}) async-start(), calls=%async_computation.5 | async-start | bytes 1179648 | tf_op jit(solution)/shard_map/psum | solution.py:172
  757.6 5.7 collective-permute-start.12
  760.9 5.9 collective-permute-start.13
  770.0 19.4 %copy-start.5 = (f32[10,4,8,1152]{3,2,1,0:T(8,128)S(1)}, f32[10,4,8,1152]{3,2,1,0:T(8,128)}, u32[]{:S(2)}) copy-start(f32[10,4,8,1152]{3,2,1,0:T(8,128)} %copy-done.4) | copy-start | bytes 4423684
  770.0 19.4 %copy-start.29 = (f32[8]{0:T(128)S(1)}, f32[8]{0:T(128)}, u32[]{:S(2)}) copy-start(f32[8]{0:T(128)} %get-tuple-element.200) | copy-start | bytes 100
  770.0 19.4 %copy-start.31 = (f32[8]{0:T(128)S(1)}, f32[8]{0:T(128)}, u32[]{:S(2)}) copy-start(f32[8]{0:T(128)} %get-tuple-element.206) | copy-start | bytes 100
  770.0 19.4 %copy-start.33 = (f32[8]{0:T(128)S(1)}, f32[8]{0:T(128)}, u32[]{:S(2)}) copy-start(f32[8]{0:T(128)} %copy-done.32) | copy-start | bytes 100
  770.0 19.4 %copy-start.35 = (f32[8]{0:T(128)S(1)}, f32[8]{0:T(128)}, u32[]{:S(2)}) copy-start(f32[8]{0:T(128)} %copy-done.34) | copy-start | bytes 100
  770.0 19.4 %copy-start.37 = (f32[8]{0:T(128)S(1)}, f32[8]{0:T(128)}, u32[]{:S(2)}) copy-start(f32[8]{0:T(128)} %copy-done.36) | copy-start | bytes 100
  770.0 19.4 %copy-start.39 = (f32[8]{0:T(128)S(1)}, f32[8]{0:T(128)}, u32[]{:S(2)}) copy-start(f32[8]{0:T(128)} %copy-done.38) | copy-start | bytes 100
  770.1 19.4 %copy-start.41 = (f32[8]{0:T(128)S(1)}, f32[8]{0:T(128)}, u32[]{:S(2)}) copy-start(f32[8]{0:T(128)} %copy-done.40) | copy-start | bytes 100
  770.1 19.4 %copy-start.43 = (f32[8]{0:T(128)S(1)}, f32[8]{0:T(128)}, u32[]{:S(2)}) copy-start(f32[8]{0:T(128)} %copy-done.42) | copy-start | bytes 100
  770.1 19.4 %copy-start.45 = (f32[8]{0:T(128)S(1)}, f32[8]{0:T(128)}, u32[]{:S(2)}) copy-start(f32[8]{0:T(128)} %copy-done.44) | copy-start | bytes 100
  770.3 17.9 %collective-permute-start.14 = (f32[10,4,4,1152]{3,2,1,0:T(4,128)S(1)}, f32[10,4,4,1152]{3,2,1,0:T(4,128)S(1)}, u32[]{:S(2)}, u32[]{:S(2)}) collective-permute-start(f32[10,4,4,1152]{3,2,1,0:T(4,128)S(1)} %get-tuple-element.90), channel_id=1, source_target_pairs={{1,0},{2,1},{3,2},{5,4},{6,5},{7,6},{9,8},{10,9},{11,10},{13,12},{... | collective-permute-start | bytes 2211848 | tf_op jit(solution)/shard_map/ppermute | solution.py:23
  771.7 17.6 %collective-permute-start.15 = (f32[10,4,4,1152]{3,2,1,0:T(4,128)S(1)}, f32[10,4,4,1152]{3,2,1,0:T(4,128)S(1)}, u32[]{:S(2)}, u32[]{:S(2)}) collective-permute-start(f32[10,4,4,1152]{3,2,1,0:T(4,128)S(1)} %get-tuple-element.91), channel_id=1, source_target_pairs={{0,1},{1,2},{2,3},{4,5},{5,6},{6,7},{8,9},{9,10},{10,11},{12,13},{... | collective-permute-start | bytes 2211848 | tf_op jit(solution)/shard_map/ppermute | solution.py:21
  (22 other events, 62.0 us)
Sparse Core Ops, SparseCore 0:
  61.2 37.6 reduce-scatter.2
  309.9 56.1 all-reduce.45
  454.3 36.1 reduce-scatter.4
  700.4 56.0 all-reduce.47
where the time goes:
time: 809 us; the launch traced here: 800 us
  local copies, waits for them, and re-layouts  260 us (32%)
  waiting for transfers between devices  238 us (29%)
  other arithmetic  220 us (27%)
  starting transfers between devices  44.6 us (6%)
  between operations  17.3 us (2%)
  matrix products  11.6 us (1%)
  blocking collectives  9.18 us (1%)
    gather x6, local copies, waits for them, and re-layouts, body(): flat_tile[obs_points[slot_index]] - values[slot_index]  138 us
    scatter-add x6, other arithmetic, body(): jnp.zeros(flat_tile.shape, jnp.float32).at[obs_points[slot_index]]  134 us
    psum x2, waiting for transfers between devices, body(): summed_back = lax.psum(folded, 'mem')  112 us
    reduce_scatter x2, waiting for transfers between devices, body(): lax.psum_scatter(chosen, 'mem', scatter_dimension=0, tiled=True)[0]  74.1 us
    another operation x12, local copies, waits for them, and re-layouts, fine_tile(): jnp.stack([even_cols, odd_cols], axis=-1)  49.8 us
    mul x6, other arithmetic, fine_tile(): odd_cols = 0.5 * (merid[..., :tile_half] + merid[..., 1:tile_half + 1])  40.8 us
    ppermute x8, waiting for transfers between devices, padded_2(): lax.ppermute(head, axis, [((i + 1) % count, i) for i in range(ends)])  37.9 us
    ppermute x8, starting transfers between devices, padded_2(): lax.ppermute(tail, axis, [(i, (i + 1) % count) for i in range(ends)])  33.5 us
  transfers between devices with their start and end apart: 20, of which 15 were waited for; matrix products, arithmetic and copies ran while one was open for 2% of the time, Pallas kernels for 0%

commit v1 on v0

v1 whole, which is shorter than its diff:
```python
import functools

import jax
import jax.numpy as jnp
import numpy as np
from jax import lax
from jax.experimental import pallas as pl
from jax.experimental.pallas import tpu as pltpu
from jax.sharding import PartitionSpec as P

TLON = 128
ITERS = 2
LANES = 128
OBS_CHUNK = 1024


step_size = 0.3


def band_exchange(to_prev, to_next):
    count = lax.axis_size("lat")
    even = lax.axis_index("lat") % 2 == 0
    first = [(i, i ^ 1) for i in range(count) if i ^ 1 < count]
    second = [(i, ((i + 1) ^ 1) - 1) for i in range(count) if 0 <= ((i + 1) ^ 1) - 1 < count]
    if to_prev is to_next:
        send_first = send_second = to_prev
    else:
        send_first = jnp.where(even, to_next, to_prev)
        send_second = jnp.where(even, to_prev, to_next)
    got_first = lax.ppermute(send_first, "lat", first)
    got_second = lax.ppermute(send_second, "lat", second)
    return jnp.where(even, got_second, got_first), jnp.where(even, got_first, got_second)


def core_swap(cells):
    count = lax.axis_size("mem")
    return lax.ppermute(cells, "mem", [(i, i ^ 1) for i in range(count)])


def chip_steps():
    count = lax.axis_size("mem")
    bits = [1 << b for b in range(1, count.bit_length() - 1)]
    return [
        [(i, i ^ bits[(step + i % 2) % len(bits)]) for i in range(count)]
        for step in range(len(bits))
    ]


def core_split(cells):
    core = lax.axis_index("mem") % 2
    half = cells.shape[0] // 2
    mine = lax.dynamic_slice_in_dim(cells, core * half, half, 0)
    other = lax.dynamic_slice_in_dim(cells, (1 - core) * half, half, 0)
    return mine, other


def member_sum(cells):
    mine, other = core_split(cells)
    total = mine + core_swap(other)
    for perm in chip_steps():
        total = total + lax.ppermute(total, "mem", perm)
    return total


def both_halves(mine):
    core = lax.axis_index("mem") % 2
    other = core_swap(mine)
    return jnp.concatenate(
        [jnp.where(core == 0, mine, other), jnp.where(core == 0, other, mine)], axis=0
    )


def split_two(x):
    top = x.astype(jnp.bfloat16)
    return top, (x - top.astype(jnp.float32)).astype(jnp.bfloat16)


def tile_kernel(tile_ref, count_ref, row_ref, lane_ref, index_ref, value_ref, weight_ref, out_ref):
    slot = pl.program_id(0)
    count = count_ref[slot]
    half = TLON // 2
    wide = half + 8
    rows = row_ref.shape[0]
    out_ref[...] = jnp.zeros_like(out_ref)
    spots = row_ref[...]
    lanes = lane_ref[...]
    coarse = 2 * lax.broadcasted_iota(jnp.int32, (wide, 1), 0)
    chunk = min(OBS_CHUNK, index_ref.shape[-1])

    def step(part, carry):
        @pl.when(part * chunk < count)
        def _():
            here = pl.ds(pl.multiple_of(part * chunk, chunk), chunk)
            index = index_ref[0, :, here]
            weight = weight_ref[0, :, here]
            place = lax.broadcasted_iota(jnp.int32, (1, chunk), 1) + part * chunk
            weight = jnp.where(place < count, weight, 0.0)
            pull = weight * value_ref[0, :, here]
            high = lax.shift_right_logical(index, TLON.bit_length() - 1)
            low = lax.bitwise_and(index, TLON - 1)
            at_row = jnp.where(spots == high, 1.0, 0.0).astype(jnp.bfloat16)
            contract = (((1,), (1,)), ((), ()))
            total = jnp.zeros((rows, TLON), jnp.float32)
            for piece in split_two(weight):
                at_lane = jnp.where(lanes == low, piece.astype(jnp.float32), 0.0)
                total += lax.dot_general(
                    at_row, at_lane.astype(jnp.bfloat16), contract, preferred_element_type=jnp.float32
                )
            apart = jnp.abs(low - coarse)
            share = jnp.where(apart == 0, 1.0, jnp.where(apart == 1, 0.5, 0.0))
            pulled = jnp.zeros((rows, wide), jnp.float32)
            for piece in split_two(pull):
                at_coarse = share * piece.astype(jnp.float32)
                pulled += lax.dot_general(
                    at_row, at_coarse.astype(jnp.bfloat16), contract, preferred_element_type=jnp.float32
                )
            pulled = jnp.concatenate(
                [pulled, jnp.zeros((rows, TLON - wide), jnp.float32)], axis=1
            )
            groups = out_ref.shape[1]
            step_rows = rows // groups
            for group in range(groups):
                mine = slice(group * step_rows, (group + 1) * step_rows)
                out_ref[0, group, :step_rows] += total[mine]
                out_ref[0, group, step_rows:] += pulled[mine]

        return carry

    lax.fori_loop(0, index_ref.shape[-1] // chunk, step, 0)
    step_rows = rows // out_ref.shape[1]
    marker = jnp.where(count > 0, tile_ref[slot] + 1, 0).astype(jnp.float32)
    lane = lax.broadcasted_iota(jnp.int32, (8, TLON), 1)
    for group in range(out_ref.shape[1]):
        block = out_ref[0, group, step_rows : step_rows + 8]
        out_ref[0, group, step_rows : step_rows + 8] = jnp.where(lane == TLON - 1, marker, block)


def tile_sums(tiles, counts, index, value, weight, var_count, lev_count, row_count):
    slots, length = index.shape
    var, par, lev, row = np.meshgrid(
        np.arange(var_count), np.arange(2), np.arange(lev_count), np.arange(row_count), indexing="ij"
    )
    spot = ((var * lev_count + lev) * row_count + row) * 2 + par
    spot = spot.reshape(-1, 1).astype(np.int32)
    lanes = np.arange(TLON).reshape(2, TLON // 2)
    lanes = (2 * (lanes % (TLON // 2)) + lanes // (TLON // 2)).reshape(-1, 1).astype(np.int32)
    rows = spot.shape[0]
    whole = lambda shape: pl.BlockSpec(shape, lambda s, *_: (0,) * len(shape))
    line = pl.BlockSpec((1, 1, length), lambda s, *_: (s, 0, 0))
    out = (slots, var_count, 2 * rows // var_count, TLON)
    return pl.pallas_call(
        tile_kernel,
        grid_spec=pltpu.PrefetchScalarGridSpec(
            num_scalar_prefetch=2,
            grid=(slots,),
            in_specs=[whole(spot.shape), whole(lanes.shape), line, line, line],
            out_specs=pl.BlockSpec((1,) + out[1:], lambda s, *_: (s, 0, 0, 0)),
        ),
        out_shape=jax.ShapeDtypeStruct(out, jnp.float32),
        compiler_params=pltpu.CompilerParams(vmem_limit_bytes=32 * 2**20),
        cost_estimate=pl.CostEstimate(
            flops=2 * slots * length * rows * 400, bytes_accessed=slots * rows * 1024, transcendentals=0
        ),
    )(
        tiles,
        counts,
        jnp.asarray(spot),
        jnp.asarray(lanes),
        index[:, None],
        value[:, None],
        weight[:, None],
    )


def field_kernel(mark_ref, slots_ref, weight_ref, pull_ref, where_ref):
    tile_count = where_ref.shape[0]
    half = TLON // 2

    def note(slot, carry):
        mark = mark_ref[slot]

        @pl.when(mark > 0)
        def _():
            where_ref[mark - 1] = slot

        return carry

    for tile in range(tile_count):
        where_ref[tile] = 0
    lax.fori_loop(0, mark_ref.shape[0], note, 0)
    rows = weight_ref.shape[1]
    lane = lax.broadcasted_iota(jnp.int32, (rows, TLON), 1)
    for pair in range(tile_count // 2):
        left = where_ref[2 * pair]
        right = where_ref[2 * pair + 1]
        before = where_ref[(2 * pair - 1) % tile_count]
        here = slice(pair * TLON, (pair + 1) * TLON)
        first, second = slots_ref[left, :rows], slots_ref[right, :rows]
        weight_ref[0, :, here] = jnp.where(lane < half, first, pltpu.roll(second, half, 1))
        weight_ref[1, :, here] = jnp.where(lane < half, pltpu.roll(first, half, 1), second)
        first, second = slots_ref[left, rows:], slots_ref[right, rows:]
        third = slots_ref[before, rows:]
        pull_ref[:, here] = (
            jnp.where(lane <= half, first, 0.0)
            + jnp.where(lane >= half, pltpu.roll(second, half, 1), 0.0)
            + jnp.where(lane == 0, pltpu.roll(third, half, 1), 0.0)
        )


def band_fields(slots, lon_cells):
    rows = slots.shape[1] // 2
    marks = slots[:, rows, TLON - 1].astype(jnp.int32)
    vmem = pl.BlockSpec(memory_space=pltpu.VMEM)
    return pl.pallas_call(
        field_kernel,
        in_specs=[pl.BlockSpec(memory_space=pltpu.SMEM), vmem],
        out_specs=[vmem, vmem],
        out_shape=[
            jax.ShapeDtypeStruct((2, rows, lon_cells), jnp.float32),
            jax.ShapeDtypeStruct((rows, lon_cells), jnp.float32),
        ],
        scratch_shapes=[pltpu.SMEM((2 * lon_cells // TLON,), jnp.int32)],
        compiler_params=pltpu.CompilerParams(vmem_limit_bytes=32 * 2**20),
        cost_estimate=pl.CostEstimate(
            flops=rows * lon_cells * 8, bytes_accessed=rows * lon_cells * 24, transcendentals=0
        ),
    )(marks, slots)


def observation_fields(tiles, counts, index, value, weight, var_count, lev_count, row_count, lon_cells):
    slots = tile_sums(tiles, counts, index, value, weight, var_count, lev_count, row_count)
    core = lax.axis_index("mem") % 2
    by_var = slots.transpose(1, 0, 2, 3)
    mine, other = core_split(by_var)
    held = jnp.concatenate([mine[0], core_swap(other)[0]], axis=0)
    for perm in chip_steps():
        held = jnp.concatenate([held, lax.ppermute(held, "mem", perm)], axis=0)
    return band_fields(held, lon_cells)


def pull_columns(weights, cells):
    odd = weights[1] * (0.5 * (cells + jnp.roll(cells, -1, axis=-1)))
    return weights[0] * cells + 0.5 * (odd + jnp.roll(odd, 1, axis=-1))


def observed_adjoint(inc, below, above, fields, rims, band_index, band_count):
    weights, pulls = fields
    south = band_index == 0
    north = band_index == band_count - 1
    first, last = inc[:, 0], inc[:, -1]
    lower = jnp.where(south, first, below)
    upper = jnp.where(north, last, above)
    down = jnp.concatenate([lower[:, None], inc[:, :-1]], axis=1)
    up = jnp.concatenate([inc[:, 1:], upper[:, None]], axis=1)
    even = pull_columns(weights[:, 0], 0.75 * inc + 0.25 * down) - pulls[0]
    odd = pull_columns(weights[:, 1], 0.75 * inc + 0.25 * up) - pulls[1]
    (rim_weight_below, rim_pull_below), (rim_weight_above, rim_pull_above) = rims
    odd_below = pull_columns(rim_weight_below, 0.75 * below + 0.25 * first) - rim_pull_below
    even_above = pull_columns(rim_weight_above, 0.75 * above + 0.25 * last) - rim_pull_above
    odd_below = jnp.where(south, even[:, 0], odd_below)
    even_above = jnp.where(north, odd[:, -1], even_above)
    odd_down = jnp.concatenate([odd_below[:, None], odd[:, :-1]], axis=1)
    even_up = jnp.concatenate([even[:, 1:], even_above[:, None]], axis=1)
    return 0.75 * (even + odd) + 0.25 * (odd_down + even_up)


def forward_rows(cells, coeffs, row_count, half_band):
    running = jnp.zeros(cells.shape[:2] + (row_count, cells.shape[3]), jnp.float32)
    for offset in range(2 * half_band + 1):
        running = running + coeffs[:, offset][None, None, :, None] * cells[:, :, offset : offset + row_count]
    return running


def backward_rows(cells, coeffs, row_count, half_band):
    running = jnp.zeros(cells.shape[:2] + (row_count, cells.shape[3]), jnp.float32)
    for offset in range(2 * half_band + 1):
        at = 2 * half_band - offset
        running = (
            running
            + coeffs[at : at + row_count, offset][None, None, :, None] * cells[:, :, at : at + row_count]
        )
    return running


def partial_increment(ext, coeffs, zonal_loc, members, half_band):
    spread = forward_rows(ext, coeffs, members.shape[3], half_band).astype(jnp.bfloat16)
    localized = jnp.dot(
        spread.reshape(-1, spread.shape[-1]), zonal_loc, preferred_element_type=jnp.float32
    ).reshape(spread.shape)
    return jnp.sum(members * localized[:, None], axis=0)


def zonal_backward(members, adjoint, zonal_loc):
    weighted = jnp.sum(members * adjoint[None], axis=1).astype(jnp.bfloat16)
    return lax.dot_general(
        weighted.reshape(-1, weighted.shape[-1]),
        zonal_loc,
        (((1,), (1,)), ((), ())),
        preferred_element_type=jnp.float32,
    ).reshape(weighted.shape)


def body(
    members, alpha, zonal_loc, merid_coef, slot_tile, obs_count, obs_index, obs_value, obs_weight
):
    half_band = merid_coef.shape[1] // 2
    _, var_count, lev_count, rows, lon_cells = members.shape
    band_index = lax.axis_index("lat")
    band_count = lax.axis_size("lat")
    slot_count = slot_tile.shape[-1]

    below, above = band_exchange(alpha[:, :, :half_band], alpha[:, :, -half_band:])
    ext = jnp.concatenate([below, alpha, above], axis=2)
    sent, below = lax.optimization_barrier((members, below))
    members_below, members_above = band_exchange(sent, sent)

    weights, pulls = observation_fields(
        slot_tile.reshape(-1),
        obs_count.reshape(-1),
        obs_index.reshape(slot_count, -1),
        obs_value.reshape(slot_count, -1),
        obs_weight.reshape(slot_count, -1),
        var_count,
        lev_count,
        rows,
        lon_cells,
    )
    weights = weights.reshape(2, 2, lev_count, rows, lon_cells)
    pulls = pulls.reshape(2, lev_count, rows, lon_cells)
    rim_below, rim_above = band_exchange(
        jnp.concatenate([weights[:, 0, :, 0], pulls[None, 0, :, 0]]),
        jnp.concatenate([weights[:, 1, :, -1], pulls[None, 1, :, -1]]),
    )
    rims = (rim_below[:2], rim_below[2]), (rim_above[:2], rim_above[2])

    coef_wide = jnp.pad(merid_coef, ((rows, rows), (0, 0)))
    coef_wide = lax.dynamic_slice_in_dim(coef_wide, band_index * rows, 3 * rows, 0)
    own_coef = coef_wide[rows : 2 * rows]
    row_at = band_index * rows + jnp.arange(-half_band, rows + half_band)
    on_grid = ((row_at >= 0) & (row_at < band_count * rows))[None, None, :, None]

    for iteration in range(ITERS):
        partial_value = partial_increment(ext, own_coef, zonal_loc, members, half_band)
        inc = member_sum(partial_value)[0]
        low, high = band_exchange(inc[:, 0], inc[:, -1])
        adjoint = observed_adjoint(inc, low, high, (weights, pulls), rims, band_index, band_count)
        if iteration + 1 < ITERS:
            low, high = band_exchange(adjoint, adjoint)
            halo = rows
        else:
            low, high = band_exchange(adjoint[:, :half_band], adjoint[:, -half_band:])
            halo = half_band
        adjoint = both_halves(jnp.concatenate([low, adjoint, high], axis=1)[None])
        wide_members = jnp.concatenate(
            [members_below[:, :, :, rows - halo :], members, members_above[:, :, :, :halo]], axis=3
        )
        zonal_back = zonal_backward(wide_members, adjoint, zonal_loc)
        coeffs = coef_wide[rows - halo : 2 * rows + halo]
        if iteration + 1 < ITERS:
            gradient = ext + backward_rows(zonal_back, coeffs, rows + 2 * half_band, half_band)
            ext = jnp.where(on_grid, ext - step_size * gradient, 0.0)
        else:
            current = ext[:, :, half_band:-half_band]
            gradient = current + backward_rows(zonal_back, coeffs, rows, half_band)
            current = current - step_size * gradient
    return current


def solution(mesh):
    in_specs = (
        P("mem", None, None, "lat", None),
        P("mem", None, "lat", None),
        P(),
        P(),
        P("lat", "mem", None),
        P("lat", "mem", None),
        P("lat", "mem", None, None),
        P("lat", "mem", None, None),
        P("lat", "mem", None, None),
    )
    out_specs = P("mem", None, "lat", None)
    return jax.shard_map(body, mesh=mesh, in_specs=in_specs, out_specs=out_specs, check_vma=False)
```

time: 809 us -> 168 us (0.21)
  local copies, waits for them, and re-layouts: 260 us -> 6.61 us
  other arithmetic: 220 us -> 34.6 us
  waiting for transfers between devices: 238 us -> 62 us
  between operations: 17.3 us -> 1.15 us
  blocking collectives: 9.18 us -> 0 us
    gather x8 -> x0, local copies, waits for them, and re-layouts: 143 us -> none  [the longest x6 138 us: body(): flat_tile[obs_points[slot_index]] - values[slot_index]]
    scatter-add x6 -> x0, other arithmetic: 134 us -> none  [body(): jnp.zeros(flat_tile.shape, jnp.float32).at[obs_points[slot_index]]]
    psum x2 -> x0, waiting for transfers between devices: 112 us -> none  [body(): summed_back = lax.psum(folded, 'mem')]
    reduce_scatter x2 -> x0, waiting for transfers between devices: 74.1 us -> none  [body(): lax.psum_scatter(chosen, 'mem', scatter_dimension=0, tiled=True)[0]]
    another operation x25 -> x0, local copies, waits for them, and re-layouts: 50.4 us -> none  [the longest x12 49.8 us: fine_tile(): jnp.stack([even_cols, odd_cols], axis=-1)]
    mul x17 -> x9, other arithmetic: 45.9 us -> 0.81 us  [the longest x8 0.66 us: pull_columns(): odd = weights[1] * (0.5 * (cells + jnp.roll(cells, -1, axis=-1)))]
    reshape x13 -> x0, local copies, waits for them, and re-layouts: 32.2 us -> none  [the longest x6 24 us: body(): flat_tile = fine_field.reshape(-1)]
    sub x2 -> x1, other arithmetic: 14.5 us -> 2.7 us  [body(): current = current - step_size * gradient]
  transfers between devices with their start and end apart: 20 -> 25, of which waited for: 15 -> 12; matrix products, arithmetic and copies ran while one was open for 2% -> 10% of each run, Pallas kernels for 0% -> 3%
where the time goes in v1:
time: 168 us; the launch traced here: 167 us
  waiting for transfers between devices  62 us (37%)
  starting transfers between devices  44.2 us (26%)
  other arithmetic  34.6 us (21%)
  matrix products  12.6 us (8%)
  local copies, waits for them, and re-layouts  6.61 us (4%)
  Pallas kernels  5.99 us (4%)
    ppermute x7, waiting for transfers between devices, band_exchange(): got_first = lax.ppermute(send_first, 'lat', first)  42 us
    ppermute x7, starting transfers between devices, band_exchange(): got_first = lax.ppermute(send_first, 'lat', first)  29.5 us
    ppermute x4, waiting for transfers between devices, member_sum(): total = total + lax.ppermute(total, 'mem', perm)  17.8 us
    reduce_sum x2, other arithmetic, zonal_backward(): weighted = jnp.sum(members * adjoint[None], axis=1).astype(jnp.bfloat16)  7.06 us
    dot_general x2, matrix products, partial_increment(): jnp.dot(spread.reshape(-1, spread.shape[-1]), zonal_loc, preferred_elemen...  6.89 us
    ppermute x7, starting transfers between devices, band_exchange(): got_second = lax.ppermute(send_second, 'lat', second)  6.84 us
    dot_general x2, matrix products, zonal_backward(): lax.dot_general(weighted.reshape(-1, weighted.shape[-1]), zonal_loc, (((1...  5.72 us
    ppermute x4, starting transfers between devices, member_sum(): total = total + lax.ppermute(total, 'mem', perm)  5.46 us
  transfers between devices with their start and end apart: 25, of which 12 were waited for; matrix products, arithmetic and copies ran while one was open for 10% of the time, Pallas kernels for 3%

profile of v1, /device:TPU:0, one launch (start us, length us, event | category | flops | bytes accessed | tf_op | source)
XLA Modules:
  0.0 167.1 jit_solution(18439069808528119829)
XLA Ops:
  0.1 3.3 %slice_select_fusion = (f32[10,4,4,1152]{3,2,1,0:T(4,128)}, f32[10,4,4,1152]{3,2,1,0:T(4,128)}) fusion(f32[10,4,8,1152]{3,2,1,0:T(8,128)} %param.12, pred[]{:T(512)S(6)} %eq.36), kind=kLoop, calls=%fused_computation.125 | loop fusion | flops 368640 | bytes 2949121 | tf_op jit(solution)/shard_map/jit(_where)/select_n | solution.py:28
  3.4 3.0 %collective-permute-start.1 = (f32[10,4,4,1152]{3,2,1,0:T(4,128)}, f32[10,4,4,1152]{3,2,1,0:T(4,128)}, u32[]{:S(2)}, u32[]{:S(2)}) collective-permute-start(f32[10,4,4,1152]{3,2,1,0:T(4,128)} %get-tuple-element.15), channel_id=1, source_target_pairs={{0,1},{1,0},{2,3},{3,2},{4,5},{5,4},{6,7},{7,6},{8,9},{9,8},{10,11... | collective-permute-start | bytes 2211848 | tf_op jit(solution)/shard_map/ppermute | solution.py:30
  6.4 1.5 collective-permute-start
  8.0 4.8 %shard_map.109 = f32[3,2,128,128]{3,2,1,0:T(8,128)S(1)} custom-call(s32[3]{0:T(128)S(1)} %bitcast.273, s32[3]{0:T(128)S(1)} %bitcast.274, s32[128,1]{1,0:T(8,128)S(1)} %copy-done.7, s32[128,1]{1,0:T(8,128)S(1)} %copy-done.6, s32[3,1,4096]{2,1,0:T(1,128)S(1)} %bitcast.270, f32[3,1,4096]{2,1,0:T(1,128)S(1)} %bitcast.271, f32[3,1,4096]{2,1,0:T(1,128)S(1)} %bitcast.272), custom_call_target="tpu_custom_call" | custom-call | flops 1258291200 | bytes 393216 | tf_op jit(solution)/shard_map/pallas_call | solution.py:151
  13.2 10.0 %collective-permute-done.1 = f32[10,4,4,1152]{3,2,1,0:T(4,128)} collective-permute-done((f32[10,4,4,1152]{3,2,1,0:T(4,128)}, f32[10,4,4,1152]{3,2,1,0:T(4,128)}, u32[]{:S(2)}, u32[]{:S(2)}) %collective-permute-start.1) | collective-permute-done | bytes 737312 | tf_op jit(solution)/shard_map/ppermute | solution.py:30
  23.2 1.6 broadcast_select_fusion.2
  25.1 3.7 %fusion.20 = f32[10,4,8,1152]{3,2,1,0:T(8,128)S(1)} fusion(bf16[1152,1152]{1,0:T(8,128)(2,1)S(1)} %copy-done, f32[10,4,8,1152]{3,2,1,0:T(8,128)S(1)} %copy-done.13, f32[10,4,4,1152]{3,2,1,0:T(4,128)S(1)} %bitcast.275, f32[10,4,4,1152]{3,2,1,0:T(4,128)S(1)} %bitcast.277, f32[8]{0:T(128)S(1)} %get-tuple-element.77, f32[8]{0:T(128)S(1)} %get-tuple-element.76, ...), kind=kOutput, calls=%fused_computation.45 | convolution fusion | flops 858931200 | bytes 7078176 | tf_op jit(solution)/shard_map/dot_general | solution.py:287
  28.7 1.8 %fusion = f32[2,4,8,1152]{3,2,1,0:T(8,128)S(1)} fusion(bf16[10,2,4,8,1152]{4,3,2,1,0:T(8,128)(2,1)} %param.11, f32[10,4,8,1152]{3,2,1,0:T(8,128)S(1)} %fusion.20), kind=kLoop, calls=%fused_computation.16 | loop fusion | flops 2138112 | bytes 3244032 | tf_op jit(solution)/shard_map/reduce_sum | solution.py:290
  30.7 0.8 pad_maximum_fusion.6
  31.5 1.7 collective-permute-start.5
  33.2 0.6 collective-permute-start.8
  33.8 7.2 %collective-permute-done.8 = f32[1,4,8,1152]{3,1,2,0:T(4,128)S(1)} collective-permute-done((f32[1,4,8,1152]{3,1,2,0:T(4,128)S(1)}, f32[1,4,8,1152]{3,1,2,0:T(4,128)S(1)}, u32[]{:S(2)}, u32[]{:S(2)}) %collective-permute-start.8) | collective-permute-done | bytes 147488 | tf_op jit(solution)/shard_map/ppermute | solution.py:61
  41.0 0.7 add.301
  41.7 1.7 %collective-permute-start.9 = (f32[1,4,8,1152]{3,1,2,0:T(4,128)}, f32[1,4,8,1152]{3,1,2,0:T(4,128)}, u32[]{:S(2)}, u32[]{:S(2)}) collective-permute-start(f32[1,4,8,1152]{3,1,2,0:T(4,128)} %add.301), channel_id=1, source_target_pairs={{0,16},{4,12},{8,24},{12,4},{16,0},{20,28},{24,8},{28,20},{1,17},{... | collective-permute-start | bytes 442376 | tf_op jit(solution)/shard_map/ppermute | solution.py:61
  43.5 0.4 collective-permute-start.6
  43.9 3.3 %collective-permute-done.9 = f32[1,4,8,1152]{3,1,2,0:T(4,128)} collective-permute-done((f32[1,4,8,1152]{3,1,2,0:T(4,128)}, f32[1,4,8,1152]{3,1,2,0:T(4,128)}, u32[]{:S(2)}, u32[]{:S(2)}) %collective-permute-start.9) | collective-permute-done | bytes 147488 | tf_op jit(solution)/shard_map/ppermute | solution.py:61
  47.2 1.0 add_bitcast_fusion.1
  48.2 0.7 collective-permute-start.10
  48.9 7.8 %collective-permute-start.11 = (f32[4,1152]{1,0:T(4,128)S(1)}, f32[4,1152]{1,0:T(4,128)S(1)}, u32[]{:S(2)}, u32[]{:S(2)}) collective-permute-start(f32[4,1152]{1,0:T(4,128)S(1)} %get-tuple-element.62), channel_id=1, source_target_pairs={{0,1},{1,0},{2,3},{3,2},{4,5},{5,4},{6,7},{7,6},{8,9},{9,8},{10,11... | collective-permute-start | bytes 55304 | tf_op jit(solution)/shard_map/ppermute | solution.py:30
  56.7 1.7 %collective-permute-done.11 = f32[4,1152]{1,0:T(4,128)S(1)} collective-permute-done((f32[4,1152]{1,0:T(4,128)S(1)}, f32[4,1152]{1,0:T(4,128)S(1)}, u32[]{:S(2)}, u32[]{:S(2)}) %collective-permute-start.11) | collective-permute-done | bytes 18464 | tf_op jit(solution)/shard_map/ppermute | solution.py:30
  59.2 0.6 fusion.135.mark_ref
  59.8 1.2 shard_map.110
  61.1 0.8 slice_bitcast_fusion
  62.0 2.1 %collective-permute-start.13 = (f32[3,4,1152]{2,1,0:T(4,128)S(1)}, f32[3,4,1152]{2,1,0:T(4,128)S(1)}, u32[]{:S(2)}, u32[]{:S(2)}) collective-permute-start(f32[3,4,1152]{2,1,0:T(4,128)S(1)} %get-tuple-element.65), channel_id=1, source_target_pairs={{0,1},{1,0},{2,3},{3,2},{4,5},{5,4},{6,7},{7,6},{8,9},{9,8},{10,11... | collective-permute-start | bytes 165896 | tf_op jit(solution)/shard_map/ppermute | solution.py:30
  64.0 0.7 collective-permute-start.12
  65.3 0.2 fusion.83
  65.6 0.6 collective-permute-done.13
  66.6 0.2 copy-done.30
  66.9 4.0 %collective-permute-start.15 = (f32[4,8,1152]{2,0,1:T(4,128)S(1)}, f32[4,8,1152]{2,0,1:T(4,128)S(1)}, u32[]{:S(2)}, u32[]{:S(2)}) collective-permute-start(f32[4,8,1152]{2,0,1:T(4,128)S(1)} %fusion.89), channel_id=1, source_target_pairs={{0,1},{1,0},{2,3},{3,2},{4,5},{5,4},{6,7},{7,6},{8,9},{9,8},{10,11... | collective-permute-start | bytes 442376 | tf_op jit(solution)/shard_map/ppermute | solution.py:30
  70.9 0.7 collective-permute-start.14
  71.6 2.2 %collective-permute-start.3 = (bf16[10,2,4,8,1152]{4,3,2,1,0:T(8,128)(2,1)}, bf16[10,2,4,8,1152]{4,3,2,1,0:T(8,128)(2,1)}, u32[]{:S(2)}, u32[]{:S(2)}) collective-permute-start(bf16[10,2,4,8,1152]{4,3,2,1,0:T(8,128)(2,1)} %param.11), channel_id=1, source_target_pairs={{0,1},{1,0},{2,3},{3,2},{4,5},{5,4},{6,7},{7,6},{8,9},{9,8},{10,11... | collective-permute-start | bytes 4423688 | tf_op jit(solution)/shard_map/ppermute | solution.py:30
  73.8 1.8 %collective-permute-start.2 = (bf16[10,2,4,8,1152]{4,3,2,1,0:T(8,128)(2,1)}, bf16[10,2,4,8,1152]{4,3,2,1,0:T(8,128)(2,1)}, u32[]{:S(2)}, u32[]{:S(2)}) collective-permute-start(bf16[10,2,4,8,1152]{4,3,2,1,0:T(8,128)(2,1)} %param.11), channel_id=1, source_target_pairs={{1,2},{2,1},{5,6},{6,5},{9,10},{10,9},{13,14},{14,13},{17,18},{18,... | collective-permute-start | bytes 4423688 | tf_op jit(solution)/shard_map/ppermute | solution.py:31
  75.7 0.9 maximum_bitcast_fusion
  76.5 0.5 compare_and_fusion
  77.2 0.7 fusion.141
  77.8 0.8 collective-permute-done.16
  78.7 1.2 broadcast_select_fusion.5
  79.9 0.2 pad_maximum_fusion.3
  80.1 25.6 %collective-permute-done.3 = bf16[10,2,4,8,1152]{4,3,2,1,0:T(8,128)(2,1)} collective-permute-done((bf16[10,2,4,8,1152]{4,3,2,1,0:T(8,128)(2,1)}, bf16[10,2,4,8,1152]{4,3,2,1,0:T(8,128)(2,1)}, u32[]{:S(2)}, u32[]{:S(2)}) %collective-permute-start.3) | collective-permute-done | bytes 1474592 | tf_op jit(solution)/shard_map/ppermute | solution.py:30
  105.8 2.1 %broadcast_select_fusion.1 = (bf16[10,2,4,8,1152]{4,3,2,1,0:T(8,128)(2,1)S(1)}, bf16[10,2,4,8,1152]{4,3,2,1,0:T(8,128)(2,1)S(1)}) fusion(bf16[10,2,4,8,1152]{4,3,2,1,0:T(8,128)(2,1)} %collective-permute-done.2, bf16[10,2,4,8,1152]{4,3,2,1,0:T(8,128)(2,1)} %collective-permute-done.3, pred[]{:T(512)S(6)} %eq.36), kind=kLoop, calls=%fused_computation.113 | loop fusion | flops 1474560 | bytes 5898241 | tf_op jit(solution)/shard_map/jit(_where)/select_n | solution.py:32
  107.9 3.5 %multiply_reduce_fusion = bf16[10,4,24,1152]{3,2,1,0:T(8,128)(2,1)S(1)} fusion(bf16[10,2,4,8,1152]{4,3,2,1,0:T(8,128)(2,1)S(1)} %get-tuple-element.12, bf16[10,2,4,8,1152]{4,3,2,1,0:T(8,128)(2,1)} %param.11, bf16[10,2,4,8,1152]{4,3,2,1,0:T(8,128)(2,1)S(1)} %get-tuple-element.11, f32[2,4,24,1152]{3,2,1,0:T(8,128)S(1)} %copy.89), kind=kLoop, calls=%fused_computation | loop fusion | flops 16588800 | bytes 7520256 | tf_op jit(solution)/shard_map/reduce_sum | solution.py:294
  111.4 3.4 %fusion.18 = f32[10,4,24,1152]{3,2,1,0:T(8,128)S(1)} fusion(bf16[1152,1152]{1,0:T(8,128)(2,1)S(1)} %copy-done, bf16[10,4,24,1152]{3,2,1,0:T(8,128)(2,1)S(1)} %multiply_reduce_fusion), kind=kOutput, calls=%fused_computation.43 | convolution fusion | flops 2548039680 | bytes 9289728 | tf_op jit(solution)/shard_map/dot_general | solution.py:295
  114.8 4.7 %fusion.6 = f32[10,4,16,1152]{3,2,1,0:T(8,128)S(1)} fusion(f32[10,4,24,1152]{3,2,1,0:T(8,128)S(1)} %fusion.18, f32[10,4,4,1152]{3,2,1,0:T(4,128)S(1)} %bitcast.276, f32[10,4,8,1152]{3,2,1,0:T(8,128)S(1)} %copy-done.14, f32[10,4,4,1152]{3,2,1,0:T(4,128)S(1)} %bitcast.278, f32[16]{0:T(128)S(1)} %get-tuple-element.92, f32[16]{0:T(128)S(1)} %get-tuple-element.91, ...), kind=kLoop, calls=%fused_computation.23 | loop fusion | flops 16957440 | bytes 32440912 | tf_op jit(solution)/shard_map/jit(_where)/select_n | solution.py:361
  119.6 3.2 %fusion.16 = f32[10,4,8,1152]{3,2,1,0:T(8,128)S(1)} fusion(bf16[1152,1152]{1,0:T(8,128)(2,1)S(1)} %copy-done, f32[10,4,16,1152]{3,2,1,0:T(8,128)S(1)} %fusion.6, f32[8]{0:T(128)} %copy-done.36, f32[8]{0:T(128)} %copy-done.35, f32[8]{0:T(128)} %copy-done.34, f32[8]{0:T(128)} %copy-done.33, f32[8]{0:T(128)S(1)} %get-tuple-element.72, f32[8]{0:T(128)} %copy-done.40, ...), kind=kOutput, calls=%fused_computation.41 | convolution fusion | flops 855982080 | bytes 17400576 | tf_op jit(solution)/shard_map/dot_general | solution.py:287
  122.8 1.7 %fusion.1 = f32[2,4,8,1152]{3,2,1,0:T(8,128)S(1)} fusion(bf16[10,2,4,8,1152]{4,3,2,1,0:T(8,128)(2,1)} %param.11, f32[10,4,8,1152]{3,2,1,0:T(8,128)S(1)} %fusion.16), kind=kLoop, calls=%fused_computation.17 | loop fusion | flops 2138112 | bytes 3244032 | tf_op jit(solution)/shard_map/reduce_sum | solution.py:290
  124.7 1.4 collective-permute-done.17
  126.1 1.6 collective-permute-start.18
  127.7 3.7 %collective-permute-done.18 = f32[1,4,8,1152]{3,1,2,0:T(4,128)S(1)} collective-permute-done((f32[1,4,8,1152]{3,1,2,0:T(4,128)S(1)}, f32[1,4,8,1152]{3,1,2,0:T(4,128)S(1)}, u32[]{:S(2)}, u32[]{:S(2)}) %collective-permute-start.18) | collective-permute-done | bytes 147488 | tf_op jit(solution)/shard_map/ppermute | solution.py:61
  131.4 1.6 collective-permute-start.19
  133.0 3.6 %collective-permute-done.19 = f32[1,4,8,1152]{3,1,2,0:T(4,128)S(1)} collective-permute-done((f32[1,4,8,1152]{3,1,2,0:T(4,128)S(1)}, f32[1,4,8,1152]{3,1,2,0:T(4,128)S(1)}, u32[]{:S(2)}, u32[]{:S(2)}) %collective-permute-start.19) | collective-permute-done | bytes 147488 | tf_op jit(solution)/shard_map/ppermute | solution.py:61
  136.7 0.7 collective-permute-start.20
  137.4 5.5 %collective-permute-start.21 = (f32[4,1152]{1,0:T(4,128)S(1)}, f32[4,1152]{1,0:T(4,128)S(1)}, u32[]{:S(2)}, u32[]{:S(2)}) collective-permute-start(f32[4,1152]{1,0:T(4,128)S(1)} %get-tuple-element.56), channel_id=1, source_target_pairs={{0,1},{1,0},{2,3},{3,2},{4,5},{5,4},{6,7},{7,6},{8,9},{9,8},{10,11... | collective-permute-start | bytes 55304 | tf_op jit(solution)/shard_map/ppermute | solution.py:30
  142.9 1.7 %collective-permute-done.21 = f32[4,1152]{1,0:T(4,128)S(1)} collective-permute-done((f32[4,1152]{1,0:T(4,128)S(1)}, f32[4,1152]{1,0:T(4,128)S(1)}, u32[]{:S(2)}, u32[]{:S(2)}) %collective-permute-start.21) | collective-permute-done | bytes 18464 | tf_op jit(solution)/shard_map/ppermute | solution.py:30
  145.7 0.2 fusion.95
  146.1 0.2 fusion.101
  146.6 0.9 collective-permute-start.22
  147.5 4.9 %collective-permute-start.23 = (f32[4,4,1152]{2,0,1:T(4,128)S(1)}, f32[4,4,1152]{2,0,1:T(4,128)S(1)}, u32[]{:S(2)}, u32[]{:S(2)}) collective-permute-start(f32[4,4,1152]{2,0,1:T(4,128)S(1)} %get-tuple-element.50), channel_id=1, source_target_pairs={{0,1},{1,0},{2,3},{3,2},{4,5},{5,4},{6,7},{7,6},{8,9},{9,8},{10,11... | collective-permute-start | bytes 221192 | tf_op jit(solution)/shard_map/ppermute | solution.py:30
  152.4 2.3 %collective-permute-done.23 = f32[4,4,1152]{2,0,1:T(4,128)S(1)} collective-permute-done((f32[4,4,1152]{2,0,1:T(4,128)S(1)}, f32[4,4,1152]{2,0,1:T(4,128)S(1)}, u32[]{:S(2)}, u32[]{:S(2)}) %collective-permute-start.23) | collective-permute-done | bytes 73760 | tf_op jit(solution)/shard_map/ppermute | solution.py:30
  155.1 1.9 %slice.670 = bf16[10,2,4,4,1152]{4,3,2,1,0:T(4,128)(2,1)S(1)} slice(bf16[10,2,4,8,1152]{4,3,2,1,0:T(8,128)(2,1)} %copy-done.10), slice={[0:10], [0:2], [0:4], [4:8], [0:1152]} | slice | bytes 1474560 | tf_op jit(solution)/shard_map/slice | solution.py:355
  157.0 0.2 slice.671
  157.2 1.1 broadcast_select_fusion.7
  158.5 3.6 %multiply_reduce_fusion.1 = bf16[10,4,16,1152]{3,2,1,0:T(8,128)(2,1)S(1)} fusion(bf16[10,2,4,4,1152]{4,3,2,1,0:T(4,128)(2,1)S(1)} %slice.671, bf16[10,2,4,8,1152]{4,3,2,1,0:T(8,128)(2,1)} %param.11, bf16[10,2,4,4,1152]{4,3,2,1,0:T(4,128)(2,1)S(1)} %slice.670, f32[2,4,16,1152]{3,2,1,0:T(8,128)S(1)} %copy.94), kind=kLoop, calls=%fused_computation.1 | loop fusion | flops 11059200 | bytes 5013504 | tf_op jit(solution)/shard_map/reduce_sum | solution.py:294
  162.1 2.3 %fusion.14 = f32[10,4,16,1152]{3,2,1,0:T(8,128)S(1)} fusion(bf16[1152,1152]{1,0:T(8,128)(2,1)S(1)} %copy-done, bf16[10,4,16,1152]{3,2,1,0:T(8,128)(2,1)S(1)} %multiply_reduce_fusion.1), kind=kOutput, calls=%fused_computation.39 | convolution fusion | flops 1698693120 | bytes 7077888 | tf_op jit(solution)/shard_map/dot_general | solution.py:295
  164.4 2.7 %fusion.47 = f32[10,4,8,1152]{3,2,1,0:T(8,128)} fusion(f32[10,4,16,1152]{3,2,1,0:T(8,128)S(1)} %fusion.14, f32[10,4,16,1152]{3,2,1,0:T(8,128)S(1)} %copy-done.12, f32[8]{0:T(128)S(1)} %get-tuple-element.83, f32[8]{0:T(128)S(1)} %get-tuple-element.82, f32[8]{0:T(128)S(1)} %get-tuple-element.81, f32[8]{0:T(128)S(1)} %get-tuple-element.80, ...), kind=kLoop, calls=%fused_computation.74 | loop fusion | flops 7372800 | bytes 16220448 | tf_op jit(solution)/shard_map/sub | solution.py:365
  (184 shorter events, 5.5 us)
Async XLA Ops:
  0.0 24.9 %copy-start = (bf16[1152,1152]{1,0:T(8,128)(2,1)S(1)}, bf16[1152,1152]{1,0:T(8,128)(2,1)}, u32[]{:S(2)}) copy-start(bf16[1152,1152]{1,0:T(8,128)(2,1)} %param.13) | copy-start | bytes 7962628
  0.0 8.0 %copy-start.1 = (s32[1,1,3,4096]{3,1,2,0:T(1,128)S(1)}, s32[1,1,3,4096]{3,1,2,0:T(1,128)}, u32[]{:S(2)}) copy-start(s32[1,1,3,4096]{3,1,2,0:T(1,128)} %param.17) | copy-start | bytes 147460
  0.0 8.0 %copy-start.2 = (f32[1,1,3,4096]{3,1,2,0:T(1,128)S(1)}, f32[1,1,3,4096]{3,1,2,0:T(1,128)}, u32[]{:S(2)}) copy-start(f32[1,1,3,4096]{3,1,2,0:T(1,128)} %param.18) | copy-start | bytes 147460
  0.0 8.0 %copy-start.3 = (f32[1,1,3,4096]{3,1,2,0:T(1,128)S(1)}, f32[1,1,3,4096]{3,1,2,0:T(1,128)}, u32[]{:S(2)}) copy-start(f32[1,1,3,4096]{3,1,2,0:T(1,128)} %param.19) | copy-start | bytes 147460
  0.0 8.0 %copy-start.4 = (s32[1,1,3]{2,1,0:T(1,128)S(1)}, s32[1,1,3]{2,1,0:T(1,128)}, u32[]{:S(2)}) copy-start(s32[1,1,3]{2,1,0:T(1,128)} %param.15) | copy-start | bytes 40
  0.0 8.0 %copy-start.5 = (s32[1,1,3]{2,1,0:T(1,128)S(1)}, s32[1,1,3]{2,1,0:T(1,128)}, u32[]{:S(2)}) copy-start(s32[1,1,3]{2,1,0:T(1,128)} %param.16) | copy-start | bytes 40
  0.0 8.0 %copy-start.6 = (s32[128,1]{1,0:T(8,128)S(1)}, s32[128,1]{1,0:T(8,128)}, u32[]{:S(2)}) copy-start(s32[128,1]{1,0:T(8,128)} %constant.80.clone.lane_ref) | copy-start | bytes 1540
  0.0 8.0 %copy-start.7 = (s32[128,1]{1,0:T(8,128)S(1)}, s32[128,1]{1,0:T(8,128)}, u32[]{:S(2)}) copy-start(s32[128,1]{1,0:T(8,128)} %constant.79.clone.row_ref) | copy-start | bytes 1540
  3.4 19.8 %collective-permute-start.1 = (f32[10,4,4,1152]{3,2,1,0:T(4,128)}, f32[10,4,4,1152]{3,2,1,0:T(4,128)}, u32[]{:S(2)}, u32[]{:S(2)}) collective-permute-start(f32[10,4,4,1152]{3,2,1,0:T(4,128)} %get-tuple-element.15), channel_id=1, source_target_pairs={{0,1},{1,0},{2,3},{3,2},{4,5},{5,4},{6,7},{7,6},{8,9},{9,8},{10,11... | collective-permute-start | bytes 2211848 | tf_op jit(solution)/shard_map/ppermute | solution.py:30
  6.4 16.8 %collective-permute-start = (f32[10,4,4,1152]{3,2,1,0:T(4,128)}, f32[10,4,4,1152]{3,2,1,0:T(4,128)}, u32[]{:S(2)}, u32[]{:S(2)}) collective-permute-start(f32[10,4,4,1152]{3,2,1,0:T(4,128)} %get-tuple-element.16), channel_id=1, source_target_pairs={{1,2},{2,1},{5,6},{6,5},{9,10},{10,9},{13,14},{14,13},{17,18},{18,... | collective-permute-start | bytes 2211848 | tf_op jit(solution)/shard_map/ppermute | solution.py:31
  8.0 5.0 %copy-start.32 = (f32[32,9]{0,1:T(8,128)S(1)}, f32[32,9]{0,1:T(8,128)}, u32[]{:S(2)}) copy-start(f32[32,9]{0,1:T(8,128)} %param.14) | copy-start | bytes 3460
  12.9 17.8 %collective-permute-start.4 = (f32[1,3,128,128]{3,2,1,0:T(8,128)S(1)}, f32[1,3,128,128]{3,2,1,0:T(8,128)S(1)}, u32[]{:S(2)}, u32[]{:S(2)}) collective-permute-start(f32[1,3,128,128]{3,2,1,0:T(8,128)S(1)} %get-tuple-element.28), channel_id=1, source_target_pairs={{0,4},{4,0},{8,12},{12,8},{16,20},{20,16},{24,28},{28,24},{1,5},{5... | collective-permute-start | bytes 589832 | tf_op jit(solution)/shard_map/ppermute | solution.py:37
  13.1 11.7 %copy-start.33 = (f32[8]{0:T(128)}, f32[8]{0:T(128)S(1)}, u32[]{:S(2)}) copy-start(f32[8]{0:T(128)S(1)} %get-tuple-element.74) | copy-start | bytes 100
  13.1 11.7 %copy-start.34 = (f32[8]{0:T(128)}, f32[8]{0:T(128)S(1)}, u32[]{:S(2)}) copy-start(f32[8]{0:T(128)S(1)} %get-tuple-element.75) | copy-start | bytes 100
  13.1 11.7 %copy-start.35 = (f32[8]{0:T(128)}, f32[8]{0:T(128)S(1)}, u32[]{:S(2)}) copy-start(f32[8]{0:T(128)S(1)} %get-tuple-element.76) | copy-start | bytes 100
  13.1 11.7 %copy-start.36 = (f32[8]{0:T(128)}, f32[8]{0:T(128)S(1)}, u32[]{:S(2)}) copy-start(f32[8]{0:T(128)S(1)} %get-tuple-element.77) | copy-start | bytes 100
  13.2 11.6 %copy-start.37 = (f32[8]{0:T(128)}, f32[8]{0:T(128)S(1)}, u32[]{:S(2)}) copy-start(f32[8]{0:T(128)S(1)} %get-tuple-element.68) | copy-start | bytes 100
  13.2 11.6 %copy-start.38 = (f32[8]{0:T(128)}, f32[8]{0:T(128)S(1)}, u32[]{:S(2)}) copy-start(f32[8]{0:T(128)S(1)} %get-tuple-element.69) | copy-start | bytes 100
  13.2 11.7 %copy-start.39 = (f32[8]{0:T(128)}, f32[8]{0:T(128)S(1)}, u32[]{:S(2)}) copy-start(f32[8]{0:T(128)S(1)} %get-tuple-element.70) | copy-start | bytes 100
  13.2 11.7 %copy-start.40 = (f32[8]{0:T(128)}, f32[8]{0:T(128)S(1)}, u32[]{:S(2)}) copy-start(f32[8]{0:T(128)S(1)} %get-tuple-element.71) | copy-start | bytes 100
  23.2 1.8 %copy-start.13 = (f32[10,4,8,1152]{3,2,1,0:T(8,128)S(1)}, f32[10,4,8,1152]{3,2,1,0:T(8,128)}, u32[]{:S(2)}) copy-start(f32[10,4,8,1152]{3,2,1,0:T(8,128)} %param.12) | copy-start | bytes 4423684
  24.8 3.9 %copy-start.15 = (f32[10,2,8,1152]{3,2,1,0:T(8,128)}, f32[10,2,8,1152]{3,2,1,0:T(8,128)S(1)}, u32[]{:S(2)}) copy-start(f32[10,2,8,1152]{3,2,1,0:T(8,128)S(1)} %get-tuple-element.95) | copy-start | bytes 2211844
  24.8 3.9 %copy-start.17 = (f32[10,2,8,1152]{3,2,1,0:T(8,128)}, f32[10,2,8,1152]{3,2,1,0:T(8,128)S(1)}, u32[]{:S(2)}) copy-start(f32[10,2,8,1152]{3,2,1,0:T(8,128)S(1)} %get-tuple-element.96) | copy-start | bytes 2211844
  30.6 2.5 %collective-permute-start.7 = (f32[1,4,8,1152]{3,1,2,0:T(4,128)S(1)}, f32[1,4,8,1152]{3,1,2,0:T(4,128)S(1)}, u32[]{:S(2)}, u32[]{:S(2)}) collective-permute-start(f32[1,4,8,1152]{3,1,2,0:T(4,128)S(1)} %copy.99), channel_id=1, source_target_pairs={{0,4},{4,0},{8,12},{12,8},{16,20},{20,16},{24,28},{28,24},{1,5},{5... | collective-permute-start | bytes 442376 | tf_op jit(solution)/shard_map/ppermute | solution.py:37
  31.5 11.9 %collective-permute-start.5 = (f32[6,128,128]{2,1,0:T(8,128)}, f32[6,128,128]{2,1,0:T(8,128)S(1)}, u32[]{:S(2)}, u32[]{:S(2)}) collective-permute-start(f32[6,128,128]{2,1,0:T(8,128)} %pad_maximum_fusion.6), channel_id=1, source_target_pairs={{0,8},{4,20},{8,0},{12,28},{16,24},{20,4},{24,16},{28,12},{1,9},{5... | collective-permute-start | bytes 1179656 | tf_op jit(solution)/shard_map/ppermute | solution.py:237
  33.2 7.9 %collective-permute-start.8 = (f32[1,4,8,1152]{3,1,2,0:T(4,128)S(1)}, f32[1,4,8,1152]{3,1,2,0:T(4,128)S(1)}, u32[]{:S(2)}, u32[]{:S(2)}) collective-permute-start(f32[1,4,8,1152]{3,1,2,0:T(4,128)S(1)} %copy_add_fusion.1), channel_id=1, source_target_pairs={{0,8},{4,20},{8,0},{12,28},{16,24},{20,4},{24,16},{28,12},{1,9},{5... | collective-permute-start | bytes 442376 | tf_op jit(solution)/shard_map/ppermute | solution.py:61
  41.7 5.5 %collective-permute-start.9 = (f32[1,4,8,1152]{3,1,2,0:T(4,128)}, f32[1,4,8,1152]{3,1,2,0:T(4,128)}, u32[]{:S(2)}, u32[]{:S(2)}) collective-permute-start(f32[1,4,8,1152]{3,1,2,0:T(4,128)} %add.301), channel_id=1, source_target_pairs={{0,16},{4,12},{8,24},{12,4},{16,0},{20,28},{24,8},{28,20},{1,17},{... | collective-permute-start | bytes 442376 | tf_op jit(solution)/shard_map/ppermute | solution.py:61
  43.5 15.6 %collective-permute-start.6 = (f32[12,128,128]{2,1,0:T(8,128)S(1)}, f32[12,128,128]{2,1,0:T(8,128)S(1)}, u32[]{:S(2)}, u32[]{:S(2)}) collective-permute-start(f32[12,128,128]{2,1,0:T(8,128)S(1)} %pad_maximum_fusion.4), channel_id=1, source_target_pairs={{0,16},{4,12},{8,24},{12,4},{16,0},{20,28},{24,8},{28,20},{1,17},{... | collective-permute-start | bytes 2359304 | tf_op jit(solution)/shard_map/ppermute | solution.py:237
  48.2 8.5 %collective-permute-start.10 = (f32[4,1152]{1,0:T(4,128)S(1)}, f32[4,1152]{1,0:T(4,128)S(1)}, u32[]{:S(2)}, u32[]{:S(2)}) collective-permute-start(f32[4,1152]{1,0:T(4,128)S(1)} %get-tuple-element.61), channel_id=1, source_target_pairs={{1,2},{2,1},{5,6},{6,5},{9,10},{10,9},{13,14},{14,13},{17,18},{18,... | collective-permute-start | bytes 55304 | tf_op jit(solution)/shard_map/ppermute | solution.py:31
  48.9 9.5 %collective-permute-start.11 = (f32[4,1152]{1,0:T(4,128)S(1)}, f32[4,1152]{1,0:T(4,128)S(1)}, u32[]{:S(2)}, u32[]{:S(2)}) collective-permute-start(f32[4,1152]{1,0:T(4,128)S(1)} %get-tuple-element.62), channel_id=1, source_target_pairs={{0,1},{1,0},{2,3},{3,2},{4,5},{5,4},{6,7},{7,6},{8,9},{9,8},{10,11... | collective-permute-start | bytes 55304 | tf_op jit(solution)/shard_map/ppermute | solution.py:30
  61.0 4.2 %copy-start.21 = (f32[1,1,4,8,1152]{4,3,2,1,0:T(8,128)}, f32[1,1,4,8,1152]{4,3,2,1,0:T(8,128)S(1)}, u32[]{:S(2)}) copy-start(f32[1,1,4,8,1152]{4,3,2,1,0:T(8,128)S(1)} %get-tuple-element.26) | copy-start | bytes 442372
  61.0 4.2 %copy-start.23 = (f32[1,1,4,8,1152]{4,3,2,1,0:T(8,128)}, f32[1,1,4,8,1152]{4,3,2,1,0:T(8,128)S(1)}, u32[]{:S(2)}) copy-start(f32[1,1,4,8,1152]{4,3,2,1,0:T(8,128)S(1)} %get-tuple-element.25) | copy-start | bytes 442372
  61.1 4.2 %copy-start.25 = (f32[1,1,4,8,1152]{4,3,2,1,0:T(8,128)}, f32[1,1,4,8,1152]{4,3,2,1,0:T(8,128)S(1)}, u32[]{:S(2)}) copy-start(f32[1,1,4,8,1152]{4,3,2,1,0:T(8,128)S(1)} %get-tuple-element.24) | copy-start | bytes 442372
  61.1 4.2 %copy-start.19 = (f32[1,1,4,8,1152]{4,3,2,1,0:T(8,128)}, f32[1,1,4,8,1152]{4,3,2,1,0:T(8,128)S(1)}, u32[]{:S(2)}) copy-start(f32[1,1,4,8,1152]{4,3,2,1,0:T(8,128)S(1)} %get-tuple-element.23) | copy-start | bytes 442372
  61.8 3.5 %copy-start.27 = (f32[4,8,1152]{2,1,0:T(8,128)}, f32[4,8,1152]{2,1,0:T(8,128)S(1)}, u32[]{:S(2)}) copy-start(f32[4,8,1152]{2,1,0:T(8,128)S(1)} %get-tuple-element.30) | copy-start | bytes 442372
  62.0 4.2 %collective-permute-start.13 = (f32[3,4,1152]{2,1,0:T(4,128)S(1)}, f32[3,4,1152]{2,1,0:T(4,128)S(1)}, u32[]{:S(2)}, u32[]{:S(2)}) collective-permute-start(f32[3,4,1152]{2,1,0:T(4,128)S(1)} %get-tuple-element.65), channel_id=1, source_target_pairs={{0,1},{1,0},{2,3},{3,2},{4,5},{5,4},{6,7},{7,6},{8,9},{9,8},{10,11... | collective-permute-start | bytes 165896 | tf_op jit(solution)/shard_map/ppermute | solution.py:30
  64.0 2.1 %collective-permute-start.12 = (f32[3,4,1152]{2,1,0:T(4,128)S(1)}, f32[3,4,1152]{2,1,0:T(4,128)S(1)}, u32[]{:S(2)}, u32[]{:S(2)}) collective-permute-start(f32[3,4,1152]{2,1,0:T(4,128)S(1)} %get-tuple-element.66), channel_id=1, source_target_pairs={{1,2},{2,1},{5,6},{6,5},{9,10},{10,9},{13,14},{14,13},{17,18},{18,... | collective-permute-start | bytes 165896 | tf_op jit(solution)/shard_map/ppermute | solution.py:31
  66.9 8.7 %collective-permute-start.15 = (f32[4,8,1152]{2,0,1:T(4,128)S(1)}, f32[4,8,1152]{2,0,1:T(4,128)S(1)}, u32[]{:S(2)}, u32[]{:S(2)}) collective-permute-start(f32[4,8,1152]{2,0,1:T(4,128)S(1)} %fusion.89), channel_id=1, source_target_pairs={{0,1},{1,0},{2,3},{3,2},{4,5},{5,4},{6,7},{7,6},{8,9},{9,8},{10,11... | collective-permute-start | bytes 442376 | tf_op jit(solution)/shard_map/ppermute | solution.py:30
  70.9 4.7 %collective-permute-start.14 = (f32[4,8,1152]{2,0,1:T(4,128)S(1)}, f32[4,8,1152]{2,0,1:T(4,128)S(1)}, u32[]{:S(2)}, u32[]{:S(2)}) collective-permute-start(f32[4,8,1152]{2,0,1:T(4,128)S(1)} %fusion.89), channel_id=1, source_target_pairs={{1,2},{2,1},{5,6},{6,5},{9,10},{10,9},{13,14},{14,13},{17,18},{18,... | collective-permute-start | bytes 442376 | tf_op jit(solution)/shard_map/ppermute | solution.py:31
  71.6 34.2 %collective-permute-start.3 = (bf16[10,2,4,8,1152]{4,3,2,1,0:T(8,128)(2,1)}, bf16[10,2,4,8,1152]{4,3,2,1,0:T(8,128)(2,1)}, u32[]{:S(2)}, u32[]{:S(2)}) collective-permute-start(bf16[10,2,4,8,1152]{4,3,2,1,0:T(8,128)(2,1)} %param.11), channel_id=1, source_target_pairs={{0,1},{1,0},{2,3},{3,2},{4,5},{5,4},{6,7},{7,6},{8,9},{9,8},{10,11... | collective-permute-start | bytes 4423688 | tf_op jit(solution)/shard_map/ppermute | solution.py:30
  73.8 31.9 %collective-permute-start.2 = (bf16[10,2,4,8,1152]{4,3,2,1,0:T(8,128)(2,1)}, bf16[10,2,4,8,1152]{4,3,2,1,0:T(8,128)(2,1)}, u32[]{:S(2)}, u32[]{:S(2)}) collective-permute-start(bf16[10,2,4,8,1152]{4,3,2,1,0:T(8,128)(2,1)} %param.11), channel_id=1, source_target_pairs={{1,2},{2,1},{5,6},{6,5},{9,10},{10,9},{13,14},{14,13},{17,18},{18,... | collective-permute-start | bytes 4423688 | tf_op jit(solution)/shard_map/ppermute | solution.py:31
  76.5 2.1 %collective-permute-start.16 = (f32[1,4,24,1152]{3,1,2,0:T(4,128)}, f32[1,4,24,1152]{3,1,2,0:T(4,128)}, u32[]{:S(2)}, u32[]{:S(2)}) collective-permute-start(f32[1,4,24,1152]{3,1,2,0:T(4,128)} %maximum_bitcast_fusion), channel_id=1, source_target_pairs={{0,4},{4,0},{8,12},{12,8},{16,20},{20,16},{24,28},{28,24},{1,5},{5... | collective-permute-start | bytes 1327112 | tf_op jit(solution)/shard_map/ppermute | solution.py:37
  107.9 3.5 %copy-start.8 = (bf16[10,2,4,8,1152]{4,3,2,1,0:T(8,128)(2,1)}, bf16[10,2,4,8,1152]{4,3,2,1,0:T(8,128)(2,1)S(1)}, u32[]{:S(2)}) copy-start(bf16[10,2,4,8,1152]{4,3,2,1,0:T(8,128)(2,1)S(1)} %get-tuple-element.12) | copy-start | bytes 4423684
  107.9 3.5 %copy-start.10 = (bf16[10,2,4,8,1152]{4,3,2,1,0:T(8,128)(2,1)}, bf16[10,2,4,8,1152]{4,3,2,1,0:T(8,128)(2,1)S(1)}, u32[]{:S(2)}) copy-start(bf16[10,2,4,8,1152]{4,3,2,1,0:T(8,128)(2,1)S(1)} %get-tuple-element.11) | copy-start | bytes 4423684
  111.4 3.4 %copy-start.14 = (f32[10,4,8,1152]{3,2,1,0:T(8,128)S(1)}, f32[10,4,8,1152]{3,2,1,0:T(8,128)}, u32[]{:S(2)}) copy-start(f32[10,4,8,1152]{3,2,1,0:T(8,128)} %param.12) | copy-start | bytes 4423684
  111.4 3.4 %copy-start.16 = (f32[10,2,8,1152]{3,2,1,0:T(8,128)S(1)}, f32[10,2,8,1152]{3,2,1,0:T(8,128)}, u32[]{:S(2)}) copy-start(f32[10,2,8,1152]{3,2,1,0:T(8,128)} %copy-done.15) | copy-start | bytes 2211844
  111.4 3.4 %copy-start.18 = (f32[10,2,8,1152]{3,2,1,0:T(8,128)S(1)}, f32[10,2,8,1152]{3,2,1,0:T(8,128)}, u32[]{:S(2)}) copy-start(f32[10,2,8,1152]{3,2,1,0:T(8,128)} %copy-done.17) | copy-start | bytes 2211844
  119.6 3.2 %copy-start.11 = (f32[10,4,16,1152]{3,2,1,0:T(8,128)}, f32[10,4,16,1152]{3,2,1,0:T(8,128)S(1)}, u32[]{:S(2)}) copy-start(f32[10,4,16,1152]{3,2,1,0:T(8,128)S(1)} %fusion.6) | copy-start | bytes 8847364
  124.6 1.4 collective-permute-start.17
  126.1 5.2 %collective-permute-start.18 = (f32[1,4,8,1152]{3,1,2,0:T(4,128)S(1)}, f32[1,4,8,1152]{3,1,2,0:T(4,128)S(1)}, u32[]{:S(2)}, u32[]{:S(2)}) collective-permute-start(f32[1,4,8,1152]{3,1,2,0:T(4,128)S(1)} %copy_add_fusion), channel_id=1, source_target_pairs={{0,8},{4,20},{8,0},{12,28},{16,24},{20,4},{24,16},{28,12},{1,9},{5... | collective-permute-start | bytes 442376 | tf_op jit(solution)/shard_map/ppermute | solution.py:61
  131.4 14.0 %copy-start.31 = (f32[3,4,1152]{2,1,0:T(4,128)S(1)}, f32[3,4,1152]{2,1,0:T(4,128)}, u32[]{:S(2)}) copy-start(f32[3,4,1152]{2,1,0:T(4,128)} %copy-done.30) | copy-start | bytes 165892
  131.4 14.2 %copy-start.26 = (f32[1,1,4,8,1152]{4,3,2,1,0:T(8,128)S(1)}, f32[1,1,4,8,1152]{4,3,2,1,0:T(8,128)}, u32[]{:S(2)}) copy-start(f32[1,1,4,8,1152]{4,3,2,1,0:T(8,128)} %copy-done.25) | copy-start | bytes 442372
  131.4 5.2 %collective-permute-start.19 = (f32[1,4,8,1152]{3,1,2,0:T(4,128)S(1)}, f32[1,4,8,1152]{3,1,2,0:T(4,128)S(1)}, u32[]{:S(2)}, u32[]{:S(2)}) collective-permute-start(f32[1,4,8,1152]{3,1,2,0:T(4,128)S(1)} %add.340), channel_id=1, source_target_pairs={{0,16},{4,12},{8,24},{12,4},{16,0},{20,28},{24,8},{28,20},{1,17},{... | collective-permute-start | bytes 442376 | tf_op jit(solution)/shard_map/ppermute | solution.py:61
  136.7 6.2 %collective-permute-start.20 = (f32[4,1152]{1,0:T(4,128)S(1)}, f32[4,1152]{1,0:T(4,128)S(1)}, u32[]{:S(2)}, u32[]{:S(2)}) collective-permute-start(f32[4,1152]{1,0:T(4,128)S(1)} %get-tuple-element.55), channel_id=1, source_target_pairs={{1,2},{2,1},{5,6},{6,5},{9,10},{10,9},{13,14},{14,13},{17,18},{18,... | collective-permute-start | bytes 55304 | tf_op jit(solution)/shard_map/ppermute | solution.py:31
  137.3 8.4 %copy-start.20 = (f32[1,1,4,8,1152]{4,3,2,1,0:T(8,128)S(1)}, f32[1,1,4,8,1152]{4,3,2,1,0:T(8,128)}, u32[]{:S(2)}) copy-start(f32[1,1,4,8,1152]{4,3,2,1,0:T(8,128)} %copy-done.19) | copy-start | bytes 442372
  137.3 8.4 %copy-start.28 = (f32[4,8,1152]{2,1,0:T(8,128)S(1)}, f32[4,8,1152]{2,1,0:T(8,128)}, u32[]{:S(2)}) copy-start(f32[4,8,1152]{2,1,0:T(8,128)} %copy-done.27) | copy-start | bytes 442372
  137.4 7.2 %collective-permute-start.21 = (f32[4,1152]{1,0:T(4,128)S(1)}, f32[4,1152]{1,0:T(4,128)S(1)}, u32[]{:S(2)}, u32[]{:S(2)}) collective-permute-start(f32[4,1152]{1,0:T(4,128)S(1)} %get-tuple-element.56), channel_id=1, source_target_pairs={{0,1},{1,0},{2,3},{3,2},{4,5},{5,4},{6,7},{7,6},{8,9},{9,8},{10,11... | collective-permute-start | bytes 55304 | tf_op jit(solution)/shard_map/ppermute | solution.py:30
  145.1 1.0 copy-start.22
  145.1 1.0 copy-start.29
  146.6 5.8 %collective-permute-start.22 = (f32[4,4,1152]{2,0,1:T(4,128)S(1)}, f32[4,4,1152]{2,0,1:T(4,128)S(1)}, u32[]{:S(2)}, u32[]{:S(2)}) collective-permute-start(f32[4,4,1152]{2,0,1:T(4,128)S(1)} %get-tuple-element.49), channel_id=1, source_target_pairs={{1,2},{2,1},{5,6},{6,5},{9,10},{10,9},{13,14},{14,13},{17,18},{18,... | collective-permute-start | bytes 221192 | tf_op jit(solution)/shard_map/ppermute | solution.py:31
  147.5 7.2 %collective-permute-start.23 = (f32[4,4,1152]{2,0,1:T(4,128)S(1)}, f32[4,4,1152]{2,0,1:T(4,128)S(1)}, u32[]{:S(2)}, u32[]{:S(2)}) collective-permute-start(f32[4,4,1152]{2,0,1:T(4,128)S(1)} %get-tuple-element.50), channel_id=1, source_target_pairs={{0,1},{1,0},{2,3},{3,2},{4,5},{5,4},{6,7},{7,6},{8,9},{9,8},{10,11... | collective-permute-start | bytes 221192 | tf_op jit(solution)/shard_map/ppermute | solution.py:30
  154.8 2.4 %collective-permute-start.24 = (f32[1,4,16,1152]{3,1,2,0:T(4,128)S(1)}, f32[1,4,16,1152]{3,1,2,0:T(4,128)}, u32[]{:S(2)}, u32[]{:S(2)}) collective-permute-start(f32[1,4,16,1152]{3,1,2,0:T(4,128)S(1)} %maximum_bitcast_fusion.1), channel_id=1, source_target_pairs={{0,4},{4,0},{8,12},{12,8},{16,20},{20,16},{24,28},{28,24},{1,5},{5... | collective-permute-start | bytes 884744 | tf_op jit(solution)/shard_map/ppermute | solution.py:37
  154.9 2.1 %copy-start.9 = (bf16[10,2,4,8,1152]{4,3,2,1,0:T(8,128)(2,1)S(1)}, bf16[10,2,4,8,1152]{4,3,2,1,0:T(8,128)(2,1)}, u32[]{:S(2)}) copy-start(bf16[10,2,4,8,1152]{4,3,2,1,0:T(8,128)(2,1)} %copy-done.8) | copy-start | bytes 4423684
  162.0 2.3 %copy-start.12 = (f32[10,4,16,1152]{3,2,1,0:T(8,128)S(1)}, f32[10,4,16,1152]{3,2,1,0:T(8,128)}, u32[]{:S(2)}) copy-start(f32[10,4,16,1152]{3,2,1,0:T(8,128)} %copy-done.11) | copy-start | bytes 8847364
  (2 other events, 1.6 us)

commit v2 on v1

--- a/solution.py
+++ b/solution.py
@@ -12,24 +12,44 @@
 ITERS = 2
 LANES = 128
 OBS_CHUNK = 1024
+PART_EVENTS = ("forward", "chip0", "chip1", "adjoint", None)
+PARTS = len(PART_EVENTS)
+EVEN, CORE, HAS_FIRST, HAS_SECOND, HAS_BELOW, HAS_ABOVE = range(6)
 
 
 step_size = 0.3
 
 
-def band_exchange(to_prev, to_next):
-    count = lax.axis_size("lat")
-    even = lax.axis_index("lat") % 2 == 0
-    first = [(i, i ^ 1) for i in range(count) if i ^ 1 < count]
-    second = [(i, ((i + 1) ^ 1) - 1) for i in range(count) if 0 <= ((i + 1) ^ 1) - 1 < count]
-    if to_prev is to_next:
-        send_first = send_second = to_prev
-    else:
-        send_first = jnp.where(even, to_next, to_prev)
-        send_second = jnp.where(even, to_prev, to_next)
-    got_first = lax.ppermute(send_first, "lat", first)
-    got_second = lax.ppermute(send_second, "lat", second)
-    return jnp.where(even, got_second, got_first), jnp.where(even, got_first, got_second)
+def band_pairs(second):
+    bands, groups = lax.axis_size("lat"), lax.axis_size("mem")
+    perm = []
+    for group in range(groups):
+        for band in range(bands):
+            other = ((band + second) ^ 1) - second
+            if 0 <= other < bands:
+                target = group * bands + other
+            else:
+                target = (group ^ 1) * bands + band
+            perm.append((group * bands + band, target))
+    return perm
+
+
+def band_swap(send_first, send_second):
+    axes = ("mem", "lat")
+    return (
+        lax.ppermute(send_first, axes, band_pairs(0)),
+        lax.ppermute(send_second, axes, band_pairs(1)),
+    )
+
+
+def band_sides():
+    band = lax.axis_index("lat")
+    return band % 2 == 0, band > 0, band < lax.axis_size("lat") - 1
+
+
+def by_partner(to_prev, to_next):
+    even, _, _ = band_sides()
+    return jnp.where(even, to_next, to_prev), jnp.where(even, to_prev, to_next)
 
 
 def core_swap(cells):
@@ -52,22 +72,6 @@
     mine = lax.dynamic_slice_in_dim(cells, core * half, half, 0)
     other = lax.dynamic_slice_in_dim(cells, (1 - core) * half, half, 0)
     return mine, other
-
-
-def member_sum(cells):
-    mine, other = core_split(cells)
-    total = mine + core_swap(other)
-    for perm in chip_steps():
-        total = total + lax.ppermute(total, "mem", perm)
-    return total
-
-
-def both_halves(mine):
-    core = lax.axis_index("mem") % 2
-    other = core_swap(mine)
-    return jnp.concatenate(
-        [jnp.where(core == 0, mine, other), jnp.where(core == 0, other, mine)], axis=0
-    )
 
 
 def split_two(x):
@@ -227,77 +231,325 @@
     )(marks, slots)
 
 
-def observation_fields(tiles, counts, index, value, weight, var_count, lev_count, row_count, lon_cells):
+def observation_slots(tiles, counts, index, value, weight, var_count, lev_count, row_count):
     slots = tile_sums(tiles, counts, index, value, weight, var_count, lev_count, row_count)
-    core = lax.axis_index("mem") % 2
-    by_var = slots.transpose(1, 0, 2, 3)
-    mine, other = core_split(by_var)
-    held = jnp.concatenate([mine[0], core_swap(other)[0]], axis=0)
-    for perm in chip_steps():
-        held = jnp.concatenate([held, lax.ppermute(held, "mem", perm)], axis=0)
-    return band_fields(held, lon_cells)
-
-
-def pull_columns(weights, cells):
-    odd = weights[1] * (0.5 * (cells + jnp.roll(cells, -1, axis=-1)))
-    return weights[0] * cells + 0.5 * (odd + jnp.roll(odd, 1, axis=-1))
-
-
-def observed_adjoint(inc, below, above, fields, rims, band_index, band_count):
-    weights, pulls = fields
-    south = band_index == 0
-    north = band_index == band_count - 1
-    first, last = inc[:, 0], inc[:, -1]
-    lower = jnp.where(south, first, below)
-    upper = jnp.where(north, last, above)
-    down = jnp.concatenate([lower[:, None], inc[:, :-1]], axis=1)
-    up = jnp.concatenate([inc[:, 1:], upper[:, None]], axis=1)
-    even = pull_columns(weights[:, 0], 0.75 * inc + 0.25 * down) - pulls[0]
-    odd = pull_columns(weights[:, 1], 0.75 * inc + 0.25 * up) - pulls[1]
-    (rim_weight_below, rim_pull_below), (rim_weight_above, rim_pull_above) = rims
-    odd_below = pull_columns(rim_weight_below, 0.75 * below + 0.25 * first) - rim_pull_below
-    even_above = pull_columns(rim_weight_above, 0.75 * above + 0.25 * last) - rim_pull_above
-    odd_below = jnp.where(south, even[:, 0], odd_below)
-    even_above = jnp.where(north, odd[:, -1], even_above)
-    odd_down = jnp.concatenate([odd_below[:, None], odd[:, :-1]], axis=1)
-    even_up = jnp.concatenate([even[:, 1:], even_above[:, None]], axis=1)
-    return 0.75 * (even + odd) + 0.25 * (odd_down + even_up)
-
-
-def forward_rows(cells, coeffs, row_count, half_band):
-    running = jnp.zeros(cells.shape[:2] + (row_count, cells.shape[3]), jnp.float32)
-    for offset in range(2 * half_band + 1):
-        running = running + coeffs[:, offset][None, None, :, None] * cells[:, :, offset : offset + row_count]
-    return running
-
-
-def backward_rows(cells, coeffs, row_count, half_band):
-    running = jnp.zeros(cells.shape[:2] + (row_count, cells.shape[3]), jnp.float32)
-    for offset in range(2 * half_band + 1):
-        at = 2 * half_band - offset
-        running = (
-            running
-            + coeffs[at : at + row_count, offset][None, None, :, None] * cells[:, :, at : at + row_count]
+    mine, other = core_split(slots.transpose(1, 0, 2, 3))
+    return jnp.concatenate([mine[0], core_swap(other)[0]], axis=0)
+
+
+def pull_columns(weight, odd_weight, cells):
+    lon = cells.shape[-1]
+    odd = odd_weight * (0.5 * (cells + pltpu.roll(cells, lon - 1, cells.ndim - 1)))
+    return weight * cells + 0.5 * (odd + pltpu.roll(odd, 1, cells.ndim - 1))
+
+
+def observe_kernel(
+    flag_ref, inc_ref, first_ref, second_ref, weight_ref, pull_ref, rim_first_ref, rim_second_ref, out_ref
+):
+    even = flag_ref[EVEN] == 1
+    has_below, has_above = flag_ref[HAS_BELOW] == 1, flag_ref[HAS_ABOVE] == 1
+    levels, rows, lon = inc_ref.shape
+    first, second = first_ref[...], second_ref[...]
+    lowest = jnp.concatenate([inc_ref[lev, 0:1] for lev in range(levels)], axis=0)
+    highest = jnp.concatenate([inc_ref[lev, rows - 1 : rows] for lev in range(levels)], axis=0)
+    below = jnp.where(has_below, jnp.where(even, second, first), lowest)
+    above = jnp.where(has_above, jnp.where(even, first, second), highest)
+    rim_below = [jnp.where(even, rim_second_ref[i], rim_first_ref[i]) for i in range(3)]
+    rim_above = [jnp.where(even, rim_first_ref[i], rim_second_ref[i]) for i in range(3)]
+    odd_below = pull_columns(rim_below[0], rim_below[1], 0.75 * below + 0.25 * lowest) - rim_below[2]
+    even_above = pull_columns(rim_above[0], rim_above[1], 0.75 * above + 0.25 * highest) - rim_above[2]
+    row = lax.broadcasted_iota(jnp.int32, (rows, lon), 0)
+    for lev in range(levels):
+        cells = inc_ref[lev]
+        down = jnp.where(row == 0, below[lev : lev + 1], pltpu.roll(cells, 1, 0))
+        up = jnp.where(row == rows - 1, above[lev : lev + 1], pltpu.roll(cells, rows - 1, 0))
+        low = pull_columns(weight_ref[0, 0, lev], weight_ref[1, 0, lev], 0.75 * cells + 0.25 * down) - pull_ref[0, lev]
+        high = pull_columns(weight_ref[0, 1, lev], weight_ref[1, 1, lev], 0.75 * cells + 0.25 * up) - pull_ref[1, lev]
+        from_below = jnp.where(has_below, odd_below[lev : lev + 1], low[0:1])
+        from_above = jnp.where(has_above, even_above[lev : lev + 1], high[rows - 1 : rows])
+        high_down = jnp.where(row == 0, from_below, pltpu.roll(high, 1, 0))
+        low_up = jnp.where(row == rows - 1, from_above, pltpu.roll(low, rows - 1, 0))
+        out_ref[lev] = 0.75 * (low + high) + 0.25 * (high_down + low_up)
+
+
+def row_groups(lines):
+    starts = list(range(0, lines - 7, 8))
+    return starts if starts[-1] + 8 == lines else starts + [lines - 8]
+
+
+def strided(ref, chunk, start, rows):
+    return ref[chunk, pl.ds(start, 8, stride=rows), :]
+
+
+def to_chunks(ref, cells):
+    for chunk in range(ref.shape[0]):
+        ref[chunk] = cells[:, chunk * LANES : (chunk + 1) * LANES]
+
+
+def spread_rows(cells, coef_ref, base, taps):
+    out = []
+    for row in range(len(cells) - taps + 1):
+        total = coef_ref[base + row * taps] * cells[row]
+        for tap in range(1, taps):
+            total += coef_ref[base + row * taps + tap] * cells[row + tap]
+        out.append(total)
+    return out
+
+
+def pull_rows(cells, coef_ref, base, taps):
+    out = []
+    for row in range(len(cells) - taps + 1):
+        total = coef_ref[base + row * taps] * cells[row + taps - 1]
+        for tap in range(1, taps):
+            total += coef_ref[base + row * taps + tap] * cells[row + taps - 1 - tap]
+        out.append(total)
+    return out
+
+
+def sum_members(spread_ref, zonal_ref, members_ref, inc_ref):
+    size, variables, levels, rows, lon = members_ref.shape
+    spread = jnp.concatenate(
+        [spread_ref[chunk].astype(jnp.bfloat16) for chunk in range(spread_ref.shape[0])], axis=1
+    )
+    wide = LANES * 3 if lon % (LANES * 3) == 0 else LANES
+    for start in range(0, lon, wide):
+        lanes = slice(start, start + wide)
+        localized = jnp.dot(spread, zonal_ref[:, lanes], preferred_element_type=jnp.float32)
+        localized = localized.reshape(size, levels, rows, wide)
+        for var in range(variables):
+            total = members_ref[0, var, :, :, lanes].astype(jnp.float32) * localized[0]
+            for k in range(1, size):
+                total += members_ref[k, var, :, :, lanes].astype(jnp.float32) * localized[k]
+            inc_ref[var, :, :, lanes] = total
+
+
+def edge_kernel(alpha_ref, first_ref, second_ref):
+    even = lax.rem(lax.axis_index("lat"), 2) == 0
+    lines, rows = alpha_ref.shape[:2]
+    half = first_ref.shape[0] // lines
+
+    def step(pair, carry):
+        one, two = alpha_ref[2 * pair], alpha_ref[2 * pair + 1]
+        here = pl.ds(pl.multiple_of(pair * 2 * half, 8), 2 * half)
+        head = jnp.concatenate([one[:half], two[:half]], axis=0)
+        tail = jnp.concatenate([one[rows - half :], two[rows - half :]], axis=0)
+        first_ref[here, :] = jnp.where(even, tail, head)
+        second_ref[here, :] = jnp.where(even, head, tail)
+        return carry
+
+    lax.fori_loop(0, lines // 2, step, 0, unroll=2)
+
+
+def forward_kernel(
+    flag_ref,
+    coef_ref,
+    alpha_ref,
+    first_ref,
+    second_ref,
+    zonal_ref,
+    members_ref,
+    inc_ref,
+    own_ref,
+    below_ref,
+    above_ref,
+    spread_ref,
+):
+    rows = members_ref.shape[3]
+    half_band = first_ref.shape[0] * rows // alpha_ref.shape[0]
+    taps = 2 * half_band + 1
+    even = flag_ref[EVEN] == 1
+    to_chunks(own_ref, alpha_ref[...])
+    first = jnp.where(flag_ref[HAS_FIRST] == 1, first_ref[...], 0.0)
+    second = jnp.where(flag_ref[HAS_SECOND] == 1, second_ref[...], 0.0)
+    to_chunks(below_ref, jnp.where(even, second, first))
+    to_chunks(above_ref, jnp.where(even, first, second))
+
+    def step(chunk, carry):
+        for start in row_groups(own_ref.shape[1] // rows):
+            cells = wide_rows(own_ref, below_ref, above_ref, chunk, start, rows, half_band)
+            for r, total in enumerate(spread_rows(cells, coef_ref, 0, taps)):
+                spread_ref[chunk, pl.ds(start * rows + r, 8, stride=rows), :] = total
+        return carry
+
+    lax.fori_loop(0, own_ref.shape[0], step, 0)
+    sum_members(spread_ref, zonal_ref, members_ref, inc_ref)
+
+
+def wide_rows(own_ref, below_ref, above_ref, chunk, start, rows, half_band):
+    below = [strided(below_ref, chunk, start * half_band + r, half_band) for r in range(half_band)]
+    own = [strided(own_ref, chunk, start * rows + r, rows) for r in range(rows)]
+    above = [strided(above_ref, chunk, start * half_band + r, half_band) for r in range(half_band)]
+    return below + own + above
+
+
+def zonal_back(flag_ref, adjoints, members, zonal_ref, weighted_ref, back_ref):
+    lines = back_ref.shape[1] // 3
+    even, core = flag_ref[EVEN], flag_ref[CORE]
+    places = (lines, even * (2 * lines), (1 - even) * (2 * lines))
+    there = (None, flag_ref[HAS_FIRST] == 1, flag_ref[HAS_SECOND] == 1)
+    for number, (place, parts) in enumerate(zip(places, members)):
+        mine_ref, other_ref = adjoints[2 * number : 2 * number + 2]
+        done = 0
+        for part_ref in parts:
+            size, _, levels, rows, lon = part_ref.shape
+            flat = levels * rows
+
+            def step(
+                k, carry, part_ref=part_ref, mine_ref=mine_ref, other_ref=other_ref, place=place, done=done, number=number
+            ):
+                total = part_ref[k, core].astype(jnp.float32) * mine_ref[...]
+                total += part_ref[k, 1 - core].astype(jnp.float32) * other_ref[...]
+                if there[number] is not None:
+                    total = jnp.where(there[number], total, 0.0)
+                at = pl.multiple_of(place + (k + done) * flat, 16)
+                weighted_ref[pl.ds(at, flat), :] = total.reshape(flat, lon).astype(jnp.bfloat16)
+                return carry
+
+            lax.fori_loop(0, size, step, 0)
+            done += size
+    lon = zonal_ref.shape[0]
+    wide = LANES * 3 if lon % (LANES * 3) == 0 else LANES
+    for tile in range(3):
+        here = slice(tile * lines, (tile + 1) * lines)
+        weighted = weighted_ref[here, :]
+        for start in range(0, lon, wide):
+            back = lax.dot_general(
+                weighted,
+                zonal_ref[start : start + wide, :],
+                (((1,), (1,)), ((), ())),
+                preferred_element_type=jnp.float32,
+            )
+            for part in range(wide // LANES):
+                back_ref[start // LANES + part, here, :] = back[:, part * LANES : (part + 1) * LANES]
+
+
+def back_rows(back_ref, chunk, start, rows, halo):
+    lines = back_ref.shape[1] // 3
+    return [
+        strided(back_ref, chunk, (at // rows) * lines + start * rows + at % rows, rows)
+        for at in range(rows - halo, 2 * rows + halo)
+    ]
+
+
+def between_kernel(parts, *refs):
+    flag_ref, coef_ref, own_ref, below_ref, above_ref, zonal_ref = refs[:6]
+    adjoints = refs[6:12]
+    members_ref = refs[12]
+    partners = refs[13 : 13 + 2 * parts]
+    inc_ref, current_ref, weighted_ref, back_ref, spread_ref = refs[13 + 2 * parts :]
+    rows = members_ref.shape[3]
+    lines = own_ref.shape[1]
+    half_band = below_ref.shape[1] * rows // lines
+    taps = 2 * half_band + 1
+    zonal_back(
+        flag_ref, adjoints, ((members_ref,), partners[:parts], partners[parts:]), zonal_ref, weighted_ref, back_ref
+    )
+
+    def step(chunk, carry):
+        for start in row_groups(lines // rows):
+            back = back_rows(back_ref, chunk, start, rows, 2 * half_band)
+            pulled = pull_rows(back, coef_ref, rows * taps, taps)
+            cells = wide_rows(own_ref, below_ref, above_ref, chunk, start, rows, half_band)
+            cells = [c - step_size * (c + p) for c, p in zip(cells, pulled)]
+            for r in range(rows):
+                current_ref[chunk, pl.ds(start * rows + r, 8, stride=rows), :] = cells[half_band + r]
+            for r, total in enumerate(spread_rows(cells, coef_ref, 0, taps)):
+                spread_ref[chunk, pl.ds(start * rows + r, 8, stride=rows), :] = total
+        return carry
+
+    lax.fori_loop(0, own_ref.shape[0], step, 0)
+    sum_members(spread_ref, zonal_ref, members_ref, inc_ref)
+
+
+def last_kernel(parts, taps, *refs):
+    flag_ref, coef_ref, own_ref, zonal_ref = refs[:4]
+    adjoints = refs[4:10]
+    members_ref = refs[10]
+    partners = refs[11 : 11 + 2 * parts]
+    out_ref, weighted_ref, back_ref, current_ref = refs[11 + 2 * parts :]
+    rows = members_ref.shape[3]
+    half_band = taps // 2
+    zonal_back(
+        flag_ref, adjoints, ((members_ref,), partners[:parts], partners[parts:]), zonal_ref, weighted_ref, back_ref
+    )
+
+    def step(chunk, carry):
+        for start in row_groups(own_ref.shape[1] // rows):
+            back = back_rows(back_ref, chunk, start, rows, half_band)
+            for r, pulled in enumerate(pull_rows(back, coef_ref, (rows + half_band) * taps, taps)):
+                here = pl.ds(start * rows + r, 8, stride=rows)
+                cell = own_ref[chunk, here, :]
+                current_ref[chunk, here, :] = cell - step_size * (cell + pulled)
+        return carry
+
+    lax.fori_loop(0, own_ref.shape[0], step, 0)
+    for chunk in range(own_ref.shape[0]):
+        out_ref[:, chunk * LANES : (chunk + 1) * LANES] = current_ref[chunk]
+
+
+def call(kernel, operands, outs, scratch, flops):
+    vmem = pl.BlockSpec(memory_space=pltpu.VMEM)
+    moved = sum(int(np.prod(x.shape)) * x.dtype.itemsize for x in list(operands) + list(outs))
+    return pl.pallas_call(
+        kernel,
+        in_specs=[pl.BlockSpec(memory_space=pltpu.SMEM)] + [vmem] * (len(operands) - 1),
+        out_specs=[vmem] * len(outs),
+        out_shape=list(outs),
+        scratch_shapes=list(scratch),
+        compiler_params=pltpu.CompilerParams(vmem_limit_bytes=28 * 2**20),
+        cost_estimate=pl.CostEstimate(flops=flops, bytes_accessed=moved, transcendentals=0),
+    )(*operands)
+
+
+def coefficient_kernel(rows, coef_ref, out_ref):
+    count, taps = coef_ref.shape
+    half_band = taps // 2
+    first = lax.axis_index("lat") * rows
+
+    def write(place, row, tap, on_grid):
+        value = jnp.where(on_grid, coef_ref[jnp.clip(row, 0, count - 1), tap], 0.0)
+        out_ref[place] = jnp.full(out_ref.shape[1:], value, jnp.float32)
+
+    def forward(row, carry):
+        for tap in range(taps):
+            write(row * taps + tap, first + row, tap, True)
+        return carry
+
+    def backward(row, carry):
+        target = first + row - half_band
+        for tap in range(taps):
+            source = target + half_band - tap
+            on_grid = (target >= 0) & (target < count) & (source >= 0) & (source < count)
+            write((rows + row) * taps + tap, source, tap, on_grid)
+        return carry
+
+    lax.fori_loop(0, rows, forward, 0)
+    lax.fori_loop(0, rows + 2 * half_band, backward, 0)
+
+
+def stencil_coefficients(merid_coef, rows):
+    taps = merid_coef.shape[1]
+    shape = ((2 * rows + taps - 1) * taps, 8, LANES)
+    return pl.pallas_call(
+        functools.partial(coefficient_kernel, rows),
+        in_specs=[pl.BlockSpec(memory_space=pltpu.SMEM)],
+        out_specs=pl.BlockSpec(memory_space=pltpu.VMEM),
+        out_shape=jax.ShapeDtypeStruct(shape, jnp.float32),
+        cost_estimate=pl.CostEstimate(flops=0, bytes_accessed=shape[0] * 4096, transcendentals=0),
+    )(merid_coef)
+
+
+def band_setup(held, lev_count, rows, lon_cells):
+    weights, pulls = band_fields(held, lon_cells)
+    weights = weights.reshape(2, 2, lev_count, rows, lon_cells)
+    pulls = pulls.reshape(2, lev_count, rows, lon_cells)
+    rims = band_swap(
+        *by_partner(
+            jnp.concatenate([weights[:, 0, :, 0], pulls[None, 0, :, 0]]),
+            jnp.concatenate([weights[:, 1, :, -1], pulls[None, 1, :, -1]]),
         )
-    return running
-
-
-def partial_increment(ext, coeffs, zonal_loc, members, half_band):
-    spread = forward_rows(ext, coeffs, members.shape[3], half_band).astype(jnp.bfloat16)
-    localized = jnp.dot(
-        spread.reshape(-1, spread.shape[-1]), zonal_loc, preferred_element_type=jnp.float32
-    ).reshape(spread.shape)
-    return jnp.sum(members * localized[:, None], axis=0)
-
-
-def zonal_backward(members, adjoint, zonal_loc):
-    weighted = jnp.sum(members * adjoint[None], axis=1).astype(jnp.bfloat16)
-    return lax.dot_general(
-        weighted.reshape(-1, weighted.shape[-1]),
-        zonal_loc,
-        (((1,), (1,)), ((), ())),
-        preferred_element_type=jnp.float32,
-    ).reshape(weighted.shape)
+    )
+    return weights, pulls, rims
 
 
 def body(
@@ -305,16 +557,38 @@
 ):
     half_band = merid_coef.shape[1] // 2
     _, var_count, lev_count, rows, lon_cells = members.shape
-    band_index = lax.axis_index("lat")
-    band_count = lax.axis_size("lat")
     slot_count = slot_tile.shape[-1]
 
-    below, above = band_exchange(alpha[:, :, :half_band], alpha[:, :, -half_band:])
-    ext = jnp.concatenate([below, alpha, above], axis=2)
-    sent, below = lax.optimization_barrier((members, below))
-    members_below, members_above = band_exchange(sent, sent)
-
-    weights, pulls = observation_fields(
+    members_per = members.shape[0]
+    lines = members_per * lev_count * rows
+    even, has_below, has_above = band_sides()
+    first_there = jnp.where(even, has_above, has_below)
+    second_there = jnp.where(even, has_below, has_above)
+    core = lax.axis_index("mem") % 2
+    flags = jnp.stack(
+        [x.astype(jnp.int32) for x in (even, core, first_there, second_there, has_below, has_above)]
+    )
+
+    edge_lines = members_per * lev_count * half_band
+    edge_shape = jax.ShapeDtypeStruct((edge_lines, lon_cells), jnp.float32)
+    vmem = pl.BlockSpec(memory_space=pltpu.VMEM)
+    sends = pl.pallas_call(
+        edge_kernel,
+        in_specs=[vmem],
+        out_specs=[vmem, vmem],
+        out_shape=[edge_shape, edge_shape],
+        compiler_params=pltpu.CompilerParams(vmem_limit_bytes=16 * 2**20),
+        cost_estimate=pl.CostEstimate(flops=0, bytes_accessed=16 * edge_lines * lon_cells, transcendentals=0),
+    )(alpha.reshape(-1, rows, lon_cells))
+    obs_index, obs_value, obs_weight, sends = lax.optimization_barrier((obs_index, obs_value, obs_weight, sends))
+    halo_first, halo_second = band_swap(*sends)
+    coeffs = stencil_coefficients(merid_coef, rows)
+    own = alpha.reshape(lines, lon_cells)
+
+    cuts = [0] + [members_per * (i + 1) // PARTS for i in range(PARTS)]
+    parts = [members[x:y] for x, y in zip(cuts[:-1], cuts[1:])]
+
+    held = observation_slots(
         slot_tile.reshape(-1),
         obs_count.reshape(-1),
         obs_index.reshape(slot_count, -1),
@@ -323,47 +597,82 @@
         var_count,
         lev_count,
         rows,
-        lon_cells,
-    )
-    weights = weights.reshape(2, 2, lev_count, rows, lon_cells)
-    pulls = pulls.reshape(2, lev_count, rows, lon_cells)
-    rim_below, rim_above = band_exchange(
-        jnp.concatenate([weights[:, 0, :, 0], pulls[None, 0, :, 0]]),
-        jnp.concatenate([weights[:, 1, :, -1], pulls[None, 1, :, -1]]),
-    )
-    rims = (rim_below[:2], rim_below[2]), (rim_above[:2], rim_above[2])
-
-    coef_wide = jnp.pad(merid_coef, ((rows, rows), (0, 0)))
-    coef_wide = lax.dynamic_slice_in_dim(coef_wide, band_index * rows, 3 * rows, 0)
-    own_coef = coef_wide[rows : 2 * rows]
-    row_at = band_index * rows + jnp.arange(-half_band, rows + half_band)
-    on_grid = ((row_at >= 0) & (row_at < band_count * rows))[None, None, :, None]
-
+    )
+    steps = chip_steps()
+    for number, perm in enumerate(steps):
+        if number == len(steps) - 1:
+            halo_first, halo_second, held = lax.optimization_barrier((halo_first, halo_second, held))
+        held = jnp.concatenate([held, lax.ppermute(held, "mem", perm)], axis=0)
+    fetched = [band_swap(part, part) for part in parts]
+
+    def pin(value, event):
+        for number, name in enumerate(PART_EVENTS):
+            if name == event:
+                value, fetched[number] = lax.optimization_barrier((value, fetched[number]))
+        return value
+
+    inc_shape = jax.ShapeDtypeStruct((var_count, lev_count, rows, lon_cells), jnp.float32)
+    line_shape = jax.ShapeDtypeStruct((lines, lon_cells), jnp.float32)
+    chunks = lon_cells // LANES
+    chunk_shape = jax.ShapeDtypeStruct((chunks, lines, LANES), jnp.float32)
+    halo_shape = jax.ShapeDtypeStruct((chunks, halo_first.shape[0], LANES), jnp.float32)
+    zonal_flops = 2 * lines * lon_cells * lon_cells
+    chunk_scratch = pltpu.VMEM((chunks, lines, LANES), jnp.float32)
+    weighted_scratch = pltpu.VMEM((3 * lines, lon_cells), jnp.bfloat16)
+    back_scratch = pltpu.VMEM((chunks, 3 * lines, LANES), jnp.float32)
+    partial_value, own, below, above = call(
+        forward_kernel,
+        (flags, coeffs, own, halo_first, halo_second, zonal_loc, members),
+        [inc_shape, chunk_shape, halo_shape, halo_shape],
+        [chunk_scratch],
+        zonal_flops,
+    )
+    partial_value = pin(partial_value, "forward")
     for iteration in range(ITERS):
-        partial_value = partial_increment(ext, own_coef, zonal_loc, members, half_band)
-        inc = member_sum(partial_value)[0]
-        low, high = band_exchange(inc[:, 0], inc[:, -1])
-        adjoint = observed_adjoint(inc, low, high, (weights, pulls), rims, band_index, band_count)
+        mine, other = core_split(partial_value)
+        inc = mine + core_swap(other)
+        if iteration == 0:
+            inc, held = lax.optimization_barrier((inc, held))
+            weights, pulls, rims = band_setup(held, lev_count, rows, lon_cells)
+        for number, perm in enumerate(steps):
+            inc = inc + lax.ppermute(inc, "mem", perm)
+            if iteration == 0 and number == len(steps) - 1:
+                inc, rims = lax.optimization_barrier((inc, rims))
+            if iteration == 0:
+                inc = pin(inc, f"chip{number}")
+        inc = inc[0]
+        edges = band_swap(*by_partner(inc[:, 0], inc[:, -1]))
+        (adjoint,) = call(
+            observe_kernel,
+            (flags, inc, *edges, weights, pulls, *rims),
+            [jax.ShapeDtypeStruct(inc.shape, jnp.float32)],
+            [],
+            40 * 2 * inc.size,
+        )
+        if iteration == 0:
+            adjoint = pin(adjoint, "adjoint")
+        first, second = band_swap(adjoint, adjoint)
+        halves = []
+        for cells in (adjoint, first, second):
+            halves += [cells, core_swap(cells)]
+        partners = [x[0] for x in fetched] + [x[1] for x in fetched]
         if iteration + 1 < ITERS:
-            low, high = band_exchange(adjoint, adjoint)
-            halo = rows
+            partial_value, own = call(
+                functools.partial(between_kernel, PARTS),
+                (flags, coeffs, own, below, above, zonal_loc, *halves, members, *partners),
+                [inc_shape, chunk_shape],
+                [weighted_scratch, back_scratch, chunk_scratch],
+                4 * zonal_flops,
+            )
         else:
-            low, high = band_exchange(adjoint[:, :half_band], adjoint[:, -half_band:])
-            halo = half_band
-        adjoint = both_halves(jnp.concatenate([low, adjoint, high], axis=1)[None])
-        wide_members = jnp.concatenate(
-            [members_below[:, :, :, rows - halo :], members, members_above[:, :, :, :halo]], axis=3
-        )
-        zonal_back = zonal_backward(wide_members, adjoint, zonal_loc)
-        coeffs = coef_wide[rows - halo : 2 * rows + halo]
-        if iteration + 1 < ITERS:
-            gradient = ext + backward_rows(zonal_back, coeffs, rows + 2 * half_band, half_band)
-            ext = jnp.where(on_grid, ext - step_size * gradient, 0.0)
-        else:
-            current = ext[:, :, half_band:-half_band]
-            gradient = current + backward_rows(zonal_back, coeffs, rows, half_band)
-            current = current - step_size * gradient
-    return current
+            (own,) = call(
+                functools.partial(last_kernel, PARTS, 2 * half_band + 1),
+                (flags, coeffs, own, zonal_loc, *halves, members, *partners),
+                [line_shape],
+                [weighted_scratch, back_scratch, chunk_scratch],
+                3 * zonal_flops,
+            )
+    return own.reshape(alpha.shape)
 
 
 def solution(mesh):

time: 168 us -> 133 us (0.79)
  other arithmetic: 34.6 us -> 3.1 us
  Pallas kernels: 5.99 us -> 36.6 us
  waiting for transfers between devices: 62 us -> 38.5 us
  matrix products: 12.6 us -> 0 us
  local copies, waits for them, and re-layouts: 6.61 us -> 12.2 us
  starting transfers between devices: 44.2 us -> 41.6 us
    pallas_call x0 -> x7, Pallas kernels: none -> 29.6 us  [the longest x5 25.7 us: call(): pl.pallas_call(kernel, in_specs=[pl.BlockSpec(memory_space=pltpu.SMEM)] +...]
    ppermute x20 -> x28, waiting for transfers between devices: 59.8 us -> 34.6 us  [the longest x11 21.4 us: band_swap(): lax.ppermute(send_first, axes, band_pairs(0))]
    select_n x13 -> x3, other arithmetic: 14.1 us -> 0.05 us  [by_partner(): jnp.where(even, to_prev, to_next)]
    dot_general x4 -> x0, matrix products: 12.6 us -> none  [the longest x2 6.89 us: partial_increment(): jnp.dot(spread.reshape(-1, spread.shape[-1]), zonal_loc, preferred_elemen...]
    reduce_sum x4 -> x0, other arithmetic: 10.5 us -> none  [the longest x2 7.06 us: zonal_backward(): weighted = jnp.sum(members * adjoint[None], axis=1).astype(jnp.bfloat16)]
    unnamed x90 -> x41, local copies, waits for them, and re-layouts: 0.72 us -> 10.6 us
    ppermute x20 -> x28, starting transfers between devices: 43.9 us -> 40.3 us  [the longest x11 28.5 us: band_swap(): lax.ppermute(send_first, axes, band_pairs(0))]
    sub x5 -> x0, other arithmetic: 3.2 us -> none  [the longest x1 2.7 us: body(): current = current - step_size * gradient]
  transfers between devices with their start and end apart: 25 -> 37, of which waited for: 12 -> 13; matrix products, arithmetic and copies ran while one was open for 10% -> 4% of each run, Pallas kernels for 3% -> 7%
where the time goes in v2:
time: 133 us; the launch traced here: 132 us
  starting transfers between devices  41.6 us (31%)
  waiting for transfers between devices  38.5 us (29%)
  Pallas kernels  36.6 us (28%)
  local copies, waits for them, and re-layouts  12.2 us (9%)
  other arithmetic  3.1 us (2%)
    ppermute x11, starting transfers between devices, band_swap(): lax.ppermute(send_first, axes, band_pairs(0))  28.5 us
    pallas_call x5, Pallas kernels, call(): pl.pallas_call(kernel, in_specs=[pl.BlockSpec(memory_space=pltpu.SMEM)] +...  25.7 us
    ppermute x11, waiting for transfers between devices, band_swap(): lax.ppermute(send_first, axes, band_pairs(0))  21.4 us
    ppermute x4, waiting for transfers between devices, body(): inc = inc + lax.ppermute(inc, 'mem', perm)  12.3 us
    unnamed x41, local copies, waits for them, and re-layouts  10.6 us
    ppermute x4, starting transfers between devices, body(): inc = inc + lax.ppermute(inc, 'mem', perm)  6.92 us
    pallas_call x1, Pallas kernels, tile_sums(): pl.pallas_call(tile_kernel, grid_spec=pltpu.PrefetchScalarGridSpec(num_sc...  5.83 us
    ppermute x9, waiting for transfers between devices, core_swap(): return lax.ppermute(cells, 'mem', [(i, i ^ 1) for i in range(count)])  3.92 us
  transfers between devices with their start and end apart: 37, of which 13 were waited for; matrix products, arithmetic and copies ran while one was open for 4% of the time, Pallas kernels for 7%

profile of v2, /device:TPU:0, one launch (start us, length us, event | category | flops | bytes accessed | tf_op | source)
XLA Modules:
  0.0 132.5 jit_solution(15391388068205563689)
XLA Ops:
  0.0 1.4 %copy-done.4 = f32[10,4,8,1152]{3,2,1,0:T(8,128)S(1)} copy-done((f32[10,4,8,1152]{3,2,1,0:T(8,128)S(1)}, f32[10,4,8,1152]{3,2,1,0:T(8,128)}, u32[]{:S(2)}) %copy-start.4) | copy-done | bytes 1474584
  1.4 1.3 %shard_map.110 = (f32[160,1152]{1,0:T(8,128)}, f32[160,1152]{1,0:T(8,128)}) custom-call(f32[40,8,1152]{2,1,0:T(8,128)S(1)} %bitcast.40), custom_call_target="tpu_custom_call" | custom-call | bytes 2949120 | tf_op jit(solution)/shard_map/pallas_call | solution.py:575
  2.7 0.8 copy-done.6
  3.5 0.8 copy-done.7
  4.3 0.8 copy-done.8
  5.1 0.7 copy-done.9
  5.8 0.7 copy-done.10
  6.4 0.8 copy-done.11
  7.3 0.8 copy-done.12
  8.1 5.8 %shard_map.111 = f32[3,2,128,128]{3,2,1,0:T(8,128)S(1)} custom-call(s32[3]{0:T(128)S(1)} %bitcast.51, s32[3]{0:T(128)S(1)} %bitcast.52, s32[128,1]{1,0:T(8,128)S(1)} %copy-done.12, s32[128,1]{1,0:T(8,128)S(1)} %copy-done.11, s32[3,1,4096]{2,1,0:T(1,128)S(1)} %bitcast.48, f32[3,1,4096]{2,1,0:T(1,128)S(1)} %bitcast.49, f32[3,1,4096]{2,1,0:T(1,128)S(1)} %bitcast.50), custom_call_target="tpu_custom_call" | custom-call | flops 1258291200 | bytes 393216 | tf_op jit(solution)/shard_map/pallas_call | solution.py:155
  14.1 2.1 %collective-permute-start = (f32[160,1152]{1,0:T(8,128)}, f32[160,1152]{1,0:T(8,128)S(1)}, u32[]{:S(2)}, u32[]{:S(2)}) collective-permute-start(f32[160,1152]{1,0:T(8,128)} %get-tuple-element.42), channel_id=1, source_target_pairs={{0,1},{1,0},{2,3},{3,2},{4,5},{5,4},{6,7},{7,6},{8,9},{9,8},{10,11... | collective-permute-start | bytes 2211848 | tf_op jit(solution)/shard_map/ppermute | solution.py:40
  16.2 0.2 collective-permute-start.1
  16.3 0.8 pad_maximum_fusion.2
  17.2 1.6 %collective-permute-start.3 = (f32[6,128,128]{2,1,0:T(8,128)}, f32[6,128,128]{2,1,0:T(8,128)}, u32[]{:S(2)}, u32[]{:S(2)}) collective-permute-start(f32[6,128,128]{2,1,0:T(8,128)} %pad_maximum_fusion.2), channel_id=1, source_target_pairs={{0,8},{4,20},{8,0},{12,28},{16,24},{20,4},{24,16},{28,12},{1,9},{5... | collective-permute-start | bytes 1179656 | tf_op jit(solution)/shard_map/ppermute | solution.py:605
  18.8 1.1 fusion.2
  19.9 2.7 %collective-permute-start.4 = (bf16[2,2,4,8,1152]{4,3,2,1,0:T(8,128)(2,1)}, bf16[2,2,4,8,1152]{4,3,2,1,0:T(8,128)(2,1)}, u32[]{:S(2)}, u32[]{:S(2)}) collective-permute-start(bf16[2,2,4,8,1152]{4,3,2,1,0:T(8,128)(2,1)} %get-tuple-element.79), channel_id=1, source_target_pairs={{0,1},{1,0},{2,3},{3,2},{4,5},{5,4},{6,7},{7,6},{8,9},{9,8},{10,11... | collective-permute-start | bytes 884744 | tf_op jit(solution)/shard_map/ppermute | solution.py:40
  22.6 0.7 copy.23.coef_ref
  23.3 2.6 %shard_map.109.coef_ref.refs_1_ = f32[216,8,128]{2,1,0:T(8,128)} custom-call(f32[32,9]{1,0:T(8,128)} %copy.23.coef_ref), custom_call_target="tpu_custom_call" | custom-call | bytes 884736 | tf_op jit(solution)/shard_map/pallas_call | solution.py:533
  25.9 0.1 stack.47.flag_ref.refs_0_
  26.0 1.3 pad_maximum_fusion.1
  27.3 6.5 %collective-permute-done.first_ref = f32[160,1152]{1,0:T(8,128)S(1)} collective-permute-done((f32[160,1152]{1,0:T(8,128)}, f32[160,1152]{1,0:T(8,128)S(1)}, u32[]{:S(2)}, u32[]{:S(2)}) %collective-permute-start) | collective-permute-done | bytes 737312 | tf_op jit(solution)/shard_map/ppermute | solution.py:40
  33.7 1.6 %collective-permute-start.7 = (f32[12,128,128]{2,1,0:T(8,128)S(1)}, f32[12,128,128]{2,1,0:T(8,128)S(1)}, u32[]{:S(2)}, u32[]{:S(2)}) collective-permute-start(f32[12,128,128]{2,1,0:T(8,128)S(1)} %pad_maximum_fusion.1), channel_id=1, source_target_pairs={{0,16},{4,12},{8,24},{12,4},{16,0},{20,28},{24,8},{28,20},{1,17},{... | collective-permute-start | bytes 2359304 | tf_op jit(solution)/shard_map/ppermute | solution.py:605
  35.4 1.7 %copy-done.1 = bf16[1152,1152]{1,0:T(8,128)(2,1)S(1)} copy-done((bf16[1152,1152]{1,0:T(8,128)(2,1)S(1)}, bf16[1152,1152]{1,0:T(8,128)(2,1)}, u32[]{:S(2)}) %copy-start.1) | copy-done | bytes 2654232
  37.1 1.4 %copy-done.5 = f32[10,4,8,1152]{3,2,1,0:T(8,128)S(1)} copy-done((f32[10,4,8,1152]{3,2,1,0:T(8,128)S(1)}, f32[10,4,8,1152]{3,2,1,0:T(8,128)}, u32[]{:S(2)}) %copy-start.5) | copy-done | bytes 1474584
  38.5 3.9 %shard_map.112 = (f32[2,4,8,1152]{3,2,1,0:T(8,128)S(1)}, f32[9,320,128]{2,1,0:T(8,128)S(1)}, f32[9,160,128]{2,1,0:T(8,128)S(1)}, f32[9,160,128]{2,1,0:T(8,128)S(1)}) custom-call(s32[6]{0:T(128)S(1)} %stack.47.flag_ref.refs_0_, f32[216,8,128]{2,1,0:T(8,128)S(1)} %copy-done.3, f32[320,1152]{1,0:T(8,128)S(1)} %bitcast.41, ...), custom_call_target="tpu_custom_call" | custom-call | flops 849346560 | bytes 11206680 | tf_op jit(solution)/shard_map/pallas_call | solution.py:493
  42.7 0.5 collective-permute-start.15
  43.2 3.9 %collective-permute-start.14 = (bf16[2,2,4,8,1152]{4,3,2,1,0:T(8,128)(2,1)S(1)}, bf16[2,2,4,8,1152]{4,3,2,1,0:T(8,128)(2,1)S(1)}, u32[]{:S(2)}, u32[]{:S(2)}) collective-permute-start(bf16[2,2,4,8,1152]{4,3,2,1,0:T(8,128)(2,1)S(1)} %copy-done.17), channel_id=1, source_target_pairs={{0,1},{1,0},{2,3},{3,2},{4,5},{5,4},{6,7},{7,6},{8,9},{9,8},{10,11... | collective-permute-start | bytes 884744 | tf_op jit(solution)/shard_map/ppermute | solution.py:40
  47.1 0.3 collective-permute-start.9
  47.4 0.1 pad_maximum_fusion.slots_ref
  47.6 0.6 convert_reduce_fusion.mark_ref
  48.2 1.2 shard_map.113
  49.4 2.7 %collective-permute-start.8 = (f32[1,4,8,1152]{3,1,2,0:T(4,128)S(1)}, f32[1,4,8,1152]{3,1,2,0:T(4,128)S(1)}, u32[]{:S(2)}, u32[]{:S(2)}) collective-permute-start(f32[1,4,8,1152]{3,1,2,0:T(4,128)S(1)} %dynamic-slice_add_fusion.1), channel_id=1, source_target_pairs={{0,8},{4,20},{8,0},{12,28},{16,24},{20,4},{24,16},{28,12},{1,9},{5... | collective-permute-start | bytes 442376 | tf_op jit(solution)/shard_map/ppermute | solution.py:638
  52.1 3.1 %collective-permute-done.8 = f32[1,4,8,1152]{3,1,2,0:T(4,128)S(1)} collective-permute-done((f32[1,4,8,1152]{3,1,2,0:T(4,128)S(1)}, f32[1,4,8,1152]{3,1,2,0:T(4,128)S(1)}, u32[]{:S(2)}, u32[]{:S(2)}) %collective-permute-start.8) | collective-permute-done | bytes 147488 | tf_op jit(solution)/shard_map/ppermute | solution.py:638
  55.3 5.4 %collective-permute-done.9.refs_14_.refs_12_ = bf16[2,2,4,8,1152]{4,3,2,1,0:T(8,128)(2,1)S(1)} collective-permute-done((bf16[2,2,4,8,1152]{4,3,2,1,0:T(8,128)(2,1)S(1)}, bf16[2,2,4,8,1152]{4,3,2,1,0:T(8,128)(2,1)S(1)}, u32[]{:S(2)}, u32[]{:S(2)}) %collective-permute-start.9) | collective-permute-done | bytes 294944 | tf_op jit(solution)/shard_map/ppermute | solution.py:40
  60.7 1.3 collective-permute-start.11
  62.0 0.7 collective-permute-start.13
  62.8 1.4 %collective-permute-start.12 = (f32[3,4,1152]{2,1,0:T(4,128)S(1)}, f32[3,4,1152]{2,1,0:T(4,128)S(1)}, u32[]{:S(2)}, u32[]{:S(2)}) collective-permute-start(f32[3,4,1152]{2,1,0:T(4,128)S(1)} %get-tuple-element.91), channel_id=1, source_target_pairs={{0,1},{1,0},{2,3},{3,2},{4,5},{5,4},{6,7},{7,6},{8,9},{9,8},{10,11... | collective-permute-start | bytes 165896 | tf_op jit(solution)/shard_map/ppermute | solution.py:40
  64.2 1.7 %collective-permute-done.11 = f32[1,4,8,1152]{3,1,2,0:T(4,128)S(1)} collective-permute-done((f32[1,4,8,1152]{3,1,2,0:T(4,128)S(1)}, f32[1,4,8,1152]{3,1,2,0:T(4,128)S(1)}, u32[]{:S(2)}, u32[]{:S(2)}) %collective-permute-start.11) | collective-permute-done | bytes 147488 | tf_op jit(solution)/shard_map/ppermute | solution.py:638
  65.9 2.1 %collective-permute-start.18 = (bf16[2,2,4,8,1152]{4,3,2,1,0:T(8,128)(2,1)S(1)}, bf16[2,2,4,8,1152]{4,3,2,1,0:T(8,128)(2,1)S(1)}, u32[]{:S(2)}, u32[]{:S(2)}) collective-permute-start(bf16[2,2,4,8,1152]{4,3,2,1,0:T(8,128)(2,1)S(1)} %copy-done.16), channel_id=1, source_target_pairs={{0,1},{1,0},{2,3},{3,2},{4,5},{5,4},{6,7},{7,6},{8,9},{9,8},{10,11... | collective-permute-start | bytes 884744 | tf_op jit(solution)/shard_map/ppermute | solution.py:40
  68.1 2.0 %collective-permute-start.16 = (f32[4,1152]{1,0:T(4,128)S(1)}, f32[4,1152]{1,0:T(4,128)S(1)}, u32[]{:S(2)}, u32[]{:S(2)}) collective-permute-start(f32[4,1152]{1,0:T(4,128)S(1)} %get-tuple-element.89), channel_id=1, source_target_pairs={{0,1},{1,0},{2,3},{3,2},{4,5},{5,4},{6,7},{7,6},{8,9},{9,8},{10,11... | collective-permute-start | bytes 55304 | tf_op jit(solution)/shard_map/ppermute | solution.py:40
  70.1 7.8 %collective-permute-start.25 = (bf16[2,2,4,8,1152]{4,3,2,1,0:T(8,128)(2,1)S(1)}, bf16[2,2,4,8,1152]{4,3,2,1,0:T(8,128)(2,1)S(1)}, u32[]{:S(2)}, u32[]{:S(2)}) collective-permute-start(bf16[2,2,4,8,1152]{4,3,2,1,0:T(8,128)(2,1)S(1)} %copy-done.15), channel_id=1, source_target_pairs={{0,1},{1,0},{2,3},{3,2},{4,5},{5,4},{6,7},{7,6},{8,9},{9,8},{10,11... | collective-permute-start | bytes 884744 | tf_op jit(solution)/shard_map/ppermute | solution.py:40
  77.9 1.0 shard_map.114.refs_6_
  79.1 0.2 collective-permute-start.21
  79.3 0.3 collective-permute-start.20
  79.6 0.9 collective-permute-done.23.refs_10_
  80.4 0.1 collective-permute-start.24
  80.6 5.2 %collective-permute-done.21.refs_8_ = f32[4,8,1152]{2,1,0:T(8,128)S(1)} collective-permute-done((f32[4,8,1152]{2,1,0:T(8,128)S(1)}, f32[4,8,1152]{2,1,0:T(8,128)S(1)}, u32[]{:S(2)}, u32[]{:S(2)}) %collective-permute-start.21) | collective-permute-done | bytes 147488 | tf_op jit(solution)/shard_map/ppermute | solution.py:40
  85.8 1.3 %collective-permute-done.22.refs_9_ = f32[4,8,1152]{2,1,0:T(8,128)S(1)} collective-permute-done((f32[4,8,1152]{2,1,0:T(8,128)S(1)}, f32[4,8,1152]{2,1,0:T(8,128)S(1)}, u32[]{:S(2)}, u32[]{:S(2)}) %collective-permute-start.22) | collective-permute-done | bytes 147488 | tf_op jit(solution)/shard_map/ppermute | solution.py:57
  87.2 11.0 %shard_map.115 = (f32[2,4,8,1152]{3,2,1,0:T(8,128)S(1)}, f32[9,320,128]{2,1,0:T(8,128)S(1)}) custom-call(s32[6]{0:T(128)S(1)} %stack.47.flag_ref.refs_0_, f32[216,8,128]{2,1,0:T(8,128)S(1)} %copy-done.3, f32[9,320,128]{2,1,0:T(8,128)S(1)} %get-tuple-element.49.refs_2_, f32[9,160,128]{2,1,0:T(8,128)S(1)} %get-tuple-element.50.refs_3_, ...), custom_call_target="tpu_custom_call" | custom-call | flops 3397386240 | bytes 13565976 | tf_op jit(solution)/shard_map/pallas_call | solution.py:493
  98.2 0.1 copy.31
  98.3 0.2 collective-permute-start.27
  98.5 1.2 collective-permute-done.27
  99.8 2.1 %collective-permute-start.28 = (f32[1,4,8,1152]{3,1,2,0:T(4,128)S(1)}, f32[1,4,8,1152]{3,1,2,0:T(4,128)S(1)}, u32[]{:S(2)}, u32[]{:S(2)}) collective-permute-start(f32[1,4,8,1152]{3,1,2,0:T(4,128)S(1)} %dynamic-slice_add_fusion), channel_id=1, source_target_pairs={{0,8},{4,20},{8,0},{12,28},{16,24},{20,4},{24,16},{28,12},{1,9},{5... | collective-permute-start | bytes 442376 | tf_op jit(solution)/shard_map/ppermute | solution.py:638
  101.9 3.1 %collective-permute-done.28 = f32[1,4,8,1152]{3,1,2,0:T(4,128)S(1)} collective-permute-done((f32[1,4,8,1152]{3,1,2,0:T(4,128)S(1)}, f32[1,4,8,1152]{3,1,2,0:T(4,128)S(1)}, u32[]{:S(2)}, u32[]{:S(2)}) %collective-permute-start.28) | collective-permute-done | bytes 147488 | tf_op jit(solution)/shard_map/ppermute | solution.py:638
  105.1 0.8 collective-permute-start.29
  105.9 4.4 %collective-permute-done.29 = f32[1,4,8,1152]{3,1,2,0:T(4,128)S(1)} collective-permute-done((f32[1,4,8,1152]{3,1,2,0:T(4,128)S(1)}, f32[1,4,8,1152]{3,1,2,0:T(4,128)S(1)}, u32[]{:S(2)}, u32[]{:S(2)}) %collective-permute-start.29) | collective-permute-done | bytes 147488 | tf_op jit(solution)/shard_map/ppermute | solution.py:638
  110.4 2.2 %collective-permute-start.30 = (f32[4,1152]{1,0:T(4,128)S(1)}, f32[4,1152]{1,0:T(4,128)S(1)}, u32[]{:S(2)}, u32[]{:S(2)}) collective-permute-start(f32[4,1152]{1,0:T(4,128)S(1)} %get-tuple-element.87), channel_id=1, source_target_pairs={{0,1},{1,0},{2,3},{3,2},{4,5},{5,4},{6,7},{7,6},{8,9},{9,8},{10,11... | collective-permute-start | bytes 55304 | tf_op jit(solution)/shard_map/ppermute | solution.py:40
  112.7 1.7 %collective-permute-done.30.first_ref = f32[4,1152]{1,0:T(4,128)S(1)} collective-permute-done((f32[4,1152]{1,0:T(4,128)S(1)}, f32[4,1152]{1,0:T(4,128)S(1)}, u32[]{:S(2)}, u32[]{:S(2)}) %collective-permute-start.30) | collective-permute-done | bytes 18464 | tf_op jit(solution)/shard_map/ppermute | solution.py:40
  114.4 1.0 shard_map.116.refs_4_
  115.5 3.8 %collective-permute-start.33 = (f32[4,8,1152]{2,1,0:T(8,128)S(1)}, f32[4,8,1152]{2,1,0:T(8,128)S(1)}, u32[]{:S(2)}, u32[]{:S(2)}) collective-permute-start(f32[4,8,1152]{2,1,0:T(8,128)S(1)} %shard_map.116.refs_4_), channel_id=1, source_target_pairs={{0,1},{1,0},{2,3},{3,2},{4,5},{5,4},{6,7},{7,6},{8,9},{9,8},{10,11... | collective-permute-start | bytes 442376 | tf_op jit(solution)/shard_map/ppermute | solution.py:40
  119.3 0.5 collective-permute-start.36
  119.8 2.6 %collective-permute-done.33.refs_6_ = f32[4,8,1152]{2,1,0:T(8,128)S(1)} collective-permute-done((f32[4,8,1152]{2,1,0:T(8,128)S(1)}, f32[4,8,1152]{2,1,0:T(8,128)S(1)}, u32[]{:S(2)}, u32[]{:S(2)}) %collective-permute-start.33) | collective-permute-done | bytes 147488 | tf_op jit(solution)/shard_map/ppermute | solution.py:40
  122.4 1.4 %collective-permute-done.34.refs_7_ = f32[4,8,1152]{2,1,0:T(8,128)S(1)} collective-permute-done((f32[4,8,1152]{2,1,0:T(8,128)S(1)}, f32[4,8,1152]{2,1,0:T(8,128)S(1)}, u32[]{:S(2)}, u32[]{:S(2)}) %collective-permute-start.34) | collective-permute-done | bytes 147488 | tf_op jit(solution)/shard_map/ppermute | solution.py:57
  123.8 8.7 %shard_map.117 = f32[320,1152]{1,0:T(8,128)} custom-call(s32[6]{0:T(128)S(1)} %stack.47.flag_ref.refs_0_, f32[216,8,128]{2,1,0:T(8,128)S(1)} %copy-done.3, f32[9,320,128]{2,1,0:T(8,128)S(1)} %get-tuple-element.73.refs_2_, bf16[1152,1152]{1,0:T(8,128)(2,1)S(1)} %copy-done.2, f32[4,8,1152]{2,1,0:T(8,128)S(1)} %shard_map.116.refs_4_, ...), custom_call_target="tpu_custom_call" | custom-call | flops 2548039680 | bytes 11796504 | tf_op jit(solution)/shard_map/pallas_call | solution.py:493
  (86 shorter events, 1.1 us)
Async XLA Ops:
  0.0 1.4 %copy-start.4 = (f32[10,4,8,1152]{3,2,1,0:T(8,128)S(1)}, f32[10,4,8,1152]{3,2,1,0:T(8,128)}, u32[]{:S(2)}) copy-start(f32[10,4,8,1152]{3,2,1,0:T(8,128)} %param.12) | copy-start | bytes 4423684
  2.7 0.8 copy-start.6
  3.5 0.8 copy-start.7
  4.3 0.8 copy-start.8
  5.1 0.7 copy-start.9
  5.8 0.7 copy-start.10
  6.4 0.8 copy-start.11
  7.2 0.8 copy-start.12
  13.9 4.8 %copy-start = (bf16[10,2,4,8,1152]{4,3,2,1,0:T(8,128)(2,1)S(1)}, bf16[10,2,4,8,1152]{4,3,2,1,0:T(8,128)(2,1)}, u32[]{:S(2)}) copy-start(bf16[10,2,4,8,1152]{4,3,2,1,0:T(8,128)(2,1)} %refs_10_.1) | copy-start | bytes 4423684
  14.0 9.3 %copy-start.13 = (f32[3,128,128]{2,1,0:T(8,128)}, f32[3,128,128]{2,1,0:T(8,128)S(1)}, u32[]{:S(2)}) copy-start(f32[3,128,128]{2,1,0:T(8,128)S(1)} %get-tuple-element.82) | copy-start | bytes 589828
  14.0 2.3 %collective-permute-start.2 = (f32[1,3,128,128]{3,2,1,0:T(8,128)S(1)}, f32[1,3,128,128]{3,2,1,0:T(8,128)S(1)}, u32[]{:S(2)}, u32[]{:S(2)}) collective-permute-start(f32[1,3,128,128]{3,2,1,0:T(8,128)S(1)} %get-tuple-element.83), channel_id=1, source_target_pairs={{0,4},{4,0},{8,12},{12,8},{16,20},{20,16},{24,28},{28,24},{1,5},{5... | collective-permute-start | bytes 589832 | tf_op jit(solution)/shard_map/ppermute | solution.py:57
  14.1 19.6 %collective-permute-start = (f32[160,1152]{1,0:T(8,128)}, f32[160,1152]{1,0:T(8,128)S(1)}, u32[]{:S(2)}, u32[]{:S(2)}) collective-permute-start(f32[160,1152]{1,0:T(8,128)} %get-tuple-element.42), channel_id=1, source_target_pairs={{0,1},{1,0},{2,3},{3,2},{4,5},{5,4},{6,7},{7,6},{8,9},{9,8},{10,11... | collective-permute-start | bytes 2211848 | tf_op jit(solution)/shard_map/ppermute | solution.py:40
  16.2 17.6 %collective-permute-start.1 = (f32[160,1152]{1,0:T(8,128)}, f32[160,1152]{1,0:T(8,128)}, u32[]{:S(2)}, u32[]{:S(2)}) collective-permute-start(f32[160,1152]{1,0:T(8,128)} %get-tuple-element.43), channel_id=1, source_target_pairs={{0,4},{1,2},{2,1},{3,7},{4,0},{5,6},{6,5},{7,3},{8,12},{9,10},{10,... | collective-permute-start | bytes 2211848 | tf_op jit(solution)/shard_map/ppermute | solution.py:41
  16.3 7.0 %copy-start.14 = (f32[1,3,128,128]{3,2,1,0:T(8,128)}, f32[1,3,128,128]{3,2,1,0:T(8,128)S(1)}, u32[]{:S(2)}) copy-start(f32[1,3,128,128]{3,2,1,0:T(8,128)S(1)} %collective-permute-done.2) | copy-start | bytes 589828
  17.2 5.5 %copy-start.19 = (f32[32,9]{0,1:T(8,128)S(1)}, f32[32,9]{0,1:T(8,128)}, u32[]{:S(2)}) copy-start(f32[32,9]{0,1:T(8,128)} %param.14) | copy-start | bytes 3460
  17.2 8.8 %collective-permute-start.3 = (f32[6,128,128]{2,1,0:T(8,128)}, f32[6,128,128]{2,1,0:T(8,128)}, u32[]{:S(2)}, u32[]{:S(2)}) collective-permute-start(f32[6,128,128]{2,1,0:T(8,128)} %pad_maximum_fusion.2), channel_id=1, source_target_pairs={{0,8},{4,20},{8,0},{12,28},{16,24},{20,4},{24,16},{28,12},{1,9},{5... | collective-permute-start | bytes 1179656 | tf_op jit(solution)/shard_map/ppermute | solution.py:605
  19.9 22.5 %collective-permute-start.5 = (bf16[2,2,4,8,1152]{4,3,2,1,0:T(8,128)(2,1)}, bf16[2,2,4,8,1152]{4,3,2,1,0:T(8,128)(2,1)S(1)}, u32[]{:S(2)}, u32[]{:S(2)}) collective-permute-start(bf16[2,2,4,8,1152]{4,3,2,1,0:T(8,128)(2,1)} %get-tuple-element.79), channel_id=1, source_target_pairs={{0,4},{1,2},{2,1},{3,7},{4,0},{5,6},{6,5},{7,3},{8,12},{9,10},{10,... | collective-permute-start | bytes 884744 | tf_op jit(solution)/shard_map/ppermute | solution.py:41
  19.9 22.5 %collective-permute-start.4 = (bf16[2,2,4,8,1152]{4,3,2,1,0:T(8,128)(2,1)}, bf16[2,2,4,8,1152]{4,3,2,1,0:T(8,128)(2,1)}, u32[]{:S(2)}, u32[]{:S(2)}) collective-permute-start(bf16[2,2,4,8,1152]{4,3,2,1,0:T(8,128)(2,1)} %get-tuple-element.79), channel_id=1, source_target_pairs={{0,1},{1,0},{2,3},{3,2},{4,5},{5,4},{6,7},{7,6},{8,9},{9,8},{10,11... | collective-permute-start | bytes 884744 | tf_op jit(solution)/shard_map/ppermute | solution.py:40
  25.9 9.5 %copy-start.3 = (f32[216,8,128]{2,1,0:T(8,128)S(1)}, f32[216,8,128]{2,1,0:T(8,128)}, u32[]{:S(2)}) copy-start(f32[216,8,128]{2,1,0:T(8,128)} %shard_map.109.coef_ref.refs_1_) | copy-start | bytes 2654212
  33.7 13.7 %collective-permute-start.7 = (f32[12,128,128]{2,1,0:T(8,128)S(1)}, f32[12,128,128]{2,1,0:T(8,128)S(1)}, u32[]{:S(2)}, u32[]{:S(2)}) collective-permute-start(f32[12,128,128]{2,1,0:T(8,128)S(1)} %pad_maximum_fusion.1), channel_id=1, source_target_pairs={{0,16},{4,12},{8,24},{12,4},{16,0},{20,28},{24,8},{28,20},{1,17},{... | collective-permute-start | bytes 2359304 | tf_op jit(solution)/shard_map/ppermute | solution.py:605
  35.4 1.8 %copy-start.1 = (bf16[1152,1152]{1,0:T(8,128)(2,1)S(1)}, bf16[1152,1152]{1,0:T(8,128)(2,1)}, u32[]{:S(2)}) copy-start(bf16[1152,1152]{1,0:T(8,128)(2,1)} %refs_3_.1) | copy-start | bytes 7962628
  37.1 1.4 %copy-start.5 = (f32[10,4,8,1152]{3,2,1,0:T(8,128)S(1)}, f32[10,4,8,1152]{3,2,1,0:T(8,128)}, u32[]{:S(2)}) copy-start(f32[10,4,8,1152]{3,2,1,0:T(8,128)} %param.12) | copy-start | bytes 4423684
  38.5 4.2 %copy-start.17 = (bf16[2,2,4,8,1152]{4,3,2,1,0:T(8,128)(2,1)S(1)}, bf16[2,2,4,8,1152]{4,3,2,1,0:T(8,128)(2,1)}, u32[]{:S(2)}) copy-start(bf16[2,2,4,8,1152]{4,3,2,1,0:T(8,128)(2,1)} %get-tuple-element.77) | copy-start | bytes 884740
  38.5 8.6 %copy-start.18 = (bf16[2,2,4,8,1152]{4,3,2,1,0:T(8,128)(2,1)S(1)}, bf16[2,2,4,8,1152]{4,3,2,1,0:T(8,128)(2,1)}, u32[]{:S(2)}) copy-start(bf16[2,2,4,8,1152]{4,3,2,1,0:T(8,128)(2,1)} %get-tuple-element.78) | copy-start | bytes 884740
  42.6 4.5 %collective-permute-start.6 = (f32[1,4,8,1152]{3,1,2,0:T(4,128)S(1)}, f32[1,4,8,1152]{3,1,2,0:T(4,128)S(1)}, u32[]{:S(2)}, u32[]{:S(2)}) collective-permute-start(f32[1,4,8,1152]{3,1,2,0:T(4,128)S(1)} %constant_dynamic-slice_fusion.1), channel_id=1, source_target_pairs={{0,4},{4,0},{8,12},{12,8},{16,20},{20,16},{24,28},{28,24},{1,5},{5... | collective-permute-start | bytes 442376 | tf_op jit(solution)/shard_map/ppermute | solution.py:57
  42.7 25.3 %collective-permute-start.15 = (bf16[2,2,4,8,1152]{4,3,2,1,0:T(8,128)(2,1)S(1)}, bf16[2,2,4,8,1152]{4,3,2,1,0:T(8,128)(2,1)S(1)}, u32[]{:S(2)}, u32[]{:S(2)}) collective-permute-start(bf16[2,2,4,8,1152]{4,3,2,1,0:T(8,128)(2,1)S(1)} %copy-done.17), channel_id=1, source_target_pairs={{0,4},{1,2},{2,1},{3,7},{4,0},{5,6},{6,5},{7,3},{8,12},{9,10},{10,... | collective-permute-start | bytes 884744 | tf_op jit(solution)/shard_map/ppermute | solution.py:41
  43.2 24.9 %collective-permute-start.14 = (bf16[2,2,4,8,1152]{4,3,2,1,0:T(8,128)(2,1)S(1)}, bf16[2,2,4,8,1152]{4,3,2,1,0:T(8,128)(2,1)S(1)}, u32[]{:S(2)}, u32[]{:S(2)}) collective-permute-start(bf16[2,2,4,8,1152]{4,3,2,1,0:T(8,128)(2,1)S(1)} %copy-done.17), channel_id=1, source_target_pairs={{0,1},{1,0},{2,3},{3,2},{4,5},{5,4},{6,7},{7,6},{8,9},{9,8},{10,11... | collective-permute-start | bytes 884744 | tf_op jit(solution)/shard_map/ppermute | solution.py:40
  47.1 8.2 %collective-permute-start.10 = (bf16[2,2,4,8,1152]{4,3,2,1,0:T(8,128)(2,1)S(1)}, bf16[2,2,4,8,1152]{4,3,2,1,0:T(8,128)(2,1)S(1)}, u32[]{:S(2)}, u32[]{:S(2)}) collective-permute-start(bf16[2,2,4,8,1152]{4,3,2,1,0:T(8,128)(2,1)S(1)} %copy-done.18), channel_id=1, source_target_pairs={{0,4},{1,2},{2,1},{3,7},{4,0},{5,6},{6,5},{7,3},{8,12},{9,10},{10,... | collective-permute-start | bytes 884744 | tf_op jit(solution)/shard_map/ppermute | solution.py:41
  47.1 13.6 %collective-permute-start.9 = (bf16[2,2,4,8,1152]{4,3,2,1,0:T(8,128)(2,1)S(1)}, bf16[2,2,4,8,1152]{4,3,2,1,0:T(8,128)(2,1)S(1)}, u32[]{:S(2)}, u32[]{:S(2)}) collective-permute-start(bf16[2,2,4,8,1152]{4,3,2,1,0:T(8,128)(2,1)S(1)} %copy-done.18), channel_id=1, source_target_pairs={{0,1},{1,0},{2,3},{3,2},{4,5},{5,4},{6,7},{7,6},{8,9},{9,8},{10,11... | collective-permute-start | bytes 884744 | tf_op jit(solution)/shard_map/ppermute | solution.py:40
  47.6 18.3 %copy-start.16 = (bf16[2,2,4,8,1152]{4,3,2,1,0:T(8,128)(2,1)S(1)}, bf16[2,2,4,8,1152]{4,3,2,1,0:T(8,128)(2,1)}, u32[]{:S(2)}) copy-start(bf16[2,2,4,8,1152]{4,3,2,1,0:T(8,128)(2,1)} %get-tuple-element.76) | copy-start | bytes 884740
  48.2 22.0 %copy-start.15 = (bf16[2,2,4,8,1152]{4,3,2,1,0:T(8,128)(2,1)S(1)}, bf16[2,2,4,8,1152]{4,3,2,1,0:T(8,128)(2,1)}, u32[]{:S(2)}) copy-start(bf16[2,2,4,8,1152]{4,3,2,1,0:T(8,128)(2,1)} %get-tuple-element.75) | copy-start | bytes 884740
  49.4 37.8 %copy-start.2 = (bf16[1152,1152]{1,0:T(8,128)(2,1)S(1)}, bf16[1152,1152]{1,0:T(8,128)(2,1)}, u32[]{:S(2)}) copy-start(bf16[1152,1152]{1,0:T(8,128)(2,1)} %refs_3_.1) | copy-start | bytes 7962628
  49.4 5.8 %collective-permute-start.8 = (f32[1,4,8,1152]{3,1,2,0:T(4,128)S(1)}, f32[1,4,8,1152]{3,1,2,0:T(4,128)S(1)}, u32[]{:S(2)}, u32[]{:S(2)}) collective-permute-start(f32[1,4,8,1152]{3,1,2,0:T(4,128)S(1)} %dynamic-slice_add_fusion.1), channel_id=1, source_target_pairs={{0,8},{4,20},{8,0},{12,28},{16,24},{20,4},{24,16},{28,12},{1,9},{5... | collective-permute-start | bytes 442376 | tf_op jit(solution)/shard_map/ppermute | solution.py:638
  60.7 5.1 %collective-permute-start.11 = (f32[1,4,8,1152]{3,1,2,0:T(4,128)S(1)}, f32[1,4,8,1152]{3,1,2,0:T(4,128)S(1)}, u32[]{:S(2)}, u32[]{:S(2)}) collective-permute-start(f32[1,4,8,1152]{3,1,2,0:T(4,128)S(1)} %add.47), channel_id=1, source_target_pairs={{0,16},{4,12},{8,24},{12,4},{16,0},{20,28},{24,8},{28,20},{1,17},{... | collective-permute-start | bytes 442376 | tf_op jit(solution)/shard_map/ppermute | solution.py:638
  62.0 3.9 %collective-permute-start.13 = (f32[3,4,1152]{2,1,0:T(4,128)S(1)}, f32[3,4,1152]{2,1,0:T(4,128)S(1)}, u32[]{:S(2)}, u32[]{:S(2)}) collective-permute-start(f32[3,4,1152]{2,1,0:T(4,128)S(1)} %get-tuple-element.90), channel_id=1, source_target_pairs={{0,4},{1,2},{2,1},{3,7},{4,0},{5,6},{6,5},{7,3},{8,12},{9,10},{10,... | collective-permute-start | bytes 165896 | tf_op jit(solution)/shard_map/ppermute | solution.py:41
  62.8 5.2 %collective-permute-start.12 = (f32[3,4,1152]{2,1,0:T(4,128)S(1)}, f32[3,4,1152]{2,1,0:T(4,128)S(1)}, u32[]{:S(2)}, u32[]{:S(2)}) collective-permute-start(f32[3,4,1152]{2,1,0:T(4,128)S(1)} %get-tuple-element.91), channel_id=1, source_target_pairs={{0,1},{1,0},{2,3},{3,2},{4,5},{5,4},{6,7},{7,6},{8,9},{9,8},{10,11... | collective-permute-start | bytes 165896 | tf_op jit(solution)/shard_map/ppermute | solution.py:40
  65.8 13.1 %collective-permute-start.19 = (bf16[2,2,4,8,1152]{4,3,2,1,0:T(8,128)(2,1)S(1)}, bf16[2,2,4,8,1152]{4,3,2,1,0:T(8,128)(2,1)S(1)}, u32[]{:S(2)}, u32[]{:S(2)}) collective-permute-start(bf16[2,2,4,8,1152]{4,3,2,1,0:T(8,128)(2,1)S(1)} %copy-done.16), channel_id=1, source_target_pairs={{0,4},{1,2},{2,1},{3,7},{4,0},{5,6},{6,5},{7,3},{8,12},{9,10},{10,... | collective-permute-start | bytes 884744 | tf_op jit(solution)/shard_map/ppermute | solution.py:41
  65.9 13.1 %collective-permute-start.18 = (bf16[2,2,4,8,1152]{4,3,2,1,0:T(8,128)(2,1)S(1)}, bf16[2,2,4,8,1152]{4,3,2,1,0:T(8,128)(2,1)S(1)}, u32[]{:S(2)}, u32[]{:S(2)}) collective-permute-start(bf16[2,2,4,8,1152]{4,3,2,1,0:T(8,128)(2,1)S(1)} %copy-done.16), channel_id=1, source_target_pairs={{0,1},{1,0},{2,3},{3,2},{4,5},{5,4},{6,7},{7,6},{8,9},{9,8},{10,11... | collective-permute-start | bytes 884744 | tf_op jit(solution)/shard_map/ppermute | solution.py:40
  68.0 2.1 %collective-permute-start.17 = (f32[4,1152]{1,0:T(4,128)S(1)}, f32[4,1152]{1,0:T(4,128)S(1)}, u32[]{:S(2)}, u32[]{:S(2)}) collective-permute-start(f32[4,1152]{1,0:T(4,128)S(1)} %get-tuple-element.88), channel_id=1, source_target_pairs={{0,4},{1,2},{2,1},{3,7},{4,0},{5,6},{6,5},{7,3},{8,12},{9,10},{10,... | collective-permute-start | bytes 55304 | tf_op jit(solution)/shard_map/ppermute | solution.py:41
  68.1 9.8 %collective-permute-start.16 = (f32[4,1152]{1,0:T(4,128)S(1)}, f32[4,1152]{1,0:T(4,128)S(1)}, u32[]{:S(2)}, u32[]{:S(2)}) collective-permute-start(f32[4,1152]{1,0:T(4,128)S(1)} %get-tuple-element.89), channel_id=1, source_target_pairs={{0,1},{1,0},{2,3},{3,2},{4,5},{5,4},{6,7},{7,6},{8,9},{9,8},{10,11... | collective-permute-start | bytes 55304 | tf_op jit(solution)/shard_map/ppermute | solution.py:40
  70.1 15.7 %collective-permute-start.26 = (bf16[2,2,4,8,1152]{4,3,2,1,0:T(8,128)(2,1)S(1)}, bf16[2,2,4,8,1152]{4,3,2,1,0:T(8,128)(2,1)S(1)}, u32[]{:S(2)}, u32[]{:S(2)}) collective-permute-start(bf16[2,2,4,8,1152]{4,3,2,1,0:T(8,128)(2,1)S(1)} %copy-done.15), channel_id=1, source_target_pairs={{0,4},{1,2},{2,1},{3,7},{4,0},{5,6},{6,5},{7,3},{8,12},{9,10},{10,... | collective-permute-start | bytes 884744 | tf_op jit(solution)/shard_map/ppermute | solution.py:41
  70.1 15.6 %collective-permute-start.25 = (bf16[2,2,4,8,1152]{4,3,2,1,0:T(8,128)(2,1)S(1)}, bf16[2,2,4,8,1152]{4,3,2,1,0:T(8,128)(2,1)S(1)}, u32[]{:S(2)}, u32[]{:S(2)}) collective-permute-start(bf16[2,2,4,8,1152]{4,3,2,1,0:T(8,128)(2,1)S(1)} %copy-done.15), channel_id=1, source_target_pairs={{0,1},{1,0},{2,3},{3,2},{4,5},{5,4},{6,7},{7,6},{8,9},{9,8},{10,11... | collective-permute-start | bytes 884744 | tf_op jit(solution)/shard_map/ppermute | solution.py:40
  79.0 1.4 %collective-permute-start.23 = (f32[4,8,1152]{2,1,0:T(8,128)S(1)}, f32[4,8,1152]{2,1,0:T(8,128)S(1)}, u32[]{:S(2)}, u32[]{:S(2)}) collective-permute-start(f32[4,8,1152]{2,1,0:T(8,128)S(1)} %shard_map.114.refs_6_), channel_id=1, source_target_pairs={{0,4},{1,2},{2,1},{3,7},{4,0},{5,6},{6,5},{7,3},{8,12},{9,10},{10,... | collective-permute-start | bytes 442376 | tf_op jit(solution)/shard_map/ppermute | solution.py:41
  79.1 6.7 %collective-permute-start.21 = (f32[4,8,1152]{2,1,0:T(8,128)S(1)}, f32[4,8,1152]{2,1,0:T(8,128)S(1)}, u32[]{:S(2)}, u32[]{:S(2)}) collective-permute-start(f32[4,8,1152]{2,1,0:T(8,128)S(1)} %shard_map.114.refs_6_), channel_id=1, source_target_pairs={{0,1},{1,0},{2,3},{3,2},{4,5},{5,4},{6,7},{7,6},{8,9},{9,8},{10,11... | collective-permute-start | bytes 442376 | tf_op jit(solution)/shard_map/ppermute | solution.py:40
  79.3 6.5 %collective-permute-start.20 = (f32[4,8,1152]{2,1,0:T(8,128)S(1)}, f32[4,8,1152]{2,1,0:T(8,128)S(1)}, u32[]{:S(2)}, u32[]{:S(2)}) collective-permute-start(f32[4,8,1152]{2,1,0:T(8,128)S(1)} %shard_map.114.refs_6_), channel_id=1, source_target_pairs={{0,4},{4,0},{8,12},{12,8},{16,20},{20,16},{24,28},{28,24},{1,5},{5... | collective-permute-start | bytes 442376 | tf_op jit(solution)/shard_map/ppermute | solution.py:57
  80.4 5.4 %collective-permute-start.24 = (f32[4,8,1152]{2,1,0:T(8,128)S(1)}, f32[4,8,1152]{2,1,0:T(8,128)S(1)}, u32[]{:S(2)}, u32[]{:S(2)}) collective-permute-start(f32[4,8,1152]{2,1,0:T(8,128)S(1)} %collective-permute-done.23.refs_10_), channel_id=1, source_target_pairs={{0,4},{4,0},{8,12},{12,8},{16,20},{20,16},{24,28},{28,24},{1,5},{5... | collective-permute-start | bytes 442376 | tf_op jit(solution)/shard_map/ppermute | solution.py:57
  85.8 1.4 %collective-permute-start.22 = (f32[4,8,1152]{2,1,0:T(8,128)S(1)}, f32[4,8,1152]{2,1,0:T(8,128)S(1)}, u32[]{:S(2)}, u32[]{:S(2)}) collective-permute-start(f32[4,8,1152]{2,1,0:T(8,128)S(1)} %collective-permute-done.21.refs_8_), channel_id=1, source_target_pairs={{0,4},{4,0},{8,12},{12,8},{16,20},{20,16},{24,28},{28,24},{1,5},{5... | collective-permute-start | bytes 442376 | tf_op jit(solution)/shard_map/ppermute | solution.py:57
  98.3 1.4 %collective-permute-start.27 = (f32[1,4,8,1152]{3,1,2,0:T(4,128)S(1)}, f32[1,4,8,1152]{3,1,2,0:T(4,128)S(1)}, u32[]{:S(2)}, u32[]{:S(2)}) collective-permute-start(f32[1,4,8,1152]{3,1,2,0:T(4,128)S(1)} %constant_dynamic-slice_fusion), channel_id=1, source_target_pairs={{0,4},{4,0},{8,12},{12,8},{16,20},{20,16},{24,28},{28,24},{1,5},{5... | collective-permute-start | bytes 442376 | tf_op jit(solution)/shard_map/ppermute | solution.py:57
  99.8 5.3 %collective-permute-start.28 = (f32[1,4,8,1152]{3,1,2,0:T(4,128)S(1)}, f32[1,4,8,1152]{3,1,2,0:T(4,128)S(1)}, u32[]{:S(2)}, u32[]{:S(2)}) collective-permute-start(f32[1,4,8,1152]{3,1,2,0:T(4,128)S(1)} %dynamic-slice_add_fusion), channel_id=1, source_target_pairs={{0,8},{4,20},{8,0},{12,28},{16,24},{20,4},{24,16},{28,12},{1,9},{5... | collective-permute-start | bytes 442376 | tf_op jit(solution)/shard_map/ppermute | solution.py:638
  105.1 5.2 %collective-permute-start.29 = (f32[1,4,8,1152]{3,1,2,0:T(4,128)S(1)}, f32[1,4,8,1152]{3,1,2,0:T(4,128)S(1)}, u32[]{:S(2)}, u32[]{:S(2)}) collective-permute-start(f32[1,4,8,1152]{3,1,2,0:T(4,128)S(1)} %add.50), channel_id=1, source_target_pairs={{0,16},{4,12},{8,24},{12,4},{16,0},{20,28},{24,8},{28,20},{1,17},{... | collective-permute-start | bytes 442376 | tf_op jit(solution)/shard_map/ppermute | solution.py:638
  110.4 2.3 %collective-permute-start.31 = (f32[4,1152]{1,0:T(4,128)S(1)}, f32[4,1152]{1,0:T(4,128)S(1)}, u32[]{:S(2)}, u32[]{:S(2)}) collective-permute-start(f32[4,1152]{1,0:T(4,128)S(1)} %get-tuple-element.86), channel_id=1, source_target_pairs={{0,4},{1,2},{2,1},{3,7},{4,0},{5,6},{6,5},{7,3},{8,12},{9,10},{10,... | collective-permute-start | bytes 55304 | tf_op jit(solution)/shard_map/ppermute | solution.py:41
  110.4 3.9 %collective-permute-start.30 = (f32[4,1152]{1,0:T(4,128)S(1)}, f32[4,1152]{1,0:T(4,128)S(1)}, u32[]{:S(2)}, u32[]{:S(2)}) collective-permute-start(f32[4,1152]{1,0:T(4,128)S(1)} %get-tuple-element.87), channel_id=1, source_target_pairs={{0,1},{1,0},{2,3},{3,2},{4,5},{5,4},{6,7},{7,6},{8,9},{9,8},{10,11... | collective-permute-start | bytes 55304 | tf_op jit(solution)/shard_map/ppermute | solution.py:40
  115.4 3.9 %collective-permute-start.35 = (f32[4,8,1152]{2,1,0:T(8,128)S(1)}, f32[4,8,1152]{2,1,0:T(8,128)S(1)}, u32[]{:S(2)}, u32[]{:S(2)}) collective-permute-start(f32[4,8,1152]{2,1,0:T(8,128)S(1)} %shard_map.116.refs_4_), channel_id=1, source_target_pairs={{0,4},{1,2},{2,1},{3,7},{4,0},{5,6},{6,5},{7,3},{8,12},{9,10},{10,... | collective-permute-start | bytes 442376 | tf_op jit(solution)/shard_map/ppermute | solution.py:41
  115.5 6.9 %collective-permute-start.33 = (f32[4,8,1152]{2,1,0:T(8,128)S(1)}, f32[4,8,1152]{2,1,0:T(8,128)S(1)}, u32[]{:S(2)}, u32[]{:S(2)}) collective-permute-start(f32[4,8,1152]{2,1,0:T(8,128)S(1)} %shard_map.116.refs_4_), channel_id=1, source_target_pairs={{0,1},{1,0},{2,3},{3,2},{4,5},{5,4},{6,7},{7,6},{8,9},{9,8},{10,11... | collective-permute-start | bytes 442376 | tf_op jit(solution)/shard_map/ppermute | solution.py:40
  119.3 3.1 %collective-permute-start.32 = (f32[4,8,1152]{2,1,0:T(8,128)S(1)}, f32[4,8,1152]{2,1,0:T(8,128)S(1)}, u32[]{:S(2)}, u32[]{:S(2)}) collective-permute-start(f32[4,8,1152]{2,1,0:T(8,128)S(1)} %shard_map.116.refs_4_), channel_id=1, source_target_pairs={{0,4},{4,0},{8,12},{12,8},{16,20},{20,16},{24,28},{28,24},{1,5},{5... | collective-permute-start | bytes 442376 | tf_op jit(solution)/shard_map/ppermute | solution.py:57
  119.3 3.1 %collective-permute-start.36 = (f32[4,8,1152]{2,1,0:T(8,128)S(1)}, f32[4,8,1152]{2,1,0:T(8,128)S(1)}, u32[]{:S(2)}, u32[]{:S(2)}) collective-permute-start(f32[4,8,1152]{2,1,0:T(8,128)S(1)} %collective-permute-done.35.refs_8_), channel_id=1, source_target_pairs={{0,4},{4,0},{8,12},{12,8},{16,20},{20,16},{24,28},{28,24},{1,5},{5... | collective-permute-start | bytes 442376 | tf_op jit(solution)/shard_map/ppermute | solution.py:57
  122.4 1.4 %collective-permute-start.34 = (f32[4,8,1152]{2,1,0:T(8,128)S(1)}, f32[4,8,1152]{2,1,0:T(8,128)S(1)}, u32[]{:S(2)}, u32[]{:S(2)}) collective-permute-start(f32[4,8,1152]{2,1,0:T(8,128)S(1)} %collective-permute-done.33.refs_6_), channel_id=1, source_target_pairs={{0,4},{4,0},{8,12},{12,8},{16,20},{20,16},{24,28},{28,24},{1,5},{5... | collective-permute-start | bytes 442376 | tf_op jit(solution)/shard_map/ppermute | solution.py:57

commit v3 on v2

--- a/solution.py
+++ b/solution.py
@@ -12,8 +12,7 @@
 ITERS = 2
 LANES = 128
 OBS_CHUNK = 1024
-PART_EVENTS = ("forward", "chip0", "chip1", "adjoint", None)
-PARTS = len(PART_EVENTS)
+PARTS = ((2, "forward"), (3, "chip0"), (3, "chip1"), (1, "adjoint"), (1, None))
 EVEN, CORE, HAS_FIRST, HAS_SECOND, HAS_BELOW, HAS_ABOVE = range(6)
 
 
@@ -161,7 +160,7 @@
             out_specs=pl.BlockSpec((1,) + out[1:], lambda s, *_: (s, 0, 0, 0)),
         ),
         out_shape=jax.ShapeDtypeStruct(out, jnp.float32),
-        compiler_params=pltpu.CompilerParams(vmem_limit_bytes=32 * 2**20),
+        compiler_params=pltpu.CompilerParams(vmem_limit_bytes=16 * 2**20),
         cost_estimate=pl.CostEstimate(
             flops=2 * slots * length * rows * 400, bytes_accessed=slots * rows * 1024, transcendentals=0
         ),
@@ -224,7 +223,7 @@
             jax.ShapeDtypeStruct((rows, lon_cells), jnp.float32),
         ],
         scratch_shapes=[pltpu.SMEM((2 * lon_cells // TLON,), jnp.int32)],
-        compiler_params=pltpu.CompilerParams(vmem_limit_bytes=32 * 2**20),
+        compiler_params=pltpu.CompilerParams(vmem_limit_bytes=16 * 2**20),
         cost_estimate=pl.CostEstimate(
             flops=rows * lon_cells * 8, bytes_accessed=rows * lon_cells * 24, transcendentals=0
         ),
@@ -343,22 +342,24 @@
 def forward_kernel(
     flag_ref,
     coef_ref,
-    alpha_ref,
+    own_ref,
     first_ref,
     second_ref,
     zonal_ref,
-    members_ref,
+    members_from,
     inc_ref,
-    own_ref,
     below_ref,
     above_ref,
     spread_ref,
+    members_ref,
+    arrived,
 ):
+    copy = pltpu.make_async_copy(members_from, members_ref, arrived)
+    copy.start()
     rows = members_ref.shape[3]
-    half_band = first_ref.shape[0] * rows // alpha_ref.shape[0]
+    half_band = first_ref.shape[0] * rows // own_ref.shape[1]
     taps = 2 * half_band + 1
     even = flag_ref[EVEN] == 1
-    to_chunks(own_ref, alpha_ref[...])
     first = jnp.where(flag_ref[HAS_FIRST] == 1, first_ref[...], 0.0)
     second = jnp.where(flag_ref[HAS_SECOND] == 1, second_ref[...], 0.0)
     to_chunks(below_ref, jnp.where(even, second, first))
@@ -372,6 +373,7 @@
         return carry
 
     lax.fori_loop(0, own_ref.shape[0], step, 0)
+    copy.wait()
     sum_members(spread_ref, zonal_ref, members_ref, inc_ref)
 
 
@@ -382,35 +384,27 @@
     return below + own + above
 
 
-def zonal_back(flag_ref, adjoints, members, zonal_ref, weighted_ref, back_ref):
-    lines = back_ref.shape[1] // 3
-    even, core = flag_ref[EVEN], flag_ref[CORE]
-    places = (lines, even * (2 * lines), (1 - even) * (2 * lines))
-    there = (None, flag_ref[HAS_FIRST] == 1, flag_ref[HAS_SECOND] == 1)
-    for number, (place, parts) in enumerate(zip(places, members)):
-        mine_ref, other_ref = adjoints[2 * number : 2 * number + 2]
-        done = 0
-        for part_ref in parts:
-            size, _, levels, rows, lon = part_ref.shape
-            flat = levels * rows
-
-            def step(
-                k, carry, part_ref=part_ref, mine_ref=mine_ref, other_ref=other_ref, place=place, done=done, number=number
-            ):
-                total = part_ref[k, core].astype(jnp.float32) * mine_ref[...]
-                total += part_ref[k, 1 - core].astype(jnp.float32) * other_ref[...]
-                if there[number] is not None:
-                    total = jnp.where(there[number], total, 0.0)
-                at = pl.multiple_of(place + (k + done) * flat, 16)
-                weighted_ref[pl.ds(at, flat), :] = total.reshape(flat, lon).astype(jnp.bfloat16)
-                return carry
-
-            lax.fori_loop(0, size, step, 0)
-            done += size
+def weigh(part_ref, core, mine_ref, other_ref, weighted_ref, place, there):
+    size, _, levels, rows, lon = part_ref.shape
+    flat = levels * rows
+
+    def step(k, carry):
+        total = part_ref[k, core].astype(jnp.float32) * mine_ref[...]
+        total += part_ref[k, 1 - core].astype(jnp.float32) * other_ref[...]
+        if there is not None:
+            total = jnp.where(there, total, 0.0)
+        at = pl.multiple_of(place + k * flat, 16)
+        weighted_ref[pl.ds(at, flat), :] = total.reshape(flat, lon).astype(jnp.bfloat16)
+        return carry
+
+    lax.fori_loop(0, size, step, 0)
+
+
+def zonal_back(weighted_ref, zonal_ref, back_ref, lines):
     lon = zonal_ref.shape[0]
     wide = LANES * 3 if lon % (LANES * 3) == 0 else LANES
-    for tile in range(3):
-        here = slice(tile * lines, (tile + 1) * lines)
+    for first in range(0, back_ref.shape[1], lines):
+        here = slice(first, first + lines)
         weighted = weighted_ref[here, :]
         for start in range(0, lon, wide):
             back = lax.dot_general(
@@ -423,31 +417,46 @@
                 back_ref[start // LANES + part, here, :] = back[:, part * LANES : (part + 1) * LANES]
 
 
-def back_rows(back_ref, chunk, start, rows, halo):
-    lines = back_ref.shape[1] // 3
-    return [
-        strided(back_ref, chunk, (at // rows) * lines + start * rows + at % rows, rows)
-        for at in range(rows - halo, 2 * rows + halo)
-    ]
-
-
-def between_kernel(parts, *refs):
-    flag_ref, coef_ref, own_ref, below_ref, above_ref, zonal_ref = refs[:6]
-    adjoints = refs[6:12]
-    members_ref = refs[12]
-    partners = refs[13 : 13 + 2 * parts]
-    inc_ref, current_ref, weighted_ref, back_ref, spread_ref = refs[13 + 2 * parts :]
-    rows = members_ref.shape[3]
+def own_kernel(flag_ref, zonal_ref, mine_ref, other_ref, members_ref, back_ref, weighted_ref):
+    weigh(members_ref, flag_ref[CORE], mine_ref, other_ref, weighted_ref, 0, None)
+    zonal_back(weighted_ref, zonal_ref, back_ref, back_ref.shape[1])
+
+
+def partner_back(flag_ref, zonal_ref, adjoints, partners, weighted_ref, back_ref):
+    lines = back_ref.shape[1] // 2
+    even, core = flag_ref[EVEN], flag_ref[CORE]
+    half = len(partners) // 2
+    for number, (place, flag) in enumerate((((even * lines), HAS_FIRST), ((1 - even) * lines, HAS_SECOND))):
+        for part_ref in partners[number * half : (number + 1) * half]:
+            mine_ref, other_ref = adjoints[2 * number : 2 * number + 2]
+            weigh(part_ref, core, mine_ref, other_ref, weighted_ref, place, flag_ref[flag] == 1)
+            place += part_ref.shape[0] * part_ref.shape[2] * part_ref.shape[3]
+    zonal_back(weighted_ref, zonal_ref, back_ref, lines)
+
+
+def back_rows(own_ref, partner_ref, chunk, start, rows, halo):
+    lines = own_ref.shape[1]
+    out = []
+    for at in range(rows - halo, 2 * rows + halo):
+        ref = own_ref if rows <= at < 2 * rows else partner_ref
+        out.append(strided(ref, chunk, (lines if at >= 2 * rows else 0) + start * rows + at % rows, rows))
+    return out
+
+
+def between_kernel(rows, parts, *refs):
+    flag_ref, coef_ref, own_ref, below_ref, above_ref, zonal_ref, own_back_ref = refs[:7]
+    adjoints = refs[7:11]
+    members_ref = refs[11]
+    partners = refs[12 : 12 + 2 * parts]
+    inc_ref, current_ref, weighted_ref, back_ref, spread_ref = refs[12 + 2 * parts :]
     lines = own_ref.shape[1]
     half_band = below_ref.shape[1] * rows // lines
     taps = 2 * half_band + 1
-    zonal_back(
-        flag_ref, adjoints, ((members_ref,), partners[:parts], partners[parts:]), zonal_ref, weighted_ref, back_ref
-    )
+    partner_back(flag_ref, zonal_ref, adjoints, partners, weighted_ref, back_ref)
 
     def step(chunk, carry):
         for start in row_groups(lines // rows):
-            back = back_rows(back_ref, chunk, start, rows, 2 * half_band)
+            back = back_rows(own_back_ref, back_ref, chunk, start, rows, 2 * half_band)
             pulled = pull_rows(back, coef_ref, rows * taps, taps)
             cells = wide_rows(own_ref, below_ref, above_ref, chunk, start, rows, half_band)
             cells = [c - step_size * (c + p) for c, p in zip(cells, pulled)]
@@ -461,21 +470,17 @@
     sum_members(spread_ref, zonal_ref, members_ref, inc_ref)
 
 
-def last_kernel(parts, taps, *refs):
-    flag_ref, coef_ref, own_ref, zonal_ref = refs[:4]
-    adjoints = refs[4:10]
-    members_ref = refs[10]
-    partners = refs[11 : 11 + 2 * parts]
-    out_ref, weighted_ref, back_ref, current_ref = refs[11 + 2 * parts :]
-    rows = members_ref.shape[3]
+def last_kernel(rows, parts, taps, *refs):
+    flag_ref, coef_ref, own_ref, zonal_ref, own_back_ref = refs[:5]
+    adjoints = refs[5:9]
+    partners = refs[9 : 9 + 2 * parts]
+    out_ref, weighted_ref, back_ref, current_ref = refs[9 + 2 * parts :]
     half_band = taps // 2
-    zonal_back(
-        flag_ref, adjoints, ((members_ref,), partners[:parts], partners[parts:]), zonal_ref, weighted_ref, back_ref
-    )
+    partner_back(flag_ref, zonal_ref, adjoints, partners, weighted_ref, back_ref)
 
     def step(chunk, carry):
         for start in row_groups(own_ref.shape[1] // rows):
-            back = back_rows(back_ref, chunk, start, rows, half_band)
+            back = back_rows(own_back_ref, back_ref, chunk, start, rows, half_band)
             for r, pulled in enumerate(pull_rows(back, coef_ref, (rows + half_band) * taps, taps)):
                 here = pl.ds(start * rows + r, 8, stride=rows)
                 cell = own_ref[chunk, here, :]
@@ -487,21 +492,23 @@
         out_ref[:, chunk * LANES : (chunk + 1) * LANES] = current_ref[chunk]
 
 
-def call(kernel, operands, outs, scratch, flops):
+def call(kernel, operands, outs, scratch, flops, anywhere=0, budget=20 * 2**20):
     vmem = pl.BlockSpec(memory_space=pltpu.VMEM)
     moved = sum(int(np.prod(x.shape)) * x.dtype.itemsize for x in list(operands) + list(outs))
     return pl.pallas_call(
         kernel,
-        in_specs=[pl.BlockSpec(memory_space=pltpu.SMEM)] + [vmem] * (len(operands) - 1),
+        in_specs=[pl.BlockSpec(memory_space=pltpu.SMEM)] + [vmem] * (len(operands) - 1 - anywhere)
+        + [pl.BlockSpec(memory_space=pl.ANY)] * anywhere,
         out_specs=[vmem] * len(outs),
         out_shape=list(outs),
         scratch_shapes=list(scratch),
-        compiler_params=pltpu.CompilerParams(vmem_limit_bytes=28 * 2**20),
+        compiler_params=pltpu.CompilerParams(vmem_limit_bytes=budget),
         cost_estimate=pl.CostEstimate(flops=flops, bytes_accessed=moved, transcendentals=0),
     )(*operands)
 
 
-def coefficient_kernel(rows, coef_ref, out_ref):
+def setup_kernel(rows, coef_ref, alpha_ref, out_ref, own_ref):
+    to_chunks(own_ref, alpha_ref[...])
     count, taps = coef_ref.shape
     half_band = taps // 2
     first = lax.axis_index("lat") * rows
@@ -527,16 +534,22 @@
     lax.fori_loop(0, rows + 2 * half_band, backward, 0)
 
 
-def stencil_coefficients(merid_coef, rows):
+def setup(merid_coef, own, rows):
     taps = merid_coef.shape[1]
     shape = ((2 * rows + taps - 1) * taps, 8, LANES)
+    lines, lon = own.shape
+    vmem = pl.BlockSpec(memory_space=pltpu.VMEM)
     return pl.pallas_call(
-        functools.partial(coefficient_kernel, rows),
-        in_specs=[pl.BlockSpec(memory_space=pltpu.SMEM)],
-        out_specs=pl.BlockSpec(memory_space=pltpu.VMEM),
-        out_shape=jax.ShapeDtypeStruct(shape, jnp.float32),
-        cost_estimate=pl.CostEstimate(flops=0, bytes_accessed=shape[0] * 4096, transcendentals=0),
-    )(merid_coef)
+        functools.partial(setup_kernel, rows),
+        in_specs=[pl.BlockSpec(memory_space=pltpu.SMEM), vmem],
+        out_specs=[vmem, vmem],
+        out_shape=[
+            jax.ShapeDtypeStruct(shape, jnp.float32),
+            jax.ShapeDtypeStruct((lon // LANES, lines, LANES), jnp.float32),
+        ],
+        compiler_params=pltpu.CompilerParams(vmem_limit_bytes=8 * 2**20),
+        cost_estimate=pl.CostEstimate(flops=0, bytes_accessed=shape[0] * 4096 + 8 * own.size, transcendentals=0),
+    )(merid_coef, own)
 
 
 def band_setup(held, lev_count, rows, lon_cells):
@@ -577,16 +590,17 @@
         in_specs=[vmem],
         out_specs=[vmem, vmem],
         out_shape=[edge_shape, edge_shape],
-        compiler_params=pltpu.CompilerParams(vmem_limit_bytes=16 * 2**20),
+        compiler_params=pltpu.CompilerParams(vmem_limit_bytes=8 * 2**20),
         cost_estimate=pl.CostEstimate(flops=0, bytes_accessed=16 * edge_lines * lon_cells, transcendentals=0),
     )(alpha.reshape(-1, rows, lon_cells))
     obs_index, obs_value, obs_weight, sends = lax.optimization_barrier((obs_index, obs_value, obs_weight, sends))
     halo_first, halo_second = band_swap(*sends)
-    coeffs = stencil_coefficients(merid_coef, rows)
-    own = alpha.reshape(lines, lon_cells)
-
-    cuts = [0] + [members_per * (i + 1) // PARTS for i in range(PARTS)]
-    parts = [members[x:y] for x, y in zip(cuts[:-1], cuts[1:])]
+    coeffs, own = setup(merid_coef, alpha.reshape(lines, lon_cells), rows)
+
+    total_share = sum(share for share, _ in PARTS)
+    cuts = [sum(share for share, _ in PARTS[:i]) * members_per // total_share for i in range(len(PARTS) + 1)]
+    pieces = [(x, y, event) for x, y, (_, event) in zip(cuts[:-1], cuts[1:], PARTS) if x < y]
+    parts = [members[x:y] for x, y, _ in pieces]
 
     held = observation_slots(
         slot_tile.reshape(-1),
@@ -601,12 +615,14 @@
     steps = chip_steps()
     for number, perm in enumerate(steps):
         if number == len(steps) - 1:
-            halo_first, halo_second, held = lax.optimization_barrier((halo_first, halo_second, held))
+            halo_first, halo_second, held, coeffs, own, parts = lax.optimization_barrier(
+                (halo_first, halo_second, held, coeffs, own, parts)
+            )
         held = jnp.concatenate([held, lax.ppermute(held, "mem", perm)], axis=0)
     fetched = [band_swap(part, part) for part in parts]
 
     def pin(value, event):
-        for number, name in enumerate(PART_EVENTS):
+        for number, (_, _, name) in enumerate(pieces):
             if name == event:
                 value, fetched[number] = lax.optimization_barrier((value, fetched[number]))
         return value
@@ -618,24 +634,25 @@
     halo_shape = jax.ShapeDtypeStruct((chunks, halo_first.shape[0], LANES), jnp.float32)
     zonal_flops = 2 * lines * lon_cells * lon_cells
     chunk_scratch = pltpu.VMEM((chunks, lines, LANES), jnp.float32)
-    weighted_scratch = pltpu.VMEM((3 * lines, lon_cells), jnp.bfloat16)
-    back_scratch = pltpu.VMEM((chunks, 3 * lines, LANES), jnp.float32)
-    partial_value, own, below, above = call(
+    weighted_scratch = pltpu.VMEM((2 * lines, lon_cells), jnp.bfloat16)
+    back_scratch = pltpu.VMEM((chunks, 2 * lines, LANES), jnp.float32)
+    partial_value, below, above = call(
         forward_kernel,
         (flags, coeffs, own, halo_first, halo_second, zonal_loc, members),
-        [inc_shape, chunk_shape, halo_shape, halo_shape],
-        [chunk_scratch],
+        [inc_shape, halo_shape, halo_shape],
+        [chunk_scratch, pltpu.VMEM(members.shape, members.dtype), pltpu.SemaphoreType.DMA],
         zonal_flops,
+        anywhere=1,
     )
     partial_value = pin(partial_value, "forward")
     for iteration in range(ITERS):
         mine, other = core_split(partial_value)
         inc = mine + core_swap(other)
-        if iteration == 0:
-            inc, held = lax.optimization_barrier((inc, held))
-            weights, pulls, rims = band_setup(held, lev_count, rows, lon_cells)
         for number, perm in enumerate(steps):
             inc = inc + lax.ppermute(inc, "mem", perm)
+            if iteration == 0 and number == 0:
+                inc, held = lax.optimization_barrier((inc, held))
+                weights, pulls, rims = band_setup(held, lev_count, rows, lon_cells)
             if iteration == 0 and number == len(steps) - 1:
                 inc, rims = lax.optimization_barrier((inc, rims))
             if iteration == 0:
@@ -652,25 +669,32 @@
         if iteration == 0:
             adjoint = pin(adjoint, "adjoint")
         first, second = band_swap(adjoint, adjoint)
-        halves = []
-        for cells in (adjoint, first, second):
-            halves += [cells, core_swap(cells)]
+        other = core_swap(adjoint)
+        (own_back,) = call(
+            own_kernel,
+            (flags, zonal_loc, adjoint, other, members),
+            [chunk_shape],
+            [pltpu.VMEM((lines, lon_cells), jnp.bfloat16)],
+            zonal_flops,
+        )
+        first, second, own_back = lax.optimization_barrier((first, second, own_back))
+        halves = (first, core_swap(first), second, core_swap(second))
         partners = [x[0] for x in fetched] + [x[1] for x in fetched]
         if iteration + 1 < ITERS:
             partial_value, own = call(
-                functools.partial(between_kernel, PARTS),
-                (flags, coeffs, own, below, above, zonal_loc, *halves, members, *partners),
+                functools.partial(between_kernel, rows, len(pieces)),
+                (flags, coeffs, own, below, above, zonal_loc, own_back, *halves, members, *partners),
                 [inc_shape, chunk_shape],
                 [weighted_scratch, back_scratch, chunk_scratch],
-                4 * zonal_flops,
+                3 * zonal_flops,
             )
         else:
             (own,) = call(
-                functools.partial(last_kernel, PARTS, 2 * half_band + 1),
-                (flags, coeffs, own, zonal_loc, *halves, members, *partners),
+                functools.partial(last_kernel, rows, len(pieces), 2 * half_band + 1),
+                (flags, coeffs, own, zonal_loc, own_back, *halves, *partners),
                 [line_shape],
                 [weighted_scratch, back_scratch, chunk_scratch],
-                3 * zonal_flops,
+                2 * zonal_flops,
             )
     return own.reshape(alpha.shape)
 

time: 133 us -> 126 us (0.947)
  starting transfers between devices: 41.6 us -> 34.3 us
  Pallas kernels: 36.6 us -> 35 us
  waiting for transfers between devices: 38.5 us -> 39.9 us
    ppermute x11, waiting for transfers between devices: 21.4 us -> 15.2 us  [band_swap(): lax.ppermute(send_first, axes, band_pairs(0))]
    ppermute x4, starting transfers between devices: 6.92 us -> 0.7 us  [body(): inc = inc + lax.ppermute(inc, 'mem', perm)]
    ppermute x4, waiting for transfers between devices: 12.3 us -> 17.6 us  [body(): inc = inc + lax.ppermute(inc, 'mem', perm)]
    ppermute x11, starting transfers between devices: 28.5 us -> 23.8 us  [band_swap(): lax.ppermute(send_first, axes, band_pairs(0))]
    ppermute x2, waiting for transfers between devices: 0.01 us -> 4.56 us  [body(): held = jnp.concatenate([held, lax.ppermute(held, 'mem', perm)], axis=0)]
    unnamed x41 -> x49, local copies, waits for them, and re-layouts: 10.6 us -> 7.46 us
    pallas_call x1, Pallas kernels: 5.83 us -> 3.32 us  [tile_sums(): pl.pallas_call(tile_kernel, grid_spec=pltpu.PrefetchScalarGridSpec(num_sc...]
    slice x1 -> x3, local copies, waits for them, and re-layouts: 1.15 us -> 3.49 us  [body(): parts = [members[x:y] for x, y, _ in pieces]]
  transfers between devices with their start and end apart: 37 -> 37, of which waited for: 13 -> 15; matrix products, arithmetic and copies ran while one was open for 4% -> 6% of each run, Pallas kernels for 7% -> 10%
where the time goes in v3:
time: 126 us
  waiting for transfers between devices  39.9 us (32%)
  Pallas kernels  35 us (28%)
  starting transfers between devices  34.3 us (27%)
  local copies, waits for them, and re-layouts  12.1 us (10%)
  other arithmetic  4.13 us (3%)
    pallas_call x7, Pallas kernels, call(): pl.pallas_call(kernel, in_specs=[pl.BlockSpec(memory_space=pltpu.SMEM)] +...  27.5 us
    ppermute x11, starting transfers between devices, band_swap(): lax.ppermute(send_first, axes, band_pairs(0))  23.8 us
    ppermute x4, waiting for transfers between devices, body(): inc = inc + lax.ppermute(inc, 'mem', perm)  17.6 us
    ppermute x11, waiting for transfers between devices, band_swap(): lax.ppermute(send_first, axes, band_pairs(0))  15.2 us
    unnamed x49, local copies, waits for them, and re-layouts  7.46 us
    ppermute x2, starting transfers between devices, body(): held = jnp.concatenate([held, lax.ppermute(held, 'mem', perm)], axis=0)  5.44 us
    ppermute x2, waiting for transfers between devices, body(): held = jnp.concatenate([held, lax.ppermute(held, 'mem', perm)], axis=0)  4.56 us
    slice x3, local copies, waits for them, and re-layouts, body(): parts = [members[x:y] for x, y, _ in pieces]  3.49 us
  transfers between devices with their start and end apart: 37, of which 15 were waited for; matrix products, arithmetic and copies ran while one was open for 6% of the time, Pallas kernels for 10%

profile of v3, /device:TPU:0, one launch (start us, length us, event | category | flops | bytes accessed | tf_op | source)
XLA Modules:
  0.0 125.9 jit_solution(14111240689569830316)
XLA Ops:
  0.0 1.4 %copy-done.7 = f32[10,4,8,1152]{3,2,1,0:T(8,128)S(1)} copy-done((f32[10,4,8,1152]{3,2,1,0:T(8,128)S(1)}, f32[10,4,8,1152]{3,2,1,0:T(8,128)}, u32[]{:S(2)}) %copy-start.7) | copy-done | bytes 1474584
  1.4 1.3 %shard_map.109 = (f32[160,1152]{1,0:T(8,128)}, f32[160,1152]{1,0:T(8,128)}) custom-call(f32[40,8,1152]{2,1,0:T(8,128)S(1)} %bitcast.40), custom_call_target="tpu_custom_call" | custom-call | bytes 2949120 | tf_op jit(solution)/shard_map/pallas_call | solution.py:588
  2.8 3.3 %shard_map.110 = f32[3,2,128,128]{3,2,1,0:T(8,128)S(1)} custom-call(s32[3]{0:T(128)S(1)} %bitcast.51, s32[3]{0:T(128)S(1)} %bitcast.52, s32[128,1]{1,0:T(8,128)S(1)} %copy-done.15, s32[128,1]{1,0:T(8,128)S(1)} %copy-done.14, s32[3,1,4096]{2,1,0:T(1,128)S(1)} %bitcast.48, f32[3,1,4096]{2,1,0:T(1,128)S(1)} %bitcast.49, f32[3,1,4096]{2,1,0:T(1,128)S(1)} %bitcast.50), custom_call_target="tpu_custom_call" | custom-call | flops 1258291200 | bytes 393216 | tf_op jit(solution)/shard_map/pallas_call | solution.py:154
  6.2 0.7 dynamic-slice_bitcast_fusion.1
  6.9 1.0 collective-permute-start.2
  7.8 3.1 %collective-permute-start = (f32[160,1152]{1,0:T(8,128)}, f32[160,1152]{1,0:T(8,128)}, u32[]{:S(2)}, u32[]{:S(2)}) collective-permute-start(f32[160,1152]{1,0:T(8,128)} %get-tuple-element.56), channel_id=1, source_target_pairs={{0,1},{1,0},{2,3},{3,2},{4,5},{5,4},{6,7},{7,6},{8,9},{9,8},{10,11... | collective-permute-start | bytes 2211848 | tf_op jit(solution)/shard_map/ppermute | solution.py:39
  10.9 0.2 collective-permute-start.1
  11.1 1.0 fusion.3
  12.2 0.7 slice.42
  12.9 0.1 copy.23.coef_ref
  13.0 1.4 %copy-done.8 = f32[10,4,8,1152]{3,2,1,0:T(8,128)S(1)} copy-done((f32[10,4,8,1152]{3,2,1,0:T(8,128)S(1)}, f32[10,4,8,1152]{3,2,1,0:T(8,128)}, u32[]{:S(2)}) %copy-start.8) | copy-done | bytes 1474584
  14.4 1.6 %shard_map.111 = (f32[216,8,128]{2,1,0:T(8,128)S(1)}, f32[9,320,128]{2,1,0:T(8,128)S(1)}) custom-call(f32[32,9]{1,0:T(8,128)S(1)} %copy.23.coef_ref, f32[320,1152]{1,0:T(8,128)S(1)} %bitcast.41), custom_call_target="tpu_custom_call" | custom-call | bytes 3833856 | tf_op jit(solution)/shard_map/pallas_call | solution.py:542
  16.0 1.1 copy-done.4
  17.1 0.7 copy-done.18
  17.8 1.2 pad_maximum_fusion.2
  19.0 1.6 %collective-permute-start.3 = (f32[6,128,128]{2,1,0:T(8,128)S(1)}, f32[6,128,128]{2,1,0:T(8,128)S(1)}, u32[]{:S(2)}, u32[]{:S(2)}) collective-permute-start(f32[6,128,128]{2,1,0:T(8,128)S(1)} %pad_maximum_fusion.2), channel_id=1, source_target_pairs={{0,8},{4,20},{8,0},{12,28},{16,24},{20,4},{24,16},{28,12},{1,9},{5... | collective-permute-start | bytes 1179656 | tf_op jit(solution)/shard_map/ppermute | solution.py:621
  20.5 1.7 %fusion.2 = (bf16[1,2,4,8,1152]{4,3,2,1,0:T(8,128)(2,1)}, bf16[1,2,4,8,1152]{4,3,2,1,0:T(8,128)(2,1)}) fusion(bf16[10,2,4,8,1152]{4,3,2,1,0:T(8,128)(2,1)} %members_ref.3), kind=kLoop, calls=%fused_computation.23 | loop fusion | bytes 589824 | tf_op jit(solution)/shard_map/slice | solution.py:603
  22.3 4.6 %collective-permute-done.3 = f32[6,128,128]{2,1,0:T(8,128)S(1)} collective-permute-done((f32[6,128,128]{2,1,0:T(8,128)S(1)}, f32[6,128,128]{2,1,0:T(8,128)S(1)}, u32[]{:S(2)}, u32[]{:S(2)}) %collective-permute-start.3) | collective-permute-done | bytes 393248 | tf_op jit(solution)/shard_map/ppermute | solution.py:621
  26.8 1.9 %pad_maximum_fusion.1 = f32[12,128,128]{2,1,0:T(8,128)} fusion(f32[6,128,128]{2,1,0:T(8,128)S(1)} %collective-permute-done.3, f32[3,128,128]{2,1,0:T(8,128)} %bitcast.54, f32[3,128,128]{2,1,0:T(8,128)S(1)} %copy-done.17), kind=kLoop, calls=%fused_computation.1 | loop fusion | flops 393216 | bytes 1572864 | tf_op jit(solution)/shard_map/concatenate | solution.py:621
  28.7 3.7 %collective-permute-start.4 = (bf16[2,2,4,8,1152]{4,3,2,1,0:T(8,128)(2,1)}, bf16[2,2,4,8,1152]{4,3,2,1,0:T(8,128)(2,1)}, u32[]{:S(2)}, u32[]{:S(2)}) collective-permute-start(bf16[2,2,4,8,1152]{4,3,2,1,0:T(8,128)(2,1)} %slice.42), channel_id=1, source_target_pairs={{0,1},{1,0},{2,3},{3,2},{4,5},{5,4},{6,7},{7,6},{8,9},{9,8},{10,11... | collective-permute-start | bytes 884744 | tf_op jit(solution)/shard_map/ppermute | solution.py:39
  32.5 0.1 stack.47.flag_ref.refs_0_
  32.6 3.9 %collective-permute-start.8 = (f32[12,128,128]{2,1,0:T(8,128)}, f32[12,128,128]{2,1,0:T(8,128)S(1)}, u32[]{:S(2)}, u32[]{:S(2)}) collective-permute-start(f32[12,128,128]{2,1,0:T(8,128)} %pad_maximum_fusion.1), channel_id=1, source_target_pairs={{0,16},{4,12},{8,24},{12,4},{16,0},{20,28},{24,8},{28,20},{1,17},{... | collective-permute-start | bytes 2359304 | tf_op jit(solution)/shard_map/ppermute | solution.py:621
  36.4 1.4 %copy-done.2 = bf16[10,2,4,8,1152]{4,3,2,1,0:T(8,128)(2,1)S(1)} copy-done((bf16[10,2,4,8,1152]{4,3,2,1,0:T(8,128)(2,1)S(1)}, bf16[10,2,4,8,1152]{4,3,2,1,0:T(8,128)(2,1)}, u32[]{:S(2)}) %copy-start.2) | copy-done | bytes 1474584
  37.8 1.4 %copy-done.5 = f32[9,320,128]{2,1,0:T(8,128)S(1)} copy-done((f32[9,320,128]{2,1,0:T(8,128)S(1)}, f32[9,320,128]{2,1,0:T(8,128)}, u32[]{:S(2)}) %copy-start.5) | copy-done | bytes 1474584
  39.2 4.3 %shard_map.112 = (f32[2,4,8,1152]{3,2,1,0:T(8,128)S(1)}, f32[9,160,128]{2,1,0:T(8,128)S(1)}, f32[9,160,128]{2,1,0:T(8,128)S(1)}) custom-call(s32[6]{0:T(128)S(1)} %stack.47.flag_ref.refs_0_, f32[216,8,128]{2,1,0:T(8,128)S(1)} %get-tuple-element.63.coef_ref.refs_1_, f32[9,320,128]{2,1,0:T(8,128)S(1)} %copy-done.5, ...), custom_call_target="tpu_custom_call" | custom-call | flops 849346560 | bytes 9732120 | tf_op jit(solution)/shard_map/pallas_call | solution.py:498
  43.8 0.5 collective-permute-start.10
  44.3 0.8 collective-permute-start.9
  45.3 0.2 collective-permute-start.15
  45.5 4.9 %collective-permute-done.7 = f32[1,4,8,1152]{3,1,2,0:T(4,128)S(1)} collective-permute-done((f32[1,4,8,1152]{3,1,2,0:T(4,128)S(1)}, f32[1,4,8,1152]{3,1,2,0:T(4,128)S(1)}, u32[]{:S(2)}, u32[]{:S(2)}) %collective-permute-start.7) | collective-permute-done | bytes 147488 | tf_op jit(solution)/shard_map/ppermute | solution.py:652
  50.4 1.2 collective-permute-start.14
  51.6 0.1 pad_maximum_fusion.slots_ref
  51.8 5.5 %collective-permute-done.9.refs_13_.refs_10_ = bf16[3,2,4,8,1152]{4,3,2,1,0:T(8,128)(2,1)S(1)} collective-permute-done((bf16[3,2,4,8,1152]{4,3,2,1,0:T(8,128)(2,1)S(1)}, bf16[3,2,4,8,1152]{4,3,2,1,0:T(8,128)(2,1)S(1)}, u32[]{:S(2)}, u32[]{:S(2)}) %collective-permute-start.9) | collective-permute-done | bytes 442400 | tf_op jit(solution)/shard_map/ppermute | solution.py:39
  57.3 0.6 convert_reduce_fusion.mark_ref
  57.9 1.2 shard_map.113
  59.2 0.1 collective-permute-start.11
  59.4 2.1 %collective-permute-start.12 = (f32[3,4,1152]{2,1,0:T(4,128)S(1)}, f32[3,4,1152]{2,1,0:T(4,128)S(1)}, u32[]{:S(2)}, u32[]{:S(2)}) collective-permute-start(f32[3,4,1152]{2,1,0:T(4,128)S(1)} %get-tuple-element.118), channel_id=1, source_target_pairs={{0,1},{1,0},{2,3},{3,2},{4,5},{5,4},{6,7},{7,6},{8,9},{9,8},{10,11... | collective-permute-start | bytes 165896 | tf_op jit(solution)/shard_map/ppermute | solution.py:39
  61.5 2.9 %collective-permute-done.11 = f32[1,4,8,1152]{3,1,2,0:T(4,128)S(1)} collective-permute-done((f32[1,4,8,1152]{3,1,2,0:T(4,128)S(1)}, f32[1,4,8,1152]{3,1,2,0:T(4,128)S(1)}, u32[]{:S(2)}, u32[]{:S(2)}) %collective-permute-start.11) | collective-permute-done | bytes 147488 | tf_op jit(solution)/shard_map/ppermute | solution.py:652
  64.4 3.1 %collective-permute-start.18 = (bf16[1,2,4,8,1152]{4,3,2,1,0:T(8,128)(2,1)S(1)}, bf16[1,2,4,8,1152]{4,3,2,1,0:T(8,128)(2,1)S(1)}, u32[]{:S(2)}, u32[]{:S(2)}) collective-permute-start(bf16[1,2,4,8,1152]{4,3,2,1,0:T(8,128)(2,1)S(1)} %copy-done.22), channel_id=1, source_target_pairs={{0,1},{1,0},{2,3},{3,2},{4,5},{5,4},{6,7},{7,6},{8,9},{9,8},{10,11... | collective-permute-start | bytes 442376 | tf_op jit(solution)/shard_map/ppermute | solution.py:39
  67.6 1.3 %collective-permute-start.16 = (f32[4,1152]{1,0:T(4,128)S(1)}, f32[4,1152]{1,0:T(4,128)S(1)}, u32[]{:S(2)}, u32[]{:S(2)}) collective-permute-start(f32[4,1152]{1,0:T(4,128)S(1)} %get-tuple-element.116), channel_id=1, source_target_pairs={{0,1},{1,0},{2,3},{3,2},{4,5},{5,4},{6,7},{7,6},{8,9},{9,8},{10,11... | collective-permute-start | bytes 55304 | tf_op jit(solution)/shard_map/ppermute | solution.py:39
  68.9 2.5 %collective-permute-done.16.first_ref = f32[4,1152]{1,0:T(4,128)S(1)} collective-permute-done((f32[4,1152]{1,0:T(4,128)S(1)}, f32[4,1152]{1,0:T(4,128)S(1)}, u32[]{:S(2)}, u32[]{:S(2)}) %collective-permute-start.16) | collective-permute-done | bytes 18464 | tf_op jit(solution)/shard_map/ppermute | solution.py:39
  71.4 1.0 shard_map.114.mine_ref
  72.6 0.5 collective-permute-start.21
  73.1 2.3 %collective-permute-start.20 = (f32[4,8,1152]{2,1,0:T(8,128)S(1)}, f32[4,8,1152]{2,1,0:T(8,128)S(1)}, u32[]{:S(2)}, u32[]{:S(2)}) collective-permute-start(f32[4,8,1152]{2,1,0:T(8,128)S(1)} %shard_map.114.mine_ref), channel_id=1, source_target_pairs={{0,1},{1,0},{2,3},{3,2},{4,5},{5,4},{6,7},{7,6},{8,9},{9,8},{10,11... | collective-permute-start | bytes 442376 | tf_op jit(solution)/shard_map/ppermute | solution.py:39
  75.4 0.9 collective-permute-start.25
  76.3 2.3 %shard_map.115.refs_6_ = f32[9,320,128]{2,1,0:T(8,128)S(1)} custom-call(s32[6]{0:T(128)S(1)} %stack.47.flag_ref.refs_0_, bf16[1152,1152]{1,0:T(8,128)(2,1)S(1)} %copy-done, f32[4,8,1152]{2,1,0:T(8,128)S(1)} %shard_map.114.mine_ref, f32[4,8,1152]{2,1,0:T(8,128)S(1)} %collective-permute-done.22.other_ref, bf16[10,2,4,8,1152]{4,3,2,1,0:T(8,128)(2,1)S(1)} %copy-done.2), custom_call_target="tpu_custom_call" | custom-call | flops 849346560 | bytes 5898264 | tf_op jit(solution)/shard_map/pallas_call | solution.py:498
  78.6 1.4 %collective-permute-done.20.refs_7_ = f32[4,8,1152]{2,1,0:T(8,128)S(1)} collective-permute-done((f32[4,8,1152]{2,1,0:T(8,128)S(1)}, f32[4,8,1152]{2,1,0:T(8,128)S(1)}, u32[]{:S(2)}, u32[]{:S(2)}) %collective-permute-start.20) | collective-permute-done | bytes 147488 | tf_op jit(solution)/shard_map/ppermute | solution.py:39
  80.0 0.5 collective-permute-start.24
  80.5 2.2 %collective-permute-done.25.refs_16_.refs_13_ = bf16[1,2,4,8,1152]{4,3,2,1,0:T(8,128)(2,1)S(1)} collective-permute-done((bf16[1,2,4,8,1152]{4,3,2,1,0:T(8,128)(2,1)S(1)}, bf16[1,2,4,8,1152]{4,3,2,1,0:T(8,128)(2,1)S(1)}, u32[]{:S(2)}, u32[]{:S(2)}) %collective-permute-start.25) | collective-permute-done | bytes 147488 | tf_op jit(solution)/shard_map/ppermute | solution.py:39
  82.7 9.4 %shard_map.116 = (f32[2,4,8,1152]{3,2,1,0:T(8,128)S(1)}, f32[9,320,128]{2,1,0:T(8,128)S(1)}) custom-call(s32[6]{0:T(128)S(1)} %stack.47.flag_ref.refs_0_, f32[216,8,128]{2,1,0:T(8,128)S(1)} %get-tuple-element.63.coef_ref.refs_1_, f32[9,320,128]{2,1,0:T(8,128)S(1)} %copy-done.6, f32[9,160,128]{2,1,0:T(8,128)S(1)} %get-tuple-element.67.refs_3_, ...), custom_call_target="tpu_custom_call" | custom-call | flops 2548039680 | bytes 14745624 | tf_op jit(solution)/shard_map/pallas_call | solution.py:498
  92.3 1.4 %collective-permute-done.27 = f32[1,4,8,1152]{3,1,2,0:T(4,128)S(1)} collective-permute-done((f32[1,4,8,1152]{3,1,2,0:T(4,128)S(1)}, f32[1,4,8,1152]{3,1,2,0:T(4,128)S(1)}, u32[]{:S(2)}, u32[]{:S(2)}) %collective-permute-start.27) | collective-permute-done | bytes 147488 | tf_op jit(solution)/shard_map/ppermute | solution.py:56
  93.8 5.1 %collective-permute-done.28 = f32[1,4,8,1152]{3,1,2,0:T(4,128)S(1)} collective-permute-done((f32[1,4,8,1152]{3,1,2,0:T(4,128)S(1)}, f32[1,4,8,1152]{3,1,2,0:T(4,128)S(1)}, u32[]{:S(2)}, u32[]{:S(2)}) %collective-permute-start.28) | collective-permute-done | bytes 147488 | tf_op jit(solution)/shard_map/ppermute | solution.py:652
  99.0 0.5 collective-permute-start.29
  99.5 4.7 %collective-permute-done.29 = f32[1,4,8,1152]{3,1,2,0:T(4,128)S(1)} collective-permute-done((f32[1,4,8,1152]{3,1,2,0:T(4,128)S(1)}, f32[1,4,8,1152]{3,1,2,0:T(4,128)S(1)}, u32[]{:S(2)}, u32[]{:S(2)}) %collective-permute-start.29) | collective-permute-done | bytes 147488 | tf_op jit(solution)/shard_map/ppermute | solution.py:652
  104.3 2.6 %collective-permute-start.30 = (f32[4,1152]{1,0:T(4,128)S(1)}, f32[4,1152]{1,0:T(4,128)S(1)}, u32[]{:S(2)}, u32[]{:S(2)}) collective-permute-start(f32[4,1152]{1,0:T(4,128)S(1)} %get-tuple-element.114), channel_id=1, source_target_pairs={{0,1},{1,0},{2,3},{3,2},{4,5},{5,4},{6,7},{7,6},{8,9},{9,8},{10,11... | collective-permute-start | bytes 55304 | tf_op jit(solution)/shard_map/ppermute | solution.py:39
  106.9 1.7 %collective-permute-done.30.first_ref = f32[4,1152]{1,0:T(4,128)S(1)} collective-permute-done((f32[4,1152]{1,0:T(4,128)S(1)}, f32[4,1152]{1,0:T(4,128)S(1)}, u32[]{:S(2)}, u32[]{:S(2)}) %collective-permute-start.30) | collective-permute-done | bytes 18464 | tf_op jit(solution)/shard_map/ppermute | solution.py:39
  108.6 1.0 shard_map.117.mine_ref
  109.7 0.5 collective-permute-start.33
  110.2 2.8 %collective-permute-start.32 = (f32[4,8,1152]{2,1,0:T(8,128)S(1)}, f32[4,8,1152]{2,1,0:T(8,128)S(1)}, u32[]{:S(2)}, u32[]{:S(2)}) collective-permute-start(f32[4,8,1152]{2,1,0:T(8,128)S(1)} %shard_map.117.mine_ref), channel_id=1, source_target_pairs={{0,1},{1,0},{2,3},{3,2},{4,5},{5,4},{6,7},{7,6},{8,9},{9,8},{10,11... | collective-permute-start | bytes 442376 | tf_op jit(solution)/shard_map/ppermute | solution.py:39
  113.0 2.3 %shard_map.118.refs_4_ = f32[9,320,128]{2,1,0:T(8,128)S(1)} custom-call(s32[6]{0:T(128)S(1)} %stack.47.flag_ref.refs_0_, bf16[1152,1152]{1,0:T(8,128)(2,1)S(1)} %copy-done, f32[4,8,1152]{2,1,0:T(8,128)S(1)} %shard_map.117.mine_ref, f32[4,8,1152]{2,1,0:T(8,128)S(1)} %collective-permute-done.34.other_ref, bf16[10,2,4,8,1152]{4,3,2,1,0:T(8,128)(2,1)S(1)} %copy-done.3), custom_call_target="tpu_custom_call" | custom-call | flops 849346560 | bytes 5898264 | tf_op jit(solution)/shard_map/pallas_call | solution.py:498
  115.4 1.9 %collective-permute-done.32.refs_5_ = f32[4,8,1152]{2,1,0:T(8,128)S(1)} collective-permute-done((f32[4,8,1152]{2,1,0:T(8,128)S(1)}, f32[4,8,1152]{2,1,0:T(8,128)S(1)}, u32[]{:S(2)}, u32[]{:S(2)}) %collective-permute-start.32) | collective-permute-done | bytes 147488 | tf_op jit(solution)/shard_map/ppermute | solution.py:39
  117.2 0.5 collective-permute-start.36
  117.7 0.9 collective-permute-done.35.refs_6_
  118.6 0.2 collective-permute-done.36.refs_8_
  118.8 7.1 %shard_map.119 = f32[320,1152]{1,0:T(8,128)} custom-call(s32[6]{0:T(128)S(1)} %stack.47.flag_ref.refs_0_, f32[216,8,128]{2,1,0:T(8,128)S(1)} %get-tuple-element.63.coef_ref.refs_1_, f32[9,320,128]{2,1,0:T(8,128)S(1)} %get-tuple-element.98.refs_2_, bf16[1152,1152]{1,0:T(8,128)(2,1)S(1)} %copy-done, f32[9,320,128]{2,1,0:T(8,128)S(1)} %shard_map.118.refs_4_, ...), custom_call_target="tpu_custom_call" | custom-call | flops 1698693120 | bytes 11501592 | tf_op jit(solution)/shard_map/pallas_call | solution.py:498
  (98 shorter events, 1.5 us)
Async XLA Ops:
  0.0 2.8 %copy-start.13 = (s32[1,1,3]{2,1,0:T(1,128)S(1)}, s32[1,1,3]{2,1,0:T(1,128)}, u32[]{:S(2)}) copy-start(s32[1,1,3]{2,1,0:T(1,128)} %param.16) | copy-start | bytes 40
  0.0 2.8 %copy-start.12 = (s32[1,1,3]{2,1,0:T(1,128)S(1)}, s32[1,1,3]{2,1,0:T(1,128)}, u32[]{:S(2)}) copy-start(s32[1,1,3]{2,1,0:T(1,128)} %param.15) | copy-start | bytes 40
  0.0 1.4 %copy-start.7 = (f32[10,4,8,1152]{3,2,1,0:T(8,128)S(1)}, f32[10,4,8,1152]{3,2,1,0:T(8,128)}, u32[]{:S(2)}) copy-start(f32[10,4,8,1152]{3,2,1,0:T(8,128)} %param.12) | copy-start | bytes 4423684
  1.4 1.4 %copy-start.9 = (s32[1,1,3,4096]{3,1,2,0:T(1,128)S(1)}, s32[1,1,3,4096]{3,1,2,0:T(1,128)}, u32[]{:S(2)}) copy-start(s32[1,1,3,4096]{3,1,2,0:T(1,128)} %param.17) | copy-start | bytes 147460
  1.4 1.4 %copy-start.10 = (f32[1,1,3,4096]{3,1,2,0:T(1,128)S(1)}, f32[1,1,3,4096]{3,1,2,0:T(1,128)}, u32[]{:S(2)}) copy-start(f32[1,1,3,4096]{3,1,2,0:T(1,128)} %param.18) | copy-start | bytes 147460
  1.4 1.4 %copy-start.11 = (f32[1,1,3,4096]{3,1,2,0:T(1,128)S(1)}, f32[1,1,3,4096]{3,1,2,0:T(1,128)}, u32[]{:S(2)}) copy-start(f32[1,1,3,4096]{3,1,2,0:T(1,128)} %param.19) | copy-start | bytes 147460
  1.4 1.4 %copy-start.14 = (s32[128,1]{1,0:T(8,128)S(1)}, s32[128,1]{1,0:T(8,128)}, u32[]{:S(2)}) copy-start(s32[128,1]{1,0:T(8,128)} %constant.48.clone.lane_ref) | copy-start | bytes 1540
  1.4 1.4 %copy-start.15 = (s32[128,1]{1,0:T(8,128)S(1)}, s32[128,1]{1,0:T(8,128)}, u32[]{:S(2)}) copy-start(s32[128,1]{1,0:T(8,128)} %constant.47.clone.row_ref) | copy-start | bytes 1540
  2.8 8.3 %copy-start.1 = (bf16[10,2,4,8,1152]{4,3,2,1,0:T(8,128)(2,1)S(1)}, bf16[10,2,4,8,1152]{4,3,2,1,0:T(8,128)(2,1)}, u32[]{:S(2)}) copy-start(bf16[10,2,4,8,1152]{4,3,2,1,0:T(8,128)(2,1)} %members_ref.3) | copy-start | bytes 4423684
  6.1 6.8 %copy-start.23 = (f32[32,9]{0,1:T(8,128)S(1)}, f32[32,9]{0,1:T(8,128)}, u32[]{:S(2)}) copy-start(f32[32,9]{0,1:T(8,128)} %param.14) | copy-start | bytes 3460
  6.9 10.2 %collective-permute-start.2 = (f32[1,3,128,128]{3,2,1,0:T(8,128)S(1)}, f32[1,3,128,128]{3,2,1,0:T(8,128)S(1)}, u32[]{:S(2)}, u32[]{:S(2)}) collective-permute-start(f32[1,3,128,128]{3,2,1,0:T(8,128)S(1)} %get-tuple-element.110), channel_id=1, source_target_pairs={{0,4},{4,0},{8,12},{12,8},{16,20},{20,16},{24,28},{28,24},{1,5},{5... | collective-permute-start | bytes 589832 | tf_op jit(solution)/shard_map/ppermute | solution.py:56
  7.8 20.9 %collective-permute-start = (f32[160,1152]{1,0:T(8,128)}, f32[160,1152]{1,0:T(8,128)}, u32[]{:S(2)}, u32[]{:S(2)}) collective-permute-start(f32[160,1152]{1,0:T(8,128)} %get-tuple-element.56), channel_id=1, source_target_pairs={{0,1},{1,0},{2,3},{3,2},{4,5},{5,4},{6,7},{7,6},{8,9},{9,8},{10,11... | collective-permute-start | bytes 2211848 | tf_op jit(solution)/shard_map/ppermute | solution.py:39
  10.9 17.8 %collective-permute-start.1 = (f32[160,1152]{1,0:T(8,128)}, f32[160,1152]{1,0:T(8,128)}, u32[]{:S(2)}, u32[]{:S(2)}) collective-permute-start(f32[160,1152]{1,0:T(8,128)} %get-tuple-element.57), channel_id=1, source_target_pairs={{0,4},{1,2},{2,1},{3,7},{4,0},{5,6},{6,5},{7,3},{8,12},{9,10},{10,... | collective-permute-start | bytes 2211848 | tf_op jit(solution)/shard_map/ppermute | solution.py:40
  13.0 1.4 %copy-start.8 = (f32[10,4,8,1152]{3,2,1,0:T(8,128)S(1)}, f32[10,4,8,1152]{3,2,1,0:T(8,128)}, u32[]{:S(2)}) copy-start(f32[10,4,8,1152]{3,2,1,0:T(8,128)} %param.12) | copy-start | bytes 4423684
  14.3 12.5 %copy-start.17 = (f32[3,128,128]{2,1,0:T(8,128)S(1)}, f32[3,128,128]{2,1,0:T(8,128)}, u32[]{:S(2)}) copy-start(f32[3,128,128]{2,1,0:T(8,128)} %get-tuple-element.109) | copy-start | bytes 589828
  16.0 1.1 copy-start.4
  17.1 0.7 copy-start.18
  17.8 18.7 %copy-start = (bf16[1152,1152]{1,0:T(8,128)(2,1)S(1)}, bf16[1152,1152]{1,0:T(8,128)(2,1)}, u32[]{:S(2)}) copy-start(bf16[1152,1152]{1,0:T(8,128)(2,1)} %refs_3_.1) | copy-start | bytes 7962628
  19.0 7.8 %collective-permute-start.3 = (f32[6,128,128]{2,1,0:T(8,128)S(1)}, f32[6,128,128]{2,1,0:T(8,128)S(1)}, u32[]{:S(2)}, u32[]{:S(2)}) collective-permute-start(f32[6,128,128]{2,1,0:T(8,128)S(1)} %pad_maximum_fusion.2), channel_id=1, source_target_pairs={{0,8},{4,20},{8,0},{12,28},{16,24},{20,4},{24,16},{28,12},{1,9},{5... | collective-permute-start | bytes 1179656 | tf_op jit(solution)/shard_map/ppermute | solution.py:621
  28.7 14.8 %collective-permute-start.5 = (bf16[2,2,4,8,1152]{4,3,2,1,0:T(8,128)(2,1)}, bf16[2,2,4,8,1152]{4,3,2,1,0:T(8,128)(2,1)}, u32[]{:S(2)}, u32[]{:S(2)}) collective-permute-start(bf16[2,2,4,8,1152]{4,3,2,1,0:T(8,128)(2,1)} %slice.42), channel_id=1, source_target_pairs={{0,4},{1,2},{2,1},{3,7},{4,0},{5,6},{6,5},{7,3},{8,12},{9,10},{10,... | collective-permute-start | bytes 884744 | tf_op jit(solution)/shard_map/ppermute | solution.py:40
  28.7 14.8 %collective-permute-start.4 = (bf16[2,2,4,8,1152]{4,3,2,1,0:T(8,128)(2,1)}, bf16[2,2,4,8,1152]{4,3,2,1,0:T(8,128)(2,1)}, u32[]{:S(2)}, u32[]{:S(2)}) collective-permute-start(bf16[2,2,4,8,1152]{4,3,2,1,0:T(8,128)(2,1)} %slice.42), channel_id=1, source_target_pairs={{0,1},{1,0},{2,3},{3,2},{4,5},{5,4},{6,7},{7,6},{8,9},{9,8},{10,11... | collective-permute-start | bytes 884744 | tf_op jit(solution)/shard_map/ppermute | solution.py:39
  32.6 19.0 %collective-permute-start.8 = (f32[12,128,128]{2,1,0:T(8,128)}, f32[12,128,128]{2,1,0:T(8,128)S(1)}, u32[]{:S(2)}, u32[]{:S(2)}) collective-permute-start(f32[12,128,128]{2,1,0:T(8,128)} %pad_maximum_fusion.1), channel_id=1, source_target_pairs={{0,16},{4,12},{8,24},{12,4},{16,0},{20,28},{24,8},{28,20},{1,17},{... | collective-permute-start | bytes 2359304 | tf_op jit(solution)/shard_map/ppermute | solution.py:621
  36.4 1.4 %copy-start.2 = (bf16[10,2,4,8,1152]{4,3,2,1,0:T(8,128)(2,1)S(1)}, bf16[10,2,4,8,1152]{4,3,2,1,0:T(8,128)(2,1)}, u32[]{:S(2)}) copy-start(bf16[10,2,4,8,1152]{4,3,2,1,0:T(8,128)(2,1)} %members_ref.3) | copy-start | bytes 4423684
  37.8 1.4 %copy-start.5 = (f32[9,320,128]{2,1,0:T(8,128)S(1)}, f32[9,320,128]{2,1,0:T(8,128)}, u32[]{:S(2)}) copy-start(f32[9,320,128]{2,1,0:T(8,128)} %copy-done.4) | copy-start | bytes 4423684
  39.2 4.6 %copy-start.20 = (bf16[3,2,4,8,1152]{4,3,2,1,0:T(8,128)(2,1)S(1)}, bf16[3,2,4,8,1152]{4,3,2,1,0:T(8,128)(2,1)}, u32[]{:S(2)}) copy-start(bf16[3,2,4,8,1152]{4,3,2,1,0:T(8,128)(2,1)} %get-tuple-element.74) | copy-start | bytes 1327108
  39.2 6.1 %copy-start.19 = (bf16[3,2,4,8,1152]{4,3,2,1,0:T(8,128)(2,1)S(1)}, bf16[3,2,4,8,1152]{4,3,2,1,0:T(8,128)(2,1)}, u32[]{:S(2)}) copy-start(bf16[3,2,4,8,1152]{4,3,2,1,0:T(8,128)(2,1)} %get-tuple-element.80) | copy-start | bytes 1327108
  43.6 8.1 %copy-start.16 = (f32[12,128,128]{2,1,0:T(8,128)S(1)}, f32[12,128,128]{2,1,0:T(8,128)}, u32[]{:S(2)}) copy-start(f32[12,128,128]{2,1,0:T(8,128)} %pad_maximum_fusion.1) | copy-start | bytes 2359300
  43.7 1.4 %collective-permute-start.6 = (f32[1,4,8,1152]{3,1,2,0:T(4,128)S(1)}, f32[1,4,8,1152]{3,1,2,0:T(4,128)S(1)}, u32[]{:S(2)}, u32[]{:S(2)}) collective-permute-start(f32[1,4,8,1152]{3,1,2,0:T(4,128)S(1)} %constant_dynamic-slice_fusion.1), channel_id=1, source_target_pairs={{0,4},{4,0},{8,12},{12,8},{16,20},{20,16},{24,28},{28,24},{1,5},{5... | collective-permute-start | bytes 442376 | tf_op jit(solution)/shard_map/ppermute | solution.py:56
  43.8 8.0 %collective-permute-start.10 = (bf16[3,2,4,8,1152]{4,3,2,1,0:T(8,128)(2,1)S(1)}, bf16[3,2,4,8,1152]{4,3,2,1,0:T(8,128)(2,1)S(1)}, u32[]{:S(2)}, u32[]{:S(2)}) collective-permute-start(bf16[3,2,4,8,1152]{4,3,2,1,0:T(8,128)(2,1)S(1)} %copy-done.20), channel_id=1, source_target_pairs={{0,4},{1,2},{2,1},{3,7},{4,0},{5,6},{6,5},{7,3},{8,12},{9,10},{10,... | collective-permute-start | bytes 1327112 | tf_op jit(solution)/shard_map/ppermute | solution.py:40
  44.3 13.0 %collective-permute-start.9 = (bf16[3,2,4,8,1152]{4,3,2,1,0:T(8,128)(2,1)S(1)}, bf16[3,2,4,8,1152]{4,3,2,1,0:T(8,128)(2,1)S(1)}, u32[]{:S(2)}, u32[]{:S(2)}) collective-permute-start(bf16[3,2,4,8,1152]{4,3,2,1,0:T(8,128)(2,1)S(1)} %copy-done.20), channel_id=1, source_target_pairs={{0,1},{1,0},{2,3},{3,2},{4,5},{5,4},{6,7},{7,6},{8,9},{9,8},{10,11... | collective-permute-start | bytes 1327112 | tf_op jit(solution)/shard_map/ppermute | solution.py:39
  45.2 5.2 %collective-permute-start.7 = (f32[1,4,8,1152]{3,1,2,0:T(4,128)S(1)}, f32[1,4,8,1152]{3,1,2,0:T(4,128)S(1)}, u32[]{:S(2)}, u32[]{:S(2)}) collective-permute-start(f32[1,4,8,1152]{3,1,2,0:T(4,128)S(1)} %dynamic-slice_add_fusion.1), channel_id=1, source_target_pairs={{0,8},{4,20},{8,0},{12,28},{16,24},{20,4},{24,16},{28,12},{1,9},{5... | collective-permute-start | bytes 442376 | tf_op jit(solution)/shard_map/ppermute | solution.py:652
  45.3 22.2 %collective-permute-start.15 = (bf16[3,2,4,8,1152]{4,3,2,1,0:T(8,128)(2,1)S(1)}, bf16[3,2,4,8,1152]{4,3,2,1,0:T(8,128)(2,1)S(1)}, u32[]{:S(2)}, u32[]{:S(2)}) collective-permute-start(bf16[3,2,4,8,1152]{4,3,2,1,0:T(8,128)(2,1)S(1)} %copy-done.19), channel_id=1, source_target_pairs={{0,4},{1,2},{2,1},{3,7},{4,0},{5,6},{6,5},{7,3},{8,12},{9,10},{10,... | collective-permute-start | bytes 1327112 | tf_op jit(solution)/shard_map/ppermute | solution.py:40
  50.4 17.1 %collective-permute-start.14 = (bf16[3,2,4,8,1152]{4,3,2,1,0:T(8,128)(2,1)S(1)}, bf16[3,2,4,8,1152]{4,3,2,1,0:T(8,128)(2,1)S(1)}, u32[]{:S(2)}, u32[]{:S(2)}) collective-permute-start(bf16[3,2,4,8,1152]{4,3,2,1,0:T(8,128)(2,1)S(1)} %copy-done.19), channel_id=1, source_target_pairs={{0,1},{1,0},{2,3},{3,2},{4,5},{5,4},{6,7},{7,6},{8,9},{9,8},{10,11... | collective-permute-start | bytes 1327112 | tf_op jit(solution)/shard_map/ppermute | solution.py:39
  51.8 12.6 %copy-start.22 = (bf16[1,2,4,8,1152]{4,3,2,1,0:T(8,128)(2,1)S(1)}, bf16[1,2,4,8,1152]{4,3,2,1,0:T(8,128)(2,1)}, u32[]{:S(2)}) copy-start(bf16[1,2,4,8,1152]{4,3,2,1,0:T(8,128)(2,1)} %get-tuple-element.84) | copy-start | bytes 442372
  59.1 16.3 %copy-start.21 = (bf16[1,2,4,8,1152]{4,3,2,1,0:T(8,128)(2,1)S(1)}, bf16[1,2,4,8,1152]{4,3,2,1,0:T(8,128)(2,1)}, u32[]{:S(2)}) copy-start(bf16[1,2,4,8,1152]{4,3,2,1,0:T(8,128)(2,1)} %get-tuple-element.93) | copy-start | bytes 442372
  59.2 5.2 %collective-permute-start.11 = (f32[1,4,8,1152]{3,1,2,0:T(4,128)S(1)}, f32[1,4,8,1152]{3,1,2,0:T(4,128)S(1)}, u32[]{:S(2)}, u32[]{:S(2)}) collective-permute-start(f32[1,4,8,1152]{3,1,2,0:T(4,128)S(1)} %add.47), channel_id=1, source_target_pairs={{0,16},{4,12},{8,24},{12,4},{16,0},{20,28},{24,8},{28,20},{1,17},{... | collective-permute-start | bytes 442376 | tf_op jit(solution)/shard_map/ppermute | solution.py:652
  59.3 5.1 %collective-permute-start.13 = (f32[3,4,1152]{2,1,0:T(4,128)S(1)}, f32[3,4,1152]{2,1,0:T(4,128)S(1)}, u32[]{:S(2)}, u32[]{:S(2)}) collective-permute-start(f32[3,4,1152]{2,1,0:T(4,128)S(1)} %get-tuple-element.117), channel_id=1, source_target_pairs={{0,4},{1,2},{2,1},{3,7},{4,0},{5,6},{6,5},{7,3},{8,12},{9,10},{10,... | collective-permute-start | bytes 165896 | tf_op jit(solution)/shard_map/ppermute | solution.py:40
  59.4 8.1 %collective-permute-start.12 = (f32[3,4,1152]{2,1,0:T(4,128)S(1)}, f32[3,4,1152]{2,1,0:T(4,128)S(1)}, u32[]{:S(2)}, u32[]{:S(2)}) collective-permute-start(f32[3,4,1152]{2,1,0:T(4,128)S(1)} %get-tuple-element.118), channel_id=1, source_target_pairs={{0,1},{1,0},{2,3},{3,2},{4,5},{5,4},{6,7},{7,6},{8,9},{9,8},{10,11... | collective-permute-start | bytes 165896 | tf_op jit(solution)/shard_map/ppermute | solution.py:39
  64.4 8.1 %collective-permute-start.19 = (bf16[1,2,4,8,1152]{4,3,2,1,0:T(8,128)(2,1)S(1)}, bf16[1,2,4,8,1152]{4,3,2,1,0:T(8,128)(2,1)S(1)}, u32[]{:S(2)}, u32[]{:S(2)}) collective-permute-start(bf16[1,2,4,8,1152]{4,3,2,1,0:T(8,128)(2,1)S(1)} %copy-done.22), channel_id=1, source_target_pairs={{0,4},{1,2},{2,1},{3,7},{4,0},{5,6},{6,5},{7,3},{8,12},{9,10},{10,... | collective-permute-start | bytes 442376 | tf_op jit(solution)/shard_map/ppermute | solution.py:40
  64.4 8.1 %collective-permute-start.18 = (bf16[1,2,4,8,1152]{4,3,2,1,0:T(8,128)(2,1)S(1)}, bf16[1,2,4,8,1152]{4,3,2,1,0:T(8,128)(2,1)S(1)}, u32[]{:S(2)}, u32[]{:S(2)}) collective-permute-start(bf16[1,2,4,8,1152]{4,3,2,1,0:T(8,128)(2,1)S(1)} %copy-done.22), channel_id=1, source_target_pairs={{0,1},{1,0},{2,3},{3,2},{4,5},{5,4},{6,7},{7,6},{8,9},{9,8},{10,11... | collective-permute-start | bytes 442376 | tf_op jit(solution)/shard_map/ppermute | solution.py:39
  67.5 1.4 %collective-permute-start.17 = (f32[4,1152]{1,0:T(4,128)S(1)}, f32[4,1152]{1,0:T(4,128)S(1)}, u32[]{:S(2)}, u32[]{:S(2)}) collective-permute-start(f32[4,1152]{1,0:T(4,128)S(1)} %get-tuple-element.115), channel_id=1, source_target_pairs={{0,4},{1,2},{2,1},{3,7},{4,0},{5,6},{6,5},{7,3},{8,12},{9,10},{10,... | collective-permute-start | bytes 55304 | tf_op jit(solution)/shard_map/ppermute | solution.py:40
  67.6 3.8 %collective-permute-start.16 = (f32[4,1152]{1,0:T(4,128)S(1)}, f32[4,1152]{1,0:T(4,128)S(1)}, u32[]{:S(2)}, u32[]{:S(2)}) collective-permute-start(f32[4,1152]{1,0:T(4,128)S(1)} %get-tuple-element.116), channel_id=1, source_target_pairs={{0,1},{1,0},{2,3},{3,2},{4,5},{5,4},{6,7},{7,6},{8,9},{9,8},{10,11... | collective-permute-start | bytes 55304 | tf_op jit(solution)/shard_map/ppermute | solution.py:39
  72.5 10.3 %copy-start.3 = (bf16[10,2,4,8,1152]{4,3,2,1,0:T(8,128)(2,1)S(1)}, bf16[10,2,4,8,1152]{4,3,2,1,0:T(8,128)(2,1)}, u32[]{:S(2)}) copy-start(bf16[10,2,4,8,1152]{4,3,2,1,0:T(8,128)(2,1)} %members_ref.3) | copy-start | bytes 4423684
  72.5 10.3 %copy-start.6 = (f32[9,320,128]{2,1,0:T(8,128)S(1)}, f32[9,320,128]{2,1,0:T(8,128)}, u32[]{:S(2)}) copy-start(f32[9,320,128]{2,1,0:T(8,128)} %copy-done.4) | copy-start | bytes 4423684
  72.5 3.8 %collective-permute-start.22 = (f32[4,8,1152]{2,1,0:T(8,128)S(1)}, f32[4,8,1152]{2,1,0:T(8,128)S(1)}, u32[]{:S(2)}, u32[]{:S(2)}) collective-permute-start(f32[4,8,1152]{2,1,0:T(8,128)S(1)} %shard_map.114.mine_ref), channel_id=1, source_target_pairs={{0,4},{4,0},{8,12},{12,8},{16,20},{20,16},{24,28},{28,24},{1,5},{5... | collective-permute-start | bytes 442376 | tf_op jit(solution)/shard_map/ppermute | solution.py:56
  72.6 6.0 %collective-permute-start.21 = (f32[4,8,1152]{2,1,0:T(8,128)S(1)}, f32[4,8,1152]{2,1,0:T(8,128)S(1)}, u32[]{:S(2)}, u32[]{:S(2)}) collective-permute-start(f32[4,8,1152]{2,1,0:T(8,128)S(1)} %shard_map.114.mine_ref), channel_id=1, source_target_pairs={{0,4},{1,2},{2,1},{3,7},{4,0},{5,6},{6,5},{7,3},{8,12},{9,10},{10,... | collective-permute-start | bytes 442376 | tf_op jit(solution)/shard_map/ppermute | solution.py:40
  73.1 6.9 %collective-permute-start.20 = (f32[4,8,1152]{2,1,0:T(8,128)S(1)}, f32[4,8,1152]{2,1,0:T(8,128)S(1)}, u32[]{:S(2)}, u32[]{:S(2)}) collective-permute-start(f32[4,8,1152]{2,1,0:T(8,128)S(1)} %shard_map.114.mine_ref), channel_id=1, source_target_pairs={{0,1},{1,0},{2,3},{3,2},{4,5},{5,4},{6,7},{7,6},{8,9},{9,8},{10,11... | collective-permute-start | bytes 442376 | tf_op jit(solution)/shard_map/ppermute | solution.py:39
  75.4 5.1 %collective-permute-start.26 = (bf16[1,2,4,8,1152]{4,3,2,1,0:T(8,128)(2,1)S(1)}, bf16[1,2,4,8,1152]{4,3,2,1,0:T(8,128)(2,1)S(1)}, u32[]{:S(2)}, u32[]{:S(2)}) collective-permute-start(bf16[1,2,4,8,1152]{4,3,2,1,0:T(8,128)(2,1)S(1)} %copy-done.21), channel_id=1, source_target_pairs={{0,4},{1,2},{2,1},{3,7},{4,0},{5,6},{6,5},{7,3},{8,12},{9,10},{10,... | collective-permute-start | bytes 442376 | tf_op jit(solution)/shard_map/ppermute | solution.py:40
  75.4 7.3 %collective-permute-start.25 = (bf16[1,2,4,8,1152]{4,3,2,1,0:T(8,128)(2,1)S(1)}, bf16[1,2,4,8,1152]{4,3,2,1,0:T(8,128)(2,1)S(1)}, u32[]{:S(2)}, u32[]{:S(2)}) collective-permute-start(bf16[1,2,4,8,1152]{4,3,2,1,0:T(8,128)(2,1)S(1)} %copy-done.21), channel_id=1, source_target_pairs={{0,1},{1,0},{2,3},{3,2},{4,5},{5,4},{6,7},{7,6},{8,9},{9,8},{10,11... | collective-permute-start | bytes 442376 | tf_op jit(solution)/shard_map/ppermute | solution.py:39
  80.0 2.7 %collective-permute-start.23 = (f32[4,8,1152]{2,1,0:T(8,128)S(1)}, f32[4,8,1152]{2,1,0:T(8,128)S(1)}, u32[]{:S(2)}, u32[]{:S(2)}) collective-permute-start(f32[4,8,1152]{2,1,0:T(8,128)S(1)} %collective-permute-done.20.refs_7_), channel_id=1, source_target_pairs={{0,4},{4,0},{8,12},{12,8},{16,20},{20,16},{24,28},{28,24},{1,5},{5... | collective-permute-start | bytes 442376 | tf_op jit(solution)/shard_map/ppermute | solution.py:56
  80.0 2.7 %collective-permute-start.24 = (f32[4,8,1152]{2,1,0:T(8,128)S(1)}, f32[4,8,1152]{2,1,0:T(8,128)S(1)}, u32[]{:S(2)}, u32[]{:S(2)}) collective-permute-start(f32[4,8,1152]{2,1,0:T(8,128)S(1)} %collective-permute-done.21.refs_9_), channel_id=1, source_target_pairs={{0,4},{4,0},{8,12},{12,8},{16,20},{20,16},{24,28},{28,24},{1,5},{5... | collective-permute-start | bytes 442376 | tf_op jit(solution)/shard_map/ppermute | solution.py:56
  92.3 1.4 %collective-permute-start.27 = (f32[1,4,8,1152]{3,1,2,0:T(4,128)S(1)}, f32[1,4,8,1152]{3,1,2,0:T(4,128)S(1)}, u32[]{:S(2)}, u32[]{:S(2)}) collective-permute-start(f32[1,4,8,1152]{3,1,2,0:T(4,128)S(1)} %constant_dynamic-slice_fusion), channel_id=1, source_target_pairs={{0,4},{4,0},{8,12},{12,8},{16,20},{20,16},{24,28},{28,24},{1,5},{5... | collective-permute-start | bytes 442376 | tf_op jit(solution)/shard_map/ppermute | solution.py:56
  93.7 5.2 %collective-permute-start.28 = (f32[1,4,8,1152]{3,1,2,0:T(4,128)S(1)}, f32[1,4,8,1152]{3,1,2,0:T(4,128)S(1)}, u32[]{:S(2)}, u32[]{:S(2)}) collective-permute-start(f32[1,4,8,1152]{3,1,2,0:T(4,128)S(1)} %dynamic-slice_add_fusion), channel_id=1, source_target_pairs={{0,8},{4,20},{8,0},{12,28},{16,24},{20,4},{24,16},{28,12},{1,9},{5... | collective-permute-start | bytes 442376 | tf_op jit(solution)/shard_map/ppermute | solution.py:652
  99.0 5.2 %collective-permute-start.29 = (f32[1,4,8,1152]{3,1,2,0:T(4,128)S(1)}, f32[1,4,8,1152]{3,1,2,0:T(4,128)S(1)}, u32[]{:S(2)}, u32[]{:S(2)}) collective-permute-start(f32[1,4,8,1152]{3,1,2,0:T(4,128)S(1)} %add.50), channel_id=1, source_target_pairs={{0,16},{4,12},{8,24},{12,4},{16,0},{20,28},{24,8},{28,20},{1,17},{... | collective-permute-start | bytes 442376 | tf_op jit(solution)/shard_map/ppermute | solution.py:652
  104.3 2.6 %collective-permute-start.31 = (f32[4,1152]{1,0:T(4,128)S(1)}, f32[4,1152]{1,0:T(4,128)S(1)}, u32[]{:S(2)}, u32[]{:S(2)}) collective-permute-start(f32[4,1152]{1,0:T(4,128)S(1)} %get-tuple-element.113), channel_id=1, source_target_pairs={{0,4},{1,2},{2,1},{3,7},{4,0},{5,6},{6,5},{7,3},{8,12},{9,10},{10,... | collective-permute-start | bytes 55304 | tf_op jit(solution)/shard_map/ppermute | solution.py:40
  104.3 4.3 %collective-permute-start.30 = (f32[4,1152]{1,0:T(4,128)S(1)}, f32[4,1152]{1,0:T(4,128)S(1)}, u32[]{:S(2)}, u32[]{:S(2)}) collective-permute-start(f32[4,1152]{1,0:T(4,128)S(1)} %get-tuple-element.114), channel_id=1, source_target_pairs={{0,1},{1,0},{2,3},{3,2},{4,5},{5,4},{6,7},{7,6},{8,9},{9,8},{10,11... | collective-permute-start | bytes 55304 | tf_op jit(solution)/shard_map/ppermute | solution.py:39
  109.7 3.4 %collective-permute-start.34 = (f32[4,8,1152]{2,1,0:T(8,128)S(1)}, f32[4,8,1152]{2,1,0:T(8,128)S(1)}, u32[]{:S(2)}, u32[]{:S(2)}) collective-permute-start(f32[4,8,1152]{2,1,0:T(8,128)S(1)} %shard_map.117.mine_ref), channel_id=1, source_target_pairs={{0,4},{4,0},{8,12},{12,8},{16,20},{20,16},{24,28},{28,24},{1,5},{5... | collective-permute-start | bytes 442376 | tf_op jit(solution)/shard_map/ppermute | solution.py:56
  109.7 5.6 %collective-permute-start.33 = (f32[4,8,1152]{2,1,0:T(8,128)S(1)}, f32[4,8,1152]{2,1,0:T(8,128)S(1)}, u32[]{:S(2)}, u32[]{:S(2)}) collective-permute-start(f32[4,8,1152]{2,1,0:T(8,128)S(1)} %shard_map.117.mine_ref), channel_id=1, source_target_pairs={{0,4},{1,2},{2,1},{3,7},{4,0},{5,6},{6,5},{7,3},{8,12},{9,10},{10,... | collective-permute-start | bytes 442376 | tf_op jit(solution)/shard_map/ppermute | solution.py:40
  110.2 7.0 %collective-permute-start.32 = (f32[4,8,1152]{2,1,0:T(8,128)S(1)}, f32[4,8,1152]{2,1,0:T(8,128)S(1)}, u32[]{:S(2)}, u32[]{:S(2)}) collective-permute-start(f32[4,8,1152]{2,1,0:T(8,128)S(1)} %shard_map.117.mine_ref), channel_id=1, source_target_pairs={{0,1},{1,0},{2,3},{3,2},{4,5},{5,4},{6,7},{7,6},{8,9},{9,8},{10,11... | collective-permute-start | bytes 442376 | tf_op jit(solution)/shard_map/ppermute | solution.py:39
  117.2 1.4 %collective-permute-start.35 = (f32[4,8,1152]{2,1,0:T(8,128)S(1)}, f32[4,8,1152]{2,1,0:T(8,128)S(1)}, u32[]{:S(2)}, u32[]{:S(2)}) collective-permute-start(f32[4,8,1152]{2,1,0:T(8,128)S(1)} %collective-permute-done.32.refs_5_), channel_id=1, source_target_pairs={{0,4},{4,0},{8,12},{12,8},{16,20},{20,16},{24,28},{28,24},{1,5},{5... | collective-permute-start | bytes 442376 | tf_op jit(solution)/shard_map/ppermute | solution.py:56
  117.2 1.6 %collective-permute-start.36 = (f32[4,8,1152]{2,1,0:T(8,128)S(1)}, f32[4,8,1152]{2,1,0:T(8,128)S(1)}, u32[]{:S(2)}, u32[]{:S(2)}) collective-permute-start(f32[4,8,1152]{2,1,0:T(8,128)S(1)} %collective-permute-done.33.refs_7_), channel_id=1, source_target_pairs={{0,4},{4,0},{8,12},{12,8},{16,20},{20,16},{24,28},{28,24},{1,5},{5... | collective-permute-start | bytes 442376 | tf_op jit(solution)/shard_map/ppermute | solution.py:56

commit v4 on v3

--- a/solution.py
+++ b/solution.py
@@ -12,7 +12,6 @@
 ITERS = 2
 LANES = 128
 OBS_CHUNK = 1024
-PARTS = ((2, "forward"), (3, "chip0"), (3, "chip1"), (1, "adjoint"), (1, None))
 EVEN, CORE, HAS_FIRST, HAS_SECOND, HAS_BELOW, HAS_ABOVE = range(6)
 
 
@@ -175,9 +174,12 @@
     )
 
 
-def field_kernel(mark_ref, slots_ref, weight_ref, pull_ref, where_ref):
+def field_kernel(mark_ref, *refs):
+    groups = refs[:-3]
+    weight_ref, pull_ref, where_ref = refs[-3:]
     tile_count = where_ref.shape[0]
     half = TLON // 2
+    size, rows = groups[0].shape[0], weight_ref.shape[1]
 
     def note(slot, carry):
         mark = mark_ref[slot]
@@ -188,21 +190,27 @@
 
         return carry
 
+    def tile_rows(slot, here):
+        at = lax.rem(slot, size)
+        out = groups[0][at, here]
+        for number in range(1, len(groups)):
+            out = jnp.where(slot >= number * size, groups[number][at, here], out)
+        return out
+
     for tile in range(tile_count):
         where_ref[tile] = 0
     lax.fori_loop(0, mark_ref.shape[0], note, 0)
-    rows = weight_ref.shape[1]
     lane = lax.broadcasted_iota(jnp.int32, (rows, TLON), 1)
+    upper, lower = slice(0, rows), slice(rows, 2 * rows)
     for pair in range(tile_count // 2):
         left = where_ref[2 * pair]
         right = where_ref[2 * pair + 1]
         before = where_ref[(2 * pair - 1) % tile_count]
         here = slice(pair * TLON, (pair + 1) * TLON)
-        first, second = slots_ref[left, :rows], slots_ref[right, :rows]
+        first, second = tile_rows(left, upper), tile_rows(right, upper)
         weight_ref[0, :, here] = jnp.where(lane < half, first, pltpu.roll(second, half, 1))
         weight_ref[1, :, here] = jnp.where(lane < half, pltpu.roll(first, half, 1), second)
-        first, second = slots_ref[left, rows:], slots_ref[right, rows:]
-        third = slots_ref[before, rows:]
+        first, second, third = tile_rows(left, lower), tile_rows(right, lower), tile_rows(before, lower)
         pull_ref[:, here] = (
             jnp.where(lane <= half, first, 0.0)
             + jnp.where(lane >= half, pltpu.roll(second, half, 1), 0.0)
@@ -210,13 +218,13 @@
         )
 
 
-def band_fields(slots, lon_cells):
-    rows = slots.shape[1] // 2
-    marks = slots[:, rows, TLON - 1].astype(jnp.int32)
+def band_fields(held, lon_cells):
+    rows = held[0].shape[1] // 2
+    marks = jnp.concatenate([slots[:, rows, TLON - 1] for slots in held]).astype(jnp.int32)
     vmem = pl.BlockSpec(memory_space=pltpu.VMEM)
     return pl.pallas_call(
         field_kernel,
-        in_specs=[pl.BlockSpec(memory_space=pltpu.SMEM), vmem],
+        in_specs=[pl.BlockSpec(memory_space=pltpu.SMEM)] + [vmem] * len(held),
         out_specs=[vmem, vmem],
         out_shape=[
             jax.ShapeDtypeStruct((2, rows, lon_cells), jnp.float32),
@@ -227,7 +235,7 @@
         cost_estimate=pl.CostEstimate(
             flops=rows * lon_cells * 8, bytes_accessed=rows * lon_cells * 24, transcendentals=0
         ),
-    )(marks, slots)
+    )(marks, *held)
 
 
 def observation_slots(tiles, counts, index, value, weight, var_count, lev_count, row_count):
@@ -248,7 +256,7 @@
     even = flag_ref[EVEN] == 1
     has_below, has_above = flag_ref[HAS_BELOW] == 1, flag_ref[HAS_ABOVE] == 1
     levels, rows, lon = inc_ref.shape
-    first, second = first_ref[...], second_ref[...]
+    first, second = first_ref[first_ref.shape[0] - 1], second_ref[second_ref.shape[0] - 1]
     lowest = jnp.concatenate([inc_ref[lev, 0:1] for lev in range(levels)], axis=0)
     highest = jnp.concatenate([inc_ref[lev, rows - 1 : rows] for lev in range(levels)], axis=0)
     below = jnp.where(has_below, jnp.where(even, second, first), lowest)
@@ -305,8 +313,8 @@
     return out
 
 
-def sum_members(spread_ref, zonal_ref, members_ref, inc_ref):
-    size, variables, levels, rows, lon = members_ref.shape
+def sum_members(core, spread_ref, zonal_ref, members_ref, mine_ref, other_ref):
+    size, _, levels, rows, lon = members_ref.shape
     spread = jnp.concatenate(
         [spread_ref[chunk].astype(jnp.bfloat16) for chunk in range(spread_ref.shape[0])], axis=1
     )
@@ -315,11 +323,11 @@
         lanes = slice(start, start + wide)
         localized = jnp.dot(spread, zonal_ref[:, lanes], preferred_element_type=jnp.float32)
         localized = localized.reshape(size, levels, rows, wide)
-        for var in range(variables):
+        for var, inc_ref in ((core, mine_ref), (1 - core, other_ref)):
             total = members_ref[0, var, :, :, lanes].astype(jnp.float32) * localized[0]
             for k in range(1, size):
                 total += members_ref[k, var, :, :, lanes].astype(jnp.float32) * localized[k]
-            inc_ref[var, :, :, lanes] = total
+            inc_ref[:, :, lanes] = total
 
 
 def edge_kernel(alpha_ref, first_ref, second_ref):
@@ -347,7 +355,8 @@
     second_ref,
     zonal_ref,
     members_from,
-    inc_ref,
+    mine_ref,
+    other_ref,
     below_ref,
     above_ref,
     spread_ref,
@@ -374,7 +383,7 @@
 
     lax.fori_loop(0, own_ref.shape[0], step, 0)
     copy.wait()
-    sum_members(spread_ref, zonal_ref, members_ref, inc_ref)
+    sum_members(flag_ref[CORE], spread_ref, zonal_ref, members_ref, mine_ref, other_ref)
 
 
 def wide_rows(own_ref, below_ref, above_ref, chunk, start, rows, half_band):
@@ -448,7 +457,7 @@
     adjoints = refs[7:11]
     members_ref = refs[11]
     partners = refs[12 : 12 + 2 * parts]
-    inc_ref, current_ref, weighted_ref, back_ref, spread_ref = refs[12 + 2 * parts :]
+    mine_ref, other_ref, current_ref, weighted_ref, back_ref, spread_ref = refs[12 + 2 * parts :]
     lines = own_ref.shape[1]
     half_band = below_ref.shape[1] * rows // lines
     taps = 2 * half_band + 1
@@ -467,7 +476,7 @@
         return carry
 
     lax.fori_loop(0, own_ref.shape[0], step, 0)
-    sum_members(spread_ref, zonal_ref, members_ref, inc_ref)
+    sum_members(flag_ref[CORE], spread_ref, zonal_ref, members_ref, mine_ref, other_ref)
 
 
 def last_kernel(rows, parts, taps, *refs):
@@ -552,17 +561,22 @@
     )(merid_coef, own)
 
 
-def band_setup(held, lev_count, rows, lon_cells):
-    weights, pulls = band_fields(held, lon_cells)
-    weights = weights.reshape(2, 2, lev_count, rows, lon_cells)
-    pulls = pulls.reshape(2, lev_count, rows, lon_cells)
-    rims = band_swap(
-        *by_partner(
-            jnp.concatenate([weights[:, 0, :, 0], pulls[None, 0, :, 0]]),
-            jnp.concatenate([weights[:, 1, :, -1], pulls[None, 1, :, -1]]),
-        )
-    )
-    return weights, pulls, rims
+def pack_kernel(flag_ref, inc_ref, weight_ref, pull_ref, first_ref, second_ref):
+    even = flag_ref[EVEN] == 1
+    levels, rows, _ = inc_ref.shape
+
+    def line(ref, *place):
+        return jnp.concatenate([ref[(*place[:-1], lev, slice(place[-1], place[-1] + 1))] for lev in range(levels)], axis=0)
+
+    for number in range(4):
+        if number < 2:
+            low, high = line(weight_ref, number, 0, 0), line(weight_ref, number, 1, rows - 1)
+        elif number == 2:
+            low, high = line(pull_ref, 0, 0), line(pull_ref, 1, rows - 1)
+        else:
+            low, high = line(inc_ref, 0), line(inc_ref, rows - 1)
+        first_ref[number] = jnp.where(even, high, low)
+        second_ref[number] = jnp.where(even, low, high)
 
 
 def body(
@@ -597,11 +611,6 @@
     halo_first, halo_second = band_swap(*sends)
     coeffs, own = setup(merid_coef, alpha.reshape(lines, lon_cells), rows)
 
-    total_share = sum(share for share, _ in PARTS)
-    cuts = [sum(share for share, _ in PARTS[:i]) * members_per // total_share for i in range(len(PARTS) + 1)]
-    pieces = [(x, y, event) for x, y, (_, event) in zip(cuts[:-1], cuts[1:], PARTS) if x < y]
-    parts = [members[x:y] for x, y, _ in pieces]
-
     held = observation_slots(
         slot_tile.reshape(-1),
         obs_count.reshape(-1),
@@ -613,21 +622,12 @@
         rows,
     )
     steps = chip_steps()
-    for number, perm in enumerate(steps):
-        if number == len(steps) - 1:
-            halo_first, halo_second, held, coeffs, own, parts = lax.optimization_barrier(
-                (halo_first, halo_second, held, coeffs, own, parts)
-            )
-        held = jnp.concatenate([held, lax.ppermute(held, "mem", perm)], axis=0)
-    fetched = [band_swap(part, part) for part in parts]
-
-    def pin(value, event):
-        for number, (_, _, name) in enumerate(pieces):
-            if name == event:
-                value, fetched[number] = lax.optimization_barrier((value, fetched[number]))
-        return value
-
-    inc_shape = jax.ShapeDtypeStruct((var_count, lev_count, rows, lon_cells), jnp.float32)
+    halo_first, halo_second, held, coeffs, own, sent = lax.optimization_barrier(
+        (halo_first, halo_second, held, coeffs, own, members)
+    )
+    fetched = band_swap(sent, sent)
+
+    inc_shape = jax.ShapeDtypeStruct((lev_count, rows, lon_cells), jnp.float32)
     line_shape = jax.ShapeDtypeStruct((lines, lon_cells), jnp.float32)
     chunks = lon_cells // LANES
     chunk_shape = jax.ShapeDtypeStruct((chunks, lines, LANES), jnp.float32)
@@ -636,29 +636,13 @@
     chunk_scratch = pltpu.VMEM((chunks, lines, LANES), jnp.float32)
     weighted_scratch = pltpu.VMEM((2 * lines, lon_cells), jnp.bfloat16)
     back_scratch = pltpu.VMEM((chunks, 2 * lines, LANES), jnp.float32)
-    partial_value, below, above = call(
-        forward_kernel,
-        (flags, coeffs, own, halo_first, halo_second, zonal_loc, members),
-        [inc_shape, halo_shape, halo_shape],
-        [chunk_scratch, pltpu.VMEM(members.shape, members.dtype), pltpu.SemaphoreType.DMA],
-        zonal_flops,
-        anywhere=1,
-    )
-    partial_value = pin(partial_value, "forward")
-    for iteration in range(ITERS):
-        mine, other = core_split(partial_value)
-        inc = mine + core_swap(other)
-        for number, perm in enumerate(steps):
-            inc = inc + lax.ppermute(inc, "mem", perm)
-            if iteration == 0 and number == 0:
-                inc, held = lax.optimization_barrier((inc, held))
-                weights, pulls, rims = band_setup(held, lev_count, rows, lon_cells)
-            if iteration == 0 and number == len(steps) - 1:
-                inc, rims = lax.optimization_barrier((inc, rims))
-            if iteration == 0:
-                inc = pin(inc, f"chip{number}")
-        inc = inc[0]
-        edges = band_swap(*by_partner(inc[:, 0], inc[:, -1]))
+    def observe(inc, weights, pulls, rims=None):
+        if rims is None:
+            send_shape = jax.ShapeDtypeStruct((4, lev_count, lon_cells), jnp.float32)
+            sends = call(pack_kernel, (flags, inc, weights, pulls), [send_shape, send_shape], [], 0)
+            edges = rims = band_swap(*sends)
+        else:
+            edges = band_swap(*by_partner(inc[None, :, 0], inc[None, :, -1]))
         (adjoint,) = call(
             observe_kernel,
             (flags, inc, *edges, weights, pulls, *rims),
@@ -666,32 +650,72 @@
             [],
             40 * 2 * inc.size,
         )
-        if iteration == 0:
-            adjoint = pin(adjoint, "adjoint")
+        return adjoint, rims
+
+    def opening(held, coeffs, own, halo_first, halo_second):
+        held = [held]
+        for perm in steps[:-1]:
+            held = held + [lax.ppermute(x, "mem", perm) for x in held]
+        got = [lax.ppermute(x, "mem", steps[-1]) for x in held]
+        mine, other, below, above = call(
+            forward_kernel,
+            (flags, coeffs, own, halo_first, halo_second, zonal_loc, members),
+            [inc_shape, inc_shape, halo_shape, halo_shape],
+            [chunk_scratch, pltpu.VMEM(members.shape, members.dtype), pltpu.SemaphoreType.DMA],
+            zonal_flops,
+            anywhere=1,
+        )
+        inc = mine + core_swap(other)
+        for number, perm in enumerate(steps):
+            inc = inc + lax.ppermute(inc, "mem", perm)
+            if number == 0:
+                inc, got = lax.optimization_barrier((inc, got))
+        weights, pulls = band_fields(held + got, lon_cells)
+        weights = weights.reshape(2, 2, lev_count, rows, lon_cells)
+        pulls = pulls.reshape(2, lev_count, rows, lon_cells)
+        adjoint, rims = observe(inc, weights, pulls)
+        return adjoint, weights, pulls, rims, below, above
+
+    operands = (held, coeffs, own, halo_first, halo_second)
+    shapes = jax.eval_shape(opening, *operands)
+    adjoint, weights, pulls, rims, below, above = lax.cond(
+        lax.axis_index("lat") < lax.axis_size("lat"),
+        opening,
+        lambda *_: jax.tree.map(lambda x: jnp.zeros(x.shape, x.dtype), shapes),
+        *operands,
+    )
+    (adjoint, weights, pulls, rims, below, above, own, coeffs), fetched = lax.optimization_barrier(
+        ((adjoint, weights, pulls, rims, below, above, own, coeffs), fetched)
+    )
+    for iteration in range(ITERS):
+        if iteration > 0:
+            inc = mine + core_swap(other)
+            for perm in steps:
+                inc = inc + lax.ppermute(inc, "mem", perm)
+            adjoint, _ = observe(inc, weights, pulls, rims)
         first, second = band_swap(adjoint, adjoint)
-        other = core_swap(adjoint)
+        adjoint_other = core_swap(adjoint)
         (own_back,) = call(
             own_kernel,
-            (flags, zonal_loc, adjoint, other, members),
+            (flags, zonal_loc, adjoint, adjoint_other, members),
             [chunk_shape],
             [pltpu.VMEM((lines, lon_cells), jnp.bfloat16)],
             zonal_flops,
         )
         first, second, own_back = lax.optimization_barrier((first, second, own_back))
         halves = (first, core_swap(first), second, core_swap(second))
-        partners = [x[0] for x in fetched] + [x[1] for x in fetched]
         if iteration + 1 < ITERS:
-            partial_value, own = call(
-                functools.partial(between_kernel, rows, len(pieces)),
-                (flags, coeffs, own, below, above, zonal_loc, own_back, *halves, members, *partners),
-                [inc_shape, chunk_shape],
+            mine, other, own = call(
+                functools.partial(between_kernel, rows, 1),
+                (flags, coeffs, own, below, above, zonal_loc, own_back, *halves, members, *fetched),
+                [inc_shape, inc_shape, chunk_shape],
                 [weighted_scratch, back_scratch, chunk_scratch],
                 3 * zonal_flops,
             )
         else:
             (own,) = call(
-                functools.partial(last_kernel, rows, len(pieces), 2 * half_band + 1),
-                (flags, coeffs, own, zonal_loc, own_back, *halves, *partners),
+                functools.partial(last_kernel, rows, 1, 2 * half_band + 1),
+                (flags, coeffs, own, zonal_loc, own_back, *halves, *fetched),
                 [line_shape],
                 [weighted_scratch, back_scratch, chunk_scratch],
                 2 * zonal_flops,

time: 126 us -> 113 us (0.90)
  local copies, waits for them, and re-layouts: 12.1 us -> 3.67 us
  Pallas kernels: 35 us -> 43 us
  starting transfers between devices: 34.3 us -> 27.5 us
  waiting for transfers between devices: 39.9 us -> 36.7 us
  other arithmetic: 4.13 us -> 1.23 us
    ppermute x4 -> x2, waiting for transfers between devices: 17.6 us -> 7.28 us  [body(): inc = inc + lax.ppermute(inc, 'mem', perm)]
    ppermute x11 -> x6, starting transfers between devices: 23.8 us -> 15.1 us  [band_swap(): lax.ppermute(send_first, axes, band_pairs(0))]
    pallas_call x7 -> x8, Pallas kernels: 27.5 us -> 34.2 us  [call(): pl.pallas_call(kernel, in_specs=[pl.BlockSpec(memory_space=pltpu.SMEM)] +...]
    ppermute x2 -> x5, waiting for transfers between devices: 4.56 us -> 10.8 us  [the longest x2 6.39 us: opening(): inc = inc + lax.ppermute(inc, 'mem', perm)]
    unnamed x49 -> x29, local copies, waits for them, and re-layouts: 7.46 us -> 2.91 us
    slice x5 -> x3, local copies, waits for them, and re-layouts: 3.57 us -> 0.59 us  [band_fields(): slots[:, rows, TLON - 1]]
    ppermute x4 -> x2, starting transfers between devices: 0.7 us -> 3.14 us  [body(): inc = inc + lax.ppermute(inc, 'mem', perm)]
    concatenate x2 -> x0, other arithmetic: 2.06 us -> none  [body(): held = jnp.concatenate([held, lax.ppermute(held, 'mem', perm)], axis=0)]
  transfers between devices with their start and end apart: 37 -> 28, of which waited for: 15 -> 16; matrix products, arithmetic and copies ran while one was open for 6% -> 2% of each run, Pallas kernels for 10% -> 22%
where the time goes in v4:
time: 113 us; the launch traced here: 112 us
  Pallas kernels  43 us (38%)
  waiting for transfers between devices  36.7 us (32%)
  starting transfers between devices  27.5 us (24%)
  local copies, waits for them, and re-layouts  3.67 us (3%)
  other arithmetic  1.23 us (1%)
    pallas_call x8, Pallas kernels, call(): pl.pallas_call(kernel, in_specs=[pl.BlockSpec(memory_space=pltpu.SMEM)] +...  34.2 us
    ppermute x6, waiting for transfers between devices, band_swap(): lax.ppermute(send_first, axes, band_pairs(0))  15.3 us
    ppermute x6, starting transfers between devices, band_swap(): lax.ppermute(send_first, axes, band_pairs(0))  15.1 us
    ppermute x2, waiting for transfers between devices, body(): inc = inc + lax.ppermute(inc, 'mem', perm)  7.28 us
    ppermute x2, waiting for transfers between devices, opening(): inc = inc + lax.ppermute(inc, 'mem', perm)  6.39 us
    ppermute x2, waiting for transfers between devices, opening(): got = [lax.ppermute(x, 'mem', steps[-1]) for x in held]  4.44 us
    pallas_call x1, Pallas kernels, tile_sums(): pl.pallas_call(tile_kernel, grid_spec=pltpu.PrefetchScalarGridSpec(num_sc...  3.31 us
    ppermute x9, waiting for transfers between devices, core_swap(): return lax.ppermute(cells, 'mem', [(i, i ^ 1) for i in range(count)])  3.25 us
  transfers between devices with their start and end apart: 28, of which 16 were waited for; matrix products, arithmetic and copies ran while one was open for 2% of the time, Pallas kernels for 22%

profile of v4, /device:TPU:0, one launch (start us, length us, event | category | flops | bytes accessed | tf_op | source)
XLA Modules:
  0.0 112.5 jit_solution(8954622084449182293)
XLA Ops:
  0.0 1.4 %copy-done = f32[10,4,8,1152]{3,2,1,0:T(8,128)S(1)} copy-done((f32[10,4,8,1152]{3,2,1,0:T(8,128)S(1)}, f32[10,4,8,1152]{3,2,1,0:T(8,128)}, u32[]{:S(2)}) %copy-start) | copy-done | bytes 1474584
  1.4 0.2 shard_map.109
  1.6 3.1 %collective-permute-start.8 = (f32[160,1152]{1,0:T(8,128)S(1)}, f32[160,1152]{1,0:T(8,128)}, u32[]{:S(2)}, u32[]{:S(2)}) collective-permute-start(f32[160,1152]{1,0:T(8,128)S(1)} %get-tuple-element.84), channel_id=1, source_target_pairs={{0,1},{1,0},{2,3},{3,2},{4,5},{5,4},{6,7},{7,6},{8,9},{9,8},{10,11... | collective-permute-start | bytes 2211848 | tf_op jit(solution)/shard_map/ppermute | solution.py:38
  4.8 3.3 %shard_map.110 = f32[3,2,128,128]{3,2,1,0:T(8,128)S(1)} custom-call(s32[3]{0:T(128)S(1)} %bitcast.30, s32[3]{0:T(128)S(1)} %bitcast.31, s32[128,1]{1,0:T(8,128)S(1)} %copy-done.8, s32[128,1]{1,0:T(8,128)S(1)} %copy-done.7, s32[3,1,4096]{2,1,0:T(1,128)S(1)} %bitcast.27, f32[3,1,4096]{2,1,0:T(1,128)S(1)} %bitcast.28, f32[3,1,4096]{2,1,0:T(1,128)S(1)} %bitcast.29), custom_call_target="tpu_custom_call" | custom-call | flops 1258291200 | bytes 393216 | tf_op jit(solution)/shard_map/pallas_call | solution.py:153
  8.2 0.1 collective-permute-start.10
  8.2 0.8 copy.16.coef_ref
  9.0 3.1 %shard_map.111 = (f32[216,8,128]{2,1,0:T(8,128)}, f32[9,320,128]{2,1,0:T(8,128)}) custom-call(f32[32,9]{1,0:T(8,128)S(1)} %copy.16.coef_ref, f32[320,1152]{1,0:T(8,128)S(1)} %bitcast.26), custom_call_target="tpu_custom_call" | custom-call | bytes 3833856 | tf_op jit(solution)/shard_map/pallas_call | solution.py:551
  12.1 0.7 copy-done.13
  12.8 1.0 pad_maximum_fusion
  13.7 7.6 %collective-permute-done.8 = f32[160,1152]{1,0:T(8,128)} collective-permute-done((f32[160,1152]{1,0:T(8,128)S(1)}, f32[160,1152]{1,0:T(8,128)}, u32[]{:S(2)}, u32[]{:S(2)}) %collective-permute-start.8) | collective-permute-done | bytes 737312 | tf_op jit(solution)/shard_map/ppermute | solution.py:38
  21.3 4.6 %collective-permute-start.11 = (bf16[10,2,4,8,1152]{4,3,2,1,0:T(8,128)(2,1)}, bf16[10,2,4,8,1152]{4,3,2,1,0:T(8,128)(2,1)S(1)}, u32[]{:S(2)}, u32[]{:S(2)}) collective-permute-start(bf16[10,2,4,8,1152]{4,3,2,1,0:T(8,128)(2,1)} %members_ref.3), channel_id=1, source_target_pairs={{0,1},{1,0},{2,3},{3,2},{4,5},{5,4},{6,7},{7,6},{8,9},{9,8},{10,11... | collective-permute-start | bytes 4423688 | tf_op jit(solution)/shard_map/ppermute | solution.py:38
  25.9 0.1 stack.47.flag_ref.refs_0_
  26.0 34.4 %conditional.1 = (f32[4,8,1152]{2,1,0:T(8,128)S(1)}, f32[2,2,4,8,1152]{4,3,2,1,0:T(8,128)}, f32[2,4,8,1152]{3,2,1,0:T(8,128)}, f32[4,4,1152]{2,1,0:T(4,128)}, f3...) conditional(s32[]{:T(128)} %convert_element_type.4, () %tuple.19, (s32[6]{0:T(128)S(1)}, ...), branch_computations={%region_0.1_spmd, %region_1.2_spmd} | conditional | flops 852996224 | bytes 22561600 | solution.py:681
  26.0 1.5 %collective-permute-start.3 = (f32[6,128,128]{2,1,0:T(8,128)S(1)}, f32[6,128,128]{2,1,0:T(8,128)S(1)}, u32[]{:S(2)}, u32[]{:S(2)}) collective-permute-start(f32[6,128,128]{2,1,0:T(8,128)S(1)} %get-tuple-element.30.refs_0_), channel_id=1, source_target_pairs={{0,8},{4,20},{8,0},{12,28},{16,24},{20,4},{24,16},{28,12},{1,9},{5... | collective-permute-start | bytes 1179656 | tf_op jit(solution)/shard_map/cond/branch_1_fun/ppermute | solution.py:658
  27.5 5.8 %branch_1_fun.4 = (f32[4,8,1152]{2,1,0:T(8,128)S(1)}, f32[4,8,1152]{2,1,0:T(8,128)S(1)}, f32[9,160,128]{2,1,0:T(8,128)}, f32[9,160,128]{2,1,0:T(8,128)}) custom-call(s32[6]{0:T(128)S(1)} %get-tuple-element.21.flag_ref, f32[216,8,128]{2,1,0:T(8,128)} %get-tuple-element.22.coef_ref, f32[9,320,128]{2,1,0:T(8,128)} %get-tuple-element.23.own_ref, ...), custom_call_target="tpu_custom_call" | custom-call | flops 849346560 | bytes 9732120 | tf_op jit(solution)/shard_map/cond/branch_1_fun/pallas_call | solution.py:507
  33.3 0.1 collective-permute-start
  33.4 1.6 %collective-permute-start.2 = (f32[6,128,128]{2,1,0:T(8,128)S(1)}, f32[6,128,128]{2,1,0:T(8,128)S(1)}, u32[]{:S(2)}, u32[]{:S(2)}) collective-permute-start(f32[6,128,128]{2,1,0:T(8,128)S(1)} %get-tuple-element.30.refs_0_), channel_id=1, source_target_pairs={{0,16},{4,12},{8,24},{12,4},{16,0},{20,28},{24,8},{28,20},{1,17},{... | collective-permute-start | bytes 1179656 | tf_op jit(solution)/shard_map/cond/branch_1_fun/ppermute | solution.py:659
  34.9 0.5 collective-permute-start.4
  35.5 1.4 %collective-permute-start.1 = (f32[4,8,1152]{2,1,0:T(8,128)S(1)}, f32[4,8,1152]{2,1,0:T(8,128)S(1)}, u32[]{:S(2)}, u32[]{:S(2)}) collective-permute-start(f32[4,8,1152]{2,1,0:T(8,128)S(1)} %add.24), channel_id=1, source_target_pairs={{0,8},{4,20},{8,0},{12,28},{16,24},{20,4},{24,16},{28,12},{1,9},{5... | collective-permute-start | bytes 442376 | tf_op jit(solution)/shard_map/cond/branch_1_fun/ppermute | solution.py:670
  36.9 0.2 slice_reduce_fusion.3
  37.1 5.2 %collective-permute-done.1 = f32[4,8,1152]{2,1,0:T(8,128)S(1)} collective-permute-done((f32[4,8,1152]{2,1,0:T(8,128)S(1)}, f32[4,8,1152]{2,1,0:T(8,128)S(1)}, u32[]{:S(2)}, u32[]{:S(2)}) %collective-permute-start.1) | collective-permute-done | bytes 147488 | tf_op jit(solution)/shard_map/cond/branch_1_fun/ppermute | solution.py:670
  42.3 0.2 slice_reduce_fusion
  42.5 0.2 collective-permute-done.2.refs_2_
  42.8 4.2 %collective-permute-done.4.refs_3_ = f32[6,128,128]{2,1,0:T(8,128)S(1)} collective-permute-done((f32[6,128,128]{2,1,0:T(8,128)S(1)}, f32[6,128,128]{2,1,0:T(8,128)S(1)}, u32[]{:S(2)}, u32[]{:S(2)}) %collective-permute-start.4) | collective-permute-done | bytes 393248 | tf_op jit(solution)/shard_map/cond/branch_1_fun/ppermute | solution.py:659
  47.0 1.5 %collective-permute-start.5 = (f32[4,8,1152]{2,1,0:T(8,128)S(1)}, f32[4,8,1152]{2,1,0:T(8,128)S(1)}, u32[]{:S(2)}, u32[]{:S(2)}) collective-permute-start(f32[4,8,1152]{2,1,0:T(8,128)S(1)} %add.25), channel_id=1, source_target_pairs={{0,16},{4,12},{8,24},{12,4},{16,0},{20,28},{24,8},{28,20},{1,17},{... | collective-permute-start | bytes 442376 | tf_op jit(solution)/shard_map/cond/branch_1_fun/ppermute | solution.py:670
  48.5 0.2 slice_reduce_fusion.1
  48.7 0.1 maximum_convert_fusion.mark_ref
  48.8 2.2 %branch_1_fun.5 = (f32[2,64,1152]{2,1,0:T(8,128)}, f32[64,1152]{1,0:T(8,128)}) custom-call(s32[24]{0:T(128)S(1)} %maximum_convert_fusion.mark_ref, f32[6,128,128]{2,1,0:T(8,128)S(1)} %get-tuple-element.30.refs_0_, f32[6,128,128]{2,1,0:T(8,128)S(1)} %collective-permute-done.3.refs_1_, f32[6,128,128]{2,1,0:T(8,128)S(1)} %collective-permute-done.2.refs_2_, ...), custom_call_target="tpu_custom_call" | custom-call | flops 589824 | bytes 1769472 | tf_op jit(solution)/shard_map/cond/branch_1_fun/pallas_call | solution.py:225
  51.0 1.2 %collective-permute-done.5 = f32[4,8,1152]{2,1,0:T(8,128)S(1)} collective-permute-done((f32[4,8,1152]{2,1,0:T(8,128)S(1)}, f32[4,8,1152]{2,1,0:T(8,128)S(1)}, u32[]{:S(2)}, u32[]{:S(2)}) %collective-permute-start.5) | collective-permute-done | bytes 147488 | tf_op jit(solution)/shard_map/cond/branch_1_fun/ppermute | solution.py:670
  52.2 1.2 %branch_1_fun.6 = (f32[4,4,1152]{2,1,0:T(4,128)S(1)}, f32[4,4,1152]{2,1,0:T(4,128)S(1)}) custom-call(s32[6]{0:T(128)S(1)} %get-tuple-element.21.flag_ref, f32[4,8,1152]{2,1,0:T(8,128)S(1)} %add.26.inc_ref, f32[2,2,4,8,1152]{4,3,2,1,0:T(8,128)} %bitcast.weight_ref, f32[2,4,8,1152]{3,2,1,0:T(8,128)} %bitcast.1.pull_ref), custom_call_target="tpu_custom_call" | custom-call | bytes 1179672 | tf_op jit(solution)/shard_map/cond/branch_1_fun/pallas_call | solution.py:507
  53.4 0.1 collective-permute-start.6
  53.5 0.1 collective-permute-start.7
  53.6 5.1 %collective-permute-done.6.first_ref.rim_first_ref = f32[4,4,1152]{2,1,0:T(4,128)} collective-permute-done((f32[4,4,1152]{2,1,0:T(4,128)S(1)}, f32[4,4,1152]{2,1,0:T(4,128)}, u32[]{:S(2)}, u32[]{:S(2)}) %collective-permute-start.6) | collective-permute-done | bytes 73760 | tf_op jit(solution)/shard_map/cond/branch_1_fun/ppermute | solution.py:38
  58.7 1.7 %branch_1_fun.7 = f32[4,8,1152]{2,1,0:T(8,128)S(1)} custom-call(s32[6]{0:T(128)S(1)} %get-tuple-element.21.flag_ref, f32[4,8,1152]{2,1,0:T(8,128)S(1)} %add.26.inc_ref, f32[4,4,1152]{2,1,0:T(4,128)} %collective-permute-done.6.first_ref.rim_first_ref, f32[4,4,1152]{2,1,0:T(4,128)} %collective-permute-done.7.second_ref.rim_second_ref, ...), custom_call_target="tpu_custom_call" | custom-call | flops 2949120 | bytes 1474584 | tf_op jit(solution)/shard_map/cond/branch_1_fun/pallas_call | solution.py:507
  60.5 0.1 collective-permute-start.15
  60.5 0.5 collective-permute-start.14
  61.0 2.0 %collective-permute-start.13 = (f32[4,8,1152]{2,1,0:T(8,128)S(1)}, f32[4,8,1152]{2,1,0:T(8,128)S(1)}, u32[]{:S(2)}, u32[]{:S(2)}) collective-permute-start(f32[4,8,1152]{2,1,0:T(8,128)S(1)} %get-tuple-element.108.mine_ref), channel_id=1, source_target_pairs={{0,1},{1,0},{2,3},{3,2},{4,5},{5,4},{6,7},{7,6},{8,9},{9,8},{10,11... | collective-permute-start | bytes 442376 | tf_op jit(solution)/shard_map/ppermute | solution.py:38
  63.0 4.1 %shard_map.112.refs_6_ = f32[9,320,128]{2,1,0:T(8,128)S(1)} custom-call(s32[6]{0:T(128)S(1)} %stack.47.flag_ref.refs_0_, bf16[1152,1152]{1,0:T(8,128)(2,1)} %refs_3_.1, f32[4,8,1152]{2,1,0:T(8,128)S(1)} %get-tuple-element.108.mine_ref, f32[4,8,1152]{2,1,0:T(8,128)S(1)} %collective-permute-done.15.other_ref, bf16[10,2,4,8,1152]{4,3,2,1,0:T(8,128)(2,1)} %members_ref.3), custom_call_target="tpu_custom_call" | custom-call | flops 849346560 | bytes 5898264 | tf_op jit(solution)/shard_map/pallas_call | solution.py:507
  67.1 0.1 collective-permute-done.13.refs_7_
  67.2 0.0 collective-permute-start.16
  67.2 0.5 collective-permute-start.17
  67.7 0.9 collective-permute-done.16.refs_8_
  68.6 0.2 collective-permute-done.17.refs_10_
  68.8 9.8 %shard_map.113 = (f32[4,8,1152]{2,1,0:T(8,128)S(1)}, f32[4,8,1152]{2,1,0:T(8,128)S(1)}, f32[9,320,128]{2,1,0:T(8,128)S(1)}) custom-call(s32[6]{0:T(128)S(1)} %stack.47.flag_ref.refs_0_, f32[216,8,128]{2,1,0:T(8,128)S(1)} %copy-done.10, f32[9,320,128]{2,1,0:T(8,128)S(1)} %copy-done.11, f32[9,160,128]{2,1,0:T(8,128)} %get-tuple-element.106.refs_3_, ...), custom_call_target="tpu_custom_call" | custom-call | flops 2548039680 | bytes 14745624 | tf_op jit(solution)/shard_map/pallas_call | solution.py:507
  78.7 0.3 collective-permute-start.18
  79.0 1.1 collective-permute-done.18
  80.1 0.1 copy_add_fusion
  80.1 1.6 %collective-permute-start.19 = (f32[4,8,1152]{2,0,1:T(4,128)S(1)}, f32[4,8,1152]{2,0,1:T(4,128)S(1)}, u32[]{:S(2)}, u32[]{:S(2)}) collective-permute-start(f32[4,8,1152]{2,0,1:T(4,128)S(1)} %copy_add_fusion), channel_id=1, source_target_pairs={{0,8},{4,20},{8,0},{12,28},{16,24},{20,4},{24,16},{28,12},{1,9},{5... | collective-permute-start | bytes 442376 | tf_op jit(solution)/shard_map/ppermute | solution.py:694
  81.7 3.7 %collective-permute-done.19 = f32[4,8,1152]{2,0,1:T(4,128)S(1)} collective-permute-done((f32[4,8,1152]{2,0,1:T(4,128)S(1)}, f32[4,8,1152]{2,0,1:T(4,128)S(1)}, u32[]{:S(2)}, u32[]{:S(2)}) %collective-permute-start.19) | collective-permute-done | bytes 147488 | tf_op jit(solution)/shard_map/ppermute | solution.py:694
  85.4 1.6 %collective-permute-start.20 = (f32[4,8,1152]{2,0,1:T(4,128)S(1)}, f32[4,8,1152]{2,0,1:T(4,128)S(1)}, u32[]{:S(2)}, u32[]{:S(2)}) collective-permute-start(f32[4,8,1152]{2,0,1:T(4,128)S(1)} %add.39), channel_id=1, source_target_pairs={{0,16},{4,12},{8,24},{12,4},{16,0},{20,28},{24,8},{28,20},{1,17},{... | collective-permute-start | bytes 442376 | tf_op jit(solution)/shard_map/ppermute | solution.py:694
  87.0 3.6 %collective-permute-done.20 = f32[4,8,1152]{2,0,1:T(4,128)S(1)} collective-permute-done((f32[4,8,1152]{2,0,1:T(4,128)S(1)}, f32[4,8,1152]{2,0,1:T(4,128)S(1)}, u32[]{:S(2)}, u32[]{:S(2)}) %collective-permute-start.20) | collective-permute-done | bytes 147488 | tf_op jit(solution)/shard_map/ppermute | solution.py:694
  90.7 0.1 collective-permute-start.22
  90.8 3.1 %collective-permute-start.21 = (f32[1,4,1152]{2,1,0:T(4,128)S(1)}, f32[1,4,1152]{2,1,0:T(4,128)S(1)}, u32[]{:S(2)}, u32[]{:S(2)}) collective-permute-start(f32[1,4,1152]{2,1,0:T(4,128)S(1)} %get-tuple-element.129), channel_id=1, source_target_pairs={{0,1},{1,0},{2,3},{3,2},{4,5},{5,4},{6,7},{7,6},{8,9},{9,8},{10,11... | collective-permute-start | bytes 55304 | tf_op jit(solution)/shard_map/ppermute | solution.py:38
  93.8 1.7 %collective-permute-done.21.first_ref = f32[1,4,1152]{2,1,0:T(4,128)S(1)} collective-permute-done((f32[1,4,1152]{2,1,0:T(4,128)S(1)}, f32[1,4,1152]{2,1,0:T(4,128)S(1)}, u32[]{:S(2)}, u32[]{:S(2)}) %collective-permute-start.21) | collective-permute-done | bytes 18464 | tf_op jit(solution)/shard_map/ppermute | solution.py:38
  95.6 1.6 %shard_map.114.mine_ref = f32[4,8,1152]{2,1,0:T(8,128)S(1)} custom-call(s32[6]{0:T(128)S(1)} %stack.47.flag_ref.refs_0_, f32[4,8,1152]{2,1,0:T(8,128)S(1)} %copy.19.inc_ref, f32[1,4,1152]{2,1,0:T(4,128)S(1)} %collective-permute-done.21.first_ref, f32[1,4,1152]{2,1,0:T(4,128)S(1)} %collective-permute-done.22.second_ref, ...), custom_call_target="tpu_custom_call" | custom-call | flops 2949120 | bytes 1363992 | tf_op jit(solution)/shard_map/pallas_call | solution.py:507
  97.2 0.1 collective-permute-start.25
  97.3 0.5 collective-permute-start.24
  97.8 2.3 %collective-permute-start.23 = (f32[4,8,1152]{2,1,0:T(8,128)S(1)}, f32[4,8,1152]{2,1,0:T(8,128)S(1)}, u32[]{:S(2)}, u32[]{:S(2)}) collective-permute-start(f32[4,8,1152]{2,1,0:T(8,128)S(1)} %shard_map.114.mine_ref), channel_id=1, source_target_pairs={{0,1},{1,0},{2,3},{3,2},{4,5},{5,4},{6,7},{7,6},{8,9},{9,8},{10,11... | collective-permute-start | bytes 442376 | tf_op jit(solution)/shard_map/ppermute | solution.py:38
  100.1 3.3 %shard_map.115.refs_4_ = f32[9,320,128]{2,1,0:T(8,128)S(1)} custom-call(s32[6]{0:T(128)S(1)} %stack.47.flag_ref.refs_0_, bf16[1152,1152]{1,0:T(8,128)(2,1)S(1)} %copy-done.9, f32[4,8,1152]{2,1,0:T(8,128)S(1)} %shard_map.114.mine_ref, f32[4,8,1152]{2,1,0:T(8,128)S(1)} %collective-permute-done.25.other_ref, bf16[10,2,4,8,1152]{4,3,2,1,0:T(8,128)(2,1)} %members_ref.3), custom_call_target="tpu_custom_call" | custom-call | flops 849346560 | bytes 5898264 | tf_op jit(solution)/shard_map/pallas_call | solution.py:507
  103.4 0.8 collective-permute-done.23.refs_5_
  104.2 0.5 collective-permute-start.27
  104.7 0.9 collective-permute-done.26.refs_6_
  105.6 0.2 collective-permute-done.27.refs_8_
  105.8 6.6 %shard_map.116 = f32[320,1152]{1,0:T(8,128)} custom-call(s32[6]{0:T(128)S(1)} %stack.47.flag_ref.refs_0_, f32[216,8,128]{2,1,0:T(8,128)S(1)} %copy-done.10, f32[9,320,128]{2,1,0:T(8,128)S(1)} %get-tuple-element.114.refs_2_, bf16[1152,1152]{1,0:T(8,128)(2,1)S(1)} %copy-done.9, f32[9,320,128]{2,1,0:T(8,128)S(1)} %shard_map.115.refs_4_, ...), custom_call_target="tpu_custom_call" | custom-call | flops 1698693120 | bytes 11501592 | tf_op jit(solution)/shard_map/pallas_call | solution.py:507
  (50 shorter events, 0.3 us)
Async XLA Ops:
  0.0 4.7 %copy-start.6 = (s32[1,1,3]{2,1,0:T(1,128)S(1)}, s32[1,1,3]{2,1,0:T(1,128)}, u32[]{:S(2)}) copy-start(s32[1,1,3]{2,1,0:T(1,128)} %param.18) | copy-start | bytes 40
  0.0 4.7 %copy-start.5 = (s32[1,1,3]{2,1,0:T(1,128)S(1)}, s32[1,1,3]{2,1,0:T(1,128)}, u32[]{:S(2)}) copy-start(s32[1,1,3]{2,1,0:T(1,128)} %param.17) | copy-start | bytes 40
  0.0 1.4 %copy-start = (f32[10,4,8,1152]{3,2,1,0:T(8,128)S(1)}, f32[10,4,8,1152]{3,2,1,0:T(8,128)}, u32[]{:S(2)}) copy-start(f32[10,4,8,1152]{3,2,1,0:T(8,128)} %param.14) | copy-start | bytes 4423684
  1.4 3.3 %copy-start.2 = (s32[1,1,3,4096]{3,1,2,0:T(1,128)S(1)}, s32[1,1,3,4096]{3,1,2,0:T(1,128)}, u32[]{:S(2)}) copy-start(s32[1,1,3,4096]{3,1,2,0:T(1,128)} %param.19) | copy-start | bytes 147460
  1.4 3.3 %copy-start.3 = (f32[1,1,3,4096]{3,1,2,0:T(1,128)S(1)}, f32[1,1,3,4096]{3,1,2,0:T(1,128)}, u32[]{:S(2)}) copy-start(f32[1,1,3,4096]{3,1,2,0:T(1,128)} %param.20) | copy-start | bytes 147460
  1.4 3.3 %copy-start.4 = (f32[1,1,3,4096]{3,1,2,0:T(1,128)S(1)}, f32[1,1,3,4096]{3,1,2,0:T(1,128)}, u32[]{:S(2)}) copy-start(f32[1,1,3,4096]{3,1,2,0:T(1,128)} %param.21) | copy-start | bytes 147460
  1.4 3.4 %copy-start.7 = (s32[128,1]{1,0:T(8,128)S(1)}, s32[128,1]{1,0:T(8,128)}, u32[]{:S(2)}) copy-start(s32[128,1]{1,0:T(8,128)} %constant.48.clone.lane_ref) | copy-start | bytes 1540
  1.4 3.4 %copy-start.8 = (s32[128,1]{1,0:T(8,128)S(1)}, s32[128,1]{1,0:T(8,128)}, u32[]{:S(2)}) copy-start(s32[128,1]{1,0:T(8,128)} %constant.47.clone.row_ref) | copy-start | bytes 1540
  1.6 19.7 %collective-permute-start.8 = (f32[160,1152]{1,0:T(8,128)S(1)}, f32[160,1152]{1,0:T(8,128)}, u32[]{:S(2)}, u32[]{:S(2)}) collective-permute-start(f32[160,1152]{1,0:T(8,128)S(1)} %get-tuple-element.84), channel_id=1, source_target_pairs={{0,1},{1,0},{2,3},{3,2},{4,5},{5,4},{6,7},{7,6},{8,9},{9,8},{10,11... | collective-permute-start | bytes 2211848 | tf_op jit(solution)/shard_map/ppermute | solution.py:38
  4.7 16.6 %collective-permute-start.9 = (f32[160,1152]{1,0:T(8,128)S(1)}, f32[160,1152]{1,0:T(8,128)}, u32[]{:S(2)}, u32[]{:S(2)}) collective-permute-start(f32[160,1152]{1,0:T(8,128)S(1)} %get-tuple-element.85), channel_id=1, source_target_pairs={{0,4},{1,2},{2,1},{3,7},{4,0},{5,6},{6,5},{7,3},{8,12},{9,10},{10,... | collective-permute-start | bytes 2211848 | tf_op jit(solution)/shard_map/ppermute | solution.py:39
  4.8 4.2 %copy-start.1 = (f32[10,4,8,1152]{3,2,1,0:T(8,128)S(1)}, f32[10,4,8,1152]{3,2,1,0:T(8,128)}, u32[]{:S(2)}) copy-start(f32[10,4,8,1152]{3,2,1,0:T(8,128)} %param.14) | copy-start | bytes 4423684
  8.2 3.9 %collective-permute-start.10 = (f32[1,3,128,128]{3,2,1,0:T(8,128)S(1)}, f32[1,3,128,128]{3,2,1,0:T(8,128)S(1)}, u32[]{:S(2)}, u32[]{:S(2)}) collective-permute-start(f32[1,3,128,128]{3,2,1,0:T(8,128)S(1)} %get-tuple-element.127), channel_id=1, source_target_pairs={{0,4},{4,0},{8,12},{12,8},{16,20},{20,16},{24,28},{28,24},{1,5},{5... | collective-permute-start | bytes 589832 | tf_op jit(solution)/shard_map/ppermute | solution.py:55
  12.1 0.7 copy-start.13
  21.3 39.1 %collective-permute-start.12 = (bf16[10,2,4,8,1152]{4,3,2,1,0:T(8,128)(2,1)}, bf16[10,2,4,8,1152]{4,3,2,1,0:T(8,128)(2,1)S(1)}, u32[]{:S(2)}, u32[]{:S(2)}) collective-permute-start(bf16[10,2,4,8,1152]{4,3,2,1,0:T(8,128)(2,1)} %members_ref.3), channel_id=1, source_target_pairs={{0,4},{1,2},{2,1},{3,7},{4,0},{5,6},{6,5},{7,3},{8,12},{9,10},{10,... | collective-permute-start | bytes 4423688 | tf_op jit(solution)/shard_map/ppermute | solution.py:39
  21.3 39.1 %collective-permute-start.11 = (bf16[10,2,4,8,1152]{4,3,2,1,0:T(8,128)(2,1)}, bf16[10,2,4,8,1152]{4,3,2,1,0:T(8,128)(2,1)S(1)}, u32[]{:S(2)}, u32[]{:S(2)}) collective-permute-start(bf16[10,2,4,8,1152]{4,3,2,1,0:T(8,128)(2,1)} %members_ref.3), channel_id=1, source_target_pairs={{0,1},{1,0},{2,3},{3,2},{4,5},{5,4},{6,7},{7,6},{8,9},{9,8},{10,11... | collective-permute-start | bytes 4423688 | tf_op jit(solution)/shard_map/ppermute | solution.py:38
  26.0 8.9 %collective-permute-start.3 = (f32[6,128,128]{2,1,0:T(8,128)S(1)}, f32[6,128,128]{2,1,0:T(8,128)S(1)}, u32[]{:S(2)}, u32[]{:S(2)}) collective-permute-start(f32[6,128,128]{2,1,0:T(8,128)S(1)} %get-tuple-element.30.refs_0_), channel_id=1, source_target_pairs={{0,8},{4,20},{8,0},{12,28},{16,24},{20,4},{24,16},{28,12},{1,9},{5... | collective-permute-start | bytes 1179656 | tf_op jit(solution)/shard_map/cond/branch_1_fun/ppermute | solution.py:658
  33.3 2.2 %collective-permute-start = (f32[4,8,1152]{2,1,0:T(8,128)S(1)}, f32[4,8,1152]{2,1,0:T(8,128)S(1)}, u32[]{:S(2)}, u32[]{:S(2)}) collective-permute-start(f32[4,8,1152]{2,1,0:T(8,128)S(1)} %get-tuple-element.29), channel_id=1, source_target_pairs={{0,4},{4,0},{8,12},{12,8},{16,20},{20,16},{24,28},{28,24},{1,5},{5... | collective-permute-start | bytes 442376 | tf_op jit(solution)/shard_map/cond/branch_1_fun/ppermute | solution.py:55
  33.4 9.4 %collective-permute-start.2 = (f32[6,128,128]{2,1,0:T(8,128)S(1)}, f32[6,128,128]{2,1,0:T(8,128)S(1)}, u32[]{:S(2)}, u32[]{:S(2)}) collective-permute-start(f32[6,128,128]{2,1,0:T(8,128)S(1)} %get-tuple-element.30.refs_0_), channel_id=1, source_target_pairs={{0,16},{4,12},{8,24},{12,4},{16,0},{20,28},{24,8},{28,20},{1,17},{... | collective-permute-start | bytes 1179656 | tf_op jit(solution)/shard_map/cond/branch_1_fun/ppermute | solution.py:659
  34.9 12.0 %collective-permute-start.4 = (f32[6,128,128]{2,1,0:T(8,128)S(1)}, f32[6,128,128]{2,1,0:T(8,128)S(1)}, u32[]{:S(2)}, u32[]{:S(2)}) collective-permute-start(f32[6,128,128]{2,1,0:T(8,128)S(1)} %collective-permute-done.3.refs_1_), channel_id=1, source_target_pairs={{0,16},{4,12},{8,24},{12,4},{16,0},{20,28},{24,8},{28,20},{1,17},{... | collective-permute-start | bytes 1179656 | tf_op jit(solution)/shard_map/cond/branch_1_fun/ppermute | solution.py:659
  35.5 6.8 %collective-permute-start.1 = (f32[4,8,1152]{2,1,0:T(8,128)S(1)}, f32[4,8,1152]{2,1,0:T(8,128)S(1)}, u32[]{:S(2)}, u32[]{:S(2)}) collective-permute-start(f32[4,8,1152]{2,1,0:T(8,128)S(1)} %add.24), channel_id=1, source_target_pairs={{0,8},{4,20},{8,0},{12,28},{16,24},{20,4},{24,16},{28,12},{1,9},{5... | collective-permute-start | bytes 442376 | tf_op jit(solution)/shard_map/cond/branch_1_fun/ppermute | solution.py:670
  47.0 5.1 %collective-permute-start.5 = (f32[4,8,1152]{2,1,0:T(8,128)S(1)}, f32[4,8,1152]{2,1,0:T(8,128)S(1)}, u32[]{:S(2)}, u32[]{:S(2)}) collective-permute-start(f32[4,8,1152]{2,1,0:T(8,128)S(1)} %add.25), channel_id=1, source_target_pairs={{0,16},{4,12},{8,24},{12,4},{16,0},{20,28},{24,8},{28,20},{1,17},{... | collective-permute-start | bytes 442376 | tf_op jit(solution)/shard_map/cond/branch_1_fun/ppermute | solution.py:670
  53.4 5.3 %collective-permute-start.6 = (f32[4,4,1152]{2,1,0:T(4,128)S(1)}, f32[4,4,1152]{2,1,0:T(4,128)}, u32[]{:S(2)}, u32[]{:S(2)}) collective-permute-start(f32[4,4,1152]{2,1,0:T(4,128)S(1)} %get-tuple-element.36), channel_id=1, source_target_pairs={{0,1},{1,0},{2,3},{3,2},{4,5},{5,4},{6,7},{7,6},{8,9},{9,8},{10,11... | collective-permute-start | bytes 221192 | tf_op jit(solution)/shard_map/cond/branch_1_fun/ppermute | solution.py:38
  53.5 5.2 %collective-permute-start.7 = (f32[4,4,1152]{2,1,0:T(4,128)S(1)}, f32[4,4,1152]{2,1,0:T(4,128)}, u32[]{:S(2)}, u32[]{:S(2)}) collective-permute-start(f32[4,4,1152]{2,1,0:T(4,128)S(1)} %get-tuple-element.37), channel_id=1, source_target_pairs={{0,4},{1,2},{2,1},{3,7},{4,0},{5,6},{6,5},{7,3},{8,12},{9,10},{10,... | collective-permute-start | bytes 221192 | tf_op jit(solution)/shard_map/cond/branch_1_fun/ppermute | solution.py:39
  60.4 8.3 %copy-start.10 = (f32[216,8,128]{2,1,0:T(8,128)S(1)}, f32[216,8,128]{2,1,0:T(8,128)}, u32[]{:S(2)}) copy-start(f32[216,8,128]{2,1,0:T(8,128)} %get-tuple-element.104.refs_1_) | copy-start | bytes 2654212
  60.4 8.3 %copy-start.11 = (f32[9,320,128]{2,1,0:T(8,128)S(1)}, f32[9,320,128]{2,1,0:T(8,128)}, u32[]{:S(2)}) copy-start(f32[9,320,128]{2,1,0:T(8,128)} %get-tuple-element.105.refs_2_) | copy-start | bytes 4423684
  60.5 8.3 %copy-start.12 = (f32[9,160,128]{2,1,0:T(8,128)S(1)}, f32[9,160,128]{2,1,0:T(8,128)}, u32[]{:S(2)}) copy-start(f32[9,160,128]{2,1,0:T(8,128)} %get-tuple-element.107.refs_4_) | copy-start | bytes 2211844
  60.5 2.5 %collective-permute-start.15 = (f32[4,8,1152]{2,1,0:T(8,128)S(1)}, f32[4,8,1152]{2,1,0:T(8,128)S(1)}, u32[]{:S(2)}, u32[]{:S(2)}) collective-permute-start(f32[4,8,1152]{2,1,0:T(8,128)S(1)} %get-tuple-element.108.mine_ref), channel_id=1, source_target_pairs={{0,4},{4,0},{8,12},{12,8},{16,20},{20,16},{24,28},{28,24},{1,5},{5... | collective-permute-start | bytes 442376 | tf_op jit(solution)/shard_map/ppermute | solution.py:55
  60.5 6.6 %collective-permute-start.14 = (f32[4,8,1152]{2,1,0:T(8,128)S(1)}, f32[4,8,1152]{2,1,0:T(8,128)S(1)}, u32[]{:S(2)}, u32[]{:S(2)}) collective-permute-start(f32[4,8,1152]{2,1,0:T(8,128)S(1)} %get-tuple-element.108.mine_ref), channel_id=1, source_target_pairs={{0,4},{1,2},{2,1},{3,7},{4,0},{5,6},{6,5},{7,3},{8,12},{9,10},{10,... | collective-permute-start | bytes 442376 | tf_op jit(solution)/shard_map/ppermute | solution.py:39
  61.0 6.1 %collective-permute-start.13 = (f32[4,8,1152]{2,1,0:T(8,128)S(1)}, f32[4,8,1152]{2,1,0:T(8,128)S(1)}, u32[]{:S(2)}, u32[]{:S(2)}) collective-permute-start(f32[4,8,1152]{2,1,0:T(8,128)S(1)} %get-tuple-element.108.mine_ref), channel_id=1, source_target_pairs={{0,1},{1,0},{2,3},{3,2},{4,5},{5,4},{6,7},{7,6},{8,9},{9,8},{10,11... | collective-permute-start | bytes 442376 | tf_op jit(solution)/shard_map/ppermute | solution.py:38
  63.0 5.8 %copy-start.9 = (bf16[1152,1152]{1,0:T(8,128)(2,1)S(1)}, bf16[1152,1152]{1,0:T(8,128)(2,1)}, u32[]{:S(2)}) copy-start(bf16[1152,1152]{1,0:T(8,128)(2,1)} %refs_3_.1) | copy-start | bytes 7962628
  67.2 1.4 %collective-permute-start.16 = (f32[4,8,1152]{2,1,0:T(8,128)S(1)}, f32[4,8,1152]{2,1,0:T(8,128)S(1)}, u32[]{:S(2)}, u32[]{:S(2)}) collective-permute-start(f32[4,8,1152]{2,1,0:T(8,128)S(1)} %collective-permute-done.13.refs_7_), channel_id=1, source_target_pairs={{0,4},{4,0},{8,12},{12,8},{16,20},{20,16},{24,28},{28,24},{1,5},{5... | collective-permute-start | bytes 442376 | tf_op jit(solution)/shard_map/ppermute | solution.py:55
  67.2 1.6 %collective-permute-start.17 = (f32[4,8,1152]{2,1,0:T(8,128)S(1)}, f32[4,8,1152]{2,1,0:T(8,128)S(1)}, u32[]{:S(2)}, u32[]{:S(2)}) collective-permute-start(f32[4,8,1152]{2,1,0:T(8,128)S(1)} %collective-permute-done.14.refs_9_), channel_id=1, source_target_pairs={{0,4},{4,0},{8,12},{12,8},{16,20},{20,16},{24,28},{28,24},{1,5},{5... | collective-permute-start | bytes 442376 | tf_op jit(solution)/shard_map/ppermute | solution.py:55
  78.7 1.4 %collective-permute-start.18 = (f32[4,8,1152]{2,0,1:T(4,128)S(1)}, f32[4,8,1152]{2,0,1:T(4,128)S(1)}, u32[]{:S(2)}, u32[]{:S(2)}) collective-permute-start(f32[4,8,1152]{2,0,1:T(4,128)S(1)} %copy.17), channel_id=1, source_target_pairs={{0,4},{4,0},{8,12},{12,8},{16,20},{20,16},{24,28},{28,24},{1,5},{5... | collective-permute-start | bytes 442376 | tf_op jit(solution)/shard_map/ppermute | solution.py:55
  80.1 5.2 %collective-permute-start.19 = (f32[4,8,1152]{2,0,1:T(4,128)S(1)}, f32[4,8,1152]{2,0,1:T(4,128)S(1)}, u32[]{:S(2)}, u32[]{:S(2)}) collective-permute-start(f32[4,8,1152]{2,0,1:T(4,128)S(1)} %copy_add_fusion), channel_id=1, source_target_pairs={{0,8},{4,20},{8,0},{12,28},{16,24},{20,4},{24,16},{28,12},{1,9},{5... | collective-permute-start | bytes 442376 | tf_op jit(solution)/shard_map/ppermute | solution.py:694
  85.4 5.2 %collective-permute-start.20 = (f32[4,8,1152]{2,0,1:T(4,128)S(1)}, f32[4,8,1152]{2,0,1:T(4,128)S(1)}, u32[]{:S(2)}, u32[]{:S(2)}) collective-permute-start(f32[4,8,1152]{2,0,1:T(4,128)S(1)} %add.39), channel_id=1, source_target_pairs={{0,16},{4,12},{8,24},{12,4},{16,0},{20,28},{24,8},{28,20},{1,17},{... | collective-permute-start | bytes 442376 | tf_op jit(solution)/shard_map/ppermute | solution.py:694
  90.7 3.2 %collective-permute-start.22 = (f32[1,4,1152]{2,1,0:T(4,128)S(1)}, f32[1,4,1152]{2,1,0:T(4,128)S(1)}, u32[]{:S(2)}, u32[]{:S(2)}) collective-permute-start(f32[1,4,1152]{2,1,0:T(4,128)S(1)} %get-tuple-element.128), channel_id=1, source_target_pairs={{0,4},{1,2},{2,1},{3,7},{4,0},{5,6},{6,5},{7,3},{8,12},{9,10},{10,... | collective-permute-start | bytes 55304 | tf_op jit(solution)/shard_map/ppermute | solution.py:39
  90.8 4.8 %collective-permute-start.21 = (f32[1,4,1152]{2,1,0:T(4,128)S(1)}, f32[1,4,1152]{2,1,0:T(4,128)S(1)}, u32[]{:S(2)}, u32[]{:S(2)}) collective-permute-start(f32[1,4,1152]{2,1,0:T(4,128)S(1)} %get-tuple-element.129), channel_id=1, source_target_pairs={{0,1},{1,0},{2,3},{3,2},{4,5},{5,4},{6,7},{7,6},{8,9},{9,8},{10,11... | collective-permute-start | bytes 55304 | tf_op jit(solution)/shard_map/ppermute | solution.py:38
  97.2 2.9 %collective-permute-start.25 = (f32[4,8,1152]{2,1,0:T(8,128)S(1)}, f32[4,8,1152]{2,1,0:T(8,128)S(1)}, u32[]{:S(2)}, u32[]{:S(2)}) collective-permute-start(f32[4,8,1152]{2,1,0:T(8,128)S(1)} %shard_map.114.mine_ref), channel_id=1, source_target_pairs={{0,4},{4,0},{8,12},{12,8},{16,20},{20,16},{24,28},{28,24},{1,5},{5... | collective-permute-start | bytes 442376 | tf_op jit(solution)/shard_map/ppermute | solution.py:55
  97.3 6.1 %collective-permute-start.24 = (f32[4,8,1152]{2,1,0:T(8,128)S(1)}, f32[4,8,1152]{2,1,0:T(8,128)S(1)}, u32[]{:S(2)}, u32[]{:S(2)}) collective-permute-start(f32[4,8,1152]{2,1,0:T(8,128)S(1)} %shard_map.114.mine_ref), channel_id=1, source_target_pairs={{0,4},{1,2},{2,1},{3,7},{4,0},{5,6},{6,5},{7,3},{8,12},{9,10},{10,... | collective-permute-start | bytes 442376 | tf_op jit(solution)/shard_map/ppermute | solution.py:39
  97.8 6.5 %collective-permute-start.23 = (f32[4,8,1152]{2,1,0:T(8,128)S(1)}, f32[4,8,1152]{2,1,0:T(8,128)S(1)}, u32[]{:S(2)}, u32[]{:S(2)}) collective-permute-start(f32[4,8,1152]{2,1,0:T(8,128)S(1)} %shard_map.114.mine_ref), channel_id=1, source_target_pairs={{0,1},{1,0},{2,3},{3,2},{4,5},{5,4},{6,7},{7,6},{8,9},{9,8},{10,11... | collective-permute-start | bytes 442376 | tf_op jit(solution)/shard_map/ppermute | solution.py:38
  104.2 1.4 %collective-permute-start.26 = (f32[4,8,1152]{2,1,0:T(8,128)S(1)}, f32[4,8,1152]{2,1,0:T(8,128)S(1)}, u32[]{:S(2)}, u32[]{:S(2)}) collective-permute-start(f32[4,8,1152]{2,1,0:T(8,128)S(1)} %collective-permute-done.23.refs_5_), channel_id=1, source_target_pairs={{0,4},{4,0},{8,12},{12,8},{16,20},{20,16},{24,28},{28,24},{1,5},{5... | collective-permute-start | bytes 442376 | tf_op jit(solution)/shard_map/ppermute | solution.py:55
  104.2 1.6 %collective-permute-start.27 = (f32[4,8,1152]{2,1,0:T(8,128)S(1)}, f32[4,8,1152]{2,1,0:T(8,128)S(1)}, u32[]{:S(2)}, u32[]{:S(2)}) collective-permute-start(f32[4,8,1152]{2,1,0:T(8,128)S(1)} %collective-permute-done.24.refs_7_), channel_id=1, source_target_pairs={{0,4},{4,0},{8,12},{12,8},{16,20},{20,16},{24,28},{28,24},{1,5},{5... | collective-permute-start | bytes 442376 | tf_op jit(solution)/shard_map/ppermute | solution.py:55

commit v5 on v4

--- a/solution.py
+++ b/solution.py
@@ -251,7 +251,7 @@
 
 
 def observe_kernel(
-    flag_ref, inc_ref, first_ref, second_ref, weight_ref, pull_ref, rim_first_ref, rim_second_ref, out_ref
+    flag_ref, inc_ref, first_ref, second_ref, weight_ref, pull_ref, rim_first_ref, rim_second_ref, out_ref, *send_refs
 ):
     even = flag_ref[EVEN] == 1
     has_below, has_above = flag_ref[HAS_BELOW] == 1, flag_ref[HAS_ABOVE] == 1
@@ -277,6 +277,15 @@
         high_down = jnp.where(row == 0, from_below, pltpu.roll(high, 1, 0))
         low_up = jnp.where(row == rows - 1, from_above, pltpu.roll(low, rows - 1, 0))
         out_ref[lev] = 0.75 * (low + high) + 0.25 * (high_down + low_up)
+    for pair in range(levels // 2 if send_refs else 0):
+        head, tail = half_rows(out_ref[2 * pair], out_ref[2 * pair + 1])
+        send_refs[0][pair] = jnp.where(even, tail, head)
+        send_refs[1][pair] = jnp.where(even, head, tail)
+
+
+def half_rows(one, two):
+    half = one.shape[0] // 2
+    return jnp.concatenate([one[:half], two[:half]], axis=0), jnp.concatenate([one[half:], two[half:]], axis=0)
 
 
 def row_groups(lines):
@@ -443,6 +452,46 @@
     zonal_back(weighted_ref, zonal_ref, back_ref, lines)
 
 
+def partner_half_back(flag_ref, zonal_ref, adjoints, partners, weighted_ref, back_ref, wide_ref):
+    lines = back_ref.shape[1] // 2
+    even, core = flag_ref[EVEN], flag_ref[CORE]
+    for number, (place, flag) in enumerate((((even * lines), HAS_FIRST), ((1 - even) * lines, HAS_SECOND))):
+        part_ref = partners[number]
+        size, _, levels, rows, _ = part_ref.shape
+        flat = levels * rows // 2
+        for which, ref in enumerate(adjoints[2 * number : 2 * number + 2]):
+            for pair in range(levels // 2):
+                packed = ref[pair]
+                upper, lower = packed[: rows // 2], packed[rows // 2 :]
+                wide_ref[which, 2 * pair] = jnp.concatenate([upper, upper], axis=0)
+                wide_ref[which, 2 * pair + 1] = jnp.concatenate([lower, lower], axis=0)
+        there = flag_ref[flag] == 1
+        is_above = even == 1 - number
+
+        def step(k, carry, part_ref=part_ref, place=place, there=there, is_above=is_above):
+            total = part_ref[k, core].astype(jnp.float32) * wide_ref[0]
+            total += part_ref[k, 1 - core].astype(jnp.float32) * wide_ref[1]
+            total = jnp.where(there, total, 0.0)
+            kept = []
+            for pair in range(levels // 2):
+                head, tail = half_rows(total[2 * pair], total[2 * pair + 1])
+                kept.append(jnp.where(is_above, head, tail))
+            at = pl.multiple_of(place + k * flat, 16)
+            weighted_ref[pl.ds(at, flat), :] = jnp.concatenate(kept, axis=0).astype(jnp.bfloat16)
+            return carry
+
+        lax.fori_loop(0, size, step, 0)
+    zonal_back(weighted_ref, zonal_ref, back_ref, 2 * lines)
+
+
+def half_back_rows(own_ref, partner_ref, chunk, start, rows):
+    half, lines = rows // 2, partner_ref.shape[1] // 2
+    below = [strided(partner_ref, chunk, start * half + r, half) for r in range(half)]
+    own = [strided(own_ref, chunk, start * rows + r, rows) for r in range(rows)]
+    above = [strided(partner_ref, chunk, lines + start * half + r, half) for r in range(half)]
+    return below + own + above
+
+
 def back_rows(own_ref, partner_ref, chunk, start, rows, halo):
     lines = own_ref.shape[1]
     out = []
@@ -483,13 +532,13 @@
     flag_ref, coef_ref, own_ref, zonal_ref, own_back_ref = refs[:5]
     adjoints = refs[5:9]
     partners = refs[9 : 9 + 2 * parts]
-    out_ref, weighted_ref, back_ref, current_ref = refs[9 + 2 * parts :]
+    out_ref, weighted_ref, back_ref, current_ref, wide_ref = refs[9 + 2 * parts :]
     half_band = taps // 2
-    partner_back(flag_ref, zonal_ref, adjoints, partners, weighted_ref, back_ref)
+    partner_half_back(flag_ref, zonal_ref, adjoints, partners, weighted_ref, back_ref, wide_ref)
 
     def step(chunk, carry):
         for start in row_groups(own_ref.shape[1] // rows):
-            back = back_rows(own_back_ref, back_ref, chunk, start, rows, half_band)
+            back = half_back_rows(own_back_ref, back_ref, chunk, start, rows)
             for r, pulled in enumerate(pull_rows(back, coef_ref, (rows + half_band) * taps, taps)):
                 here = pl.ds(start * rows + r, 8, stride=rows)
                 cell = own_ref[chunk, here, :]
@@ -643,14 +692,12 @@
             edges = rims = band_swap(*sends)
         else:
             edges = band_swap(*by_partner(inc[None, :, 0], inc[None, :, -1]))
-        (adjoint,) = call(
-            observe_kernel,
-            (flags, inc, *edges, weights, pulls, *rims),
-            [jax.ShapeDtypeStruct(inc.shape, jnp.float32)],
-            [],
-            40 * 2 * inc.size,
+        half_shape = jax.ShapeDtypeStruct((lev_count // 2, rows, lon_cells), jnp.float32)
+        out_shapes = [inc_shape] if rims is edges else [inc_shape, half_shape, half_shape]
+        adjoint, *sends = call(
+            observe_kernel, (flags, inc, *edges, weights, pulls, *rims), out_shapes, [], 40 * 2 * inc.size
         )
-        return adjoint, rims
+        return adjoint, sends or rims
 
     def opening(held, coeffs, own, halo_first, halo_second):
         held = [held]
@@ -692,8 +739,8 @@
             inc = mine + core_swap(other)
             for perm in steps:
                 inc = inc + lax.ppermute(inc, "mem", perm)
-            adjoint, _ = observe(inc, weights, pulls, rims)
-        first, second = band_swap(adjoint, adjoint)
+            adjoint, sends = observe(inc, weights, pulls, rims)
+        first, second = band_swap(*((adjoint, adjoint) if iteration == 0 else sends))
         adjoint_other = core_swap(adjoint)
         (own_back,) = call(
             own_kernel,
@@ -717,8 +764,13 @@
                 functools.partial(last_kernel, rows, 1, 2 * half_band + 1),
                 (flags, coeffs, own, zonal_loc, own_back, *halves, *fetched),
                 [line_shape],
-                [weighted_scratch, back_scratch, chunk_scratch],
-                2 * zonal_flops,
+                [
+                    pltpu.VMEM((lines, lon_cells), jnp.bfloat16),
+                    chunk_scratch,
+                    chunk_scratch,
+                    pltpu.VMEM((2,) + inc_shape.shape, jnp.float32),
+                ],
+                zonal_flops,
             )
     return own.reshape(alpha.shape)
 

time: 113 us -> 110 us (0.973)
  Pallas kernels: 43 us -> 40.4 us
    pallas_call x1, Pallas kernels: 3.31 us -> 1.8 us  [tile_sums(): pl.pallas_call(tile_kernel, grid_spec=pltpu.PrefetchScalarGridSpec(num_sc...]
  transfers between devices with their start and end apart: 28 -> 28, of which waited for: 16 -> 15; matrix products, arithmetic and copies ran while one was open for 2% -> 2% of each run, Pallas kernels for 22% -> 21%
where the time goes in v5:
time: 110 us
  Pallas kernels  40.4 us (37%)
  waiting for transfers between devices  36.4 us (33%)
  starting transfers between devices  28.1 us (26%)
  local copies, waits for them, and re-layouts  3.67 us (3%)
  other arithmetic  1.23 us (1%)
    pallas_call x8, Pallas kernels, call(): pl.pallas_call(kernel, in_specs=[pl.BlockSpec(memory_space=pltpu.SMEM)] +...  33.1 us
    ppermute x6, waiting for transfers between devices, band_swap(): lax.ppermute(send_first, axes, band_pairs(0))  15 us
    ppermute x6, starting transfers between devices, band_swap(): lax.ppermute(send_first, axes, band_pairs(0))  14.9 us
    ppermute x2, waiting for transfers between devices, body(): inc = inc + lax.ppermute(inc, 'mem', perm)  7.28 us
    ppermute x2, waiting for transfers between devices, opening(): inc = inc + lax.ppermute(inc, 'mem', perm)  6.38 us
    ppermute x2, waiting for transfers between devices, opening(): got = [lax.ppermute(x, 'mem', steps[-1]) for x in held]  4.44 us
    ppermute x9, waiting for transfers between devices, core_swap(): return lax.ppermute(cells, 'mem', [(i, i ^ 1) for i in range(count)])  3.29 us
    ppermute x2, starting transfers between devices, body(): inc = inc + lax.ppermute(inc, 'mem', perm)  3.14 us
  transfers between devices with their start and end apart: 28, of which 15 were waited for; matrix products, arithmetic and copies ran while one was open for 2% of the time, Pallas kernels for 21%

profile of v5, /device:TPU:0, one launch (start us, length us, event | category | flops | bytes accessed | tf_op | source)
XLA Modules:
  0.0 110.1 jit_solution(14177348819533546884)
XLA Ops:
  0.0 1.4 %copy-done = f32[10,4,8,1152]{3,2,1,0:T(8,128)S(1)} copy-done((f32[10,4,8,1152]{3,2,1,0:T(8,128)S(1)}, f32[10,4,8,1152]{3,2,1,0:T(8,128)}, u32[]{:S(2)}) %copy-start) | copy-done | bytes 1474584
  1.4 0.2 shard_map.109
  1.6 3.1 %collective-permute-start.8 = (f32[160,1152]{1,0:T(8,128)S(1)}, f32[160,1152]{1,0:T(8,128)}, u32[]{:S(2)}, u32[]{:S(2)}) collective-permute-start(f32[160,1152]{1,0:T(8,128)S(1)} %get-tuple-element.87), channel_id=1, source_target_pairs={{0,1},{1,0},{2,3},{3,2},{4,5},{5,4},{6,7},{7,6},{8,9},{9,8},{10,11... | collective-permute-start | bytes 2211848 | tf_op jit(solution)/shard_map/ppermute | solution.py:38
  4.8 1.8 %shard_map.110 = f32[3,2,128,128]{3,2,1,0:T(8,128)S(1)} custom-call(s32[3]{0:T(128)S(1)} %bitcast.30, s32[3]{0:T(128)S(1)} %bitcast.31, s32[128,1]{1,0:T(8,128)S(1)} %copy-done.8, s32[128,1]{1,0:T(8,128)S(1)} %copy-done.7, s32[3,1,4096]{2,1,0:T(1,128)S(1)} %bitcast.27, f32[3,1,4096]{2,1,0:T(1,128)S(1)} %bitcast.28, f32[3,1,4096]{2,1,0:T(1,128)S(1)} %bitcast.29), custom_call_target="tpu_custom_call" | custom-call | flops 1258291200 | bytes 393216 | tf_op jit(solution)/shard_map/pallas_call | solution.py:153
  6.6 1.1 collective-permute-start.10
  7.7 0.8 copy.16.coef_ref
  8.5 3.1 %shard_map.111 = (f32[216,8,128]{2,1,0:T(8,128)}, f32[9,320,128]{2,1,0:T(8,128)}) custom-call(f32[32,9]{1,0:T(8,128)S(1)} %copy.16.coef_ref, f32[320,1152]{1,0:T(8,128)S(1)} %bitcast.26), custom_call_target="tpu_custom_call" | custom-call | bytes 3833856 | tf_op jit(solution)/shard_map/pallas_call | solution.py:600
  11.6 0.7 copy-done.13
  12.2 1.0 pad_maximum_fusion
  13.2 8.1 %collective-permute-done.8 = f32[160,1152]{1,0:T(8,128)} collective-permute-done((f32[160,1152]{1,0:T(8,128)S(1)}, f32[160,1152]{1,0:T(8,128)}, u32[]{:S(2)}, u32[]{:S(2)}) %collective-permute-start.8) | collective-permute-done | bytes 737312 | tf_op jit(solution)/shard_map/ppermute | solution.py:38
  21.3 4.6 %collective-permute-start.11 = (bf16[10,2,4,8,1152]{4,3,2,1,0:T(8,128)(2,1)}, bf16[10,2,4,8,1152]{4,3,2,1,0:T(8,128)(2,1)S(1)}, u32[]{:S(2)}, u32[]{:S(2)}) collective-permute-start(bf16[10,2,4,8,1152]{4,3,2,1,0:T(8,128)(2,1)} %members_ref.3), channel_id=1, source_target_pairs={{0,1},{1,0},{2,3},{3,2},{4,5},{5,4},{6,7},{7,6},{8,9},{9,8},{10,11... | collective-permute-start | bytes 4423688 | tf_op jit(solution)/shard_map/ppermute | solution.py:38
  25.9 0.1 stack.47.flag_ref.refs_0_
  26.0 34.4 %conditional.1 = (f32[4,8,1152]{2,1,0:T(8,128)S(1)}, f32[2,2,4,8,1152]{4,3,2,1,0:T(8,128)}, f32[2,4,8,1152]{3,2,1,0:T(8,128)}, f32[4,4,1152]{2,1,0:T(4,128)}, f3...) conditional(s32[]{:T(128)} %convert_element_type.4, () %tuple.19, (s32[6]{0:T(128)S(1)}, ...), branch_computations={%region_0.1_spmd, %region_1.2_spmd} | conditional | flops 852996224 | bytes 22561600 | solution.py:728
  26.0 1.5 %collective-permute-start.3 = (f32[6,128,128]{2,1,0:T(8,128)S(1)}, f32[6,128,128]{2,1,0:T(8,128)S(1)}, u32[]{:S(2)}, u32[]{:S(2)}) collective-permute-start(f32[6,128,128]{2,1,0:T(8,128)S(1)} %get-tuple-element.30.refs_0_), channel_id=1, source_target_pairs={{0,8},{4,20},{8,0},{12,28},{16,24},{20,4},{24,16},{28,12},{1,9},{5... | collective-permute-start | bytes 1179656 | tf_op jit(solution)/shard_map/cond/branch_1_fun/ppermute | solution.py:705
  27.5 5.8 %branch_1_fun.4 = (f32[4,8,1152]{2,1,0:T(8,128)S(1)}, f32[4,8,1152]{2,1,0:T(8,128)S(1)}, f32[9,160,128]{2,1,0:T(8,128)}, f32[9,160,128]{2,1,0:T(8,128)}) custom-call(s32[6]{0:T(128)S(1)} %get-tuple-element.21.flag_ref, f32[216,8,128]{2,1,0:T(8,128)} %get-tuple-element.22.coef_ref, f32[9,320,128]{2,1,0:T(8,128)} %get-tuple-element.23.own_ref, ...), custom_call_target="tpu_custom_call" | custom-call | flops 849346560 | bytes 9732120 | tf_op jit(solution)/shard_map/cond/branch_1_fun/pallas_call | solution.py:556
  33.3 0.1 collective-permute-start
  33.4 1.6 %collective-permute-start.2 = (f32[6,128,128]{2,1,0:T(8,128)S(1)}, f32[6,128,128]{2,1,0:T(8,128)S(1)}, u32[]{:S(2)}, u32[]{:S(2)}) collective-permute-start(f32[6,128,128]{2,1,0:T(8,128)S(1)} %get-tuple-element.30.refs_0_), channel_id=1, source_target_pairs={{0,16},{4,12},{8,24},{12,4},{16,0},{20,28},{24,8},{28,20},{1,17},{... | collective-permute-start | bytes 1179656 | tf_op jit(solution)/shard_map/cond/branch_1_fun/ppermute | solution.py:706
  34.9 0.5 collective-permute-start.4
  35.5 1.4 %collective-permute-start.1 = (f32[4,8,1152]{2,1,0:T(8,128)S(1)}, f32[4,8,1152]{2,1,0:T(8,128)S(1)}, u32[]{:S(2)}, u32[]{:S(2)}) collective-permute-start(f32[4,8,1152]{2,1,0:T(8,128)S(1)} %add.24), channel_id=1, source_target_pairs={{0,8},{4,20},{8,0},{12,28},{16,24},{20,4},{24,16},{28,12},{1,9},{5... | collective-permute-start | bytes 442376 | tf_op jit(solution)/shard_map/cond/branch_1_fun/ppermute | solution.py:717
  36.9 0.2 slice_reduce_fusion.3
  37.1 5.2 %collective-permute-done.1 = f32[4,8,1152]{2,1,0:T(8,128)S(1)} collective-permute-done((f32[4,8,1152]{2,1,0:T(8,128)S(1)}, f32[4,8,1152]{2,1,0:T(8,128)S(1)}, u32[]{:S(2)}, u32[]{:S(2)}) %collective-permute-start.1) | collective-permute-done | bytes 147488 | tf_op jit(solution)/shard_map/cond/branch_1_fun/ppermute | solution.py:717
  42.3 0.2 slice_reduce_fusion
  42.5 0.2 collective-permute-done.2.refs_2_
  42.8 4.2 %collective-permute-done.4.refs_3_ = f32[6,128,128]{2,1,0:T(8,128)S(1)} collective-permute-done((f32[6,128,128]{2,1,0:T(8,128)S(1)}, f32[6,128,128]{2,1,0:T(8,128)S(1)}, u32[]{:S(2)}, u32[]{:S(2)}) %collective-permute-start.4) | collective-permute-done | bytes 393248 | tf_op jit(solution)/shard_map/cond/branch_1_fun/ppermute | solution.py:706
  47.0 1.5 %collective-permute-start.5 = (f32[4,8,1152]{2,1,0:T(8,128)S(1)}, f32[4,8,1152]{2,1,0:T(8,128)S(1)}, u32[]{:S(2)}, u32[]{:S(2)}) collective-permute-start(f32[4,8,1152]{2,1,0:T(8,128)S(1)} %add.25), channel_id=1, source_target_pairs={{0,16},{4,12},{8,24},{12,4},{16,0},{20,28},{24,8},{28,20},{1,17},{... | collective-permute-start | bytes 442376 | tf_op jit(solution)/shard_map/cond/branch_1_fun/ppermute | solution.py:717
  48.5 0.2 slice_reduce_fusion.1
  48.7 0.1 maximum_convert_fusion.mark_ref
  48.8 2.2 %branch_1_fun.5 = (f32[2,64,1152]{2,1,0:T(8,128)}, f32[64,1152]{1,0:T(8,128)}) custom-call(s32[24]{0:T(128)S(1)} %maximum_convert_fusion.mark_ref, f32[6,128,128]{2,1,0:T(8,128)S(1)} %get-tuple-element.30.refs_0_, f32[6,128,128]{2,1,0:T(8,128)S(1)} %collective-permute-done.3.refs_1_, f32[6,128,128]{2,1,0:T(8,128)S(1)} %collective-permute-done.2.refs_2_, ...), custom_call_target="tpu_custom_call" | custom-call | flops 589824 | bytes 1769472 | tf_op jit(solution)/shard_map/cond/branch_1_fun/pallas_call | solution.py:225
  51.0 1.1 %collective-permute-done.5 = f32[4,8,1152]{2,1,0:T(8,128)S(1)} collective-permute-done((f32[4,8,1152]{2,1,0:T(8,128)S(1)}, f32[4,8,1152]{2,1,0:T(8,128)S(1)}, u32[]{:S(2)}, u32[]{:S(2)}) %collective-permute-start.5) | collective-permute-done | bytes 147488 | tf_op jit(solution)/shard_map/cond/branch_1_fun/ppermute | solution.py:717
  52.2 1.2 %branch_1_fun.6 = (f32[4,4,1152]{2,1,0:T(4,128)S(1)}, f32[4,4,1152]{2,1,0:T(4,128)S(1)}) custom-call(s32[6]{0:T(128)S(1)} %get-tuple-element.21.flag_ref, f32[4,8,1152]{2,1,0:T(8,128)S(1)} %add.26.inc_ref, f32[2,2,4,8,1152]{4,3,2,1,0:T(8,128)} %bitcast.weight_ref, f32[2,4,8,1152]{3,2,1,0:T(8,128)} %bitcast.1.pull_ref), custom_call_target="tpu_custom_call" | custom-call | bytes 1179672 | tf_op jit(solution)/shard_map/cond/branch_1_fun/pallas_call | solution.py:556
  53.4 0.1 collective-permute-start.6
  53.5 0.1 collective-permute-start.7
  53.6 5.1 %collective-permute-done.6.first_ref.rim_first_ref = f32[4,4,1152]{2,1,0:T(4,128)} collective-permute-done((f32[4,4,1152]{2,1,0:T(4,128)S(1)}, f32[4,4,1152]{2,1,0:T(4,128)}, u32[]{:S(2)}, u32[]{:S(2)}) %collective-permute-start.6) | collective-permute-done | bytes 73760 | tf_op jit(solution)/shard_map/cond/branch_1_fun/ppermute | solution.py:38
  58.7 1.7 %branch_1_fun.7 = f32[4,8,1152]{2,1,0:T(8,128)S(1)} custom-call(s32[6]{0:T(128)S(1)} %get-tuple-element.21.flag_ref, f32[4,8,1152]{2,1,0:T(8,128)S(1)} %add.26.inc_ref, f32[4,4,1152]{2,1,0:T(4,128)} %collective-permute-done.6.first_ref.rim_first_ref, f32[4,4,1152]{2,1,0:T(4,128)} %collective-permute-done.7.second_ref.rim_second_ref, ...), custom_call_target="tpu_custom_call" | custom-call | flops 2949120 | bytes 1474584 | tf_op jit(solution)/shard_map/cond/branch_1_fun/pallas_call | solution.py:556
  60.5 0.1 collective-permute-start.15
  60.5 0.5 collective-permute-start.14
  61.0 2.0 %collective-permute-start.13 = (f32[4,8,1152]{2,1,0:T(8,128)S(1)}, f32[4,8,1152]{2,1,0:T(8,128)S(1)}, u32[]{:S(2)}, u32[]{:S(2)}) collective-permute-start(f32[4,8,1152]{2,1,0:T(8,128)S(1)} %get-tuple-element.111.mine_ref), channel_id=1, source_target_pairs={{0,1},{1,0},{2,3},{3,2},{4,5},{5,4},{6,7},{7,6},{8,9},{9,8},{10,11... | collective-permute-start | bytes 442376 | tf_op jit(solution)/shard_map/ppermute | solution.py:38
  63.0 4.1 %shard_map.112.refs_6_ = f32[9,320,128]{2,1,0:T(8,128)S(1)} custom-call(s32[6]{0:T(128)S(1)} %stack.47.flag_ref.refs_0_, bf16[1152,1152]{1,0:T(8,128)(2,1)} %refs_3_.1, f32[4,8,1152]{2,1,0:T(8,128)S(1)} %get-tuple-element.111.mine_ref, f32[4,8,1152]{2,1,0:T(8,128)S(1)} %collective-permute-done.15.other_ref, bf16[10,2,4,8,1152]{4,3,2,1,0:T(8,128)(2,1)} %members_ref.3), custom_call_target="tpu_custom_call" | custom-call | flops 849346560 | bytes 5898264 | tf_op jit(solution)/shard_map/pallas_call | solution.py:556
  67.1 0.1 collective-permute-done.13.refs_7_
  67.2 0.0 collective-permute-start.16
  67.2 0.5 collective-permute-start.17
  67.7 0.9 collective-permute-done.16.refs_8_
  68.6 0.2 collective-permute-done.17.refs_10_
  68.8 9.8 %shard_map.113 = (f32[4,8,1152]{2,1,0:T(8,128)S(1)}, f32[4,8,1152]{2,1,0:T(8,128)S(1)}, f32[9,320,128]{2,1,0:T(8,128)S(1)}) custom-call(s32[6]{0:T(128)S(1)} %stack.47.flag_ref.refs_0_, f32[216,8,128]{2,1,0:T(8,128)S(1)} %copy-done.10, f32[9,320,128]{2,1,0:T(8,128)S(1)} %copy-done.11, f32[9,160,128]{2,1,0:T(8,128)} %get-tuple-element.109.refs_3_, ...), custom_call_target="tpu_custom_call" | custom-call | flops 2548039680 | bytes 14745624 | tf_op jit(solution)/shard_map/pallas_call | solution.py:556
  78.7 0.3 collective-permute-start.18
  79.0 1.1 %collective-permute-done.18 = f32[4,8,1152]{2,0,1:T(4,128)S(1)} collective-permute-done((f32[4,8,1152]{2,0,1:T(4,128)S(1)}, f32[4,8,1152]{2,0,1:T(4,128)S(1)}, u32[]{:S(2)}, u32[]{:S(2)}) %collective-permute-start.18) | collective-permute-done | bytes 147488 | tf_op jit(solution)/shard_map/ppermute | solution.py:55
  80.1 0.1 copy_add_fusion
  80.1 1.6 %collective-permute-start.19 = (f32[4,8,1152]{2,0,1:T(4,128)S(1)}, f32[4,8,1152]{2,0,1:T(4,128)S(1)}, u32[]{:S(2)}, u32[]{:S(2)}) collective-permute-start(f32[4,8,1152]{2,0,1:T(4,128)S(1)} %copy_add_fusion), channel_id=1, source_target_pairs={{0,8},{4,20},{8,0},{12,28},{16,24},{20,4},{24,16},{28,12},{1,9},{5... | collective-permute-start | bytes 442376 | tf_op jit(solution)/shard_map/ppermute | solution.py:741
  81.7 3.7 %collective-permute-done.19 = f32[4,8,1152]{2,0,1:T(4,128)S(1)} collective-permute-done((f32[4,8,1152]{2,0,1:T(4,128)S(1)}, f32[4,8,1152]{2,0,1:T(4,128)S(1)}, u32[]{:S(2)}, u32[]{:S(2)}) %collective-permute-start.19) | collective-permute-done | bytes 147488 | tf_op jit(solution)/shard_map/ppermute | solution.py:741
  85.4 1.6 %collective-permute-start.20 = (f32[4,8,1152]{2,0,1:T(4,128)S(1)}, f32[4,8,1152]{2,0,1:T(4,128)S(1)}, u32[]{:S(2)}, u32[]{:S(2)}) collective-permute-start(f32[4,8,1152]{2,0,1:T(4,128)S(1)} %add.39), channel_id=1, source_target_pairs={{0,16},{4,12},{8,24},{12,4},{16,0},{20,28},{24,8},{28,20},{1,17},{... | collective-permute-start | bytes 442376 | tf_op jit(solution)/shard_map/ppermute | solution.py:741
  87.0 3.6 %collective-permute-done.20 = f32[4,8,1152]{2,0,1:T(4,128)S(1)} collective-permute-done((f32[4,8,1152]{2,0,1:T(4,128)S(1)}, f32[4,8,1152]{2,0,1:T(4,128)S(1)}, u32[]{:S(2)}, u32[]{:S(2)}) %collective-permute-start.20) | collective-permute-done | bytes 147488 | tf_op jit(solution)/shard_map/ppermute | solution.py:741
  90.7 0.1 collective-permute-start.22
  90.8 3.1 %collective-permute-start.21 = (f32[1,4,1152]{2,1,0:T(4,128)S(1)}, f32[1,4,1152]{2,1,0:T(4,128)S(1)}, u32[]{:S(2)}, u32[]{:S(2)}) collective-permute-start(f32[1,4,1152]{2,1,0:T(4,128)S(1)} %get-tuple-element.135), channel_id=1, source_target_pairs={{0,1},{1,0},{2,3},{3,2},{4,5},{5,4},{6,7},{7,6},{8,9},{9,8},{10,11... | collective-permute-start | bytes 55304 | tf_op jit(solution)/shard_map/ppermute | solution.py:38
  93.8 1.7 %collective-permute-done.21.first_ref = f32[1,4,1152]{2,1,0:T(4,128)S(1)} collective-permute-done((f32[1,4,1152]{2,1,0:T(4,128)S(1)}, f32[1,4,1152]{2,1,0:T(4,128)S(1)}, u32[]{:S(2)}, u32[]{:S(2)}) %collective-permute-start.21) | collective-permute-done | bytes 18464 | tf_op jit(solution)/shard_map/ppermute | solution.py:38
  95.6 1.7 %shard_map.114 = (f32[4,8,1152]{2,1,0:T(8,128)S(1)}, f32[2,8,1152]{2,1,0:T(8,128)S(1)}, f32[2,8,1152]{2,1,0:T(8,128)S(1)}) custom-call(s32[6]{0:T(128)S(1)} %stack.47.flag_ref.refs_0_, f32[4,8,1152]{2,1,0:T(8,128)S(1)} %copy.19.inc_ref, f32[1,4,1152]{2,1,0:T(4,128)S(1)} %collective-permute-done.21.first_ref, ...), custom_call_target="tpu_custom_call" | custom-call | flops 2949120 | bytes 1511448 | tf_op jit(solution)/shard_map/pallas_call | solution.py:556
  97.2 0.1 collective-permute-start.25
  97.3 2.1 %collective-permute-start.23 = (f32[2,8,1152]{2,1,0:T(8,128)S(1)}, f32[2,8,1152]{2,1,0:T(8,128)S(1)}, u32[]{:S(2)}, u32[]{:S(2)}) collective-permute-start(f32[2,8,1152]{2,1,0:T(8,128)S(1)} %get-tuple-element.124), channel_id=1, source_target_pairs={{0,1},{1,0},{2,3},{3,2},{4,5},{5,4},{6,7},{7,6},{8,9},{9,8},{10,11... | collective-permute-start | bytes 221192 | tf_op jit(solution)/shard_map/ppermute | solution.py:38
  99.4 0.2 collective-permute-start.24
  99.6 3.3 %shard_map.115.refs_4_ = f32[9,320,128]{2,1,0:T(8,128)S(1)} custom-call(s32[6]{0:T(128)S(1)} %stack.47.flag_ref.refs_0_, bf16[1152,1152]{1,0:T(8,128)(2,1)S(1)} %copy-done.9, f32[4,8,1152]{2,1,0:T(8,128)S(1)} %get-tuple-element.126.mine_ref, f32[4,8,1152]{2,1,0:T(8,128)S(1)} %collective-permute-done.25.other_ref, bf16[10,2,4,8,1152]{4,3,2,1,0:T(8,128)(2,1)} %members_ref.3), custom_call_target="tpu_custom_call" | custom-call | flops 849346560 | bytes 5898264 | tf_op jit(solution)/shard_map/pallas_call | solution.py:556
  102.9 0.4 collective-permute-start.26
  103.3 0.2 collective-permute-start.27
  103.5 0.8 collective-permute-done.26.refs_6_
  104.2 0.4 collective-permute-done.27.refs_8_
  104.6 5.5 %shard_map.116 = f32[320,1152]{1,0:T(8,128)} custom-call(s32[6]{0:T(128)S(1)} %stack.47.flag_ref.refs_0_, f32[216,8,128]{2,1,0:T(8,128)S(1)} %copy-done.10, f32[9,320,128]{2,1,0:T(8,128)S(1)} %get-tuple-element.117.refs_2_, bf16[1152,1152]{1,0:T(8,128)(2,1)S(1)} %copy-done.9, f32[9,320,128]{2,1,0:T(8,128)S(1)} %shard_map.115.refs_4_, ...), custom_call_target="tpu_custom_call" | custom-call | flops 849346560 | bytes 11206680 | tf_op jit(solution)/shard_map/pallas_call | solution.py:556
  (50 shorter events, 0.3 us)
Async XLA Ops:
  0.0 4.7 %copy-start.6 = (s32[1,1,3]{2,1,0:T(1,128)S(1)}, s32[1,1,3]{2,1,0:T(1,128)}, u32[]{:S(2)}) copy-start(s32[1,1,3]{2,1,0:T(1,128)} %param.18) | copy-start | bytes 40
  0.0 4.7 %copy-start.5 = (s32[1,1,3]{2,1,0:T(1,128)S(1)}, s32[1,1,3]{2,1,0:T(1,128)}, u32[]{:S(2)}) copy-start(s32[1,1,3]{2,1,0:T(1,128)} %param.17) | copy-start | bytes 40
  0.0 1.4 %copy-start = (f32[10,4,8,1152]{3,2,1,0:T(8,128)S(1)}, f32[10,4,8,1152]{3,2,1,0:T(8,128)}, u32[]{:S(2)}) copy-start(f32[10,4,8,1152]{3,2,1,0:T(8,128)} %param.14) | copy-start | bytes 4423684
  1.4 3.3 %copy-start.2 = (s32[1,1,3,4096]{3,1,2,0:T(1,128)S(1)}, s32[1,1,3,4096]{3,1,2,0:T(1,128)}, u32[]{:S(2)}) copy-start(s32[1,1,3,4096]{3,1,2,0:T(1,128)} %param.19) | copy-start | bytes 147460
  1.4 3.3 %copy-start.3 = (f32[1,1,3,4096]{3,1,2,0:T(1,128)S(1)}, f32[1,1,3,4096]{3,1,2,0:T(1,128)}, u32[]{:S(2)}) copy-start(f32[1,1,3,4096]{3,1,2,0:T(1,128)} %param.20) | copy-start | bytes 147460
  1.4 3.3 %copy-start.4 = (f32[1,1,3,4096]{3,1,2,0:T(1,128)S(1)}, f32[1,1,3,4096]{3,1,2,0:T(1,128)}, u32[]{:S(2)}) copy-start(f32[1,1,3,4096]{3,1,2,0:T(1,128)} %param.21) | copy-start | bytes 147460
  1.4 3.4 %copy-start.7 = (s32[128,1]{1,0:T(8,128)S(1)}, s32[128,1]{1,0:T(8,128)}, u32[]{:S(2)}) copy-start(s32[128,1]{1,0:T(8,128)} %constant.48.clone.lane_ref) | copy-start | bytes 1540
  1.4 3.4 %copy-start.8 = (s32[128,1]{1,0:T(8,128)S(1)}, s32[128,1]{1,0:T(8,128)}, u32[]{:S(2)}) copy-start(s32[128,1]{1,0:T(8,128)} %constant.47.clone.row_ref) | copy-start | bytes 1540
  1.6 19.7 %collective-permute-start.8 = (f32[160,1152]{1,0:T(8,128)S(1)}, f32[160,1152]{1,0:T(8,128)}, u32[]{:S(2)}, u32[]{:S(2)}) collective-permute-start(f32[160,1152]{1,0:T(8,128)S(1)} %get-tuple-element.87), channel_id=1, source_target_pairs={{0,1},{1,0},{2,3},{3,2},{4,5},{5,4},{6,7},{7,6},{8,9},{9,8},{10,11... | collective-permute-start | bytes 2211848 | tf_op jit(solution)/shard_map/ppermute | solution.py:38
  4.7 16.6 %collective-permute-start.9 = (f32[160,1152]{1,0:T(8,128)S(1)}, f32[160,1152]{1,0:T(8,128)}, u32[]{:S(2)}, u32[]{:S(2)}) collective-permute-start(f32[160,1152]{1,0:T(8,128)S(1)} %get-tuple-element.88), channel_id=1, source_target_pairs={{0,4},{1,2},{2,1},{3,7},{4,0},{5,6},{6,5},{7,3},{8,12},{9,10},{10,... | collective-permute-start | bytes 2211848 | tf_op jit(solution)/shard_map/ppermute | solution.py:39
  4.8 3.7 %copy-start.1 = (f32[10,4,8,1152]{3,2,1,0:T(8,128)S(1)}, f32[10,4,8,1152]{3,2,1,0:T(8,128)}, u32[]{:S(2)}) copy-start(f32[10,4,8,1152]{3,2,1,0:T(8,128)} %param.14) | copy-start | bytes 4423684
  6.6 4.9 %collective-permute-start.10 = (f32[1,3,128,128]{3,2,1,0:T(8,128)S(1)}, f32[1,3,128,128]{3,2,1,0:T(8,128)S(1)}, u32[]{:S(2)}, u32[]{:S(2)}) collective-permute-start(f32[1,3,128,128]{3,2,1,0:T(8,128)S(1)} %get-tuple-element.133), channel_id=1, source_target_pairs={{0,4},{4,0},{8,12},{12,8},{16,20},{20,16},{24,28},{28,24},{1,5},{5... | collective-permute-start | bytes 589832 | tf_op jit(solution)/shard_map/ppermute | solution.py:55
  11.6 0.7 copy-start.13
  21.3 39.1 %collective-permute-start.12 = (bf16[10,2,4,8,1152]{4,3,2,1,0:T(8,128)(2,1)}, bf16[10,2,4,8,1152]{4,3,2,1,0:T(8,128)(2,1)S(1)}, u32[]{:S(2)}, u32[]{:S(2)}) collective-permute-start(bf16[10,2,4,8,1152]{4,3,2,1,0:T(8,128)(2,1)} %members_ref.3), channel_id=1, source_target_pairs={{0,4},{1,2},{2,1},{3,7},{4,0},{5,6},{6,5},{7,3},{8,12},{9,10},{10,... | collective-permute-start | bytes 4423688 | tf_op jit(solution)/shard_map/ppermute | solution.py:39
  21.3 39.1 %collective-permute-start.11 = (bf16[10,2,4,8,1152]{4,3,2,1,0:T(8,128)(2,1)}, bf16[10,2,4,8,1152]{4,3,2,1,0:T(8,128)(2,1)S(1)}, u32[]{:S(2)}, u32[]{:S(2)}) collective-permute-start(bf16[10,2,4,8,1152]{4,3,2,1,0:T(8,128)(2,1)} %members_ref.3), channel_id=1, source_target_pairs={{0,1},{1,0},{2,3},{3,2},{4,5},{5,4},{6,7},{7,6},{8,9},{9,8},{10,11... | collective-permute-start | bytes 4423688 | tf_op jit(solution)/shard_map/ppermute | solution.py:38
  26.0 8.9 %collective-permute-start.3 = (f32[6,128,128]{2,1,0:T(8,128)S(1)}, f32[6,128,128]{2,1,0:T(8,128)S(1)}, u32[]{:S(2)}, u32[]{:S(2)}) collective-permute-start(f32[6,128,128]{2,1,0:T(8,128)S(1)} %get-tuple-element.30.refs_0_), channel_id=1, source_target_pairs={{0,8},{4,20},{8,0},{12,28},{16,24},{20,4},{24,16},{28,12},{1,9},{5... | collective-permute-start | bytes 1179656 | tf_op jit(solution)/shard_map/cond/branch_1_fun/ppermute | solution.py:705
  33.3 2.2 %collective-permute-start = (f32[4,8,1152]{2,1,0:T(8,128)S(1)}, f32[4,8,1152]{2,1,0:T(8,128)S(1)}, u32[]{:S(2)}, u32[]{:S(2)}) collective-permute-start(f32[4,8,1152]{2,1,0:T(8,128)S(1)} %get-tuple-element.29), channel_id=1, source_target_pairs={{0,4},{4,0},{8,12},{12,8},{16,20},{20,16},{24,28},{28,24},{1,5},{5... | collective-permute-start | bytes 442376 | tf_op jit(solution)/shard_map/cond/branch_1_fun/ppermute | solution.py:55
  33.4 9.4 %collective-permute-start.2 = (f32[6,128,128]{2,1,0:T(8,128)S(1)}, f32[6,128,128]{2,1,0:T(8,128)S(1)}, u32[]{:S(2)}, u32[]{:S(2)}) collective-permute-start(f32[6,128,128]{2,1,0:T(8,128)S(1)} %get-tuple-element.30.refs_0_), channel_id=1, source_target_pairs={{0,16},{4,12},{8,24},{12,4},{16,0},{20,28},{24,8},{28,20},{1,17},{... | collective-permute-start | bytes 1179656 | tf_op jit(solution)/shard_map/cond/branch_1_fun/ppermute | solution.py:706
  34.9 12.0 %collective-permute-start.4 = (f32[6,128,128]{2,1,0:T(8,128)S(1)}, f32[6,128,128]{2,1,0:T(8,128)S(1)}, u32[]{:S(2)}, u32[]{:S(2)}) collective-permute-start(f32[6,128,128]{2,1,0:T(8,128)S(1)} %collective-permute-done.3.refs_1_), channel_id=1, source_target_pairs={{0,16},{4,12},{8,24},{12,4},{16,0},{20,28},{24,8},{28,20},{1,17},{... | collective-permute-start | bytes 1179656 | tf_op jit(solution)/shard_map/cond/branch_1_fun/ppermute | solution.py:706
  35.5 6.8 %collective-permute-start.1 = (f32[4,8,1152]{2,1,0:T(8,128)S(1)}, f32[4,8,1152]{2,1,0:T(8,128)S(1)}, u32[]{:S(2)}, u32[]{:S(2)}) collective-permute-start(f32[4,8,1152]{2,1,0:T(8,128)S(1)} %add.24), channel_id=1, source_target_pairs={{0,8},{4,20},{8,0},{12,28},{16,24},{20,4},{24,16},{28,12},{1,9},{5... | collective-permute-start | bytes 442376 | tf_op jit(solution)/shard_map/cond/branch_1_fun/ppermute | solution.py:717
  47.0 5.1 %collective-permute-start.5 = (f32[4,8,1152]{2,1,0:T(8,128)S(1)}, f32[4,8,1152]{2,1,0:T(8,128)S(1)}, u32[]{:S(2)}, u32[]{:S(2)}) collective-permute-start(f32[4,8,1152]{2,1,0:T(8,128)S(1)} %add.25), channel_id=1, source_target_pairs={{0,16},{4,12},{8,24},{12,4},{16,0},{20,28},{24,8},{28,20},{1,17},{... | collective-permute-start | bytes 442376 | tf_op jit(solution)/shard_map/cond/branch_1_fun/ppermute | solution.py:717
  53.4 5.3 %collective-permute-start.6 = (f32[4,4,1152]{2,1,0:T(4,128)S(1)}, f32[4,4,1152]{2,1,0:T(4,128)}, u32[]{:S(2)}, u32[]{:S(2)}) collective-permute-start(f32[4,4,1152]{2,1,0:T(4,128)S(1)} %get-tuple-element.36), channel_id=1, source_target_pairs={{0,1},{1,0},{2,3},{3,2},{4,5},{5,4},{6,7},{7,6},{8,9},{9,8},{10,11... | collective-permute-start | bytes 221192 | tf_op jit(solution)/shard_map/cond/branch_1_fun/ppermute | solution.py:38
  53.5 5.2 %collective-permute-start.7 = (f32[4,4,1152]{2,1,0:T(4,128)S(1)}, f32[4,4,1152]{2,1,0:T(4,128)}, u32[]{:S(2)}, u32[]{:S(2)}) collective-permute-start(f32[4,4,1152]{2,1,0:T(4,128)S(1)} %get-tuple-element.37), channel_id=1, source_target_pairs={{0,4},{1,2},{2,1},{3,7},{4,0},{5,6},{6,5},{7,3},{8,12},{9,10},{10,... | collective-permute-start | bytes 221192 | tf_op jit(solution)/shard_map/cond/branch_1_fun/ppermute | solution.py:39
  60.4 8.3 %copy-start.10 = (f32[216,8,128]{2,1,0:T(8,128)S(1)}, f32[216,8,128]{2,1,0:T(8,128)}, u32[]{:S(2)}) copy-start(f32[216,8,128]{2,1,0:T(8,128)} %get-tuple-element.107.refs_1_) | copy-start | bytes 2654212
  60.4 8.3 %copy-start.11 = (f32[9,320,128]{2,1,0:T(8,128)S(1)}, f32[9,320,128]{2,1,0:T(8,128)}, u32[]{:S(2)}) copy-start(f32[9,320,128]{2,1,0:T(8,128)} %get-tuple-element.108.refs_2_) | copy-start | bytes 4423684
  60.5 8.3 %copy-start.12 = (f32[9,160,128]{2,1,0:T(8,128)S(1)}, f32[9,160,128]{2,1,0:T(8,128)}, u32[]{:S(2)}) copy-start(f32[9,160,128]{2,1,0:T(8,128)} %get-tuple-element.110.refs_4_) | copy-start | bytes 2211844
  60.5 2.5 %collective-permute-start.15 = (f32[4,8,1152]{2,1,0:T(8,128)S(1)}, f32[4,8,1152]{2,1,0:T(8,128)S(1)}, u32[]{:S(2)}, u32[]{:S(2)}) collective-permute-start(f32[4,8,1152]{2,1,0:T(8,128)S(1)} %get-tuple-element.111.mine_ref), channel_id=1, source_target_pairs={{0,4},{4,0},{8,12},{12,8},{16,20},{20,16},{24,28},{28,24},{1,5},{5... | collective-permute-start | bytes 442376 | tf_op jit(solution)/shard_map/ppermute | solution.py:55
  60.5 6.6 %collective-permute-start.14 = (f32[4,8,1152]{2,1,0:T(8,128)S(1)}, f32[4,8,1152]{2,1,0:T(8,128)S(1)}, u32[]{:S(2)}, u32[]{:S(2)}) collective-permute-start(f32[4,8,1152]{2,1,0:T(8,128)S(1)} %get-tuple-element.111.mine_ref), channel_id=1, source_target_pairs={{0,4},{1,2},{2,1},{3,7},{4,0},{5,6},{6,5},{7,3},{8,12},{9,10},{10,... | collective-permute-start | bytes 442376 | tf_op jit(solution)/shard_map/ppermute | solution.py:39
  61.0 6.1 %collective-permute-start.13 = (f32[4,8,1152]{2,1,0:T(8,128)S(1)}, f32[4,8,1152]{2,1,0:T(8,128)S(1)}, u32[]{:S(2)}, u32[]{:S(2)}) collective-permute-start(f32[4,8,1152]{2,1,0:T(8,128)S(1)} %get-tuple-element.111.mine_ref), channel_id=1, source_target_pairs={{0,1},{1,0},{2,3},{3,2},{4,5},{5,4},{6,7},{7,6},{8,9},{9,8},{10,11... | collective-permute-start | bytes 442376 | tf_op jit(solution)/shard_map/ppermute | solution.py:38
  63.0 5.8 %copy-start.9 = (bf16[1152,1152]{1,0:T(8,128)(2,1)S(1)}, bf16[1152,1152]{1,0:T(8,128)(2,1)}, u32[]{:S(2)}) copy-start(bf16[1152,1152]{1,0:T(8,128)(2,1)} %refs_3_.1) | copy-start | bytes 7962628
  67.2 1.4 %collective-permute-start.16 = (f32[4,8,1152]{2,1,0:T(8,128)S(1)}, f32[4,8,1152]{2,1,0:T(8,128)S(1)}, u32[]{:S(2)}, u32[]{:S(2)}) collective-permute-start(f32[4,8,1152]{2,1,0:T(8,128)S(1)} %collective-permute-done.13.refs_7_), channel_id=1, source_target_pairs={{0,4},{4,0},{8,12},{12,8},{16,20},{20,16},{24,28},{28,24},{1,5},{5... | collective-permute-start | bytes 442376 | tf_op jit(solution)/shard_map/ppermute | solution.py:55
  67.2 1.6 %collective-permute-start.17 = (f32[4,8,1152]{2,1,0:T(8,128)S(1)}, f32[4,8,1152]{2,1,0:T(8,128)S(1)}, u32[]{:S(2)}, u32[]{:S(2)}) collective-permute-start(f32[4,8,1152]{2,1,0:T(8,128)S(1)} %collective-permute-done.14.refs_9_), channel_id=1, source_target_pairs={{0,4},{4,0},{8,12},{12,8},{16,20},{20,16},{24,28},{28,24},{1,5},{5... | collective-permute-start | bytes 442376 | tf_op jit(solution)/shard_map/ppermute | solution.py:55
  78.7 1.4 %collective-permute-start.18 = (f32[4,8,1152]{2,0,1:T(4,128)S(1)}, f32[4,8,1152]{2,0,1:T(4,128)S(1)}, u32[]{:S(2)}, u32[]{:S(2)}) collective-permute-start(f32[4,8,1152]{2,0,1:T(4,128)S(1)} %copy.17), channel_id=1, source_target_pairs={{0,4},{4,0},{8,12},{12,8},{16,20},{20,16},{24,28},{28,24},{1,5},{5... | collective-permute-start | bytes 442376 | tf_op jit(solution)/shard_map/ppermute | solution.py:55
  80.1 5.2 %collective-permute-start.19 = (f32[4,8,1152]{2,0,1:T(4,128)S(1)}, f32[4,8,1152]{2,0,1:T(4,128)S(1)}, u32[]{:S(2)}, u32[]{:S(2)}) collective-permute-start(f32[4,8,1152]{2,0,1:T(4,128)S(1)} %copy_add_fusion), channel_id=1, source_target_pairs={{0,8},{4,20},{8,0},{12,28},{16,24},{20,4},{24,16},{28,12},{1,9},{5... | collective-permute-start | bytes 442376 | tf_op jit(solution)/shard_map/ppermute | solution.py:741
  85.4 5.2 %collective-permute-start.20 = (f32[4,8,1152]{2,0,1:T(4,128)S(1)}, f32[4,8,1152]{2,0,1:T(4,128)S(1)}, u32[]{:S(2)}, u32[]{:S(2)}) collective-permute-start(f32[4,8,1152]{2,0,1:T(4,128)S(1)} %add.39), channel_id=1, source_target_pairs={{0,16},{4,12},{8,24},{12,4},{16,0},{20,28},{24,8},{28,20},{1,17},{... | collective-permute-start | bytes 442376 | tf_op jit(solution)/shard_map/ppermute | solution.py:741
  90.7 3.2 %collective-permute-start.22 = (f32[1,4,1152]{2,1,0:T(4,128)S(1)}, f32[1,4,1152]{2,1,0:T(4,128)S(1)}, u32[]{:S(2)}, u32[]{:S(2)}) collective-permute-start(f32[1,4,1152]{2,1,0:T(4,128)S(1)} %get-tuple-element.134), channel_id=1, source_target_pairs={{0,4},{1,2},{2,1},{3,7},{4,0},{5,6},{6,5},{7,3},{8,12},{9,10},{10,... | collective-permute-start | bytes 55304 | tf_op jit(solution)/shard_map/ppermute | solution.py:39
  90.8 4.8 %collective-permute-start.21 = (f32[1,4,1152]{2,1,0:T(4,128)S(1)}, f32[1,4,1152]{2,1,0:T(4,128)S(1)}, u32[]{:S(2)}, u32[]{:S(2)}) collective-permute-start(f32[1,4,1152]{2,1,0:T(4,128)S(1)} %get-tuple-element.135), channel_id=1, source_target_pairs={{0,1},{1,0},{2,3},{3,2},{4,5},{5,4},{6,7},{7,6},{8,9},{9,8},{10,11... | collective-permute-start | bytes 55304 | tf_op jit(solution)/shard_map/ppermute | solution.py:38
  97.2 2.3 %collective-permute-start.25 = (f32[4,8,1152]{2,1,0:T(8,128)S(1)}, f32[4,8,1152]{2,1,0:T(8,128)S(1)}, u32[]{:S(2)}, u32[]{:S(2)}) collective-permute-start(f32[4,8,1152]{2,1,0:T(8,128)S(1)} %get-tuple-element.126.mine_ref), channel_id=1, source_target_pairs={{0,4},{4,0},{8,12},{12,8},{16,20},{20,16},{24,28},{28,24},{1,5},{5... | collective-permute-start | bytes 442376 | tf_op jit(solution)/shard_map/ppermute | solution.py:55
  97.3 5.6 %collective-permute-start.23 = (f32[2,8,1152]{2,1,0:T(8,128)S(1)}, f32[2,8,1152]{2,1,0:T(8,128)S(1)}, u32[]{:S(2)}, u32[]{:S(2)}) collective-permute-start(f32[2,8,1152]{2,1,0:T(8,128)S(1)} %get-tuple-element.124), channel_id=1, source_target_pairs={{0,1},{1,0},{2,3},{3,2},{4,5},{5,4},{6,7},{7,6},{8,9},{9,8},{10,11... | collective-permute-start | bytes 221192 | tf_op jit(solution)/shard_map/ppermute | solution.py:38
  99.4 3.5 %collective-permute-start.24 = (f32[2,8,1152]{2,1,0:T(8,128)S(1)}, f32[2,8,1152]{2,1,0:T(8,128)S(1)}, u32[]{:S(2)}, u32[]{:S(2)}) collective-permute-start(f32[2,8,1152]{2,1,0:T(8,128)S(1)} %get-tuple-element.125), channel_id=1, source_target_pairs={{0,4},{1,2},{2,1},{3,7},{4,0},{5,6},{6,5},{7,3},{8,12},{9,10},{10,... | collective-permute-start | bytes 221192 | tf_op jit(solution)/shard_map/ppermute | solution.py:39
  102.9 1.3 %collective-permute-start.26 = (f32[2,8,1152]{2,1,0:T(8,128)S(1)}, f32[2,8,1152]{2,1,0:T(8,128)S(1)}, u32[]{:S(2)}, u32[]{:S(2)}) collective-permute-start(f32[2,8,1152]{2,1,0:T(8,128)S(1)} %collective-permute-done.23.refs_5_), channel_id=1, source_target_pairs={{0,4},{4,0},{8,12},{12,8},{16,20},{20,16},{24,28},{28,24},{1,5},{5... | collective-permute-start | bytes 221192 | tf_op jit(solution)/shard_map/ppermute | solution.py:55
  103.3 1.3 %collective-permute-start.27 = (f32[2,8,1152]{2,1,0:T(8,128)S(1)}, f32[2,8,1152]{2,1,0:T(8,128)S(1)}, u32[]{:S(2)}, u32[]{:S(2)}) collective-permute-start(f32[2,8,1152]{2,1,0:T(8,128)S(1)} %collective-permute-done.24.refs_7_), channel_id=1, source_target_pairs={{0,4},{4,0},{8,12},{12,8},{16,20},{20,16},{24,28},{28,24},{1,5},{5... | collective-permute-start | bytes 221192 | tf_op jit(solution)/shard_map/ppermute | solution.py:55

commit v6 on v5

--- a/solution.py
+++ b/solution.py
@@ -532,7 +532,7 @@
     flag_ref, coef_ref, own_ref, zonal_ref, own_back_ref = refs[:5]
     adjoints = refs[5:9]
     partners = refs[9 : 9 + 2 * parts]
-    out_ref, weighted_ref, back_ref, current_ref, wide_ref = refs[9 + 2 * parts :]
+    out_ref, weighted_ref, back_ref, current_ref, wide_ref, sent = refs[9 + 2 * parts :]
     half_band = taps // 2
     partner_half_back(flag_ref, zonal_ref, adjoints, partners, weighted_ref, back_ref, wide_ref)
 
@@ -543,21 +543,26 @@
                 here = pl.ds(start * rows + r, 8, stride=rows)
                 cell = own_ref[chunk, here, :]
                 current_ref[chunk, here, :] = cell - step_size * (cell + pulled)
-        return carry
+        out_copy(chunk).start()
+        return carry
+
+    def out_copy(chunk):
+        lanes = pl.ds(pl.multiple_of(chunk * LANES, LANES), LANES)
+        return pltpu.make_async_copy(current_ref.at[chunk], out_ref.at[:, lanes], sent.at[chunk])
 
     lax.fori_loop(0, own_ref.shape[0], step, 0)
     for chunk in range(own_ref.shape[0]):
-        out_ref[:, chunk * LANES : (chunk + 1) * LANES] = current_ref[chunk]
-
-
-def call(kernel, operands, outs, scratch, flops, anywhere=0, budget=20 * 2**20):
+        out_copy(chunk).wait()
+
+
+def call(kernel, operands, outs, scratch, flops, anywhere=0, out_anywhere=False, budget=20 * 2**20):
     vmem = pl.BlockSpec(memory_space=pltpu.VMEM)
     moved = sum(int(np.prod(x.shape)) * x.dtype.itemsize for x in list(operands) + list(outs))
     return pl.pallas_call(
         kernel,
         in_specs=[pl.BlockSpec(memory_space=pltpu.SMEM)] + [vmem] * (len(operands) - 1 - anywhere)
         + [pl.BlockSpec(memory_space=pl.ANY)] * anywhere,
-        out_specs=[vmem] * len(outs),
+        out_specs=[pl.BlockSpec(memory_space=pl.ANY) if out_anywhere else vmem] * len(outs),
         out_shape=list(outs),
         scratch_shapes=list(scratch),
         compiler_params=pltpu.CompilerParams(vmem_limit_bytes=budget),
@@ -769,8 +774,10 @@
                     chunk_scratch,
                     chunk_scratch,
                     pltpu.VMEM((2,) + inc_shape.shape, jnp.float32),
+                    pltpu.SemaphoreType.DMA((chunks,)),
                 ],
                 zonal_flops,
+                out_anywhere=True,
             )
     return own.reshape(alpha.shape)
 

time: 110 us -> 110 us (level)
  transfers between devices with their start and end apart: 28 -> 28, of which waited for: 15 -> 15; matrix products, arithmetic and copies ran while one was open for 2% -> 2% of each run, Pallas kernels for 21% -> 22%
where the time goes in v6:
time: 110 us
  Pallas kernels  40.4 us (37%)
  waiting for transfers between devices  36.9 us (34%)
  starting transfers between devices  27.1 us (25%)
  local copies, waits for them, and re-layouts  3.68 us (3%)
  other arithmetic  1.23 us (1%)
    pallas_call x8, Pallas kernels, call(): pl.pallas_call(kernel, in_specs=[pl.BlockSpec(memory_space=pltpu.SMEM)] +...  32.7 us
    ppermute x6, waiting for transfers between devices, band_swap(): lax.ppermute(send_first, axes, band_pairs(0))  15.5 us
    ppermute x6, starting transfers between devices, band_swap(): lax.ppermute(send_first, axes, band_pairs(0))  14.9 us
    ppermute x2, waiting for transfers between devices, body(): inc = inc + lax.ppermute(inc, 'mem', perm)  7.28 us
    ppermute x2, waiting for transfers between devices, opening(): inc = inc + lax.ppermute(inc, 'mem', perm)  6.38 us
    ppermute x2, waiting for transfers between devices, opening(): got = [lax.ppermute(x, 'mem', steps[-1]) for x in held]  4.44 us
    ppermute x9, waiting for transfers between devices, core_swap(): return lax.ppermute(cells, 'mem', [(i, i ^ 1) for i in range(count)])  3.29 us
    ppermute x2, starting transfers between devices, body(): inc = inc + lax.ppermute(inc, 'mem', perm)  3.14 us
  transfers between devices with their start and end apart: 28, of which 15 were waited for; matrix products, arithmetic and copies ran while one was open for 2% of the time, Pallas kernels for 22%

profile of v6, /device:TPU:0, one launch (start us, length us, event | category | flops | bytes accessed | tf_op | source)
XLA Modules:
  0.0 109.8 jit_solution(1936222811546700861)
XLA Ops:
  0.0 1.4 %copy-done = f32[10,4,8,1152]{3,2,1,0:T(8,128)S(1)} copy-done((f32[10,4,8,1152]{3,2,1,0:T(8,128)S(1)}, f32[10,4,8,1152]{3,2,1,0:T(8,128)}, u32[]{:S(2)}) %copy-start) | copy-done | bytes 1474584
  1.4 0.2 shard_map.109
  1.6 3.1 %collective-permute-start.8 = (f32[160,1152]{1,0:T(8,128)S(1)}, f32[160,1152]{1,0:T(8,128)}, u32[]{:S(2)}, u32[]{:S(2)}) collective-permute-start(f32[160,1152]{1,0:T(8,128)S(1)} %get-tuple-element.87), channel_id=1, source_target_pairs={{0,1},{1,0},{2,3},{3,2},{4,5},{5,4},{6,7},{7,6},{8,9},{9,8},{10,11... | collective-permute-start | bytes 2211848 | tf_op jit(solution)/shard_map/ppermute | solution.py:38
  4.8 2.3 %shard_map.110 = f32[3,2,128,128]{3,2,1,0:T(8,128)S(1)} custom-call(s32[3]{0:T(128)S(1)} %bitcast.30, s32[3]{0:T(128)S(1)} %bitcast.31, s32[128,1]{1,0:T(8,128)S(1)} %copy-done.8, s32[128,1]{1,0:T(8,128)S(1)} %copy-done.7, s32[3,1,4096]{2,1,0:T(1,128)S(1)} %bitcast.27, f32[3,1,4096]{2,1,0:T(1,128)S(1)} %bitcast.28, f32[3,1,4096]{2,1,0:T(1,128)S(1)} %bitcast.29), custom_call_target="tpu_custom_call" | custom-call | flops 1258291200 | bytes 393216 | tf_op jit(solution)/shard_map/pallas_call | solution.py:153
  7.2 0.1 collective-permute-start.10
  7.2 0.8 copy.16.coef_ref
  8.0 3.1 %shard_map.111 = (f32[216,8,128]{2,1,0:T(8,128)}, f32[9,320,128]{2,1,0:T(8,128)}) custom-call(f32[32,9]{1,0:T(8,128)S(1)} %copy.16.coef_ref, f32[320,1152]{1,0:T(8,128)S(1)} %bitcast.26), custom_call_target="tpu_custom_call" | custom-call | bytes 3833856 | tf_op jit(solution)/shard_map/pallas_call | solution.py:605
  11.1 0.7 copy-done.13
  11.8 1.0 pad_maximum_fusion
  12.7 8.6 %collective-permute-done.8 = f32[160,1152]{1,0:T(8,128)} collective-permute-done((f32[160,1152]{1,0:T(8,128)S(1)}, f32[160,1152]{1,0:T(8,128)}, u32[]{:S(2)}, u32[]{:S(2)}) %collective-permute-start.8) | collective-permute-done | bytes 737312 | tf_op jit(solution)/shard_map/ppermute | solution.py:38
  21.3 4.6 %collective-permute-start.11 = (bf16[10,2,4,8,1152]{4,3,2,1,0:T(8,128)(2,1)}, bf16[10,2,4,8,1152]{4,3,2,1,0:T(8,128)(2,1)S(1)}, u32[]{:S(2)}, u32[]{:S(2)}) collective-permute-start(bf16[10,2,4,8,1152]{4,3,2,1,0:T(8,128)(2,1)} %members_ref.3), channel_id=1, source_target_pairs={{0,1},{1,0},{2,3},{3,2},{4,5},{5,4},{6,7},{7,6},{8,9},{9,8},{10,11... | collective-permute-start | bytes 4423688 | tf_op jit(solution)/shard_map/ppermute | solution.py:38
  25.9 0.1 stack.47.flag_ref.refs_0_
  26.0 34.4 %conditional.1 = (f32[4,8,1152]{2,1,0:T(8,128)S(1)}, f32[2,2,4,8,1152]{4,3,2,1,0:T(8,128)}, f32[2,4,8,1152]{3,2,1,0:T(8,128)}, f32[4,4,1152]{2,1,0:T(4,128)}, f3...) conditional(s32[]{:T(128)} %convert_element_type.4, () %tuple.19, (s32[6]{0:T(128)S(1)}, ...), branch_computations={%region_0.1_spmd, %region_1.2_spmd} | conditional | flops 852996224 | bytes 22561600 | solution.py:733
  26.0 1.5 %collective-permute-start.3 = (f32[6,128,128]{2,1,0:T(8,128)S(1)}, f32[6,128,128]{2,1,0:T(8,128)S(1)}, u32[]{:S(2)}, u32[]{:S(2)}) collective-permute-start(f32[6,128,128]{2,1,0:T(8,128)S(1)} %get-tuple-element.30.refs_0_), channel_id=1, source_target_pairs={{0,8},{4,20},{8,0},{12,28},{16,24},{20,4},{24,16},{28,12},{1,9},{5... | collective-permute-start | bytes 1179656 | tf_op jit(solution)/shard_map/cond/branch_1_fun/ppermute | solution.py:710
  27.5 5.8 %branch_1_fun.4 = (f32[4,8,1152]{2,1,0:T(8,128)S(1)}, f32[4,8,1152]{2,1,0:T(8,128)S(1)}, f32[9,160,128]{2,1,0:T(8,128)}, f32[9,160,128]{2,1,0:T(8,128)}) custom-call(s32[6]{0:T(128)S(1)} %get-tuple-element.21.flag_ref, f32[216,8,128]{2,1,0:T(8,128)} %get-tuple-element.22.coef_ref, f32[9,320,128]{2,1,0:T(8,128)} %get-tuple-element.23.own_ref, ...), custom_call_target="tpu_custom_call" | custom-call | flops 849346560 | bytes 9732120 | tf_op jit(solution)/shard_map/cond/branch_1_fun/pallas_call | solution.py:561
  33.3 0.1 collective-permute-start
  33.4 1.6 %collective-permute-start.2 = (f32[6,128,128]{2,1,0:T(8,128)S(1)}, f32[6,128,128]{2,1,0:T(8,128)S(1)}, u32[]{:S(2)}, u32[]{:S(2)}) collective-permute-start(f32[6,128,128]{2,1,0:T(8,128)S(1)} %get-tuple-element.30.refs_0_), channel_id=1, source_target_pairs={{0,16},{4,12},{8,24},{12,4},{16,0},{20,28},{24,8},{28,20},{1,17},{... | collective-permute-start | bytes 1179656 | tf_op jit(solution)/shard_map/cond/branch_1_fun/ppermute | solution.py:711
  34.9 0.5 collective-permute-start.4
  35.5 1.4 %collective-permute-start.1 = (f32[4,8,1152]{2,1,0:T(8,128)S(1)}, f32[4,8,1152]{2,1,0:T(8,128)S(1)}, u32[]{:S(2)}, u32[]{:S(2)}) collective-permute-start(f32[4,8,1152]{2,1,0:T(8,128)S(1)} %add.24), channel_id=1, source_target_pairs={{0,8},{4,20},{8,0},{12,28},{16,24},{20,4},{24,16},{28,12},{1,9},{5... | collective-permute-start | bytes 442376 | tf_op jit(solution)/shard_map/cond/branch_1_fun/ppermute | solution.py:722
  36.9 0.2 slice_reduce_fusion.3
  37.1 5.2 %collective-permute-done.1 = f32[4,8,1152]{2,1,0:T(8,128)S(1)} collective-permute-done((f32[4,8,1152]{2,1,0:T(8,128)S(1)}, f32[4,8,1152]{2,1,0:T(8,128)S(1)}, u32[]{:S(2)}, u32[]{:S(2)}) %collective-permute-start.1) | collective-permute-done | bytes 147488 | tf_op jit(solution)/shard_map/cond/branch_1_fun/ppermute | solution.py:722
  42.3 0.2 slice_reduce_fusion
  42.5 0.2 collective-permute-done.2.refs_2_
  42.8 4.2 %collective-permute-done.4.refs_3_ = f32[6,128,128]{2,1,0:T(8,128)S(1)} collective-permute-done((f32[6,128,128]{2,1,0:T(8,128)S(1)}, f32[6,128,128]{2,1,0:T(8,128)S(1)}, u32[]{:S(2)}, u32[]{:S(2)}) %collective-permute-start.4) | collective-permute-done | bytes 393248 | tf_op jit(solution)/shard_map/cond/branch_1_fun/ppermute | solution.py:711
  47.0 1.5 %collective-permute-start.5 = (f32[4,8,1152]{2,1,0:T(8,128)S(1)}, f32[4,8,1152]{2,1,0:T(8,128)S(1)}, u32[]{:S(2)}, u32[]{:S(2)}) collective-permute-start(f32[4,8,1152]{2,1,0:T(8,128)S(1)} %add.25), channel_id=1, source_target_pairs={{0,16},{4,12},{8,24},{12,4},{16,0},{20,28},{24,8},{28,20},{1,17},{... | collective-permute-start | bytes 442376 | tf_op jit(solution)/shard_map/cond/branch_1_fun/ppermute | solution.py:722
  48.5 0.2 slice_reduce_fusion.1
  48.7 0.1 maximum_convert_fusion.mark_ref
  48.8 2.2 %branch_1_fun.5 = (f32[2,64,1152]{2,1,0:T(8,128)}, f32[64,1152]{1,0:T(8,128)}) custom-call(s32[24]{0:T(128)S(1)} %maximum_convert_fusion.mark_ref, f32[6,128,128]{2,1,0:T(8,128)S(1)} %get-tuple-element.30.refs_0_, f32[6,128,128]{2,1,0:T(8,128)S(1)} %collective-permute-done.3.refs_1_, f32[6,128,128]{2,1,0:T(8,128)S(1)} %collective-permute-done.2.refs_2_, ...), custom_call_target="tpu_custom_call" | custom-call | flops 589824 | bytes 1769472 | tf_op jit(solution)/shard_map/cond/branch_1_fun/pallas_call | solution.py:225
  51.0 1.1 %collective-permute-done.5 = f32[4,8,1152]{2,1,0:T(8,128)S(1)} collective-permute-done((f32[4,8,1152]{2,1,0:T(8,128)S(1)}, f32[4,8,1152]{2,1,0:T(8,128)S(1)}, u32[]{:S(2)}, u32[]{:S(2)}) %collective-permute-start.5) | collective-permute-done | bytes 147488 | tf_op jit(solution)/shard_map/cond/branch_1_fun/ppermute | solution.py:722
  52.2 1.2 %branch_1_fun.6 = (f32[4,4,1152]{2,1,0:T(4,128)S(1)}, f32[4,4,1152]{2,1,0:T(4,128)S(1)}) custom-call(s32[6]{0:T(128)S(1)} %get-tuple-element.21.flag_ref, f32[4,8,1152]{2,1,0:T(8,128)S(1)} %add.26.inc_ref, f32[2,2,4,8,1152]{4,3,2,1,0:T(8,128)} %bitcast.weight_ref, f32[2,4,8,1152]{3,2,1,0:T(8,128)} %bitcast.1.pull_ref), custom_call_target="tpu_custom_call" | custom-call | bytes 1179672 | tf_op jit(solution)/shard_map/cond/branch_1_fun/pallas_call | solution.py:561
  53.4 0.1 collective-permute-start.6
  53.5 0.1 collective-permute-start.7
  53.6 5.1 %collective-permute-done.6.first_ref.rim_first_ref = f32[4,4,1152]{2,1,0:T(4,128)} collective-permute-done((f32[4,4,1152]{2,1,0:T(4,128)S(1)}, f32[4,4,1152]{2,1,0:T(4,128)}, u32[]{:S(2)}, u32[]{:S(2)}) %collective-permute-start.6) | collective-permute-done | bytes 73760 | tf_op jit(solution)/shard_map/cond/branch_1_fun/ppermute | solution.py:38
  58.7 1.7 %branch_1_fun.7 = f32[4,8,1152]{2,1,0:T(8,128)S(1)} custom-call(s32[6]{0:T(128)S(1)} %get-tuple-element.21.flag_ref, f32[4,8,1152]{2,1,0:T(8,128)S(1)} %add.26.inc_ref, f32[4,4,1152]{2,1,0:T(4,128)} %collective-permute-done.6.first_ref.rim_first_ref, f32[4,4,1152]{2,1,0:T(4,128)} %collective-permute-done.7.second_ref.rim_second_ref, ...), custom_call_target="tpu_custom_call" | custom-call | flops 2949120 | bytes 1474584 | tf_op jit(solution)/shard_map/cond/branch_1_fun/pallas_call | solution.py:561
  60.5 0.1 collective-permute-start.15
  60.5 0.5 collective-permute-start.14
  61.0 2.0 %collective-permute-start.13 = (f32[4,8,1152]{2,1,0:T(8,128)S(1)}, f32[4,8,1152]{2,1,0:T(8,128)S(1)}, u32[]{:S(2)}, u32[]{:S(2)}) collective-permute-start(f32[4,8,1152]{2,1,0:T(8,128)S(1)} %get-tuple-element.111.mine_ref), channel_id=1, source_target_pairs={{0,1},{1,0},{2,3},{3,2},{4,5},{5,4},{6,7},{7,6},{8,9},{9,8},{10,11... | collective-permute-start | bytes 442376 | tf_op jit(solution)/shard_map/ppermute | solution.py:38
  63.0 4.1 %shard_map.112.refs_6_ = f32[9,320,128]{2,1,0:T(8,128)S(1)} custom-call(s32[6]{0:T(128)S(1)} %stack.47.flag_ref.refs_0_, bf16[1152,1152]{1,0:T(8,128)(2,1)} %refs_3_.1, f32[4,8,1152]{2,1,0:T(8,128)S(1)} %get-tuple-element.111.mine_ref, f32[4,8,1152]{2,1,0:T(8,128)S(1)} %collective-permute-done.15.other_ref, bf16[10,2,4,8,1152]{4,3,2,1,0:T(8,128)(2,1)} %members_ref.3), custom_call_target="tpu_custom_call" | custom-call | flops 849346560 | bytes 5898264 | tf_op jit(solution)/shard_map/pallas_call | solution.py:561
  67.1 0.1 collective-permute-done.13.refs_7_
  67.2 0.0 collective-permute-start.16
  67.2 0.5 collective-permute-start.17
  67.7 0.9 collective-permute-done.16.refs_8_
  68.6 0.2 collective-permute-done.17.refs_10_
  68.8 9.8 %shard_map.113 = (f32[4,8,1152]{2,1,0:T(8,128)S(1)}, f32[4,8,1152]{2,1,0:T(8,128)S(1)}, f32[9,320,128]{2,1,0:T(8,128)S(1)}) custom-call(s32[6]{0:T(128)S(1)} %stack.47.flag_ref.refs_0_, f32[216,8,128]{2,1,0:T(8,128)S(1)} %copy-done.10, f32[9,320,128]{2,1,0:T(8,128)S(1)} %copy-done.11, f32[9,160,128]{2,1,0:T(8,128)} %get-tuple-element.109.refs_3_, ...), custom_call_target="tpu_custom_call" | custom-call | flops 2548039680 | bytes 14745624 | tf_op jit(solution)/shard_map/pallas_call | solution.py:561
  78.7 0.3 collective-permute-start.18
  79.0 1.1 %collective-permute-done.18 = f32[4,8,1152]{2,0,1:T(4,128)S(1)} collective-permute-done((f32[4,8,1152]{2,0,1:T(4,128)S(1)}, f32[4,8,1152]{2,0,1:T(4,128)S(1)}, u32[]{:S(2)}, u32[]{:S(2)}) %collective-permute-start.18) | collective-permute-done | bytes 147488 | tf_op jit(solution)/shard_map/ppermute | solution.py:55
  80.1 0.1 copy_add_fusion
  80.1 1.6 %collective-permute-start.19 = (f32[4,8,1152]{2,0,1:T(4,128)S(1)}, f32[4,8,1152]{2,0,1:T(4,128)S(1)}, u32[]{:S(2)}, u32[]{:S(2)}) collective-permute-start(f32[4,8,1152]{2,0,1:T(4,128)S(1)} %copy_add_fusion), channel_id=1, source_target_pairs={{0,8},{4,20},{8,0},{12,28},{16,24},{20,4},{24,16},{28,12},{1,9},{5... | collective-permute-start | bytes 442376 | tf_op jit(solution)/shard_map/ppermute | solution.py:746
  81.7 3.7 %collective-permute-done.19 = f32[4,8,1152]{2,0,1:T(4,128)S(1)} collective-permute-done((f32[4,8,1152]{2,0,1:T(4,128)S(1)}, f32[4,8,1152]{2,0,1:T(4,128)S(1)}, u32[]{:S(2)}, u32[]{:S(2)}) %collective-permute-start.19) | collective-permute-done | bytes 147488 | tf_op jit(solution)/shard_map/ppermute | solution.py:746
  85.4 1.6 %collective-permute-start.20 = (f32[4,8,1152]{2,0,1:T(4,128)S(1)}, f32[4,8,1152]{2,0,1:T(4,128)S(1)}, u32[]{:S(2)}, u32[]{:S(2)}) collective-permute-start(f32[4,8,1152]{2,0,1:T(4,128)S(1)} %add.39), channel_id=1, source_target_pairs={{0,16},{4,12},{8,24},{12,4},{16,0},{20,28},{24,8},{28,20},{1,17},{... | collective-permute-start | bytes 442376 | tf_op jit(solution)/shard_map/ppermute | solution.py:746
  87.0 3.6 %collective-permute-done.20 = f32[4,8,1152]{2,0,1:T(4,128)S(1)} collective-permute-done((f32[4,8,1152]{2,0,1:T(4,128)S(1)}, f32[4,8,1152]{2,0,1:T(4,128)S(1)}, u32[]{:S(2)}, u32[]{:S(2)}) %collective-permute-start.20) | collective-permute-done | bytes 147488 | tf_op jit(solution)/shard_map/ppermute | solution.py:746
  90.7 0.1 collective-permute-start.22
  90.8 3.1 %collective-permute-start.21 = (f32[1,4,1152]{2,1,0:T(4,128)S(1)}, f32[1,4,1152]{2,1,0:T(4,128)S(1)}, u32[]{:S(2)}, u32[]{:S(2)}) collective-permute-start(f32[1,4,1152]{2,1,0:T(4,128)S(1)} %get-tuple-element.135), channel_id=1, source_target_pairs={{0,1},{1,0},{2,3},{3,2},{4,5},{5,4},{6,7},{7,6},{8,9},{9,8},{10,11... | collective-permute-start | bytes 55304 | tf_op jit(solution)/shard_map/ppermute | solution.py:38
  93.8 1.7 %collective-permute-done.21.first_ref = f32[1,4,1152]{2,1,0:T(4,128)S(1)} collective-permute-done((f32[1,4,1152]{2,1,0:T(4,128)S(1)}, f32[1,4,1152]{2,1,0:T(4,128)S(1)}, u32[]{:S(2)}, u32[]{:S(2)}) %collective-permute-start.21) | collective-permute-done | bytes 18464 | tf_op jit(solution)/shard_map/ppermute | solution.py:38
  95.6 1.7 %shard_map.114 = (f32[4,8,1152]{2,1,0:T(8,128)S(1)}, f32[2,8,1152]{2,1,0:T(8,128)S(1)}, f32[2,8,1152]{2,1,0:T(8,128)S(1)}) custom-call(s32[6]{0:T(128)S(1)} %stack.47.flag_ref.refs_0_, f32[4,8,1152]{2,1,0:T(8,128)S(1)} %copy.19.inc_ref, f32[1,4,1152]{2,1,0:T(4,128)S(1)} %collective-permute-done.21.first_ref, ...), custom_call_target="tpu_custom_call" | custom-call | flops 2949120 | bytes 1511448 | tf_op jit(solution)/shard_map/pallas_call | solution.py:561
  97.2 0.1 collective-permute-start.25
  97.3 2.1 %collective-permute-start.23 = (f32[2,8,1152]{2,1,0:T(8,128)S(1)}, f32[2,8,1152]{2,1,0:T(8,128)S(1)}, u32[]{:S(2)}, u32[]{:S(2)}) collective-permute-start(f32[2,8,1152]{2,1,0:T(8,128)S(1)} %get-tuple-element.124), channel_id=1, source_target_pairs={{0,1},{1,0},{2,3},{3,2},{4,5},{5,4},{6,7},{7,6},{8,9},{9,8},{10,11... | collective-permute-start | bytes 221192 | tf_op jit(solution)/shard_map/ppermute | solution.py:38
  99.4 0.2 collective-permute-start.24
  99.6 3.3 %shard_map.115.refs_4_ = f32[9,320,128]{2,1,0:T(8,128)S(1)} custom-call(s32[6]{0:T(128)S(1)} %stack.47.flag_ref.refs_0_, bf16[1152,1152]{1,0:T(8,128)(2,1)S(1)} %copy-done.9, f32[4,8,1152]{2,1,0:T(8,128)S(1)} %get-tuple-element.126.mine_ref, f32[4,8,1152]{2,1,0:T(8,128)S(1)} %collective-permute-done.25.other_ref, bf16[10,2,4,8,1152]{4,3,2,1,0:T(8,128)(2,1)} %members_ref.3), custom_call_target="tpu_custom_call" | custom-call | flops 849346560 | bytes 5898264 | tf_op jit(solution)/shard_map/pallas_call | solution.py:561
  102.9 0.4 collective-permute-start.26
  103.3 0.2 collective-permute-start.27
  103.5 0.8 collective-permute-done.26.refs_6_
  104.2 0.4 collective-permute-done.27.refs_8_
  104.6 5.1 %shard_map.116 = f32[320,1152]{1,0:T(8,128)} custom-call(s32[6]{0:T(128)S(1)} %stack.47.flag_ref.refs_0_, f32[216,8,128]{2,1,0:T(8,128)S(1)} %copy-done.10, f32[9,320,128]{2,1,0:T(8,128)S(1)} %get-tuple-element.117.refs_2_, bf16[1152,1152]{1,0:T(8,128)(2,1)S(1)} %copy-done.9, f32[9,320,128]{2,1,0:T(8,128)S(1)} %shard_map.115.refs_4_, ...), custom_call_target="tpu_custom_call" | custom-call | flops 849346560 | bytes 11206680 | tf_op jit(solution)/shard_map/pallas_call | solution.py:561
  (50 shorter events, 0.3 us)
Async XLA Ops:
  0.0 4.7 %copy-start.6 = (s32[1,1,3]{2,1,0:T(1,128)S(1)}, s32[1,1,3]{2,1,0:T(1,128)}, u32[]{:S(2)}) copy-start(s32[1,1,3]{2,1,0:T(1,128)} %param.18) | copy-start | bytes 40
  0.0 4.7 %copy-start.5 = (s32[1,1,3]{2,1,0:T(1,128)S(1)}, s32[1,1,3]{2,1,0:T(1,128)}, u32[]{:S(2)}) copy-start(s32[1,1,3]{2,1,0:T(1,128)} %param.17) | copy-start | bytes 40
  0.0 1.4 %copy-start = (f32[10,4,8,1152]{3,2,1,0:T(8,128)S(1)}, f32[10,4,8,1152]{3,2,1,0:T(8,128)}, u32[]{:S(2)}) copy-start(f32[10,4,8,1152]{3,2,1,0:T(8,128)} %param.14) | copy-start | bytes 4423684
  1.4 3.3 %copy-start.2 = (s32[1,1,3,4096]{3,1,2,0:T(1,128)S(1)}, s32[1,1,3,4096]{3,1,2,0:T(1,128)}, u32[]{:S(2)}) copy-start(s32[1,1,3,4096]{3,1,2,0:T(1,128)} %param.19) | copy-start | bytes 147460
  1.4 3.3 %copy-start.3 = (f32[1,1,3,4096]{3,1,2,0:T(1,128)S(1)}, f32[1,1,3,4096]{3,1,2,0:T(1,128)}, u32[]{:S(2)}) copy-start(f32[1,1,3,4096]{3,1,2,0:T(1,128)} %param.20) | copy-start | bytes 147460
  1.4 3.3 %copy-start.4 = (f32[1,1,3,4096]{3,1,2,0:T(1,128)S(1)}, f32[1,1,3,4096]{3,1,2,0:T(1,128)}, u32[]{:S(2)}) copy-start(f32[1,1,3,4096]{3,1,2,0:T(1,128)} %param.21) | copy-start | bytes 147460
  1.4 3.4 %copy-start.7 = (s32[128,1]{1,0:T(8,128)S(1)}, s32[128,1]{1,0:T(8,128)}, u32[]{:S(2)}) copy-start(s32[128,1]{1,0:T(8,128)} %constant.48.clone.lane_ref) | copy-start | bytes 1540
  1.4 3.4 %copy-start.8 = (s32[128,1]{1,0:T(8,128)S(1)}, s32[128,1]{1,0:T(8,128)}, u32[]{:S(2)}) copy-start(s32[128,1]{1,0:T(8,128)} %constant.47.clone.row_ref) | copy-start | bytes 1540
  1.6 19.7 %collective-permute-start.8 = (f32[160,1152]{1,0:T(8,128)S(1)}, f32[160,1152]{1,0:T(8,128)}, u32[]{:S(2)}, u32[]{:S(2)}) collective-permute-start(f32[160,1152]{1,0:T(8,128)S(1)} %get-tuple-element.87), channel_id=1, source_target_pairs={{0,1},{1,0},{2,3},{3,2},{4,5},{5,4},{6,7},{7,6},{8,9},{9,8},{10,11... | collective-permute-start | bytes 2211848 | tf_op jit(solution)/shard_map/ppermute | solution.py:38
  4.7 16.6 %collective-permute-start.9 = (f32[160,1152]{1,0:T(8,128)S(1)}, f32[160,1152]{1,0:T(8,128)}, u32[]{:S(2)}, u32[]{:S(2)}) collective-permute-start(f32[160,1152]{1,0:T(8,128)S(1)} %get-tuple-element.88), channel_id=1, source_target_pairs={{0,4},{1,2},{2,1},{3,7},{4,0},{5,6},{6,5},{7,3},{8,12},{9,10},{10,... | collective-permute-start | bytes 2211848 | tf_op jit(solution)/shard_map/ppermute | solution.py:39
  4.8 3.2 %copy-start.1 = (f32[10,4,8,1152]{3,2,1,0:T(8,128)S(1)}, f32[10,4,8,1152]{3,2,1,0:T(8,128)}, u32[]{:S(2)}) copy-start(f32[10,4,8,1152]{3,2,1,0:T(8,128)} %param.14) | copy-start | bytes 4423684
  7.2 3.9 %collective-permute-start.10 = (f32[1,3,128,128]{3,2,1,0:T(8,128)S(1)}, f32[1,3,128,128]{3,2,1,0:T(8,128)S(1)}, u32[]{:S(2)}, u32[]{:S(2)}) collective-permute-start(f32[1,3,128,128]{3,2,1,0:T(8,128)S(1)} %get-tuple-element.133), channel_id=1, source_target_pairs={{0,4},{4,0},{8,12},{12,8},{16,20},{20,16},{24,28},{28,24},{1,5},{5... | collective-permute-start | bytes 589832 | tf_op jit(solution)/shard_map/ppermute | solution.py:55
  11.1 0.7 copy-start.13
  21.3 39.1 %collective-permute-start.12 = (bf16[10,2,4,8,1152]{4,3,2,1,0:T(8,128)(2,1)}, bf16[10,2,4,8,1152]{4,3,2,1,0:T(8,128)(2,1)S(1)}, u32[]{:S(2)}, u32[]{:S(2)}) collective-permute-start(bf16[10,2,4,8,1152]{4,3,2,1,0:T(8,128)(2,1)} %members_ref.3), channel_id=1, source_target_pairs={{0,4},{1,2},{2,1},{3,7},{4,0},{5,6},{6,5},{7,3},{8,12},{9,10},{10,... | collective-permute-start | bytes 4423688 | tf_op jit(solution)/shard_map/ppermute | solution.py:39
  21.3 39.1 %collective-permute-start.11 = (bf16[10,2,4,8,1152]{4,3,2,1,0:T(8,128)(2,1)}, bf16[10,2,4,8,1152]{4,3,2,1,0:T(8,128)(2,1)S(1)}, u32[]{:S(2)}, u32[]{:S(2)}) collective-permute-start(bf16[10,2,4,8,1152]{4,3,2,1,0:T(8,128)(2,1)} %members_ref.3), channel_id=1, source_target_pairs={{0,1},{1,0},{2,3},{3,2},{4,5},{5,4},{6,7},{7,6},{8,9},{9,8},{10,11... | collective-permute-start | bytes 4423688 | tf_op jit(solution)/shard_map/ppermute | solution.py:38
  26.0 8.9 %collective-permute-start.3 = (f32[6,128,128]{2,1,0:T(8,128)S(1)}, f32[6,128,128]{2,1,0:T(8,128)S(1)}, u32[]{:S(2)}, u32[]{:S(2)}) collective-permute-start(f32[6,128,128]{2,1,0:T(8,128)S(1)} %get-tuple-element.30.refs_0_), channel_id=1, source_target_pairs={{0,8},{4,20},{8,0},{12,28},{16,24},{20,4},{24,16},{28,12},{1,9},{5... | collective-permute-start | bytes 1179656 | tf_op jit(solution)/shard_map/cond/branch_1_fun/ppermute | solution.py:710
  33.3 2.2 %collective-permute-start = (f32[4,8,1152]{2,1,0:T(8,128)S(1)}, f32[4,8,1152]{2,1,0:T(8,128)S(1)}, u32[]{:S(2)}, u32[]{:S(2)}) collective-permute-start(f32[4,8,1152]{2,1,0:T(8,128)S(1)} %get-tuple-element.29), channel_id=1, source_target_pairs={{0,4},{4,0},{8,12},{12,8},{16,20},{20,16},{24,28},{28,24},{1,5},{5... | collective-permute-start | bytes 442376 | tf_op jit(solution)/shard_map/cond/branch_1_fun/ppermute | solution.py:55
  33.4 9.4 %collective-permute-start.2 = (f32[6,128,128]{2,1,0:T(8,128)S(1)}, f32[6,128,128]{2,1,0:T(8,128)S(1)}, u32[]{:S(2)}, u32[]{:S(2)}) collective-permute-start(f32[6,128,128]{2,1,0:T(8,128)S(1)} %get-tuple-element.30.refs_0_), channel_id=1, source_target_pairs={{0,16},{4,12},{8,24},{12,4},{16,0},{20,28},{24,8},{28,20},{1,17},{... | collective-permute-start | bytes 1179656 | tf_op jit(solution)/shard_map/cond/branch_1_fun/ppermute | solution.py:711
  34.9 12.0 %collective-permute-start.4 = (f32[6,128,128]{2,1,0:T(8,128)S(1)}, f32[6,128,128]{2,1,0:T(8,128)S(1)}, u32[]{:S(2)}, u32[]{:S(2)}) collective-permute-start(f32[6,128,128]{2,1,0:T(8,128)S(1)} %collective-permute-done.3.refs_1_), channel_id=1, source_target_pairs={{0,16},{4,12},{8,24},{12,4},{16,0},{20,28},{24,8},{28,20},{1,17},{... | collective-permute-start | bytes 1179656 | tf_op jit(solution)/shard_map/cond/branch_1_fun/ppermute | solution.py:711
  35.5 6.8 %collective-permute-start.1 = (f32[4,8,1152]{2,1,0:T(8,128)S(1)}, f32[4,8,1152]{2,1,0:T(8,128)S(1)}, u32[]{:S(2)}, u32[]{:S(2)}) collective-permute-start(f32[4,8,1152]{2,1,0:T(8,128)S(1)} %add.24), channel_id=1, source_target_pairs={{0,8},{4,20},{8,0},{12,28},{16,24},{20,4},{24,16},{28,12},{1,9},{5... | collective-permute-start | bytes 442376 | tf_op jit(solution)/shard_map/cond/branch_1_fun/ppermute | solution.py:722
  47.0 5.1 %collective-permute-start.5 = (f32[4,8,1152]{2,1,0:T(8,128)S(1)}, f32[4,8,1152]{2,1,0:T(8,128)S(1)}, u32[]{:S(2)}, u32[]{:S(2)}) collective-permute-start(f32[4,8,1152]{2,1,0:T(8,128)S(1)} %add.25), channel_id=1, source_target_pairs={{0,16},{4,12},{8,24},{12,4},{16,0},{20,28},{24,8},{28,20},{1,17},{... | collective-permute-start | bytes 442376 | tf_op jit(solution)/shard_map/cond/branch_1_fun/ppermute | solution.py:722
  53.4 5.3 %collective-permute-start.6 = (f32[4,4,1152]{2,1,0:T(4,128)S(1)}, f32[4,4,1152]{2,1,0:T(4,128)}, u32[]{:S(2)}, u32[]{:S(2)}) collective-permute-start(f32[4,4,1152]{2,1,0:T(4,128)S(1)} %get-tuple-element.36), channel_id=1, source_target_pairs={{0,1},{1,0},{2,3},{3,2},{4,5},{5,4},{6,7},{7,6},{8,9},{9,8},{10,11... | collective-permute-start | bytes 221192 | tf_op jit(solution)/shard_map/cond/branch_1_fun/ppermute | solution.py:38
  53.5 5.2 %collective-permute-start.7 = (f32[4,4,1152]{2,1,0:T(4,128)S(1)}, f32[4,4,1152]{2,1,0:T(4,128)}, u32[]{:S(2)}, u32[]{:S(2)}) collective-permute-start(f32[4,4,1152]{2,1,0:T(4,128)S(1)} %get-tuple-element.37), channel_id=1, source_target_pairs={{0,4},{1,2},{2,1},{3,7},{4,0},{5,6},{6,5},{7,3},{8,12},{9,10},{10,... | collective-permute-start | bytes 221192 | tf_op jit(solution)/shard_map/cond/branch_1_fun/ppermute | solution.py:39
  60.4 8.3 %copy-start.10 = (f32[216,8,128]{2,1,0:T(8,128)S(1)}, f32[216,8,128]{2,1,0:T(8,128)}, u32[]{:S(2)}) copy-start(f32[216,8,128]{2,1,0:T(8,128)} %get-tuple-element.107.refs_1_) | copy-start | bytes 2654212
  60.4 8.3 %copy-start.11 = (f32[9,320,128]{2,1,0:T(8,128)S(1)}, f32[9,320,128]{2,1,0:T(8,128)}, u32[]{:S(2)}) copy-start(f32[9,320,128]{2,1,0:T(8,128)} %get-tuple-element.108.refs_2_) | copy-start | bytes 4423684
  60.5 8.3 %copy-start.12 = (f32[9,160,128]{2,1,0:T(8,128)S(1)}, f32[9,160,128]{2,1,0:T(8,128)}, u32[]{:S(2)}) copy-start(f32[9,160,128]{2,1,0:T(8,128)} %get-tuple-element.110.refs_4_) | copy-start | bytes 2211844
  60.5 2.5 %collective-permute-start.15 = (f32[4,8,1152]{2,1,0:T(8,128)S(1)}, f32[4,8,1152]{2,1,0:T(8,128)S(1)}, u32[]{:S(2)}, u32[]{:S(2)}) collective-permute-start(f32[4,8,1152]{2,1,0:T(8,128)S(1)} %get-tuple-element.111.mine_ref), channel_id=1, source_target_pairs={{0,4},{4,0},{8,12},{12,8},{16,20},{20,16},{24,28},{28,24},{1,5},{5... | collective-permute-start | bytes 442376 | tf_op jit(solution)/shard_map/ppermute | solution.py:55
  60.5 6.6 %collective-permute-start.14 = (f32[4,8,1152]{2,1,0:T(8,128)S(1)}, f32[4,8,1152]{2,1,0:T(8,128)S(1)}, u32[]{:S(2)}, u32[]{:S(2)}) collective-permute-start(f32[4,8,1152]{2,1,0:T(8,128)S(1)} %get-tuple-element.111.mine_ref), channel_id=1, source_target_pairs={{0,4},{1,2},{2,1},{3,7},{4,0},{5,6},{6,5},{7,3},{8,12},{9,10},{10,... | collective-permute-start | bytes 442376 | tf_op jit(solution)/shard_map/ppermute | solution.py:39
  61.0 6.1 %collective-permute-start.13 = (f32[4,8,1152]{2,1,0:T(8,128)S(1)}, f32[4,8,1152]{2,1,0:T(8,128)S(1)}, u32[]{:S(2)}, u32[]{:S(2)}) collective-permute-start(f32[4,8,1152]{2,1,0:T(8,128)S(1)} %get-tuple-element.111.mine_ref), channel_id=1, source_target_pairs={{0,1},{1,0},{2,3},{3,2},{4,5},{5,4},{6,7},{7,6},{8,9},{9,8},{10,11... | collective-permute-start | bytes 442376 | tf_op jit(solution)/shard_map/ppermute | solution.py:38
  63.0 5.8 %copy-start.9 = (bf16[1152,1152]{1,0:T(8,128)(2,1)S(1)}, bf16[1152,1152]{1,0:T(8,128)(2,1)}, u32[]{:S(2)}) copy-start(bf16[1152,1152]{1,0:T(8,128)(2,1)} %refs_3_.1) | copy-start | bytes 7962628
  67.2 1.4 %collective-permute-start.16 = (f32[4,8,1152]{2,1,0:T(8,128)S(1)}, f32[4,8,1152]{2,1,0:T(8,128)S(1)}, u32[]{:S(2)}, u32[]{:S(2)}) collective-permute-start(f32[4,8,1152]{2,1,0:T(8,128)S(1)} %collective-permute-done.13.refs_7_), channel_id=1, source_target_pairs={{0,4},{4,0},{8,12},{12,8},{16,20},{20,16},{24,28},{28,24},{1,5},{5... | collective-permute-start | bytes 442376 | tf_op jit(solution)/shard_map/ppermute | solution.py:55
  67.2 1.6 %collective-permute-start.17 = (f32[4,8,1152]{2,1,0:T(8,128)S(1)}, f32[4,8,1152]{2,1,0:T(8,128)S(1)}, u32[]{:S(2)}, u32[]{:S(2)}) collective-permute-start(f32[4,8,1152]{2,1,0:T(8,128)S(1)} %collective-permute-done.14.refs_9_), channel_id=1, source_target_pairs={{0,4},{4,0},{8,12},{12,8},{16,20},{20,16},{24,28},{28,24},{1,5},{5... | collective-permute-start | bytes 442376 | tf_op jit(solution)/shard_map/ppermute | solution.py:55
  78.7 1.4 %collective-permute-start.18 = (f32[4,8,1152]{2,0,1:T(4,128)S(1)}, f32[4,8,1152]{2,0,1:T(4,128)S(1)}, u32[]{:S(2)}, u32[]{:S(2)}) collective-permute-start(f32[4,8,1152]{2,0,1:T(4,128)S(1)} %copy.17), channel_id=1, source_target_pairs={{0,4},{4,0},{8,12},{12,8},{16,20},{20,16},{24,28},{28,24},{1,5},{5... | collective-permute-start | bytes 442376 | tf_op jit(solution)/shard_map/ppermute | solution.py:55
  80.1 5.2 %collective-permute-start.19 = (f32[4,8,1152]{2,0,1:T(4,128)S(1)}, f32[4,8,1152]{2,0,1:T(4,128)S(1)}, u32[]{:S(2)}, u32[]{:S(2)}) collective-permute-start(f32[4,8,1152]{2,0,1:T(4,128)S(1)} %copy_add_fusion), channel_id=1, source_target_pairs={{0,8},{4,20},{8,0},{12,28},{16,24},{20,4},{24,16},{28,12},{1,9},{5... | collective-permute-start | bytes 442376 | tf_op jit(solution)/shard_map/ppermute | solution.py:746
  85.4 5.2 %collective-permute-start.20 = (f32[4,8,1152]{2,0,1:T(4,128)S(1)}, f32[4,8,1152]{2,0,1:T(4,128)S(1)}, u32[]{:S(2)}, u32[]{:S(2)}) collective-permute-start(f32[4,8,1152]{2,0,1:T(4,128)S(1)} %add.39), channel_id=1, source_target_pairs={{0,16},{4,12},{8,24},{12,4},{16,0},{20,28},{24,8},{28,20},{1,17},{... | collective-permute-start | bytes 442376 | tf_op jit(solution)/shard_map/ppermute | solution.py:746
  90.7 3.2 %collective-permute-start.22 = (f32[1,4,1152]{2,1,0:T(4,128)S(1)}, f32[1,4,1152]{2,1,0:T(4,128)S(1)}, u32[]{:S(2)}, u32[]{:S(2)}) collective-permute-start(f32[1,4,1152]{2,1,0:T(4,128)S(1)} %get-tuple-element.134), channel_id=1, source_target_pairs={{0,4},{1,2},{2,1},{3,7},{4,0},{5,6},{6,5},{7,3},{8,12},{9,10},{10,... | collective-permute-start | bytes 55304 | tf_op jit(solution)/shard_map/ppermute | solution.py:39
  90.8 4.8 %collective-permute-start.21 = (f32[1,4,1152]{2,1,0:T(4,128)S(1)}, f32[1,4,1152]{2,1,0:T(4,128)S(1)}, u32[]{:S(2)}, u32[]{:S(2)}) collective-permute-start(f32[1,4,1152]{2,1,0:T(4,128)S(1)} %get-tuple-element.135), channel_id=1, source_target_pairs={{0,1},{1,0},{2,3},{3,2},{4,5},{5,4},{6,7},{7,6},{8,9},{9,8},{10,11... | collective-permute-start | bytes 55304 | tf_op jit(solution)/shard_map/ppermute | solution.py:38
  97.2 2.3 %collective-permute-start.25 = (f32[4,8,1152]{2,1,0:T(8,128)S(1)}, f32[4,8,1152]{2,1,0:T(8,128)S(1)}, u32[]{:S(2)}, u32[]{:S(2)}) collective-permute-start(f32[4,8,1152]{2,1,0:T(8,128)S(1)} %get-tuple-element.126.mine_ref), channel_id=1, source_target_pairs={{0,4},{4,0},{8,12},{12,8},{16,20},{20,16},{24,28},{28,24},{1,5},{5... | collective-permute-start | bytes 442376 | tf_op jit(solution)/shard_map/ppermute | solution.py:55
  97.3 5.6 %collective-permute-start.23 = (f32[2,8,1152]{2,1,0:T(8,128)S(1)}, f32[2,8,1152]{2,1,0:T(8,128)S(1)}, u32[]{:S(2)}, u32[]{:S(2)}) collective-permute-start(f32[2,8,1152]{2,1,0:T(8,128)S(1)} %get-tuple-element.124), channel_id=1, source_target_pairs={{0,1},{1,0},{2,3},{3,2},{4,5},{5,4},{6,7},{7,6},{8,9},{9,8},{10,11... | collective-permute-start | bytes 221192 | tf_op jit(solution)/shard_map/ppermute | solution.py:38
  99.4 3.5 %collective-permute-start.24 = (f32[2,8,1152]{2,1,0:T(8,128)S(1)}, f32[2,8,1152]{2,1,0:T(8,128)S(1)}, u32[]{:S(2)}, u32[]{:S(2)}) collective-permute-start(f32[2,8,1152]{2,1,0:T(8,128)S(1)} %get-tuple-element.125), channel_id=1, source_target_pairs={{0,4},{1,2},{2,1},{3,7},{4,0},{5,6},{6,5},{7,3},{8,12},{9,10},{10,... | collective-permute-start | bytes 221192 | tf_op jit(solution)/shard_map/ppermute | solution.py:39
  102.9 1.3 %collective-permute-start.26 = (f32[2,8,1152]{2,1,0:T(8,128)S(1)}, f32[2,8,1152]{2,1,0:T(8,128)S(1)}, u32[]{:S(2)}, u32[]{:S(2)}) collective-permute-start(f32[2,8,1152]{2,1,0:T(8,128)S(1)} %collective-permute-done.23.refs_5_), channel_id=1, source_target_pairs={{0,4},{4,0},{8,12},{12,8},{16,20},{20,16},{24,28},{28,24},{1,5},{5... | collective-permute-start | bytes 221192 | tf_op jit(solution)/shard_map/ppermute | solution.py:55
  103.3 1.3 %collective-permute-start.27 = (f32[2,8,1152]{2,1,0:T(8,128)S(1)}, f32[2,8,1152]{2,1,0:T(8,128)S(1)}, u32[]{:S(2)}, u32[]{:S(2)}) collective-permute-start(f32[2,8,1152]{2,1,0:T(8,128)S(1)} %collective-permute-done.24.refs_7_), channel_id=1, source_target_pairs={{0,4},{4,0},{8,12},{12,8},{16,20},{20,16},{24,28},{28,24},{1,5},{5... | collective-permute-start | bytes 221192 | tf_op jit(solution)/shard_map/ppermute | solution.py:55
